TPU v7x, 32 devices: a whole 2x2x4 slice. The times are simulated.
32 devices in a mesh: queue: 8 (over z, core), tensor: 4 (over y, x).
Axes of the slice: x: 2, y: 2, z: 4, core: 2. Of those that a mesh axis runs over, the one named last changes fastest.
Arguments:
- latents: bfloat16 [8, 768, 3072], P('queue'), may hold values from -6 to 6
- levels: int32 [8], P('queue'), may hold values from 0 to 49
- mod_table: bfloat16 [50, 9216], replicated, may hold values from -3 to 3
- step_size: float32 [50], replicated, may hold values from 0.2 to 1
- qkv_weight: bfloat16 [3, 3072, 3072], P(None, None, 'tensor'), may hold values from -0.109375 to 0.109375
- q_gain: float32 [128], replicated, may hold values from 0.8 to 4, as said below
- k_gain: float32 [128], replicated, may hold values from 0.8 to 4, as said below
- out_weight: bfloat16 [3072, 3072], P('tensor'), may hold values from -0.109375 to 0.109375
- fresh_noise: bfloat16 [2, 768, 3072], P(None, 'tensor'), may hold values from -6 to 6
Outputs:
- queue_out: bfloat16 [8, 768, 3072], P('queue')
Inputs may be any that keep to these rules, and one draw needn't show every extreme that they name: `q_gain`: positive gains. `k_gain`: positive gains.
All inputs are finite; a program needn't handle non-finite values.
Results may differ from a plain program's by a relative error of at most 0.03.
Values may be sent and summed in bfloat16 or wider, within the bound.
No kernel may reach another device: no remote copies, remote signals or barrier semaphores. Data moves between devices by JAX's collectives and lax.ppermute only.
A program may use at most 128 MiB of HBM per device.

v0:
```python
import jax
import jax.numpy as jnp
from jax import lax
from jax.sharding import PartitionSpec as P

HD = 128
STEPS = 2


def shifted(block, axis, distance):
    devices = range(lax.axis_size(axis))
    route = [(i - distance, i) for i in devices if i - distance in devices]
    return lax.ppermute(block, axis, route)


def normalize(values, epsilon):
    return values * lax.rsqrt(jnp.mean(values * values, axis=-1, keepdims=True) + epsilon)


def body(
    latents, levels, mod_table, step_size, qkv_weight, q_gain, k_gain, out_weight, fresh_noise
):
    frame_rows = latents.shape[1]
    model_width = latents.shape[2]
    head_cols = qkv_weight.shape[2]
    heads_here = head_cols // HD
    first_owner = lax.axis_index("queue") == 0
    onehot = (jnp.arange(mod_table.shape[0], dtype=jnp.int32) == levels[0]).astype(jnp.bfloat16)
    modulation = jnp.dot(onehot[None, :], mod_table, preferred_element_type=jnp.float32)[0]
    rate = jnp.sum(onehot.astype(jnp.float32) * step_size)
    shift_vec = modulation[:model_width]
    scale_vec = modulation[model_width : 2 * model_width]
    gate_vec = modulation[2 * model_width :]
    key_valid = jnp.logical_or(
        jnp.arange(2 * frame_rows) >= frame_rows, jnp.logical_not(first_owner)
    )
    noise_full = lax.all_gather(fresh_noise, "tensor", axis=1, tiled=True)
    frame = latents[0]
    for step_index in range(STEPS):
        arrived = shifted(frame, "queue", 1)
        frame = jnp.where(first_owner, noise_full[step_index], arrived)
        state = frame.astype(jnp.float32)
        normed = (normalize(state, 1e-06) * (1.0 + scale_vec) + shift_vec).astype(jnp.bfloat16)
        query = jnp.dot(normed, qkv_weight[0], preferred_element_type=jnp.float32).reshape(
            frame_rows, heads_here, HD
        )
        keys = jnp.dot(normed, qkv_weight[1], preferred_element_type=jnp.float32).reshape(
            frame_rows, heads_here, HD
        )
        values = jnp.dot(normed, qkv_weight[2], preferred_element_type=jnp.float32).astype(
            jnp.bfloat16
        )
        query = (normalize(query, 1e-06) * q_gain).astype(jnp.bfloat16)
        keys = (normalize(keys, 1e-06) * k_gain).astype(jnp.bfloat16)
        key_value = jnp.stack([keys.reshape(frame_rows, head_cols), values], axis=0)
        earlier = shifted(key_value, "queue", 1)
        all_keys = jnp.concatenate([earlier[0], key_value[0]], axis=0).reshape(
            2 * frame_rows, heads_here, HD
        )
        all_values = jnp.concatenate([earlier[1], key_value[1]], axis=0).reshape(
            2 * frame_rows, heads_here, HD
        )
        scores = jnp.einsum("qhd,khd->hqk", query, all_keys, preferred_element_type=jnp.float32)
        scores = scores * (1.0 / jnp.sqrt(jnp.float32(HD)))
        scores = jnp.where(key_valid[None, None, :], scores, jnp.float32(-1e30))
        row_top = jnp.max(scores, axis=-1, keepdims=True)
        raised = jnp.exp(scores - row_top)
        weights = (raised / jnp.sum(raised, axis=-1, keepdims=True)).astype(jnp.bfloat16)
        attended = jnp.einsum(
            "hqk,khd->qhd", weights, all_values, preferred_element_type=jnp.float32
        )
        attended = attended.astype(jnp.bfloat16).reshape(frame_rows, head_cols)
        partial_term = jnp.dot(attended, out_weight, preferred_element_type=jnp.float32)
        update = lax.psum(partial_term.astype(jnp.bfloat16), "tensor").astype(jnp.float32)
        frame = (state + rate * gate_vec * update).astype(jnp.bfloat16)
    return frame[None]


def solution(mesh):
    return jax.shard_map(
        body,
        mesh=mesh,
        in_specs=(
            P("queue", None, None),
            P("queue"),
            P(),
            P(),
            P(None, None, "tensor"),
            P(),
            P(),
            P("tensor", None),
            P(None, "tensor", None),
        ),
        out_specs=P("queue", None, None),
        check_vma=False,
    )
```

profile of v0, /device:TPU:0, one launch (start us, length us, event | category | flops | bytes accessed | tf_op | source)
XLA Modules:
  0.0 584.7 jit_solution(3101824913338581023)
XLA Ops:
  7.3 4.5 collective-permute-start
  12.4 8.9 %slice_bitcast_fusion.3 = (bf16[768,3072]{0,1:T(8,128)(2,1)}, bf16[768,3072]{0,1:T(8,128)(2,1)}) fusion(bf16[3,3072,768]{2,1,0:T(8,128)(2,1)} %param.13), kind=kLoop, calls=%fused_computation.56 | loop fusion | bytes 18874368 | tf_op jit(solution)/shard_map/dot_general | solution.py:47
  21.3 6.8 %copy.10 = bf16[768,3072]{1,0:T(8,128)(2,1)} copy(bf16[768,3072]{0,1:T(8,128)(2,1)} %get-tuple-element.9) | data formatting | bytes 9437184 | tf_op jit(solution)/shard_map/dot_general | solution.py:47
  28.1 6.6 %copy.11 = bf16[768,3072]{1,0:T(8,128)(2,1)} copy(bf16[768,3072]{0,1:T(8,128)(2,1)} %get-tuple-element.10) | data formatting | bytes 9437184 | tf_op jit(solution)/shard_map/dot_general | solution.py:44
  36.3 72.0 %all-gather.2.cloned.1.call-done = bf16[2,768,3072]{2,1,0:T(8,128)(2,1)} async-done(((bf16[2,192,3072]{2,1,0:T(8,128)(2,1)}), bf16[2,768,3072]{2,1,0:T(8,128)(2,1)}) %all-gather.2.cloned.1.call-update) | async-done | bytes 9437200 | tf_op jit(solution)/shard_map/all_gather | solution.py:37
  108.3 4.7 fusion.12
  113.1 8.4 %fusion.49 = bf16[768,768]{0,1:T(8,128)(2,1)S(1)} fusion(bf16[3,3072,768]{2,1,0:T(8,128)(2,1)} %param.13, bf16[768,3072]{1,0:T(8,128)(2,1)S(1)} %get-tuple-element.8, f32[3072]{0:T(1024)S(1)} %get-tuple-element.16, f32[3072]{0:T(1024)S(1)} %get-tuple-element.17, f32[768]{0:T(1024)S(1)} %add_rsqrt_fusion.5), kind=kOutput, calls=%fused_computation.77 | convolution fusion | flops 3636264960 | bytes 10644480 | tf_op jit(solution)/shard_map/dot_general | solution.py:50
  121.5 4.1 multiply_reduce_fusion.3
  125.7 4.3 multiply_reduce_fusion.2
  130.0 1.7 multiply_convert_fusion.2
  131.8 1.7 pad_maximum_fusion
  133.4 4.5 collective-permute-start.1
  138.0 3.1 collective-permute-done.1
  141.1 3.2 fusion.107
  144.3 10.1 %fusion.108 = f32[6,768]{1,0:T(8,128)S(1)} fusion(pred[1536]{0:T(1024)(128)(4,1)S(1)} %fusion.63, bf16[768,6,128]{0,2,1:T(8,128)(2,1)} %get-tuple-element.26, bf16[768,6,128]{0,2,1:T(8,128)(2,1)S(1)} %get-tuple-element.27, bf16[768,6,128]{0,2,1:T(8,128)(2,1)} %bitcast.105), kind=kOutput, calls=%fused_computation.120 | convolution fusion | flops 1844971008 | bytes 3558912 | tf_op jit(solution)/shard_map/sub | solution.py:67
  154.4 14.4 %fusion.58 = bf16[6,128,768]{2,1,0:T(8,128)(2,1)} fusion(f32[6,768]{1,0:T(8,128)S(1)} %fusion.108, bf16[768,6,128]{0,2,1:T(8,128)(2,1)S(1)} %bitcast.101, bf16[768,6,128]{0,2,1:T(8,128)(2,1)} %bitcast.104, pred[1536]{0:T(1024)(128)(4,1)S(1)} %fusion.63, bf16[768,6,128]{0,2,1:T(8,128)(2,1)} %get-tuple-element.26, ...), kind=kOutput, calls=%fused_computation.80 | convolution fusion | flops 3669301248 | bytes 7097856 | tf_op jit(solution)/shard_map/hqk,khd->qhd/dot_general | solution.py:69
  168.7 8.8 %convolution_convert_fusion.1 = bf16[768,3072]{1,0:T(8,128)(2,1)} fusion(bf16[768,768]{0,1:T(8,128)(2,1)} %bitcast.113, bf16[768,3072]{1,0:T(8,128)(2,1)} %param.16), kind=kOutput, calls=%fused_computation.37 | convolution fusion | flops 3626237952 | bytes 10616832 | tf_op jit(solution)/shard_map/dot_general | solution.py:73
  177.7 136.9 %all-reduce.3.cloned.1.call-done = bf16[768,3072]{1,0:T(8,128)(2,1)} async-done(((bf16[768,3072]{1,0:T(8,128)(2,1)}), bf16[768,3072]{1,0:T(8,128)(2,1)}) %all-reduce.3.cloned.1.call-update) | async-done | bytes 4718608 | tf_op jit(solution)/shard_map/psum | solution.py:74
  314.5 6.0 %fusion.16 = bf16[768,3072]{1,0:T(8,128)(2,1)S(1)} fusion(bf16[768,3072]{1,0:T(8,128)(2,1)} %copy-done.2, bf16[768,3072]{1,0:T(8,128)(2,1)} %all-reduce.3.cloned.1.call-done, f32[3072]{0:T(1024)S(1)} %get-tuple-element.15), kind=kLoop, calls=%fused_computation.28 | loop fusion | flops 11796480 | bytes 14168064 | tf_op jit(solution)/shard_map/convert_element_type | solution.py:75
  320.5 2.3 collective-permute-start.2
  322.8 7.0 %collective-permute-done.2 = bf16[768,3072]{1,0:T(8,128)(2,1)S(1)} collective-permute-done((bf16[768,3072]{1,0:T(8,128)(2,1)S(1)}, bf16[768,3072]{1,0:T(8,128)(2,1)S(1)}, u32[]{:S(2)}, u32[]{:S(2)}) %collective-permute-start.2) | collective-permute-done | bytes 4718624 | tf_op jit(solution)/shard_map/ppermute | solution.py:13
  329.9 4.6 fusion.17
  334.6 4.1 multiply_reduce_fusion.1
  338.7 6.7 %fusion.52 = bf16[768,768]{0,1:T(8,128)(2,1)S(1)} fusion(bf16[3,3072,768]{2,1,0:T(8,128)(2,1)} %param.13, bf16[768,3072]{1,0:T(8,128)(2,1)S(1)} %get-tuple-element.6, f32[768]{0:T(1024)S(1)} %add_rsqrt_fusion.4, f32[3072]{0:T(1024)S(1)} %get-tuple-element.16, f32[3072]{0:T(1024)S(1)} %get-tuple-element.17), kind=kOutput, calls=%fused_computation.78 | convolution fusion | flops 3636264960 | bytes 10644480 | tf_op jit(solution)/shard_map/dot_general | solution.py:50
  346.1 47.6 %collective-permute-start.3 = (bf16[2,768,768]{1,2,0:T(8,128)(2,1)S(1)}, bf16[2,768,768]{1,2,0:T(8,128)(2,1)S(1)}, u32[]{:S(2)}, u32[]{:S(2)}) collective-permute-start(bf16[2,768,768]{1,2,0:T(8,128)(2,1)S(1)} %pad_maximum_fusion.2), channel_id=1, source_target_pairs={{0,4},{4,8},{8,12},{12,16},{16,20},{20,24},{24,28},{1,5},{5,9},{9,... | collective-permute-start | bytes 7077896 | tf_op jit(solution)/shard_map/ppermute | solution.py:13
  393.7 4.1 multiply_reduce_fusion
  399.2 1.6 fusion.106
  400.8 10.1 %fusion.109 = f32[6,768]{1,0:T(8,128)S(1)} fusion(pred[1536]{0:T(1024)(128)(4,1)S(1)} %fusion.63, bf16[768,6,128]{0,2,1:T(8,128)(2,1)} %multiply_convert_fusion, bf16[768,6,128]{0,2,1:T(8,128)(2,1)S(1)} %multiply_convert_fusion.1, bf16[768,6,128]{0,2,1:T(8,128)(2,1)} %bitcast.108), kind=kOutput, calls=%fused_computation.121 | convolution fusion | flops 1844971008 | bytes 3558912 | tf_op jit(solution)/shard_map/sub | solution.py:67
  410.8 14.2 %fusion.55 = bf16[6,128,768]{2,1,0:T(8,128)(2,1)} fusion(f32[6,768]{1,0:T(8,128)S(1)} %fusion.109, bf16[768,6,128]{0,2,1:T(8,128)(2,1)S(1)} %bitcast.103, bf16[768,6,128]{0,2,1:T(8,128)(2,1)} %bitcast.107, pred[1536]{0:T(1024)(128)(4,1)S(1)} %fusion.63, bf16[768,6,128]{0,2,1:T(8,128)(2,1)} %multiply_convert_fusion, ...), kind=kOutput, calls=%fused_computation.79 | convolution fusion | flops 3669301248 | bytes 7097856 | tf_op jit(solution)/shard_map/hqk,khd->qhd/dot_general | solution.py:69
  425.1 8.8 %convolution_convert_fusion = bf16[768,3072]{1,0:T(8,128)(2,1)} fusion(bf16[768,768]{0,1:T(8,128)(2,1)} %bitcast.112, bf16[768,3072]{1,0:T(8,128)(2,1)} %param.16), kind=kOutput, calls=%fused_computation.36 | convolution fusion | flops 3626237952 | bytes 10616832 | tf_op jit(solution)/shard_map/dot_general | solution.py:73
  433.9 135.9 %all-reduce.5.cloned.1.call-done = bf16[768,3072]{1,0:T(8,128)(2,1)} async-done(((bf16[768,3072]{1,0:T(8,128)(2,1)}), bf16[768,3072]{1,0:T(8,128)(2,1)}) %all-reduce.5.cloned.1.call-update) | async-done | bytes 4718608 | tf_op jit(solution)/shard_map/psum | solution.py:74
  569.8 8.0 %fusion.26 = bf16[1,768,3072]{2,1,0:T(8,128)(2,1)} fusion(bf16[768,3072]{1,0:T(8,128)(2,1)} %all-reduce.5.cloned.1.call-done, bf16[768,3072]{1,0:T(8,128)(2,1)} %copy-done.3, f32[3072]{0:T(1024)S(1)} %get-tuple-element.15), kind=kLoop, calls=%fused_computation.38 | loop fusion | flops 11796480 | bytes 14168064 | tf_op jit(solution)/shard_map/broadcast_in_dim | solution.py:76
  (55 shorter events, 4.6 us)
Async XLA Ops:
  6.5 28.8 %copy-start = (bf16[50,9216]{1,0:T(8,128)(2,1)S(1)}, bf16[50,9216]{1,0:T(8,128)(2,1)}, u32[]{:S(2)}) copy-start(bf16[50,9216]{1,0:T(8,128)(2,1)} %param.11) | copy-start | bytes 2764804
  6.5 101.7 %all-gather.2.cloned.1.call-start = ((), (), s32[]{:S(2)}) async-start(), calls=%async_computation | async-start | bytes 11796480 | tf_op jit(solution)/shard_map/all_gather | solution.py:37
  7.3 307.3 %all-reduce.3.cloned.1.call-start = ((), (), s32[]{:S(2)}) async-start(), calls=%async_computation.1 | async-start | bytes 9437184 | tf_op jit(solution)/shard_map/psum | solution.py:74
  7.3 29.0 %collective-permute-start = (bf16[768,3072]{1,0:T(8,128)(2,1)}, bf16[768,3072]{1,0:T(8,128)(2,1)}, u32[]{:S(2)}, u32[]{:S(2)}) collective-permute-start(bf16[768,3072]{1,0:T(8,128)(2,1)} %bitcast.111), channel_id=1, source_target_pairs={{0,4},{4,8},{8,12},{12,16},{16,20},{20,24},{24,28},{1,5},{5,9},{9,... | collective-permute-start | bytes 14155784 | tf_op jit(solution)/shard_map/ppermute | solution.py:13
  28.1 6.6 %copy-start.6 = (f32[50]{0:T(128)S(1)}, f32[50]{0:T(128)}, u32[]{:S(2)}) copy-start(f32[50]{0:T(128)} %param.12) | copy-start | bytes 604
  108.3 13.2 %slice-start.4 = ((s8[4718592]{0:T(1024)(128)(4,1)}), s8[4194304]{0:T(1024)(128)(4,1)S(1)}, s32[]{:S(2)}) async-start(s8[4718592]{0:T(1024)(128)(4,1)} %bitcast.92), calls=%async_computation.7 | async-start | bytes 8388608
  113.0 12.6 %copy-start.2 = (bf16[768,3072]{1,0:T(8,128)(2,1)}, bf16[768,3072]{1,0:T(8,128)(2,1)S(1)}, u32[]{:S(2)}) copy-start(bf16[768,3072]{1,0:T(8,128)(2,1)S(1)} %get-tuple-element.8) | copy-start | bytes 14155780
  113.0 8.5 %slice-start.5 = ((s8[4718592]{0:T(1024)(128)(4,1)}), s8[524288]{0:T(1024)(128)(4,1)S(1)}, s32[]{:S(2)}) async-start(s8[4718592]{0:T(1024)(128)(4,1)} %bitcast.92), calls=%async_computation.8 | async-start | bytes 1048576
  113.0 12.6 %slice-start = ((s8[4718592]{0:T(1024)(128)(4,1)}), s8[524288]{0:T(1024)(128)(4,1)S(1)}, s32[]{:S(2)}) async-start(s8[4718592]{0:T(1024)(128)(4,1)} %bitcast.86), calls=%async_computation.3 | async-start | bytes 1048576
  121.5 4.1 slice-start.1
  125.7 4.4 copy-start.4
  125.7 4.4 copy-start.5
  133.4 7.6 %collective-permute-start.1 = (bf16[2,768,768]{1,2,0:T(8,128)(2,1)}, bf16[2,768,768]{1,2,0:T(8,128)(2,1)}, u32[]{:S(2)}, u32[]{:S(2)}) collective-permute-start(bf16[2,768,768]{1,2,0:T(8,128)(2,1)} %pad_maximum_fusion), channel_id=1, source_target_pairs={{0,4},{4,8},{8,12},{12,16},{16,20},{20,24},{24,28},{1,5},{5,9},{9,... | collective-permute-start | bytes 7077896 | tf_op jit(solution)/shard_map/ppermute | solution.py:13
  177.6 392.1 %all-reduce.5.cloned.1.call-start = ((), (), s32[]{:S(2)}) async-start(), calls=%async_computation.2 | async-start | bytes 9437184 | tf_op jit(solution)/shard_map/psum | solution.py:74
  314.5 20.0 %slice-start.6 = ((s8[4718592]{0:T(1024)(128)(4,1)}), s8[4194304]{0:T(1024)(128)(4,1)S(1)}, s32[]{:S(2)}) async-start(s8[4718592]{0:T(1024)(128)(4,1)} %bitcast.95), calls=%async_computation.9 | async-start | bytes 8388608
  320.5 14.1 %slice-start.7 = ((s8[4718592]{0:T(1024)(128)(4,1)}), s8[524288]{0:T(1024)(128)(4,1)S(1)}, s32[]{:S(2)}) async-start(s8[4718592]{0:T(1024)(128)(4,1)} %bitcast.95), calls=%async_computation.10 | async-start | bytes 1048576
  320.5 9.4 %collective-permute-start.2 = (bf16[768,3072]{1,0:T(8,128)(2,1)S(1)}, bf16[768,3072]{1,0:T(8,128)(2,1)S(1)}, u32[]{:S(2)}, u32[]{:S(2)}) collective-permute-start(bf16[768,3072]{1,0:T(8,128)(2,1)S(1)} %fusion.16), channel_id=1, source_target_pairs={{0,4},{4,8},{8,12},{12,16},{16,20},{20,24},{24,28},{1,5},{5,9},{9,... | collective-permute-start | bytes 14155784 | tf_op jit(solution)/shard_map/ppermute | solution.py:13
  334.5 59.1 %copy-start.3 = (bf16[768,3072]{1,0:T(8,128)(2,1)}, bf16[768,3072]{1,0:T(8,128)(2,1)S(1)}, u32[]{:S(2)}) copy-start(bf16[768,3072]{1,0:T(8,128)(2,1)S(1)} %get-tuple-element.6) | copy-start | bytes 14155780
  334.5 59.1 %slice-start.2 = ((s8[4718592]{0:T(1024)(128)(4,1)}), s8[4194304]{0:T(1024)(128)(4,1)S(1)}, s32[]{:S(2)}) async-start(s8[4718592]{0:T(1024)(128)(4,1)} %bitcast.89), calls=%async_computation.5 | async-start | bytes 8388608
  334.6 59.1 %slice-start.3 = ((s8[4718592]{0:T(1024)(128)(4,1)}), s8[524288]{0:T(1024)(128)(4,1)S(1)}, s32[]{:S(2)}) async-start(s8[4718592]{0:T(1024)(128)(4,1)} %bitcast.89), calls=%async_computation.6 | async-start | bytes 1048576
  346.1 53.1 %collective-permute-start.3 = (bf16[2,768,768]{1,2,0:T(8,128)(2,1)S(1)}, bf16[2,768,768]{1,2,0:T(8,128)(2,1)S(1)}, u32[]{:S(2)}, u32[]{:S(2)}) collective-permute-start(bf16[2,768,768]{1,2,0:T(8,128)(2,1)S(1)} %pad_maximum_fusion.2), channel_id=1, source_target_pairs={{0,4},{4,8},{8,12},{12,16},{16,20},{20,24},{24,28},{1,5},{5,9},{9,... | collective-permute-start | bytes 7077896 | tf_op jit(solution)/shard_map/ppermute | solution.py:13
  433.9 143.9 %copy-start.1 = (bf16[50,9216]{1,0:T(8,128)(2,1)S(1)}, bf16[50,9216]{1,0:T(8,128)(2,1)}, u32[]{:S(2)}) copy-start(bf16[50,9216]{1,0:T(8,128)(2,1)} %param.11) | copy-start | bytes 2764804
Sparse Core Ops, SparseCore 0:
  9.2 99.0 all-gather.1
  177.7 136.7 all-reduce.2
  434.0 135.7 all-reduce.4
where the time goes:
time: 595 us; the launch traced here: 585 us
  waiting for transfers between devices  356 us (60%)
  matrix products  98.3 us (17%)
  starting transfers between devices  59 us (10%)
  other arithmetic  30.1 us (5%)
  local copies, waits for them, and re-layouts  27.2 us (5%)
  between operations  14.6 us (2%)
    psum x2, waiting for transfers between devices, body(): lax.psum(partial_term.astype(jnp.bfloat16), 'tensor').astype(jnp.float32)  273 us
    all_gather x1, waiting for transfers between devices, body(): noise_full = lax.all_gather(fresh_noise, 'tensor', axis=1, tiled=True)  72 us
    ppermute x4, starting transfers between devices, shifted(): return lax.ppermute(block, axis, route)  58.9 us
    dot_general x2, matrix products, body(): jnp.einsum('hqk,khd->qhd', weights, all_values, preferred_element_type=jn...  28.6 us
    sub x2, matrix products, body(): raised = jnp.exp(scores - row_top)  20.1 us
    dot_general x2, matrix products, body(): jnp.dot(attended, out_weight, preferred_element_type=jnp.float32)  17.6 us
    dot_general x2, local copies, waits for them, and re-layouts, body(): jnp.dot(normed, qkv_weight[1], preferred_element_type=jnp.float32)  15.7 us
    dot_general x2, matrix products, body(): jnp.dot(normed, qkv_weight[2], preferred_element_type=jnp.float32)  15.1 us
  transfers between devices with their start and end apart: 7, of which 5 were waited for; matrix products, arithmetic and copies ran while one was open for 5% of the time, Pallas kernels for 0%

commit v1 on v0

v1 whole, which is shorter than its diff:
```python
import functools
import math

import jax
import jax.numpy as jnp
from jax import lax
from jax.experimental import pallas as pl
from jax.experimental.pallas import tpu as pltpu
from jax.sharding import PartitionSpec as P

HD = 128
STEPS = 2
CHUNKS = 2
EPS = 1e-6
AXES = ("queue", "tensor")
F32 = jnp.float32
BF16 = jnp.bfloat16
SCORE_SCALE = math.log2(math.e) / math.sqrt(HD)


def compiler_params(mib):
    return pltpu.CompilerParams(vmem_limit_bytes=mib * 2**20)


def cost(flops, nbytes, transcendentals=0):
    return pl.CostEstimate(
        flops=int(flops), bytes_accessed=int(nbytes), transcendentals=int(transcendentals)
    )


def head_normalize(values, gain):
    parts = []
    for h in range(values.shape[1] // HD):
        part = values[:, h * HD : (h + 1) * HD]
        mean = jnp.mean(part * part, axis=-1, keepdims=True)
        parts.append(part * lax.rsqrt(mean + EPS) * gain)
    return parts[0] if len(parts) == 1 else jnp.concatenate(parts, axis=1)


def key_value_kernel(z_ref, scale_ref, shift_ref, w_ref, gain_ref, kv_ref, normed_ref, *, blocks):
    step = pl.program_id(0)
    rows = z_ref.shape[0]

    @pl.when(step == 0)
    def _():
        def one(i, carry):
            at = pl.ds(pl.multiple_of(i * 16, 16), 16)
            state = z_ref[at, :].astype(F32)
            mean = jnp.mean(state * state, axis=-1, keepdims=True)
            state = state * lax.rsqrt(mean + EPS) * scale_ref[...] + shift_ref[...]
            normed_ref[at, :] = state.astype(BF16)
            return carry

        lax.fori_loop(0, rows // 16, one, 0)

    product = jnp.dot(normed_ref[...], w_ref[0], preferred_element_type=F32)

    @pl.when(step < blocks)
    def _():
        kv_ref[0] = head_normalize(product, gain_ref[...]).astype(BF16)

    @pl.when(step >= blocks)
    def _():
        kv_ref[0] = product.astype(BF16)


def key_value(z, scale1, shift, qkv_weight, k_gain):
    rows, width = z.shape
    head_cols = qkv_weight.shape[2]
    cols = 256 if head_cols % 256 == 0 else HD
    blocks = head_cols // cols
    return pl.pallas_call(
        functools.partial(key_value_kernel, blocks=blocks),
        grid=(2 * blocks,),
        in_specs=[
            pl.BlockSpec((rows, width), lambda j: (0, 0)),
            pl.BlockSpec((1, width), lambda j: (0, 0)),
            pl.BlockSpec((1, width), lambda j: (0, 0)),
            pl.BlockSpec((1, width, cols), lambda j: (1 + j // blocks, 0, j % blocks)),
            pl.BlockSpec((1, HD), lambda j: (0, 0)),
        ],
        out_specs=[
            pl.BlockSpec((1, rows, cols), lambda j: (j // blocks, 0, j % blocks)),
            pl.BlockSpec((rows, width), lambda j: (0, 0)),
        ],
        out_shape=[
            jax.ShapeDtypeStruct((2, rows, head_cols), BF16),
            jax.ShapeDtypeStruct((rows, width), BF16),
        ],
        compiler_params=compiler_params(48),
        cost_estimate=cost(
            4 * rows * width * head_cols, 4 * (rows * width + width * head_cols + rows * head_cols)
        ),
        name="norm_keys_values",
    )(z, scale1, shift, qkv_weight, k_gain)


def attend_parts(query, kv_refs, at):
    scores = [
        lax.dot_general(
            query, ref[0, :, at], (((1,), (1,)), ((), ())), preferred_element_type=F32
        )
        for ref in kv_refs
    ]
    tops = [jnp.max(s, axis=-1, keepdims=True) for s in scores]
    return scores, functools.reduce(jnp.maximum, tops)


def weigh_parts(scores, top, kv_refs, at):
    total = None
    for s, ref in zip(scores, kv_refs):
        weights = jnp.exp2(s - top).astype(BF16)
        values = ref[1, :, at]
        extended = jnp.concatenate([values, jnp.ones_like(values)], axis=1)
        term = jnp.dot(weights, extended, preferred_element_type=F32)
        total = term if total is None else total + term
    return total[:, :HD], total[:, HD:]


def own_kernel(*refs, chunks):
    normed_ref, w_ref, gain_ref = refs[:3]
    kv_refs = refs[3 : 3 + chunks]
    query_ref, acc_ref, top_ref, total_ref = refs[3 + chunks :]
    product = jnp.dot(normed_ref[...], w_ref[0], preferred_element_type=F32)
    query = head_normalize(product, gain_ref[...]).astype(BF16)
    query_ref[...] = query
    for h in range(query.shape[1] // HD):
        at = slice(h * HD, (h + 1) * HD)
        scores, top = attend_parts(query[:, at], kv_refs, at)
        acc, total = weigh_parts(scores, top, kv_refs, at)
        acc_ref[:, at] = acc
        total_ref[:, at] = total
        top_ref[:, at] = jnp.broadcast_to(top, acc.shape)


def own_attention(normed, qkv_weight, q_gain, kvs):
    rows, width = normed.shape
    head_cols = qkv_weight.shape[2]
    cols = 256 if head_cols % 256 == 0 else HD
    chunks = len(kvs)
    key_rows = kvs[0].shape[1]
    keys = chunks * key_rows
    by_heads = pl.BlockSpec((rows, cols), lambda j: (0, j))
    return pl.pallas_call(
        functools.partial(own_kernel, chunks=chunks),
        grid=(head_cols // cols,),
        in_specs=[
            pl.BlockSpec((rows, width), lambda j: (0, 0)),
            pl.BlockSpec((1, width, cols), lambda j: (0, 0, j)),
            pl.BlockSpec((1, HD), lambda j: (0, 0)),
        ]
        + [pl.BlockSpec((2, key_rows, cols), lambda j: (0, 0, j))] * chunks,
        out_specs=[by_heads] * 4,
        out_shape=[jax.ShapeDtypeStruct((rows, head_cols), BF16)]
        + [jax.ShapeDtypeStruct((rows, head_cols), F32)] * 3,
        compiler_params=compiler_params(48),
        cost_estimate=cost(
            2 * rows * width * head_cols + 8 * rows * keys * head_cols,
            2 * (rows * width + width * head_cols) + 14 * rows * head_cols + 4 * keys * head_cols,
            rows * keys * head_cols // HD,
        ),
        name="queries_own_frame",
    )(normed, qkv_weight, q_gain, *kvs)


def earlier_kernel(*refs, chunks):
    has_earlier_ref, query_ref, acc_ref, top_ref, total_ref = refs[:5]
    kv_refs = refs[5 : 5 + chunks]
    out_ref = refs[5 + chunks]
    heads = query_ref.shape[1] // HD

    @pl.when(has_earlier_ref[0] == 0)
    def _():
        out_ref[...] = (acc_ref[...] / total_ref[...]).astype(BF16)

    @pl.when(has_earlier_ref[0] != 0)
    def _():
        for h in range(heads):
            at = slice(h * HD, (h + 1) * HD)
            old_top = top_ref[:, at][:, :1]
            scores, top = attend_parts(query_ref[:, at], kv_refs, at)
            top = jnp.maximum(top, old_top)
            acc, total = weigh_parts(scores, top, kv_refs, at)
            kept = jnp.exp2(old_top - top)
            acc = acc + acc_ref[:, at] * kept
            total = total + total_ref[:, at] * kept
            out_ref[:, at] = (acc / total).astype(BF16)


def earlier_attention(has_earlier, query, acc, top, total, kvs):
    rows, head_cols = query.shape
    cols = 256 if head_cols % 256 == 0 else HD
    chunks = len(kvs)
    key_rows = kvs[0].shape[1]
    keys = chunks * key_rows
    by_heads = pl.BlockSpec((rows, cols), lambda j, flag: (0, j))
    return pl.pallas_call(
        functools.partial(earlier_kernel, chunks=chunks),
        grid_spec=pltpu.PrefetchScalarGridSpec(
            num_scalar_prefetch=1,
            grid=(head_cols // cols,),
            in_specs=[by_heads] * 4
            + [pl.BlockSpec((2, key_rows, cols), lambda j, flag: (0, 0, j))] * chunks,
            out_specs=by_heads,
        ),
        out_shape=jax.ShapeDtypeStruct((rows, head_cols), BF16),
        compiler_params=compiler_params(48),
        cost_estimate=cost(
            8 * rows * keys * head_cols,
            16 * rows * head_cols + 4 * keys * head_cols,
            rows * keys * head_cols // HD,
        ),
        name="earlier_frame",
    )(has_earlier, query, acc, top, total, *kvs)


def output_kernel(*refs, piece_counts, half_blocks):
    parity_ref, resid_ref, gate_ref = refs[:3]
    del parity_ref
    step = pl.program_id(0)
    at = 3
    pieces = []
    for count in piece_counts:
        pieces.append(refs[at : at + count])
        at += count
    others = len(piece_counts) - 1
    own_w = refs[at]
    mine = refs[at + 1 : at + 1 + others]
    sibling = refs[at + 1 + others : at + 1 + 2 * others]
    out_ref, held_ref = refs[at + 1 + 2 * others :]

    @pl.when(step == 0)
    def _():
        for k, parts in enumerate(pieces):
            row = 0
            for part in parts:
                held_ref[k, row : row + part.shape[0], :] = part[...]
                row += part.shape[0]

    def run(weights):
        update = jnp.dot(held_ref[0], own_w[...], preferred_element_type=F32)
        for k, w_ref in enumerate(weights):
            update += jnp.dot(held_ref[k + 1], w_ref[...], preferred_element_type=F32)
        out_ref[...] = (resid_ref[...].astype(F32) + gate_ref[...] * update).astype(BF16)

    @pl.when(step < half_blocks)
    def _():
        run(mine)

    @pl.when(step >= half_blocks)
    def _():
        run(sibling)


def output_projection(parity, resid, resid_chunk, gate, pieces, own_w, mine, sibling):
    head_cols, width = own_w.shape
    rows = pieces[0][0].shape[0]
    cols = 512 if (width // 2) % 512 == 0 else HD
    half_blocks = width // 2 // cols

    def column(j, parity):
        return (j // half_blocks) ^ parity[0], j % half_blocks

    def absolute(j, parity):
        half, block = column(j, parity)
        return half * half_blocks + block

    flat = [part for parts in pieces for part in parts]
    return pl.pallas_call(
        functools.partial(
            output_kernel,
            piece_counts=tuple(len(parts) for parts in pieces),
            half_blocks=half_blocks,
        ),
        grid_spec=pltpu.PrefetchScalarGridSpec(
            num_scalar_prefetch=1,
            grid=(2 * half_blocks,),
            in_specs=[
                pl.BlockSpec((rows, cols), lambda j, p: (resid_chunk, absolute(j, p))),
                pl.BlockSpec((1, cols), lambda j, p: (0, absolute(j, p))),
            ]
            + [pl.BlockSpec(part.shape, lambda j, p: (0, 0)) for part in flat]
            + [pl.BlockSpec((head_cols, cols), lambda j, p: (0, absolute(j, p)))]
            + [
                pl.BlockSpec((head_cols, cols), lambda j, p: (0, jnp.minimum(j, half_blocks - 1)))
                for _ in mine
            ]
            + [
                pl.BlockSpec((head_cols, cols), lambda j, p: (0, jnp.maximum(j - half_blocks, 0)))
                for _ in sibling
            ],
            out_specs=pl.BlockSpec((rows, cols), lambda j, p: (0, absolute(j, p))),
            scratch_shapes=[pltpu.VMEM((len(pieces), rows, head_cols), BF16)],
        ),
        out_shape=jax.ShapeDtypeStruct((rows, width), BF16),
        compiler_params=compiler_params(52),
        cost_estimate=cost(
            2 * rows * width * head_cols * len(pieces),
            2 * (2 * rows * width + head_cols * width * len(pieces)),
        ),
        name="output_projection",
    )(parity, resid, gate, *flat, own_w, *mine, *sibling)


def send(block, move, queue_size, tensor_size, frames=None):
    pairs = []
    for q in range(queue_size) if frames is None else frames:
        for t in range(tensor_size):
            to_q, to_t = move(q, t)
            pairs.append((q * tensor_size + t, to_q * tensor_size + to_t))
    return lax.ppermute(block, AXES, pairs)


def gather_pieces(block, queue_size, tensor_size, frames=None):
    half = tensor_size // 2

    def low(q, t):
        return q, t ^ 1

    def high(j):
        return lambda q, t: (q, (t // 2 - j) % half * 2 + t % 2)

    args = (queue_size, tensor_size, frames)
    rows = block.shape[0] // 2
    near = send(block, low, *args)
    far = [send(block, high(j), *args) for j in range(1, half)]
    pieces = [[block], [near]]
    for j in range(1, half):
        top = send(near[:rows], high(j), *args)
        bottom = send(far[j - 1][rows:], low, *args)
        pieces += [[far[j - 1]], [top, bottom]]
    return pieces


def gather_noise(noise, queue_size, tensor_size):
    index = lax.axis_index("tensor")
    last = [queue_size - 1]
    rows = noise.shape[0]
    frame = jnp.zeros((tensor_size,) + noise.shape, noise.dtype)
    frame = lax.dynamic_update_slice(frame, noise[None], (index, 0, 0))
    for d in range(1, tensor_size):
        came = send(
            noise, lambda q, t: (q, (t - d) % tensor_size), queue_size, tensor_size, last
        )
        frame = lax.dynamic_update_slice(
            frame, came[None], ((index + d) % tensor_size, 0, 0)
        )
    return frame.reshape(tensor_size * rows, noise.shape[1])


def body(
    latents, levels, mod_table, step_size, qkv_weight, q_gain, k_gain, out_weight, fresh_noise
):
    queue_size = lax.axis_size("queue")
    tensor_size = lax.axis_size("tensor")
    rows, width = latents.shape[1:]
    mesh_sizes = (queue_size, tensor_size)
    queue_index = lax.axis_index("queue")
    is_last = queue_index == queue_size - 1
    parity = (queue_index % 2).astype(jnp.int32)

    def ring(block):
        return send(block, lambda q, t: ((q + 1) % queue_size, t), *mesh_sizes)

    def sibling(block):
        return send(block, lambda q, t: (q ^ 1, t), *mesh_sizes)

    worked_level = send(levels, lambda q, t: ((q - 1) % queue_size, t), *mesh_sizes)[0]
    held_level = levels[0]

    def modulation(level):
        row = lax.dynamic_slice(mod_table, (level, 0), (1, 3 * width)).astype(F32)
        return row[:, :width], row[:, width : 2 * width], row[:, 2 * width :]

    shift, scale, _ = modulation(worked_level)
    _, _, gate = modulation(held_level)
    gate = gate * lax.dynamic_slice(step_size, (held_level,), (1,))[:, None]
    scale1 = 1.0 + scale
    has_earlier = jnp.where(is_last, 0, 1).astype(jnp.int32)[None]

    noise = [gather_noise(fresh_noise[s], *mesh_sizes) for s in range(STEPS)]

    half_weight = lax.dynamic_slice(
        out_weight, (0, parity * (width // 2)), (out_weight.shape[0], width // 2)
    )
    gathered = gather_pieces(half_weight, *mesh_sizes)[1:]
    mine = [jnp.concatenate(parts, axis=0) if len(parts) > 1 else parts[0] for parts in gathered]
    theirs = [sibling(block) for block in mine]

    q_gain = (q_gain * SCORE_SCALE)[None]
    k_gain = k_gain[None]
    chunk_rows = rows // CHUNKS
    frame = jnp.where(is_last, noise[0], latents[0])
    frames = [frame[c * chunk_rows : (c + 1) * chunk_rows] for c in range(CHUNKS)]
    for step_index in range(STEPS):
        final = step_index == STEPS - 1
        made = [key_value(part, scale1, shift, qkv_weight, k_gain) for part in frames]
        kvs = [kv for kv, _ in made]
        earlier = [ring(kv) for kv in kvs]
        own = [own_attention(normed, qkv_weight, q_gain, kvs) for _, normed in made]
        attended = [earlier_attention(has_earlier, *parts, earlier) for parts in own]
        resid = [ring(part) for part in frames]
        targets = range(queue_size) if final else range(queue_size - 1)
        pieces = [gather_pieces(ring(block), *mesh_sizes, targets) for block in attended]
        step_gate = gate
        if not final:
            step_gate = jnp.where(is_last, 0.0, gate)
            resid = [
                jnp.where(
                    is_last,
                    noise[step_index + 1][c * chunk_rows : (c + 1) * chunk_rows],
                    part,
                )
                for c, part in enumerate(resid)
            ]
        frames = [
            output_projection(
                parity[None], part, 0, step_gate, block, out_weight, mine, theirs
            )
            for part, block in zip(resid, pieces)
        ]
    return jnp.concatenate(frames, axis=0)[None]


def solution(mesh):
    return jax.shard_map(
        body,
        mesh=mesh,
        in_specs=(
            P("queue", None, None),
            P("queue"),
            P(),
            P(),
            P(None, None, "tensor"),
            P(),
            P(),
            P("tensor", None),
            P(None, "tensor", None),
        ),
        out_specs=P("queue", None, None),
        check_vma=False,
    )
```

time: 595 us -> 475 us (0.80); the launches traced: 585 us -> 473 us
  waiting for transfers between devices: 356 us -> 173 us
  Pallas kernels: 0 us -> 179 us
  matrix products: 98.3 us -> 0 us
  local copies, waits for them, and re-layouts: 27.2 us -> 47 us
  other arithmetic: 30.1 us -> 16.6 us
  between operations: 14.6 us -> 3 us
    psum x2 -> x0, waiting for transfers between devices: 273 us -> none  [body(): lax.psum(partial_term.astype(jnp.bfloat16), 'tensor').astype(jnp.float32)]
    pallas_call x0 -> x16, Pallas kernels: none -> 179 us  [the longest x4 58.3 us: output_projection(): pl.pallas_call(functools.partial(output_kernel, piece_counts=tuple((len(p...]
    ppermute x4 -> x42, waiting for transfers between devices: 10.1 us -> 173 us  [send(): return lax.ppermute(block, AXES, pairs)]
    dot_general x11 -> x0, matrix products: 78.2 us -> none  [the longest x2 28.6 us: body(): jnp.einsum('hqk,khd->qhd', weights, all_values, preferred_element_type=jn...]
    all_gather x1 -> x0, waiting for transfers between devices: 72 us -> none  [body(): noise_full = lax.all_gather(fresh_noise, 'tensor', axis=1, tiled=True)]
    dot_general x3 -> x0, local copies, waits for them, and re-layouts: 22.3 us -> none  [the longest x2 15.7 us: body(): jnp.dot(normed, qkv_weight[1], preferred_element_type=jnp.float32)]
    sub x2 -> x0, matrix products: 20.1 us -> none  [body(): raised = jnp.exp(scores - row_top)]
    unnamed x30 -> x63, local copies, waits for them, and re-layouts: 0.08 us -> 14 us
  transfers between devices with their start and end apart: 7 -> 42, of which waited for: 5 -> 19; matrix products, arithmetic and copies ran while one was open for 5% -> 9% of each run, Pallas kernels for 0% -> 29%
where the time goes in v1:
time: 475 us; the launch traced here: 473 us
  Pallas kernels  179 us (38%)
  waiting for transfers between devices  173 us (36%)
  starting transfers between devices  54.4 us (11%)
  local copies, waits for them, and re-layouts  47 us (10%)
  other arithmetic  16.6 us (3%)
    ppermute x42, waiting for transfers between devices, send(): return lax.ppermute(block, AXES, pairs)  173 us
    pallas_call x4, Pallas kernels, output_projection(): pl.pallas_call(functools.partial(output_kernel, piece_counts=tuple((len(p...  58.3 us
    ppermute x42, starting transfers between devices, send(): return lax.ppermute(block, AXES, pairs)  54.4 us
    pallas_call x4, Pallas kernels, own_attention(): pl.pallas_call(functools.partial(own_kernel, chunks=chunks), grid=(head_c...  49.7 us
    pallas_call x4, Pallas kernels, key_value(): pl.pallas_call(functools.partial(key_value_kernel, blocks=blocks), grid=(...  49.2 us
    pallas_call x4, Pallas kernels, earlier_attention(): pl.pallas_call(functools.partial(earlier_kernel, chunks=chunks), grid_spe...  22.2 us
    unnamed x63, local copies, waits for them, and re-layouts  14 us
    dynamic_update_slice x5, local copies, waits for them, and re-layouts, gather_noise(): lax.dynamic_update_slice(frame, came[None], ((index + d) % tensor_size, 0...  11.2 us
  transfers between devices with their start and end apart: 42, of which 19 were waited for; matrix products, arithmetic and copies ran while one was open for 9% of the time, Pallas kernels for 29%

profile of v1, /device:TPU:0, one launch (start us, length us, event | category | flops | bytes accessed | tf_op | source)
XLA Modules:
  0.0 473.2 jit_solution(13932490138652392804)
XLA Ops:
  10.7 11.1 %collective-permute-start.7 = (s32[1]{0:T(128)}, s32[1]{0:T(128)}, u32[]{:S(2)}, u32[]{:S(2)}) collective-permute-start(s32[1]{0:T(128)} %param.10), channel_id=1, source_target_pairs={{0,28},{1,29},{2,30},{3,31},{4,0},{5,1},{6,2},{7,3},{8,4},{9,5},{1... | collective-permute-start | bytes 20 | tf_op jit(solution)/shard_map/ppermute | solution.py:311
  50.5 12.8 %norm_keys_values.5 = (bf16[2,384,768]{2,1,0:T(8,128)(2,1)}, bf16[384,3072]{1,0:T(8,128)(2,1)S(1)}) custom-call(bf16[384,3072]{1,0:T(8,128)(2,1)S(1)} %get-tuple-element.58.z_ref, f32[1,3072]{1,0:T(1,128)S(1)} %get-tuple-element.63.scale_ref, f32[1,3072]{1,0:T(1,128)S(1)} %get-tuple-element.62.shift_ref, bf16[3,3072,768]{2,1,0:T(8,128)(2,1)} %refs_1_.7, ...), custom_call_target="tpu_custom_call" | custom-call | flops 3623878656 | bytes 15335424 | tf_op jit(solution)/shard_map/norm_keys_values/pallas_call | solution.py:72
  64.7 12.3 %norm_keys_values.4 = (bf16[2,384,768]{2,1,0:T(8,128)(2,1)}, bf16[384,3072]{1,0:T(8,128)(2,1)S(1)}) custom-call(bf16[384,3072]{1,0:T(8,128)(2,1)S(1)} %get-tuple-element.57.z_ref, f32[1,3072]{1,0:T(1,128)S(1)} %get-tuple-element.63.scale_ref, f32[1,3072]{1,0:T(1,128)S(1)} %get-tuple-element.62.shift_ref, bf16[3,3072,768]{2,1,0:T(8,128)(2,1)} %refs_1_.7, ...), custom_call_target="tpu_custom_call" | custom-call | flops 3623878656 | bytes 15335424 | tf_op jit(solution)/shard_map/norm_keys_values/pallas_call | solution.py:72
  77.0 3.7 collective-permute-done.15.refs_9_
  83.9 9.7 %collective-permute-done.16.refs_10_ = bf16[768,1536]{1,0:T(8,128)(2,1)} collective-permute-done((bf16[768,1536]{1,0:T(8,128)(2,1)}, bf16[768,1536]{1,0:T(8,128)(2,1)}, u32[]{:S(2)}, u32[]{:S(2)}) %collective-permute-start.16) | collective-permute-done | bytes 2359328 | tf_op jit(solution)/shard_map/ppermute | solution.py:311
  97.2 12.5 %queries_own_frame.5 = (bf16[384,768]{1,0:T(8,128)(2,1)S(1)}, f32[384,768]{1,0:T(8,128)S(1)}, f32[384,768]{1,0:T(8,128)S(1)}, f32[384,768]{1,0:T(8,128)S(1)}) custom-call(bf16[384,3072]{1,0:T(8,128)(2,1)} %copy-done.7, bf16[3,3072,768]{2,1,0:T(8,128)(2,1)} %refs_1_.7, f32[1,128]{1,0:T(1,128)S(1)} %copy-done.11, ...), custom_call_target="tpu_custom_call" | custom-call | flops 3623878656 | bytes 13565952 | tf_op jit(solution)/shard_map/queries_own_frame/pallas_call | solution.py:144
  109.7 26.8 %collective-permute-done.8.refs_5_ = bf16[2,384,768]{2,1,0:T(8,128)(2,1)S(1)} collective-permute-done((bf16[2,384,768]{2,1,0:T(8,128)(2,1)}, bf16[2,384,768]{2,1,0:T(8,128)(2,1)S(1)}, u32[]{:S(2)}, u32[]{:S(2)}) %collective-permute-start.8) | collective-permute-done | bytes 1179680 | tf_op jit(solution)/shard_map/ppermute | solution.py:311
  136.5 12.7 %collective-permute-done.9.refs_6_ = bf16[2,384,768]{2,1,0:T(8,128)(2,1)} collective-permute-done((bf16[2,384,768]{2,1,0:T(8,128)(2,1)}, bf16[2,384,768]{2,1,0:T(8,128)(2,1)}, u32[]{:S(2)}, u32[]{:S(2)}) %collective-permute-start.9) | collective-permute-done | bytes 1179680 | tf_op jit(solution)/shard_map/ppermute | solution.py:311
  149.3 6.0 %earlier_frame.5 = bf16[384,768]{1,0:T(8,128)(2,1)} custom-call(s32[1]{0:T(128)} %bitcast.14.refs_0_, bf16[384,768]{1,0:T(8,128)(2,1)S(1)} %get-tuple-element.39.refs_1_, f32[384,768]{1,0:T(8,128)S(1)} %get-tuple-element.40.refs_2_, f32[384,768]{1,0:T(8,128)S(1)} %get-tuple-element.41.refs_3_, f32[384,768]{1,0:T(8,128)S(1)} %get-tuple-element.42.refs_4_, ...), custom_call_target="tpu_custom_call" | custom-call | flops 1811939328 | bytes 7077888 | tf_op jit(solution)/shard_map/earlier_frame/pallas_call | solution.py:197
  157.8 12.5 %queries_own_frame.4 = (bf16[384,768]{1,0:T(8,128)(2,1)S(1)}, f32[384,768]{1,0:T(8,128)S(1)}, f32[384,768]{1,0:T(8,128)S(1)}, f32[384,768]{1,0:T(8,128)S(1)}) custom-call(bf16[384,3072]{1,0:T(8,128)(2,1)} %copy-done.4, bf16[3,3072,768]{2,1,0:T(8,128)(2,1)} %refs_1_.7, f32[1,128]{1,0:T(1,128)S(1)} %copy-done.12, ...), custom_call_target="tpu_custom_call" | custom-call | flops 3623878656 | bytes 13565952 | tf_op jit(solution)/shard_map/queries_own_frame/pallas_call | solution.py:144
  170.3 5.4 %earlier_frame.4 = bf16[384,768]{1,0:T(8,128)(2,1)S(1)} custom-call(s32[1]{0:T(128)} %bitcast.14.refs_0_, bf16[384,768]{1,0:T(8,128)(2,1)S(1)} %get-tuple-element.32.refs_1_, f32[384,768]{1,0:T(8,128)S(1)} %get-tuple-element.33.refs_2_, f32[384,768]{1,0:T(8,128)S(1)} %get-tuple-element.34.refs_3_, f32[384,768]{1,0:T(8,128)S(1)} %get-tuple-element.35.refs_4_, ...), custom_call_target="tpu_custom_call" | custom-call | flops 1811939328 | bytes 7077888 | tf_op jit(solution)/shard_map/earlier_frame/pallas_call | solution.py:197
  175.7 30.4 %collective-permute-done.24.refs_3_ = bf16[384,768]{1,0:T(8,128)(2,1)} collective-permute-done((bf16[384,768]{1,0:T(8,128)(2,1)}, bf16[384,768]{1,0:T(8,128)(2,1)}, u32[]{:S(2)}, u32[]{:S(2)}) %collective-permute-start.24) | collective-permute-done | bytes 589856 | tf_op jit(solution)/shard_map/ppermute | solution.py:311
  206.2 3.7 collective-permute-start.25
  218.1 3.7 collective-permute-done.26.refs_5_
  232.8 9.5 %collective-permute-done.11.refs_4_ = bf16[384,768]{1,0:T(8,128)(2,1)S(1)} collective-permute-done((bf16[384,768]{1,0:T(8,128)(2,1)S(1)}, bf16[384,768]{1,0:T(8,128)(2,1)S(1)}, u32[]{:S(2)}, u32[]{:S(2)}) %collective-permute-start.11) | collective-permute-done | bytes 589856 | tf_op jit(solution)/shard_map/ppermute | solution.py:311
  260.6 14.6 %output_projection.5.z_ref = bf16[384,3072]{1,0:T(8,128)(2,1)} custom-call(s32[1]{0:T(128)} %bitcast.refs_0_, bf16[384,3072]{1,0:T(8,128)(2,1)} %bitcast_select_fusion.1.refs_1_, f32[1,3072]{1,0:T(1,128)S(1)} %get-tuple-element.53.refs_2_, bf16[384,768]{1,0:T(8,128)(2,1)} %collective-permute-done.24.refs_3_, ...), custom_call_target="tpu_custom_call" | custom-call | flops 7247757312 | bytes 23592960 | tf_op jit(solution)/shard_map/output_projection/pallas_call | solution.py:269
  276.9 11.6 %norm_keys_values.7 = (bf16[2,384,768]{2,1,0:T(8,128)(2,1)S(1)}, bf16[384,3072]{1,0:T(8,128)(2,1)S(1)}) custom-call(bf16[384,3072]{1,0:T(8,128)(2,1)S(1)} %copy-done.2, f32[1,3072]{1,0:T(1,128)S(1)} %copy-done.9, f32[1,3072]{1,0:T(1,128)S(1)} %get-tuple-element.62.shift_ref, bf16[3,3072,768]{2,1,0:T(8,128)(2,1)} %refs_1_.7, f32[1,128]{1,0:T(1,128)S(1)} %bitcast.39), custom_call_target="tpu_custom_call" | custom-call | flops 3623878656 | bytes 15335424 | tf_op jit(solution)/shard_map/norm_keys_values/pallas_call | solution.py:72
  289.9 14.8 %output_projection.4.z_ref = bf16[384,3072]{1,0:T(8,128)(2,1)} custom-call(s32[1]{0:T(128)} %bitcast.refs_0_, bf16[384,3072]{1,0:T(8,128)(2,1)} %bitcast_select_fusion.2.refs_1_, f32[1,3072]{1,0:T(1,128)S(1)} %get-tuple-element.53.refs_2_, bf16[384,768]{1,0:T(8,128)(2,1)S(1)} %collective-permute-done.10.refs_3_, ...), custom_call_target="tpu_custom_call" | custom-call | flops 7247757312 | bytes 23592960 | tf_op jit(solution)/shard_map/output_projection/pallas_call | solution.py:269
  304.8 12.5 %norm_keys_values.6 = (bf16[2,384,768]{2,1,0:T(8,128)(2,1)S(1)}, bf16[384,3072]{1,0:T(8,128)(2,1)S(1)}) custom-call(bf16[384,3072]{1,0:T(8,128)(2,1)} %output_projection.4.z_ref, f32[1,3072]{1,0:T(1,128)S(1)} %copy-done.9, f32[1,3072]{1,0:T(1,128)S(1)} %get-tuple-element.62.shift_ref, bf16[3,3072,768]{2,1,0:T(8,128)(2,1)} %refs_1_.7, f32[1,128]{1,0:T(1,128)S(1)} %bitcast.40), custom_call_target="tpu_custom_call" | custom-call | flops 3623878656 | bytes 15335424 | tf_op jit(solution)/shard_map/norm_keys_values/pallas_call | solution.py:72
  319.1 12.3 %queries_own_frame.7 = (bf16[384,768]{1,0:T(8,128)(2,1)S(1)}, f32[384,768]{1,0:T(8,128)S(1)}, f32[384,768]{1,0:T(8,128)S(1)}, f32[384,768]{1,0:T(8,128)S(1)}) custom-call(bf16[384,3072]{1,0:T(8,128)(2,1)} %copy-done.6, bf16[3,3072,768]{2,1,0:T(8,128)(2,1)} %refs_1_.7, f32[1,128]{1,0:T(1,128)S(1)} %copy-done.13, ...), custom_call_target="tpu_custom_call" | custom-call | flops 3623878656 | bytes 13565952 | tf_op jit(solution)/shard_map/queries_own_frame/pallas_call | solution.py:144
  331.3 4.8 %collective-permute-done.29.refs_5_ = bf16[2,384,768]{2,1,0:T(8,128)(2,1)S(1)} collective-permute-done((bf16[2,384,768]{2,1,0:T(8,128)(2,1)S(1)}, bf16[2,384,768]{2,1,0:T(8,128)(2,1)S(1)}, u32[]{:S(2)}, u32[]{:S(2)}) %collective-permute-start.29) | collective-permute-done | bytes 1179680 | tf_op jit(solution)/shard_map/ppermute | solution.py:311
  336.1 12.6 %collective-permute-done.30.refs_6_ = bf16[2,384,768]{2,1,0:T(8,128)(2,1)S(1)} collective-permute-done((bf16[2,384,768]{2,1,0:T(8,128)(2,1)S(1)}, bf16[2,384,768]{2,1,0:T(8,128)(2,1)S(1)}, u32[]{:S(2)}, u32[]{:S(2)}) %collective-permute-start.30) | collective-permute-done | bytes 1179680 | tf_op jit(solution)/shard_map/ppermute | solution.py:311
  349.7 5.4 %earlier_frame.7 = bf16[384,768]{1,0:T(8,128)(2,1)S(1)} custom-call(s32[1]{0:T(128)} %bitcast.14.refs_0_, bf16[384,768]{1,0:T(8,128)(2,1)S(1)} %get-tuple-element.49.refs_1_, f32[384,768]{1,0:T(8,128)S(1)} %get-tuple-element.50.refs_2_, f32[384,768]{1,0:T(8,128)S(1)} %get-tuple-element.51.refs_3_, f32[384,768]{1,0:T(8,128)S(1)} %get-tuple-element.52.refs_4_, ...), custom_call_target="tpu_custom_call" | custom-call | flops 1811939328 | bytes 7077888 | tf_op jit(solution)/shard_map/earlier_frame/pallas_call | solution.py:197
  355.2 12.3 %queries_own_frame.6 = (bf16[384,768]{1,0:T(8,128)(2,1)S(1)}, f32[384,768]{1,0:T(8,128)S(1)}, f32[384,768]{1,0:T(8,128)S(1)}, f32[384,768]{1,0:T(8,128)S(1)}) custom-call(bf16[384,3072]{1,0:T(8,128)(2,1)} %copy-done.5, bf16[3,3072,768]{2,1,0:T(8,128)(2,1)} %refs_1_.7, f32[1,128]{1,0:T(1,128)S(1)} %copy-done.13, ...), custom_call_target="tpu_custom_call" | custom-call | flops 3623878656 | bytes 13565952 | tf_op jit(solution)/shard_map/queries_own_frame/pallas_call | solution.py:144
  367.5 5.4 %earlier_frame.6 = bf16[384,768]{1,0:T(8,128)(2,1)S(1)} custom-call(s32[1]{0:T(128)} %bitcast.14.refs_0_, bf16[384,768]{1,0:T(8,128)(2,1)S(1)} %get-tuple-element.44.refs_1_, f32[384,768]{1,0:T(8,128)S(1)} %get-tuple-element.45.refs_2_, f32[384,768]{1,0:T(8,128)S(1)} %get-tuple-element.46.refs_3_, f32[384,768]{1,0:T(8,128)S(1)} %get-tuple-element.47.refs_4_, ...), custom_call_target="tpu_custom_call" | custom-call | flops 1811939328 | bytes 7077888 | tf_op jit(solution)/shard_map/earlier_frame/pallas_call | solution.py:197
  373.0 32.7 %collective-permute-done.37.refs_3_ = bf16[384,768]{1,0:T(8,128)(2,1)S(1)} collective-permute-done((bf16[384,768]{1,0:T(8,128)(2,1)S(1)}, bf16[384,768]{1,0:T(8,128)(2,1)S(1)}, u32[]{:S(2)}, u32[]{:S(2)}) %collective-permute-start.37) | collective-permute-done | bytes 589856 | tf_op jit(solution)/shard_map/ppermute | solution.py:311
  408.2 3.7 collective-permute-done.31.refs_3_
  413.0 7.8 %collective-permute-done.38.refs_4_ = bf16[384,768]{1,0:T(8,128)(2,1)S(1)} collective-permute-done((bf16[384,768]{1,0:T(8,128)(2,1)S(1)}, bf16[384,768]{1,0:T(8,128)(2,1)S(1)}, u32[]{:S(2)}, u32[]{:S(2)}) %collective-permute-start.38) | collective-permute-done | bytes 589856 | tf_op jit(solution)/shard_map/ppermute | solution.py:311
  424.3 7.3 %collective-permute-done.32.refs_4_ = bf16[384,768]{1,0:T(8,128)(2,1)S(1)} collective-permute-done((bf16[384,768]{1,0:T(8,128)(2,1)S(1)}, bf16[384,768]{1,0:T(8,128)(2,1)S(1)}, u32[]{:S(2)}, u32[]{:S(2)}) %collective-permute-start.32) | collective-permute-done | bytes 589856 | tf_op jit(solution)/shard_map/ppermute | solution.py:311
  438.7 14.4 %output_projection.7 = bf16[384,3072]{1,0:T(8,128)(2,1)} custom-call(s32[1]{0:T(128)} %bitcast.refs_0_, bf16[384,3072]{1,0:T(8,128)(2,1)} %collective-permute-done.36.refs_1_, f32[1,3072]{1,0:T(1,128)S(1)} %get-tuple-element.54.refs_2_, bf16[384,768]{1,0:T(8,128)(2,1)S(1)} %collective-permute-done.37.refs_3_, ...), custom_call_target="tpu_custom_call" | custom-call | flops 7247757312 | bytes 23592960 | tf_op jit(solution)/shard_map/output_projection/pallas_call | solution.py:269
  454.5 14.5 %output_projection.6 = bf16[384,3072]{1,0:T(8,128)(2,1)} custom-call(s32[1]{0:T(128)} %bitcast.refs_0_, bf16[384,3072]{1,0:T(8,128)(2,1)} %copy-done.27, f32[1,3072]{1,0:T(1,128)S(1)} %get-tuple-element.54.refs_2_, bf16[384,768]{1,0:T(8,128)(2,1)S(1)} %collective-permute-done.31.refs_3_, bf16[384,768]{1,0:T(8,128)(2,1)S(1)} %collective-permute-done.32.refs_4_, ...), custom_call_target="tpu_custom_call" | custom-call | flops 7247757312 | bytes 23592960 | tf_op jit(solution)/shard_map/output_projection/pallas_call | solution.py:269
  469.0 4.2 maximum_bitcast_fusion
  (164 shorter events, 106.5 us)
Async XLA Ops:
  4.9 28.5 %collective-permute-start.3 = (bf16[192,3072]{1,0:T(8,128)(2,1)}, bf16[192,3072]{1,0:T(8,128)(2,1)}, u32[]{:S(2)}, u32[]{:S(2)}) collective-permute-start(bf16[192,3072]{1,0:T(8,128)(2,1)} %get-tuple-element.60), channel_id=1, source_target_pairs={{28,31},{29,28},{30,29},{31,30}} | collective-permute-start | bytes 3538952 | tf_op jit(solution)/shard_map/ppermute | solution.py:311
  6.6 32.8 %collective-permute-start.4 = (bf16[192,3072]{1,0:T(8,128)(2,1)}, bf16[192,3072]{1,0:T(8,128)(2,1)}, u32[]{:S(2)}, u32[]{:S(2)}) collective-permute-start(bf16[192,3072]{1,0:T(8,128)(2,1)} %get-tuple-element.60), channel_id=1, source_target_pairs={{28,30},{29,31},{30,28},{31,29}} | collective-permute-start | bytes 3538952 | tf_op jit(solution)/shard_map/ppermute | solution.py:311
  8.3 37.1 %collective-permute-start.5 = (bf16[192,3072]{1,0:T(8,128)(2,1)}, bf16[192,3072]{1,0:T(8,128)(2,1)S(1)}, u32[]{:S(2)}, u32[]{:S(2)}) collective-permute-start(bf16[192,3072]{1,0:T(8,128)(2,1)} %get-tuple-element.60), channel_id=1, source_target_pairs={{28,29},{29,30},{30,31},{31,28}} | collective-permute-start | bytes 3538952 | tf_op jit(solution)/shard_map/ppermute | solution.py:311
  9.0 27.5 %collective-permute-start = (bf16[192,3072]{1,0:T(8,128)(2,1)}, bf16[192,3072]{1,0:T(8,128)(2,1)}, u32[]{:S(2)}, u32[]{:S(2)}) collective-permute-start(bf16[192,3072]{1,0:T(8,128)(2,1)} %get-tuple-element.59), channel_id=1, source_target_pairs={{28,31},{29,28},{30,29},{31,30}} | collective-permute-start | bytes 3538952 | tf_op jit(solution)/shard_map/ppermute | solution.py:311
  10.7 18.3 %collective-permute-start.7 = (s32[1]{0:T(128)}, s32[1]{0:T(128)}, u32[]{:S(2)}, u32[]{:S(2)}) collective-permute-start(s32[1]{0:T(128)} %param.10), channel_id=1, source_target_pairs={{0,28},{1,29},{2,30},{3,31},{4,0},{5,1},{6,2},{7,3},{8,4},{9,5},{1... | collective-permute-start | bytes 20 | tf_op jit(solution)/shard_map/ppermute | solution.py:311
  36.6 44.1 %collective-permute-start.15 = (bf16[768,1536]{1,0:T(8,128)(2,1)}, bf16[768,1536]{1,0:T(8,128)(2,1)S(1)}, u32[]{:S(2)}, u32[]{:S(2)}) collective-permute-start(bf16[768,1536]{1,0:T(8,128)(2,1)} %constant_dynamic-slice_fusion), channel_id=1, source_target_pairs={{0,1},{1,0},{2,3},{3,2},{4,5},{5,4},{6,7},{7,6},{8,9},{9,8},{10,11... | collective-permute-start | bytes 7077896 | tf_op jit(solution)/shard_map/ppermute | solution.py:311
  39.5 54.1 %collective-permute-start.16 = (bf16[768,1536]{1,0:T(8,128)(2,1)}, bf16[768,1536]{1,0:T(8,128)(2,1)}, u32[]{:S(2)}, u32[]{:S(2)}) collective-permute-start(bf16[768,1536]{1,0:T(8,128)(2,1)} %constant_dynamic-slice_fusion), channel_id=1, source_target_pairs={{0,2},{1,3},{2,0},{3,1},{4,6},{5,7},{6,4},{7,5},{8,10},{9,11},{10,... | collective-permute-start | bytes 7077896 | tf_op jit(solution)/shard_map/ppermute | solution.py:311
  77.0 59.6 %collective-permute-start.8 = (bf16[2,384,768]{2,1,0:T(8,128)(2,1)}, bf16[2,384,768]{2,1,0:T(8,128)(2,1)S(1)}, u32[]{:S(2)}, u32[]{:S(2)}) collective-permute-start(bf16[2,384,768]{2,1,0:T(8,128)(2,1)} %get-tuple-element.30.refs_3_), channel_id=1, source_target_pairs={{0,4},{1,5},{2,6},{3,7},{4,8},{5,9},{6,10},{7,11},{8,12},{9,13},{1... | collective-permute-start | bytes 3538952 | tf_op jit(solution)/shard_map/ppermute | solution.py:311
  77.0 72.3 %collective-permute-start.9 = (bf16[2,384,768]{2,1,0:T(8,128)(2,1)}, bf16[2,384,768]{2,1,0:T(8,128)(2,1)}, u32[]{:S(2)}, u32[]{:S(2)}) collective-permute-start(bf16[2,384,768]{2,1,0:T(8,128)(2,1)} %get-tuple-element.31.refs_4_), channel_id=1, source_target_pairs={{0,4},{1,5},{2,6},{3,7},{4,8},{5,9},{6,10},{7,11},{8,12},{9,13},{1... | collective-permute-start | bytes 3538952 | tf_op jit(solution)/shard_map/ppermute | solution.py:311
  82.0 124.2 %collective-permute-start.17 = (bf16[384,1536]{1,0:T(8,128)(2,1)}, bf16[384,1536]{1,0:T(8,128)(2,1)}, u32[]{:S(2)}, u32[]{:S(2)}) collective-permute-start(bf16[384,1536]{1,0:T(8,128)(2,1)} %slice.95), channel_id=1, source_target_pairs={{0,2},{1,3},{2,0},{3,1},{4,6},{5,7},{6,4},{7,5},{8,10},{9,11},{10,... | collective-permute-start | bytes 3538952 | tf_op jit(solution)/shard_map/ppermute | solution.py:311
  96.0 113.8 %collective-permute-start.18 = (bf16[384,1536]{1,0:T(8,128)(2,1)}, bf16[384,1536]{1,0:T(8,128)(2,1)}, u32[]{:S(2)}, u32[]{:S(2)}) collective-permute-start(bf16[384,1536]{1,0:T(8,128)(2,1)} %slice.96), channel_id=1, source_target_pairs={{0,1},{1,0},{2,3},{3,2},{4,5},{5,4},{6,7},{7,6},{8,9},{9,8},{10,11... | collective-permute-start | bytes 3538952 | tf_op jit(solution)/shard_map/ppermute | solution.py:311
  96.5 128.3 %collective-permute-start.23 = (bf16[384,3072]{1,0:T(8,128)(2,1)}, bf16[384,3072]{1,0:T(8,128)(2,1)}, u32[]{:S(2)}, u32[]{:S(2)}) collective-permute-start(bf16[384,3072]{1,0:T(8,128)(2,1)} %copy-done), channel_id=1, source_target_pairs={{0,4},{1,5},{2,6},{3,7},{4,8},{5,9},{6,10},{7,11},{8,12},{9,13},{1... | collective-permute-start | bytes 7077896 | tf_op jit(solution)/shard_map/ppermute | solution.py:311
  136.5 90.5 %collective-permute-start.6 = (bf16[384,3072]{1,0:T(8,128)(2,1)S(1)}, bf16[384,3072]{1,0:T(8,128)(2,1)}, u32[]{:S(2)}, u32[]{:S(2)}) collective-permute-start(bf16[384,3072]{1,0:T(8,128)(2,1)S(1)} %get-tuple-element.57.z_ref), channel_id=1, source_target_pairs={{0,4},{1,5},{2,6},{3,7},{4,8},{5,9},{6,10},{7,11},{8,12},{9,13},{1... | collective-permute-start | bytes 7077896 | tf_op jit(solution)/shard_map/ppermute | solution.py:311
  155.3 50.9 %collective-permute-start.24 = (bf16[384,768]{1,0:T(8,128)(2,1)}, bf16[384,768]{1,0:T(8,128)(2,1)}, u32[]{:S(2)}, u32[]{:S(2)}) collective-permute-start(bf16[384,768]{1,0:T(8,128)(2,1)} %earlier_frame.5), channel_id=1, source_target_pairs={{0,4},{1,5},{2,6},{3,7},{4,8},{5,9},{6,10},{7,11},{8,12},{9,13},{1... | collective-permute-start | bytes 1769480 | tf_op jit(solution)/shard_map/ppermute | solution.py:311
  217.3 40.6 %collective-permute-start.19 = (bf16[768,1536]{1,0:T(8,128)(2,1)S(1)}, bf16[768,1536]{1,0:T(8,128)(2,1)S(1)}, u32[]{:S(2)}, u32[]{:S(2)}) collective-permute-start(bf16[768,1536]{1,0:T(8,128)(2,1)S(1)} %copy-done.18), channel_id=1, source_target_pairs={{0,4},{1,5},{2,6},{3,7},{4,0},{5,1},{6,2},{7,3},{8,12},{9,13},{10,... | collective-permute-start | bytes 7077896 | tf_op jit(solution)/shard_map/ppermute | solution.py:311
  218.1 39.7 %collective-permute-start.20 = (bf16[768,1536]{1,0:T(8,128)(2,1)}, bf16[768,1536]{1,0:T(8,128)(2,1)S(1)}, u32[]{:S(2)}, u32[]{:S(2)}) collective-permute-start(bf16[768,1536]{1,0:T(8,128)(2,1)} %collective-permute-done.16.refs_10_), channel_id=1, source_target_pairs={{0,4},{1,5},{2,6},{3,7},{4,0},{5,1},{6,2},{7,3},{8,12},{9,13},{10,... | collective-permute-start | bytes 7077896 | tf_op jit(solution)/shard_map/ppermute | solution.py:311
  221.8 36.0 %collective-permute-start.21 = (bf16[768,1536]{1,0:T(8,128)(2,1)S(1)}, bf16[768,1536]{1,0:T(8,128)(2,1)S(1)}, u32[]{:S(2)}, u32[]{:S(2)}) collective-permute-start(bf16[768,1536]{1,0:T(8,128)(2,1)S(1)} %constant_dynamic-update-slice_fusion.refs_11_), channel_id=1, source_target_pairs={{0,4},{1,5},{2,6},{3,7},{4,0},{5,1},{6,2},{7,3},{8,12},{9,13},{10,... | collective-permute-start | bytes 7077896 | tf_op jit(solution)/shard_map/ppermute | solution.py:311
  224.9 17.4 %collective-permute-start.11 = (bf16[384,768]{1,0:T(8,128)(2,1)S(1)}, bf16[384,768]{1,0:T(8,128)(2,1)S(1)}, u32[]{:S(2)}, u32[]{:S(2)}) collective-permute-start(bf16[384,768]{1,0:T(8,128)(2,1)S(1)} %collective-permute-done.10.refs_3_), channel_id=1, source_target_pairs={{0,1},{1,0},{2,3},{3,2},{4,5},{5,4},{6,7},{7,6},{8,9},{9,8},{10,11... | collective-permute-start | bytes 1769480 | tf_op jit(solution)/shard_map/ppermute | solution.py:311
  227.0 17.7 %collective-permute-start.12 = (bf16[384,768]{1,0:T(8,128)(2,1)S(1)}, bf16[384,768]{1,0:T(8,128)(2,1)S(1)}, u32[]{:S(2)}, u32[]{:S(2)}) collective-permute-start(bf16[384,768]{1,0:T(8,128)(2,1)S(1)} %collective-permute-done.10.refs_3_), channel_id=1, source_target_pairs={{0,2},{1,3},{2,0},{3,1},{4,6},{5,7},{6,4},{7,5},{8,10},{9,11},{10,... | collective-permute-start | bytes 1769480 | tf_op jit(solution)/shard_map/ppermute | solution.py:311
  252.6 37.4 %collective-permute-start.13 = (bf16[192,768]{1,0:T(8,128)(2,1)S(1)}, bf16[192,768]{1,0:T(8,128)(2,1)S(1)}, u32[]{:S(2)}, u32[]{:S(2)}) collective-permute-start(bf16[192,768]{1,0:T(8,128)(2,1)S(1)} %slice.93), channel_id=1, source_target_pairs={{0,2},{1,3},{2,0},{3,1},{4,6},{5,7},{6,4},{7,5},{8,10},{9,11},{10,... | collective-permute-start | bytes 884744 | tf_op jit(solution)/shard_map/ppermute | solution.py:311
  255.0 34.9 %collective-permute-start.14 = (bf16[192,768]{1,0:T(8,128)(2,1)S(1)}, bf16[192,768]{1,0:T(8,128)(2,1)S(1)}, u32[]{:S(2)}, u32[]{:S(2)}) collective-permute-start(bf16[192,768]{1,0:T(8,128)(2,1)S(1)} %slice.94), channel_id=1, source_target_pairs={{0,1},{1,0},{2,3},{3,2},{4,5},{5,4},{6,7},{7,6},{8,9},{9,8},{10,11... | collective-permute-start | bytes 884744 | tf_op jit(solution)/shard_map/ppermute | solution.py:311
  318.7 17.4 %collective-permute-start.29 = (bf16[2,384,768]{2,1,0:T(8,128)(2,1)S(1)}, bf16[2,384,768]{2,1,0:T(8,128)(2,1)S(1)}, u32[]{:S(2)}, u32[]{:S(2)}) collective-permute-start(bf16[2,384,768]{2,1,0:T(8,128)(2,1)S(1)} %get-tuple-element.37.refs_3_), channel_id=1, source_target_pairs={{0,4},{1,5},{2,6},{3,7},{4,8},{5,9},{6,10},{7,11},{8,12},{9,13},{1... | collective-permute-start | bytes 3538952 | tf_op jit(solution)/shard_map/ppermute | solution.py:311
  318.7 30.1 %collective-permute-start.30 = (bf16[2,384,768]{2,1,0:T(8,128)(2,1)S(1)}, bf16[2,384,768]{2,1,0:T(8,128)(2,1)S(1)}, u32[]{:S(2)}, u32[]{:S(2)}) collective-permute-start(bf16[2,384,768]{2,1,0:T(8,128)(2,1)S(1)} %get-tuple-element.43.refs_4_), channel_id=1, source_target_pairs={{0,4},{1,5},{2,6},{3,7},{4,8},{5,9},{6,10},{7,11},{8,12},{9,13},{1... | collective-permute-start | bytes 3538952 | tf_op jit(solution)/shard_map/ppermute | solution.py:311
  318.7 118.4 %collective-permute-start.36 = (bf16[384,3072]{1,0:T(8,128)(2,1)S(1)}, bf16[384,3072]{1,0:T(8,128)(2,1)}, u32[]{:S(2)}, u32[]{:S(2)}) collective-permute-start(bf16[384,3072]{1,0:T(8,128)(2,1)S(1)} %copy-done.3), channel_id=1, source_target_pairs={{0,4},{1,5},{2,6},{3,7},{4,8},{5,9},{6,10},{7,11},{8,12},{9,13},{1... | collective-permute-start | bytes 7077896 | tf_op jit(solution)/shard_map/ppermute | solution.py:311
  318.8 134.4 %collective-permute-start.22 = (bf16[384,3072]{1,0:T(8,128)(2,1)}, bf16[384,3072]{1,0:T(8,128)(2,1)S(1)}, u32[]{:S(2)}, u32[]{:S(2)}) collective-permute-start(bf16[384,3072]{1,0:T(8,128)(2,1)} %output_projection.4.z_ref), channel_id=1, source_target_pairs={{0,4},{1,5},{2,6},{3,7},{4,8},{5,9},{6,10},{7,11},{8,12},{9,13},{1... | collective-permute-start | bytes 7077896 | tf_op jit(solution)/shard_map/ppermute | solution.py:311
  355.1 50.5 %collective-permute-start.37 = (bf16[384,768]{1,0:T(8,128)(2,1)S(1)}, bf16[384,768]{1,0:T(8,128)(2,1)S(1)}, u32[]{:S(2)}, u32[]{:S(2)}) collective-permute-start(bf16[384,768]{1,0:T(8,128)(2,1)S(1)} %earlier_frame.7), channel_id=1, source_target_pairs={{0,4},{1,5},{2,6},{3,7},{4,8},{5,9},{6,10},{7,11},{8,12},{9,13},{1... | collective-permute-start | bytes 1769480 | tf_op jit(solution)/shard_map/ppermute | solution.py:311
  372.9 39.0 %collective-permute-start.31 = (bf16[384,768]{1,0:T(8,128)(2,1)S(1)}, bf16[384,768]{1,0:T(8,128)(2,1)S(1)}, u32[]{:S(2)}, u32[]{:S(2)}) collective-permute-start(bf16[384,768]{1,0:T(8,128)(2,1)S(1)} %earlier_frame.6), channel_id=1, source_target_pairs={{0,4},{1,5},{2,6},{3,7},{4,8},{5,9},{6,10},{7,11},{8,12},{9,13},{1... | collective-permute-start | bytes 1769480 | tf_op jit(solution)/shard_map/ppermute | solution.py:311
  406.7 15.6 %collective-permute-start.39 = (bf16[384,768]{1,0:T(8,128)(2,1)S(1)}, bf16[384,768]{1,0:T(8,128)(2,1)S(1)}, u32[]{:S(2)}, u32[]{:S(2)}) collective-permute-start(bf16[384,768]{1,0:T(8,128)(2,1)S(1)} %collective-permute-done.37.refs_3_), channel_id=1, source_target_pairs={{0,2},{1,3},{2,0},{3,1},{4,6},{5,7},{6,4},{7,5},{8,10},{9,11},{10,... | collective-permute-start | bytes 1769480 | tf_op jit(solution)/shard_map/ppermute | solution.py:311
  411.9 19.7 %collective-permute-start.32 = (bf16[384,768]{1,0:T(8,128)(2,1)S(1)}, bf16[384,768]{1,0:T(8,128)(2,1)S(1)}, u32[]{:S(2)}, u32[]{:S(2)}) collective-permute-start(bf16[384,768]{1,0:T(8,128)(2,1)S(1)} %collective-permute-done.31.refs_3_), channel_id=1, source_target_pairs={{0,1},{1,0},{2,3},{3,2},{4,5},{5,4},{6,7},{7,6},{8,9},{9,8},{10,11... | collective-permute-start | bytes 1769480 | tf_op jit(solution)/shard_map/ppermute | solution.py:311
  422.4 16.4 %collective-permute-start.40 = (bf16[192,768]{1,0:T(8,128)(2,1)S(1)}, bf16[192,768]{1,0:T(8,128)(2,1)S(1)}, u32[]{:S(2)}, u32[]{:S(2)}) collective-permute-start(bf16[192,768]{1,0:T(8,128)(2,1)S(1)} %slice.102), channel_id=1, source_target_pairs={{0,2},{1,3},{2,0},{3,1},{4,6},{5,7},{6,4},{7,5},{8,10},{9,11},{10,... | collective-permute-start | bytes 884744 | tf_op jit(solution)/shard_map/ppermute | solution.py:311
  435.6 17.6 %collective-permute-start.34 = (bf16[192,768]{1,0:T(8,128)(2,1)S(1)}, bf16[192,768]{1,0:T(8,128)(2,1)S(1)}, u32[]{:S(2)}, u32[]{:S(2)}) collective-permute-start(bf16[192,768]{1,0:T(8,128)(2,1)S(1)} %slice.100), channel_id=1, source_target_pairs={{0,2},{1,3},{2,0},{3,1},{4,6},{5,7},{6,4},{7,5},{8,10},{9,11},{10,... | collective-permute-start | bytes 884744 | tf_op jit(solution)/shard_map/ppermute | solution.py:311
  437.1 16.0 %collective-permute-start.35 = (bf16[192,768]{1,0:T(8,128)(2,1)S(1)}, bf16[192,768]{1,0:T(8,128)(2,1)S(1)}, u32[]{:S(2)}, u32[]{:S(2)}) collective-permute-start(bf16[192,768]{1,0:T(8,128)(2,1)S(1)} %slice.101), channel_id=1, source_target_pairs={{0,1},{1,0},{2,3},{3,2},{4,5},{5,4},{6,7},{7,6},{8,9},{9,8},{10,11... | collective-permute-start | bytes 884744 | tf_op jit(solution)/shard_map/ppermute | solution.py:311
  (41 other events, 409.7 us)

commit v2 on v1

v2 whole, which is shorter than its diff:
```python
import functools
import math

import jax
import jax.numpy as jnp
from jax import lax
from jax.experimental import pallas as pl
from jax.experimental.pallas import tpu as pltpu
from jax.sharding import PartitionSpec as P

HD = 128
STEPS = 2
CHUNKS = 2
EPS = 1e-6
AXES = ("queue", "tensor")
F32 = jnp.float32
BF16 = jnp.bfloat16
SCORE_SCALE = math.log2(math.e) / math.sqrt(HD)
ANY = pl.BlockSpec(memory_space=pl.ANY)


def compiler_params(mib):
    return pltpu.CompilerParams(vmem_limit_bytes=mib * 2**20)


def cost(flops, nbytes, transcendentals=0):
    return pl.CostEstimate(
        flops=int(flops), bytes_accessed=int(nbytes), transcendentals=int(transcendentals)
    )


def qkv_kernel(*refs, tensor_size, first_row, noise_first_row, noise_step, k_blocks):
    info_ref, scale_ref, shift_ref, w_ref, gain_ref, z_any, noise_any = refs[:7]
    piece_refs = refs[7 : 7 + tensor_size - 1]
    kv_ref, query_ref, state_ref, normed_ref, acc_ref, sem = refs[6 + tensor_size :]
    part, block = pl.program_id(0), pl.program_id(1)
    rows, width = state_ref.shape
    piece_rows = noise_any.shape[1]
    block_width = width // k_blocks

    @pl.when(jnp.logical_and(part == 0, block == 0))
    def _():
        @pl.when(info_ref[0] == 0)
        def _():
            copy = pltpu.make_async_copy(z_any.at[pl.ds(first_row, rows)], state_ref, sem.at[0])
            copy.start()
            copy.wait()

        @pl.when(info_ref[0] != 0)
        def _():
            unit = math.gcd(rows, piece_rows)
            for b in range(rows // unit):
                row = noise_first_row + b * unit
                away = lax.rem(row // piece_rows + tensor_size - info_ref[1], tensor_size)
                inside = pl.ds(row % piece_rows, unit)
                for d in range(tensor_size):
                    source = noise_any.at[noise_step] if d == 0 else piece_refs[d - 1]

                    @pl.when(away == d)
                    def _():
                        copy = pltpu.make_async_copy(
                            source.at[inside], state_ref.at[pl.ds(b * unit, unit)], sem.at[0]
                        )
                        copy.start()
                        copy.wait()

        def one(i, carry):
            at = pl.ds(pl.multiple_of(i * 16, 16), 16)
            state = state_ref[at, :].astype(F32)
            mean = jnp.mean(state * state, axis=-1, keepdims=True)
            state = state * lax.rsqrt(mean + EPS) * scale_ref[...] + shift_ref[...]
            state = state.astype(BF16)
            for k in range(k_blocks):
                normed_ref[k, at, :] = state[:, k * block_width : (k + 1) * block_width]
            return carry

        lax.fori_loop(0, rows // 16, one, 0)

    product = jnp.dot(normed_ref[block], w_ref[0], preferred_element_type=F32)

    @pl.when(block == 0)
    def _():
        acc_ref[...] = product

    @pl.when(jnp.logical_and(block > 0, block < k_blocks - 1))
    def _():
        acc_ref[...] += product

    @pl.when(block == k_blocks - 1)
    def _():
        def normalized(gain):
            for h in range(product.shape[1] // HD):
                at = slice(h * HD, (h + 1) * HD)
                head = acc_ref[:, at] + product[:, at]
                mean = jnp.mean(head * head, axis=-1, keepdims=True)
                yield at, (head * lax.rsqrt(mean + EPS) * gain).astype(BF16)

        @pl.when(part == 0)
        def _():
            for at, head in normalized(gain_ref[1:2]):
                kv_ref[0, :, at] = head

        @pl.when(part == 1)
        def _():
            kv_ref[0] = (acc_ref[...] + product).astype(BF16)

        @pl.when(part == 2)
        def _():
            for at, head in normalized(gain_ref[0:1]):
                query_ref[:, at] = head


def project_qkv(info, scale1, shift, qkv_weight, gains, z, first_row, rows, noise):
    width, head_cols = qkv_weight.shape[1:]
    noise_all, noise_step, pieces, noise_first_row = noise
    tensor_size = len(pieces) + 1
    k_blocks = 4
    block_width = width // k_blocks
    return pl.pallas_call(
        functools.partial(
            qkv_kernel,
            tensor_size=tensor_size,
            first_row=first_row,
            noise_first_row=noise_first_row,
            noise_step=noise_step,
            k_blocks=k_blocks,
        ),
        grid_spec=pltpu.PrefetchScalarGridSpec(
            num_scalar_prefetch=1,
            grid=(3, k_blocks),
            in_specs=[
                pl.BlockSpec((1, width), lambda p, k, i: (0, 0)),
                pl.BlockSpec((1, width), lambda p, k, i: (0, 0)),
                pl.BlockSpec((1, block_width, head_cols), lambda p, k, i: ((p + 1) % 3, k, 0)),
                pl.BlockSpec((2, HD), lambda p, k, i: (0, 0)),
            ]
            + [ANY] * (1 + tensor_size),
            out_specs=[
                pl.BlockSpec((1, rows, head_cols), lambda p, k, i: (jnp.minimum(p, 1), 0, 0)),
                pl.BlockSpec((rows, head_cols), lambda p, k, i: (0, 0)),
                pl.BlockSpec((rows, width), lambda p, k, i: (0, 0)),
            ],
            scratch_shapes=[
                pltpu.VMEM((k_blocks, rows, block_width), BF16),
                pltpu.VMEM((rows, head_cols), F32),
                pltpu.SemaphoreType.DMA((1,)),
            ],
        ),
        out_shape=[
            jax.ShapeDtypeStruct((2, rows, head_cols), BF16),
            jax.ShapeDtypeStruct((rows, head_cols), BF16),
            jax.ShapeDtypeStruct((rows, width), BF16),
        ],
        compiler_params=compiler_params(32),
        cost_estimate=cost(
            6 * rows * width * head_cols,
            4 * rows * width + 6 * width * head_cols + 6 * rows * head_cols,
        ),
        name="norm_qkv",
    )(info, scale1, shift, qkv_weight, gains, z, noise_all, *pieces)


def attend_parts(query, kv_refs, at):
    scores = [
        lax.dot_general(
            query, ref[0, :, at], (((1,), (1,)), ((), ())), preferred_element_type=F32
        )
        for ref in kv_refs
    ]
    tops = [jnp.max(s, axis=-1, keepdims=True) for s in scores]
    return scores, functools.reduce(jnp.maximum, tops)


def weigh_parts(scores, top, kv_refs, at):
    total = None
    for s, ref in zip(scores, kv_refs):
        weights = jnp.exp2(s - top).astype(BF16)
        values = ref[1, :, at]
        extended = jnp.concatenate([values, jnp.ones_like(values)], axis=1)
        term = jnp.dot(weights, extended, preferred_element_type=F32)
        total = term if total is None else total + term
    return total[:, :HD], total[:, HD:]


def own_kernel(*refs, chunks):
    query_ref = refs[0]
    kv_refs = refs[1 : 1 + chunks]
    acc_ref, top_ref, total_ref = refs[1 + chunks :]
    for h in range(query_ref.shape[1] // HD):
        at = slice(h * HD, (h + 1) * HD)
        scores, top = attend_parts(query_ref[:, at], kv_refs, at)
        acc, total = weigh_parts(scores, top, kv_refs, at)
        acc_ref[:, at] = acc
        total_ref[:, at] = total
        top_ref[:, at] = jnp.broadcast_to(top, acc.shape)


def own_attention(query, kvs):
    rows, head_cols = query.shape
    cols = 256 if head_cols % 256 == 0 else HD
    chunks = len(kvs)
    key_rows = kvs[0].shape[1]
    keys = chunks * key_rows
    by_heads = pl.BlockSpec((rows, cols), lambda j: (0, j))
    return pl.pallas_call(
        functools.partial(own_kernel, chunks=chunks),
        grid=(head_cols // cols,),
        in_specs=[by_heads] + [pl.BlockSpec((2, key_rows, cols), lambda j: (0, 0, j))] * chunks,
        out_specs=[by_heads] * 3,
        out_shape=[jax.ShapeDtypeStruct((rows, head_cols), F32)] * 3,
        compiler_params=compiler_params(32),
        cost_estimate=cost(
            8 * rows * keys * head_cols,
            14 * rows * head_cols + 4 * keys * head_cols,
            rows * keys * head_cols // HD,
        ),
        name="own_frame",
    )(query, *kvs)


def earlier_kernel(*refs, chunks):
    info_ref, query_ref, acc_ref, top_ref, total_ref = refs[:5]
    kv_refs = refs[5 : 5 + chunks]
    out_ref = refs[5 + chunks]
    heads = query_ref.shape[1] // HD

    @pl.when(info_ref[0] != 0)
    def _():
        out_ref[...] = (acc_ref[...] / total_ref[...]).astype(BF16)

    @pl.when(info_ref[0] == 0)
    def _():
        for h in range(heads):
            at = slice(h * HD, (h + 1) * HD)
            old_top = top_ref[:, at][:, :1]
            scores, top = attend_parts(query_ref[:, at], kv_refs, at)
            top = jnp.maximum(top, old_top)
            acc, total = weigh_parts(scores, top, kv_refs, at)
            kept = jnp.exp2(old_top - top)
            acc = acc + acc_ref[:, at] * kept
            total = total + total_ref[:, at] * kept
            out_ref[:, at] = (acc / total).astype(BF16)


def earlier_attention(info, query, acc, top, total, kvs):
    rows, head_cols = query.shape
    cols = 256 if head_cols % 256 == 0 else HD
    chunks = len(kvs)
    key_rows = kvs[0].shape[1]
    keys = chunks * key_rows
    by_heads = pl.BlockSpec((rows, cols), lambda j, i: (0, j))
    return pl.pallas_call(
        functools.partial(earlier_kernel, chunks=chunks),
        grid_spec=pltpu.PrefetchScalarGridSpec(
            num_scalar_prefetch=1,
            grid=(head_cols // cols,),
            in_specs=[by_heads] * 4
            + [pl.BlockSpec((2, key_rows, cols), lambda j, i: (0, 0, j))] * chunks,
            out_specs=by_heads,
        ),
        out_shape=jax.ShapeDtypeStruct((rows, head_cols), BF16),
        compiler_params=compiler_params(32),
        cost_estimate=cost(
            8 * rows * keys * head_cols,
            16 * rows * head_cols + 4 * keys * head_cols,
            rows * keys * head_cols // HD,
        ),
        name="earlier_frame",
    )(info, query, acc, top, total, *kvs)


def output_kernel(*refs, piece_counts, aliased):
    parity_ref, resid_ref, gate_ref = refs[:3]
    at = 3
    pieces = []
    for count in piece_counts:
        pieces.append(refs[at : at + count])
        at += count
    size = len(piece_counts)
    own_w = refs[at]
    others = refs[at + 1 : at + 2 * size - 1]
    at += 2 * size - 1 + aliased
    out_ref, held_ref, w_buf, acc_ref, held_sems, w_sems = refs[at:]
    step = pl.program_id(0)
    slots = w_buf.shape[0]
    half_width = w_buf.shape[2]

    def weight_copy(i):
        if i % size == 0:
            column = (parity_ref[0] ^ (i // size)) * half_width
            source = own_w.at[:, pl.ds(pl.multiple_of(column, HD), half_width)]
        else:
            source = others[i // size * (size - 1) + i % size - 1]
        return pltpu.make_async_copy(source, w_buf.at[i % slots], w_sems.at[i % slots])

    def held_copies(k):
        row = 0
        for number, part in enumerate(pieces[k]):
            count = part.shape[0]
            yield pltpu.make_async_copy(
                part, held_ref.at[k, pl.ds(row, count)], held_sems.at[k, number]
            )
            row += count

    @pl.when(step == 0)
    def _():
        for i in range(slots - 1):
            weight_copy(i).start()
            for copy in held_copies(i):
                copy.start()
        for k in range(slots - 1, size):
            for copy in held_copies(k):
                copy.start()

    for i in range(slots - 1, 2 * size):

        @pl.when(step == i - (slots - 1))
        def _():
            weight_copy(i).start()

    for k in range(size):

        @pl.when(step == k)
        def _():
            for copy in held_copies(k):
                copy.wait()

    for i in range(2 * size):

        @pl.when(step == i)
        def _():
            weight_copy(i).wait()

    k = lax.rem(step, size)
    product = jnp.dot(held_ref[k], w_buf[lax.rem(step, slots)], preferred_element_type=F32)

    @pl.when(k == 0)
    def _():
        acc_ref[...] = product

    @pl.when(jnp.logical_and(k > 0, k < size - 1))
    def _():
        acc_ref[...] += product

    @pl.when(k == size - 1)
    def _():
        update = acc_ref[...] + product
        out_ref[...] = (resid_ref[...].astype(F32) + gate_ref[...] * update).astype(BF16)


def output_projection(parity, resid, gate, pieces, own_w, mine, theirs, out_rows, chunk, into):
    head_cols, width = own_w.shape
    rows = resid.shape[0]
    size = len(pieces)
    half_width = width // 2
    parts = max(len(p) for p in pieces)
    flat = [part for group in pieces for part in group]
    alias = [] if into is None else [into]
    operands = [parity, resid, gate, *flat, own_w, *mine, *theirs, *alias]

    def column(j, parity):
        return (j // size) ^ parity[0]

    return pl.pallas_call(
        functools.partial(
            output_kernel,
            piece_counts=tuple(len(p) for p in pieces),
            aliased=len(alias),
        ),
        grid_spec=pltpu.PrefetchScalarGridSpec(
            num_scalar_prefetch=1,
            grid=(2 * size,),
            in_specs=[
                pl.BlockSpec((rows, half_width), lambda j, p: (0, column(j, p))),
                pl.BlockSpec((1, half_width), lambda j, p: (0, column(j, p))),
            ]
            + [ANY] * (len(operands) - 3),
            out_specs=pl.BlockSpec((rows, half_width), lambda j, p: (chunk, column(j, p))),
            scratch_shapes=[
                pltpu.VMEM((size, rows, head_cols), BF16),
                pltpu.VMEM((3, head_cols, half_width), BF16),
                pltpu.VMEM((rows, half_width), F32),
                pltpu.SemaphoreType.DMA((size, parts)),
                pltpu.SemaphoreType.DMA((3,)),
            ],
        ),
        out_shape=jax.ShapeDtypeStruct((out_rows, width), BF16),
        input_output_aliases={} if into is None else {len(operands) - 1: 0},
        compiler_params=compiler_params(36),
        cost_estimate=cost(
            2 * rows * width * head_cols * size,
            2 * (2 * rows * width + head_cols * width * size),
        ),
        name="output_projection",
    )(*operands)


def send(block, move, queue_size, tensor_size, frames=None):
    pairs = []
    for q in range(queue_size) if frames is None else frames:
        for t in range(tensor_size):
            to_q, to_t = move(q, t)
            pairs.append((q * tensor_size + t, to_q * tensor_size + to_t))
    return lax.ppermute(block, AXES, pairs)


def gather_pieces(block, queue_size, tensor_size, frames=None):
    half = tensor_size // 2

    def low(q, t):
        return q, t ^ 1

    def high(j):
        return lambda q, t: (q, (t // 2 - j) % half * 2 + t % 2)

    args = (queue_size, tensor_size, frames)
    rows = block.shape[0] // 2
    near = send(block, low, *args)
    far = [send(block, high(j), *args) for j in range(1, half)]
    pieces = [[block], [near]]
    for j in range(1, half):
        top = send(near[:rows], high(j), *args)
        bottom = send(far[j - 1][rows:], low, *args)
        pieces += [[far[j - 1]], [top, bottom]]
    return pieces


def body(
    latents, levels, mod_table, step_size, qkv_weight, q_gain, k_gain, out_weight, fresh_noise
):
    queue_size = lax.axis_size("queue")
    tensor_size = lax.axis_size("tensor")
    rows, width = latents.shape[1:]
    mesh_sizes = (queue_size, tensor_size)
    queue_index = lax.axis_index("queue")
    tensor_index = lax.axis_index("tensor")
    parity = (queue_index % 2).astype(jnp.int32)[None]

    def ahead(block):
        return send(block, lambda q, t: (q + 1, t), *mesh_sizes, range(queue_size - 1))

    def sibling(block):
        return send(block, lambda q, t: (q ^ 1, t), *mesh_sizes)

    def noise_pieces(block):
        return [
            send(block, lambda q, t: (q, (t - d) % tensor_size), *mesh_sizes, [0])
            for d in range(1, tensor_size)
        ]

    frame = ahead(latents[0])
    half_weight = lax.dynamic_slice(
        out_weight, (0, parity[0] * (width // 2)), (out_weight.shape[0], width // 2)
    )
    half_weight, fresh_noise, levels = lax.optimization_barrier(
        (half_weight, fresh_noise, levels)
    )
    gathered = gather_pieces(half_weight, *mesh_sizes)[1:]
    mine = [jnp.concatenate(parts, axis=0) if len(parts) > 1 else parts[0] for parts in gathered]
    theirs = [sibling(block) for block in mine]

    arriving_level = ahead(levels)[0]

    def modulation(level):
        row = lax.dynamic_slice(mod_table, (level, 0), (1, 3 * width)).astype(F32)
        rate = lax.dynamic_slice(step_size, (level,), (1,))[:, None]
        return row[:, :width], 1.0 + row[:, width : 2 * width], rate * row[:, 2 * width :]

    shift, scale1, gate = modulation(levels[0])
    arriving_gate = modulation(arriving_level)[2]
    info = jnp.stack([(queue_index == 0).astype(jnp.int32), tensor_index.astype(jnp.int32)])
    gains = jnp.stack([q_gain * SCORE_SCALE, k_gain])

    chunk_rows = rows // CHUNKS
    noise = noise_pieces(fresh_noise[0])
    frames = [(frame, c * chunk_rows) for c in range(CHUNKS)]
    for step_index in range(STEPS):
        final = step_index == STEPS - 1
        made = [
            project_qkv(
                info,
                scale1,
                shift,
                qkv_weight,
                gains,
                part,
                first_row,
                chunk_rows,
                (fresh_noise, step_index, noise, c * chunk_rows),
            )
            for c, (part, first_row) in enumerate(frames)
        ]
        kvs = [kv for kv, _, _ in made]
        earlier = [ahead(kv) for kv in kvs]
        own = [own_attention(query, kvs) for _, query, _ in made]
        attended = [
            earlier_attention(info, query, *parts, earlier)
            for (_, query, _), parts in zip(made, own)
        ]
        resid = [state for _, _, state in made]
        if final:
            pieces = [gather_pieces(block, *mesh_sizes) for block in attended]
            result = None
            for c in range(CHUNKS):
                result = output_projection(
                    parity, resid[c], gate, pieces[c], out_weight, mine, theirs, rows, c, result
                )
        else:
            attended = [ahead(block) for block in attended]
            attended, resid = lax.optimization_barrier((attended, resid))
            resid = [ahead(state) for state in resid]
            pieces = [
                gather_pieces(block, *mesh_sizes, range(1, queue_size)) for block in attended
            ]
            later_noise, _ = lax.optimization_barrier(
                (fresh_noise[step_index + 1], pieces[-1][1][0])
            )
            noise = noise_pieces(later_noise)
            frames = [
                (
                    output_projection(
                        parity,
                        resid[c],
                        arriving_gate,
                        pieces[c],
                        out_weight,
                        mine,
                        theirs,
                        chunk_rows,
                        0,
                        None,
                    ),
                    0,
                )
                for c in range(CHUNKS)
            ]
    return result[None]


def solution(mesh):
    return jax.shard_map(
        body,
        mesh=mesh,
        in_specs=(
            P("queue", None, None),
            P("queue"),
            P(),
            P(),
            P(None, None, "tensor"),
            P(),
            P(),
            P("tensor", None),
            P(None, "tensor", None),
        ),
        out_specs=P("queue", None, None),
        check_vma=False,
    )
```

time: 475 us -> 391 us (0.82)
  the two profiles are of different devices: /device:TPU:0 before, /device:TPU:1 now
where the time goes in v2:
time: 391 us; the launch traced here: 389 us
  Pallas kernels  173 us (44%)
  starting transfers between devices  106 us (27%)
  waiting for transfers between devices  77.4 us (20%)
  local copies, waits for them, and re-layouts  22.2 us (6%)
  other arithmetic  6.29 us (2%)
    ppermute x39, starting transfers between devices, send(): return lax.ppermute(block, AXES, pairs)  106 us
    pallas_call x4, Pallas kernels, project_qkv(): pl.pallas_call(functools.partial(qkv_kernel, tensor_size=tensor_size, fir...  77.5 us
    ppermute x39, waiting for transfers between devices, send(): return lax.ppermute(block, AXES, pairs)  77.4 us
    pallas_call x4, Pallas kernels, output_projection(): pl.pallas_call(functools.partial(output_kernel, piece_counts=tuple((len(p...  58.5 us
    pallas_call x4, Pallas kernels, earlier_attention(): pl.pallas_call(functools.partial(earlier_kernel, chunks=chunks), grid_spe...  20.7 us
    pallas_call x4, Pallas kernels, own_attention(): pl.pallas_call(functools.partial(own_kernel, chunks=chunks), grid=(head_c...  16.4 us
    unnamed x71, local copies, waits for them, and re-layouts  11.8 us
  transfers between devices with their start and end apart: 39, of which 11 were waited for; matrix products, arithmetic and copies ran while one was open for 4% of the time, Pallas kernels for 39%

profile of v2, /device:TPU:1, one launch (start us, length us, event | category | flops | bytes accessed | tf_op | source)
XLA Modules:
  0.0 388.8 jit_solution(3177542352747718306)
XLA Ops:
  0.0 4.6 %collective-permute-start = (bf16[768,3072]{1,0:T(8,128)(2,1)}, bf16[768,3072]{1,0:T(8,128)(2,1)}, u32[]{:S(2)}, u32[]{:S(2)}) collective-permute-start(bf16[768,3072]{1,0:T(8,128)(2,1)} %bitcast.20), channel_id=1, source_target_pairs={{0,4},{1,5},{2,6},{3,7},{4,8},{5,9},{6,10},{7,11},{8,12},{9,13},{1... | collective-permute-start | bytes 14155784 | tf_op jit(solution)/shard_map/ppermute | solution.py:404
  4.6 3.4 constant_dynamic-slice_fusion
  15.9 40.0 %collective-permute-done.9 = s32[1]{0:T(128)} collective-permute-done((s32[1]{0:T(128)}, s32[1]{0:T(128)}, u32[]{:S(2)}, u32[]{:S(2)}) %collective-permute-start.9) | collective-permute-done | bytes 36 | tf_op jit(solution)/shard_map/ppermute | solution.py:404
  57.7 3.2 collective-permute-done.14.refs_9_
  74.3 20.9 %norm_qkv.4 = (bf16[2,384,768]{2,1,0:T(8,128)(2,1)S(1)}, bf16[384,768]{1,0:T(8,128)(2,1)S(1)}, bf16[384,3072]{1,0:T(8,128)(2,1)}) custom-call(s32[2]{0:T(128)S(1)} %pad_add_fusion.refs_0_, f32[1,3072]{1,0:T(1,128)S(1)} %get-tuple-element.73.refs_1_, f32[1,3072]{1,0:T(1,128)S(1)} %get-tuple-element.72.refs_2_, bf16[3,3072,768]{2,1,0:T(8,128)(2,1)} %refs_3_.7, ...), custom_call_target="tpu_custom_call" | custom-call | flops 5435817984 | bytes 20643840 | tf_op jit(solution)/shard_map/norm_qkv/pallas_call | solution.py:119
  95.2 4.0 %collective-permute-start.4 = (bf16[2,384,768]{2,1,0:T(8,128)(2,1)S(1)}, bf16[2,384,768]{2,1,0:T(8,128)(2,1)S(1)}, u32[]{:S(2)}, u32[]{:S(2)}) collective-permute-start(bf16[2,384,768]{2,1,0:T(8,128)(2,1)S(1)} %get-tuple-element.40.refs_1_), channel_id=1, source_target_pairs={{0,4},{1,5},{2,6},{3,7},{4,8},{5,9},{6,10},{7,11},{8,12},{9,13},{1... | collective-permute-start | bytes 3538952 | tf_op jit(solution)/shard_map/ppermute | solution.py:404
  99.2 20.9 %norm_qkv.5 = (bf16[2,384,768]{2,1,0:T(8,128)(2,1)S(1)}, bf16[384,768]{1,0:T(8,128)(2,1)S(1)}, bf16[384,3072]{1,0:T(8,128)(2,1)}) custom-call(s32[2]{0:T(128)S(1)} %pad_add_fusion.refs_0_, f32[1,3072]{1,0:T(1,128)S(1)} %get-tuple-element.73.refs_1_, f32[1,3072]{1,0:T(1,128)S(1)} %get-tuple-element.72.refs_2_, bf16[3,3072,768]{2,1,0:T(8,128)(2,1)} %refs_3_.7, ...), custom_call_target="tpu_custom_call" | custom-call | flops 5435817984 | bytes 20643840 | tf_op jit(solution)/shard_map/norm_qkv/pallas_call | solution.py:119
  122.2 21.7 %collective-permute-start.18 = (bf16[768,1536]{1,0:T(8,128)(2,1)}, bf16[768,1536]{1,0:T(8,128)(2,1)S(1)}, u32[]{:S(2)}, u32[]{:S(2)}) collective-permute-start(bf16[768,1536]{1,0:T(8,128)(2,1)} %collective-permute-done.14.refs_9_), channel_id=1, source_target_pairs={{0,4},{1,5},{2,6},{3,7},{4,0},{5,1},{6,2},{7,3},{8,12},{9,13},{10,... | collective-permute-start | bytes 7077896 | tf_op jit(solution)/shard_map/ppermute | solution.py:404
  144.7 4.1 %own_frame.4 = (f32[384,768]{1,0:T(8,128)S(1)}, f32[384,768]{1,0:T(8,128)S(1)}, f32[384,768]{1,0:T(8,128)S(1)}) custom-call(bf16[384,768]{1,0:T(8,128)(2,1)S(1)} %get-tuple-element.39.refs_0_.refs_1_, bf16[2,384,768]{2,1,0:T(8,128)(2,1)S(1)} %get-tuple-element.40.refs_1_, bf16[2,384,768]{2,1,0:T(8,128)(2,1)S(1)} %get-tuple-element.41.refs_2_), custom_call_target="tpu_custom_call" | custom-call | flops 1811939328 | bytes 6488064 | tf_op jit(solution)/shard_map/own_frame/pallas_call | solution.py:205
  148.8 4.1 %own_frame.5 = (f32[384,768]{1,0:T(8,128)S(1)}, f32[384,768]{1,0:T(8,128)S(1)}, f32[384,768]{1,0:T(8,128)S(1)}) custom-call(bf16[384,768]{1,0:T(8,128)(2,1)S(1)} %get-tuple-element.45.refs_0_.refs_1_, bf16[2,384,768]{2,1,0:T(8,128)(2,1)S(1)} %get-tuple-element.40.refs_1_, bf16[2,384,768]{2,1,0:T(8,128)(2,1)S(1)} %get-tuple-element.41.refs_2_), custom_call_target="tpu_custom_call" | custom-call | flops 1811939328 | bytes 6488064 | tf_op jit(solution)/shard_map/own_frame/pallas_call | solution.py:205
  152.9 5.2 %earlier_frame.4 = bf16[384,768]{1,0:T(8,128)(2,1)S(1)} custom-call(s32[2]{0:T(128)S(1)} %pad_add_fusion.refs_0_, bf16[384,768]{1,0:T(8,128)(2,1)S(1)} %get-tuple-element.39.refs_0_.refs_1_, f32[384,768]{1,0:T(8,128)S(1)} %get-tuple-element.42.refs_2_, f32[384,768]{1,0:T(8,128)S(1)} %get-tuple-element.43.refs_3_, f32[384,768]{1,0:T(8,128)S(1)} %get-tuple-element.44.refs_4_, ...), custom_call_target="tpu_custom_call" | custom-call | flops 1811939328 | bytes 7077888 | tf_op jit(solution)/shard_map/earlier_frame/pallas_call | solution.py:252
  160.1 5.2 %earlier_frame.5 = bf16[384,768]{1,0:T(8,128)(2,1)S(1)} custom-call(s32[2]{0:T(128)S(1)} %pad_add_fusion.refs_0_, bf16[384,768]{1,0:T(8,128)(2,1)S(1)} %get-tuple-element.45.refs_0_.refs_1_, f32[384,768]{1,0:T(8,128)S(1)} %get-tuple-element.46.refs_2_, f32[384,768]{1,0:T(8,128)S(1)} %get-tuple-element.47.refs_3_, f32[384,768]{1,0:T(8,128)S(1)} %get-tuple-element.48.refs_4_, ...), custom_call_target="tpu_custom_call" | custom-call | flops 1811939328 | bytes 7077888 | tf_op jit(solution)/shard_map/earlier_frame/pallas_call | solution.py:252
  167.2 6.8 %collective-permute-done.7.refs_3_ = bf16[384,768]{1,0:T(8,128)(2,1)S(1)} collective-permute-done((bf16[384,768]{1,0:T(8,128)(2,1)S(1)}, bf16[384,768]{1,0:T(8,128)(2,1)S(1)}, u32[]{:S(2)}, u32[]{:S(2)}) %collective-permute-start.7) | collective-permute-done | bytes 589856 | tf_op jit(solution)/shard_map/ppermute | solution.py:404
  174.0 4.4 %collective-permute-start.24 = (bf16[384,3072]{1,0:T(8,128)(2,1)}, bf16[384,3072]{1,0:T(8,128)(2,1)}, u32[]{:S(2)}, u32[]{:S(2)}) collective-permute-start(bf16[384,3072]{1,0:T(8,128)(2,1)} %get-tuple-element.57), channel_id=1, source_target_pairs={{0,4},{1,5},{2,6},{3,7},{4,8},{5,9},{6,10},{7,11},{8,12},{9,13},{1... | collective-permute-start | bytes 7077896 | tf_op jit(solution)/shard_map/ppermute | solution.py:404
  182.5 4.0 %collective-permute-start.26 = (bf16[384,768]{1,0:T(8,128)(2,1)S(1)}, bf16[384,768]{1,0:T(8,128)(2,1)S(1)}, u32[]{:S(2)}, u32[]{:S(2)}) collective-permute-start(bf16[384,768]{1,0:T(8,128)(2,1)S(1)} %collective-permute-done.6.refs_3_), channel_id=1, source_target_pairs={{4,6},{5,7},{6,4},{7,5},{8,10},{9,11},{10,8},{11,9},{12,14},{13,15... | collective-permute-start | bytes 1769480 | tf_op jit(solution)/shard_map/ppermute | solution.py:404
  189.3 2.9 collective-permute-start.8
  193.8 3.4 collective-permute-start.11
  217.1 3.7 collective-permute-start.12
  227.2 14.6 %output_projection.5.refs_5_ = bf16[384,3072]{1,0:T(8,128)(2,1)S(1)} custom-call(s32[1]{0:T(128)} %bitcast.refs_0_, bf16[384,3072]{1,0:T(8,128)(2,1)} %collective-permute-done.24.refs_1_, f32[1,3072]{1,0:T(1,128)S(1)} %fusion.refs_2_, bf16[384,768]{1,0:T(8,128)(2,1)S(1)} %copy-done.27, bf16[384,768]{1,0:T(8,128)(2,1)S(1)} %copy-done.18, ...), custom_call_target="tpu_custom_call" | custom-call | flops 7247757312 | bytes 23592960 | tf_op jit(solution)/shard_map/output_projection/pallas_call | solution.py:364
  241.9 15.8 %collective-permute-start.13 = (bf16[192,768]{1,0:T(8,128)(2,1)S(1)}, bf16[192,768]{1,0:T(8,128)(2,1)S(1)}, u32[]{:S(2)}, u32[]{:S(2)}) collective-permute-start(bf16[192,768]{1,0:T(8,128)(2,1)S(1)} %slice.71), channel_id=1, source_target_pairs={{4,5},{5,4},{6,7},{7,6},{8,9},{9,8},{10,11},{11,10},{12,13},{13,12... | collective-permute-start | bytes 884744 | tf_op jit(solution)/shard_map/ppermute | solution.py:404
  257.8 17.9 %norm_qkv.7 = (bf16[2,384,768]{2,1,0:T(8,128)(2,1)S(1)}, bf16[384,768]{1,0:T(8,128)(2,1)S(1)}, bf16[384,3072]{1,0:T(8,128)(2,1)S(1)}) custom-call(s32[2]{0:T(128)S(1)} %pad_add_fusion.refs_0_, f32[1,3072]{1,0:T(1,128)S(1)} %copy-done.12, f32[1,3072]{1,0:T(1,128)S(1)} %get-tuple-element.72.refs_2_, bf16[3,3072,768]{2,1,0:T(8,128)(2,1)} %refs_3_.7, ...), custom_call_target="tpu_custom_call" | custom-call | flops 5435817984 | bytes 20643840 | tf_op jit(solution)/shard_map/norm_qkv/pallas_call | solution.py:119
  277.7 14.6 %output_projection.4.refs_5_ = bf16[384,3072]{1,0:T(8,128)(2,1)S(1)} custom-call(s32[1]{0:T(128)} %bitcast.refs_0_, bf16[384,3072]{1,0:T(8,128)(2,1)} %collective-permute-done.8.refs_1_, f32[1,3072]{1,0:T(1,128)S(1)} %fusion.refs_2_, bf16[384,768]{1,0:T(8,128)(2,1)S(1)} %copy-done.25, bf16[384,768]{1,0:T(8,128)(2,1)S(1)} %copy-done.14, ...), custom_call_target="tpu_custom_call" | custom-call | flops 7247757312 | bytes 23592960 | tf_op jit(solution)/shard_map/output_projection/pallas_call | solution.py:364
  292.3 17.9 %norm_qkv.6 = (bf16[2,384,768]{2,1,0:T(8,128)(2,1)S(1)}, bf16[384,768]{1,0:T(8,128)(2,1)S(1)}, bf16[384,3072]{1,0:T(8,128)(2,1)S(1)}) custom-call(s32[2]{0:T(128)S(1)} %pad_add_fusion.refs_0_, f32[1,3072]{1,0:T(1,128)S(1)} %copy-done.12, f32[1,3072]{1,0:T(1,128)S(1)} %get-tuple-element.72.refs_2_, bf16[3,3072,768]{2,1,0:T(8,128)(2,1)} %refs_3_.7, ...), custom_call_target="tpu_custom_call" | custom-call | flops 5435817984 | bytes 20643840 | tf_op jit(solution)/shard_map/norm_qkv/pallas_call | solution.py:119
  312.3 4.1 %own_frame.7 = (f32[384,768]{1,0:T(8,128)S(1)}, f32[384,768]{1,0:T(8,128)S(1)}, f32[384,768]{1,0:T(8,128)S(1)}) custom-call(bf16[384,768]{1,0:T(8,128)(2,1)S(1)} %get-tuple-element.65.refs_0_.refs_1_, bf16[2,384,768]{2,1,0:T(8,128)(2,1)S(1)} %get-tuple-element.59.refs_1_, bf16[2,384,768]{2,1,0:T(8,128)(2,1)S(1)} %get-tuple-element.60.refs_2_), custom_call_target="tpu_custom_call" | custom-call | flops 1811939328 | bytes 6488064 | tf_op jit(solution)/shard_map/own_frame/pallas_call | solution.py:205
  316.4 8.8 %collective-permute-done.30.refs_6_ = bf16[2,384,768]{2,1,0:T(8,128)(2,1)S(1)} collective-permute-done((bf16[2,384,768]{2,1,0:T(8,128)(2,1)S(1)}, bf16[2,384,768]{2,1,0:T(8,128)(2,1)S(1)}, u32[]{:S(2)}, u32[]{:S(2)}) %collective-permute-start.30) | collective-permute-done | bytes 1179680 | tf_op jit(solution)/shard_map/ppermute | solution.py:404
  325.2 5.2 %earlier_frame.7.refs_3_ = bf16[384,768]{1,0:T(8,128)(2,1)S(1)} custom-call(s32[2]{0:T(128)S(1)} %pad_add_fusion.refs_0_, bf16[384,768]{1,0:T(8,128)(2,1)S(1)} %get-tuple-element.65.refs_0_.refs_1_, f32[384,768]{1,0:T(8,128)S(1)} %get-tuple-element.66.refs_2_, f32[384,768]{1,0:T(8,128)S(1)} %get-tuple-element.67.refs_3_, ...), custom_call_target="tpu_custom_call" | custom-call | flops 1811939328 | bytes 7077888 | tf_op jit(solution)/shard_map/earlier_frame/pallas_call | solution.py:252
  330.8 4.1 %own_frame.6 = (f32[384,768]{1,0:T(8,128)S(1)}, f32[384,768]{1,0:T(8,128)S(1)}, f32[384,768]{1,0:T(8,128)S(1)}) custom-call(bf16[384,768]{1,0:T(8,128)(2,1)S(1)} %get-tuple-element.56.refs_0_.refs_1_, bf16[2,384,768]{2,1,0:T(8,128)(2,1)S(1)} %get-tuple-element.59.refs_1_, bf16[2,384,768]{2,1,0:T(8,128)(2,1)S(1)} %get-tuple-element.60.refs_2_), custom_call_target="tpu_custom_call" | custom-call | flops 1811939328 | bytes 6488064 | tf_op jit(solution)/shard_map/own_frame/pallas_call | solution.py:205
  334.9 5.2 %earlier_frame.6.refs_3_ = bf16[384,768]{1,0:T(8,128)(2,1)S(1)} custom-call(s32[2]{0:T(128)S(1)} %pad_add_fusion.refs_0_, bf16[384,768]{1,0:T(8,128)(2,1)S(1)} %get-tuple-element.56.refs_0_.refs_1_, f32[384,768]{1,0:T(8,128)S(1)} %get-tuple-element.61.refs_2_, f32[384,768]{1,0:T(8,128)S(1)} %get-tuple-element.62.refs_3_, ...), custom_call_target="tpu_custom_call" | custom-call | flops 1811939328 | bytes 7077888 | tf_op jit(solution)/shard_map/earlier_frame/pallas_call | solution.py:252
  342.7 2.9 collective-permute-done.35.refs_4_
  347.4 7.4 %collective-permute-done.31.refs_4_ = bf16[384,768]{1,0:T(8,128)(2,1)S(1)} collective-permute-done((bf16[384,768]{1,0:T(8,128)(2,1)S(1)}, bf16[384,768]{1,0:T(8,128)(2,1)S(1)}, u32[]{:S(2)}, u32[]{:S(2)}) %collective-permute-start.31) | collective-permute-done | bytes 589856 | tf_op jit(solution)/shard_map/ppermute | solution.py:404
  359.2 14.7 %output_projection.6.refs_15_ = bf16[768,3072]{1,0:T(8,128)(2,1)} custom-call(s32[1]{0:T(128)} %bitcast.refs_0_, bf16[384,3072]{1,0:T(8,128)(2,1)S(1)} %get-tuple-element.64.refs_1_, f32[1,3072]{1,0:T(1,128)S(1)} %copy-done.21, bf16[384,768]{1,0:T(8,128)(2,1)S(1)} %earlier_frame.7.refs_3_, bf16[384,768]{1,0:T(8,128)(2,1)S(1)} %collective-permute-done.35.refs_4_, ...), custom_call_target="tpu_custom_call" | custom-call | flops 7247757312 | bytes 23592960 | tf_op jit(solution)/shard_map/output_projection/pallas_call | solution.py:364
  374.0 14.6 %output_projection.7 = bf16[768,3072]{1,0:T(8,128)(2,1)} custom-call(s32[1]{0:T(128)} %bitcast.refs_0_, bf16[384,3072]{1,0:T(8,128)(2,1)S(1)} %copy-done.10, f32[1,3072]{1,0:T(1,128)S(1)} %copy-done.21, bf16[384,768]{1,0:T(8,128)(2,1)S(1)} %earlier_frame.6.refs_3_, ...), custom_call_target="tpu_custom_call", output_to_operand_aliasing={{}: (15, {})} | custom-call | flops 7247757312 | bytes 23592960 | tf_op jit(solution)/shard_map/output_projection/pallas_call | solution.py:364
  (153 shorter events, 75.4 us)
Async XLA Ops:
  0.0 74.3 %collective-permute-start = (bf16[768,3072]{1,0:T(8,128)(2,1)}, bf16[768,3072]{1,0:T(8,128)(2,1)}, u32[]{:S(2)}, u32[]{:S(2)}) collective-permute-start(bf16[768,3072]{1,0:T(8,128)(2,1)} %bitcast.20), channel_id=1, source_target_pairs={{0,4},{1,5},{2,6},{3,7},{4,8},{5,9},{6,10},{7,11},{8,12},{9,13},{1... | collective-permute-start | bytes 14155784 | tf_op jit(solution)/shard_map/ppermute | solution.py:404
  8.0 52.9 %collective-permute-start.14 = (bf16[768,1536]{1,0:T(8,128)(2,1)}, bf16[768,1536]{1,0:T(8,128)(2,1)}, u32[]{:S(2)}, u32[]{:S(2)}) collective-permute-start(bf16[768,1536]{1,0:T(8,128)(2,1)} %constant_dynamic-slice_fusion), channel_id=1, source_target_pairs={{0,1},{1,0},{2,3},{3,2},{4,5},{5,4},{6,7},{7,6},{8,9},{9,8},{10,11... | collective-permute-start | bytes 7077896 | tf_op jit(solution)/shard_map/ppermute | solution.py:404
  9.2 61.7 %collective-permute-start.15 = (bf16[768,1536]{1,0:T(8,128)(2,1)}, bf16[768,1536]{1,0:T(8,128)(2,1)}, u32[]{:S(2)}, u32[]{:S(2)}) collective-permute-start(bf16[768,1536]{1,0:T(8,128)(2,1)} %constant_dynamic-slice_fusion), channel_id=1, source_target_pairs={{0,2},{1,3},{2,0},{3,1},{4,6},{5,7},{6,4},{7,5},{8,10},{9,11},{10,... | collective-permute-start | bytes 7077896 | tf_op jit(solution)/shard_map/ppermute | solution.py:404
  10.5 45.5 %collective-permute-start.9 = (s32[1]{0:T(128)}, s32[1]{0:T(128)}, u32[]{:S(2)}, u32[]{:S(2)}) collective-permute-start(s32[1]{0:T(128)} %param.10), channel_id=1, source_target_pairs={{0,4},{1,5},{2,6},{3,7},{4,8},{5,9},{6,10},{7,11},{8,12},{9,13},{1... | collective-permute-start | bytes 20 | tf_op jit(solution)/shard_map/ppermute | solution.py:404
  14.5 58.5 %collective-permute-start.1 = (bf16[192,3072]{1,0:T(8,128)(2,1)}, bf16[192,3072]{1,0:T(8,128)(2,1)S(1)}, u32[]{:S(2)}, u32[]{:S(2)}) collective-permute-start(bf16[192,3072]{1,0:T(8,128)(2,1)} %get-tuple-element.70), channel_id=1, source_target_pairs={{0,3},{1,0},{2,1},{3,2}} | collective-permute-start | bytes 3538952 | tf_op jit(solution)/shard_map/ppermute | solution.py:404
  56.0 18.3 %collective-permute-start.2 = (bf16[192,3072]{1,0:T(8,128)(2,1)}, bf16[192,3072]{1,0:T(8,128)(2,1)}, u32[]{:S(2)}, u32[]{:S(2)}) collective-permute-start(bf16[192,3072]{1,0:T(8,128)(2,1)} %get-tuple-element.70), channel_id=1, source_target_pairs={{0,2},{1,3},{2,0},{3,1}} | collective-permute-start | bytes 3538952 | tf_op jit(solution)/shard_map/ppermute | solution.py:404
  60.9 13.4 %collective-permute-start.3 = (bf16[192,3072]{1,0:T(8,128)(2,1)}, bf16[192,3072]{1,0:T(8,128)(2,1)}, u32[]{:S(2)}, u32[]{:S(2)}) collective-permute-start(bf16[192,3072]{1,0:T(8,128)(2,1)} %get-tuple-element.70), channel_id=1, source_target_pairs={{0,1},{1,2},{2,3},{3,0}} | collective-permute-start | bytes 3538952 | tf_op jit(solution)/shard_map/ppermute | solution.py:404
  70.9 73.0 %collective-permute-start.16 = (bf16[384,1536]{1,0:T(8,128)(2,1)S(1)}, bf16[384,1536]{1,0:T(8,128)(2,1)S(1)}, u32[]{:S(2)}, u32[]{:S(2)}) collective-permute-start(bf16[384,1536]{1,0:T(8,128)(2,1)S(1)} %slice.72), channel_id=1, source_target_pairs={{0,2},{1,3},{2,0},{3,1},{4,6},{5,7},{6,4},{7,5},{8,10},{9,11},{10,... | collective-permute-start | bytes 3538952 | tf_op jit(solution)/shard_map/ppermute | solution.py:404
  73.0 71.1 %collective-permute-start.17 = (bf16[384,1536]{1,0:T(8,128)(2,1)S(1)}, bf16[384,1536]{1,0:T(8,128)(2,1)S(1)}, u32[]{:S(2)}, u32[]{:S(2)}) collective-permute-start(bf16[384,1536]{1,0:T(8,128)(2,1)S(1)} %slice.73), channel_id=1, source_target_pairs={{0,1},{1,0},{2,3},{3,2},{4,5},{5,4},{6,7},{7,6},{8,9},{9,8},{10,11... | collective-permute-start | bytes 3538952 | tf_op jit(solution)/shard_map/ppermute | solution.py:404
  95.2 57.7 %collective-permute-start.4 = (bf16[2,384,768]{2,1,0:T(8,128)(2,1)S(1)}, bf16[2,384,768]{2,1,0:T(8,128)(2,1)S(1)}, u32[]{:S(2)}, u32[]{:S(2)}) collective-permute-start(bf16[2,384,768]{2,1,0:T(8,128)(2,1)S(1)} %get-tuple-element.40.refs_1_), channel_id=1, source_target_pairs={{0,4},{1,5},{2,6},{3,7},{4,8},{5,9},{6,10},{7,11},{8,12},{9,13},{1... | collective-permute-start | bytes 3538952 | tf_op jit(solution)/shard_map/ppermute | solution.py:404
  120.1 32.9 %collective-permute-start.5 = (bf16[2,384,768]{2,1,0:T(8,128)(2,1)S(1)}, bf16[2,384,768]{2,1,0:T(8,128)(2,1)S(1)}, u32[]{:S(2)}, u32[]{:S(2)}) collective-permute-start(bf16[2,384,768]{2,1,0:T(8,128)(2,1)S(1)} %get-tuple-element.41.refs_2_), channel_id=1, source_target_pairs={{0,4},{1,5},{2,6},{3,7},{4,8},{5,9},{6,10},{7,11},{8,12},{9,13},{1... | collective-permute-start | bytes 3538952 | tf_op jit(solution)/shard_map/ppermute | solution.py:404
  122.2 58.9 %collective-permute-start.18 = (bf16[768,1536]{1,0:T(8,128)(2,1)}, bf16[768,1536]{1,0:T(8,128)(2,1)S(1)}, u32[]{:S(2)}, u32[]{:S(2)}) collective-permute-start(bf16[768,1536]{1,0:T(8,128)(2,1)} %collective-permute-done.14.refs_9_), channel_id=1, source_target_pairs={{0,4},{1,5},{2,6},{3,7},{4,0},{5,1},{6,2},{7,3},{8,12},{9,13},{10,... | collective-permute-start | bytes 7077896 | tf_op jit(solution)/shard_map/ppermute | solution.py:404
  143.9 43.4 %collective-permute-start.19 = (bf16[768,1536]{1,0:T(8,128)(2,1)}, bf16[768,1536]{1,0:T(8,128)(2,1)S(1)}, u32[]{:S(2)}, u32[]{:S(2)}) collective-permute-start(bf16[768,1536]{1,0:T(8,128)(2,1)} %collective-permute-done.15.refs_10_), channel_id=1, source_target_pairs={{0,4},{1,5},{2,6},{3,7},{4,0},{5,1},{6,2},{7,3},{8,12},{9,13},{10,... | collective-permute-start | bytes 7077896 | tf_op jit(solution)/shard_map/ppermute | solution.py:404
  144.2 53.8 %collective-permute-start.20 = (bf16[768,1536]{1,0:T(8,128)(2,1)S(1)}, bf16[768,1536]{1,0:T(8,128)(2,1)S(1)}, u32[]{:S(2)}, u32[]{:S(2)}) collective-permute-start(bf16[768,1536]{1,0:T(8,128)(2,1)S(1)} %constant_dynamic-update-slice_fusion.refs_11_), channel_id=1, source_target_pairs={{0,4},{1,5},{2,6},{3,7},{4,0},{5,1},{6,2},{7,3},{8,12},{9,13},{10,... | collective-permute-start | bytes 7077896 | tf_op jit(solution)/shard_map/ppermute | solution.py:404
  174.0 43.2 %collective-permute-start.24 = (bf16[384,3072]{1,0:T(8,128)(2,1)}, bf16[384,3072]{1,0:T(8,128)(2,1)}, u32[]{:S(2)}, u32[]{:S(2)}) collective-permute-start(bf16[384,3072]{1,0:T(8,128)(2,1)} %get-tuple-element.57), channel_id=1, source_target_pairs={{0,4},{1,5},{2,6},{3,7},{4,8},{5,9},{6,10},{7,11},{8,12},{9,13},{1... | collective-permute-start | bytes 7077896 | tf_op jit(solution)/shard_map/ppermute | solution.py:404
  187.4 12.6 %collective-permute-start.10 = (bf16[384,768]{1,0:T(8,128)(2,1)S(1)}, bf16[384,768]{1,0:T(8,128)(2,1)S(1)}, u32[]{:S(2)}, u32[]{:S(2)}) collective-permute-start(bf16[384,768]{1,0:T(8,128)(2,1)S(1)} %collective-permute-done.7.refs_3_), channel_id=1, source_target_pairs={{4,5},{5,4},{6,7},{7,6},{8,9},{9,8},{10,11},{11,10},{12,13},{13,12... | collective-permute-start | bytes 1769480 | tf_op jit(solution)/shard_map/ppermute | solution.py:404
  189.3 88.3 %collective-permute-start.8 = (bf16[384,3072]{1,0:T(8,128)(2,1)}, bf16[384,3072]{1,0:T(8,128)(2,1)}, u32[]{:S(2)}, u32[]{:S(2)}) collective-permute-start(bf16[384,3072]{1,0:T(8,128)(2,1)} %get-tuple-element.51), channel_id=1, source_target_pairs={{0,4},{1,5},{2,6},{3,7},{4,8},{5,9},{6,10},{7,11},{8,12},{9,13},{1... | collective-permute-start | bytes 7077896 | tf_op jit(solution)/shard_map/ppermute | solution.py:404
  205.6 36.3 %collective-permute-start.21 = (bf16[192,3072]{1,0:T(8,128)(2,1)}, bf16[192,3072]{1,0:T(8,128)(2,1)S(1)}, u32[]{:S(2)}, u32[]{:S(2)}) collective-permute-start(bf16[192,3072]{1,0:T(8,128)(2,1)} %get-tuple-element.54), channel_id=1, source_target_pairs={{0,3},{1,0},{2,1},{3,2}} | collective-permute-start | bytes 3538952 | tf_op jit(solution)/shard_map/ppermute | solution.py:404
  208.9 48.8 %collective-permute-start.22 = (bf16[192,3072]{1,0:T(8,128)(2,1)}, bf16[192,3072]{1,0:T(8,128)(2,1)}, u32[]{:S(2)}, u32[]{:S(2)}) collective-permute-start(bf16[192,3072]{1,0:T(8,128)(2,1)} %get-tuple-element.54), channel_id=1, source_target_pairs={{0,2},{1,3},{2,0},{3,1}} | collective-permute-start | bytes 3538952 | tf_op jit(solution)/shard_map/ppermute | solution.py:404
  211.8 45.9 %collective-permute-start.23 = (bf16[192,3072]{1,0:T(8,128)(2,1)}, bf16[192,3072]{1,0:T(8,128)(2,1)}, u32[]{:S(2)}, u32[]{:S(2)}) collective-permute-start(bf16[192,3072]{1,0:T(8,128)(2,1)} %get-tuple-element.54), channel_id=1, source_target_pairs={{0,1},{1,2},{2,3},{3,0}} | collective-permute-start | bytes 3538952 | tf_op jit(solution)/shard_map/ppermute | solution.py:404
  217.1 60.4 %collective-permute-start.12 = (bf16[192,768]{1,0:T(8,128)(2,1)S(1)}, bf16[192,768]{1,0:T(8,128)(2,1)S(1)}, u32[]{:S(2)}, u32[]{:S(2)}) collective-permute-start(bf16[192,768]{1,0:T(8,128)(2,1)S(1)} %slice.70), channel_id=1, source_target_pairs={{4,6},{5,7},{6,4},{7,5},{8,10},{9,11},{10,8},{11,9},{12,14},{13,15... | collective-permute-start | bytes 884744 | tf_op jit(solution)/shard_map/ppermute | solution.py:404
  241.9 35.7 %collective-permute-start.13 = (bf16[192,768]{1,0:T(8,128)(2,1)S(1)}, bf16[192,768]{1,0:T(8,128)(2,1)S(1)}, u32[]{:S(2)}, u32[]{:S(2)}) collective-permute-start(bf16[192,768]{1,0:T(8,128)(2,1)S(1)} %slice.71), channel_id=1, source_target_pairs={{4,5},{5,4},{6,7},{7,6},{8,9},{9,8},{10,11},{11,10},{12,13},{13,12... | collective-permute-start | bytes 884744 | tf_op jit(solution)/shard_map/ppermute | solution.py:404
  275.6 40.8 %collective-permute-start.29 = (bf16[2,384,768]{2,1,0:T(8,128)(2,1)S(1)}, bf16[2,384,768]{2,1,0:T(8,128)(2,1)S(1)}, u32[]{:S(2)}, u32[]{:S(2)}) collective-permute-start(bf16[2,384,768]{2,1,0:T(8,128)(2,1)S(1)} %get-tuple-element.59.refs_1_), channel_id=1, source_target_pairs={{0,4},{1,5},{2,6},{3,7},{4,8},{5,9},{6,10},{7,11},{8,12},{9,13},{1... | collective-permute-start | bytes 3538952 | tf_op jit(solution)/shard_map/ppermute | solution.py:404
  310.2 15.1 %collective-permute-start.30 = (bf16[2,384,768]{2,1,0:T(8,128)(2,1)S(1)}, bf16[2,384,768]{2,1,0:T(8,128)(2,1)S(1)}, u32[]{:S(2)}, u32[]{:S(2)}) collective-permute-start(bf16[2,384,768]{2,1,0:T(8,128)(2,1)S(1)} %get-tuple-element.60.refs_2_), channel_id=1, source_target_pairs={{0,4},{1,5},{2,6},{3,7},{4,8},{5,9},{6,10},{7,11},{8,12},{9,13},{1... | collective-permute-start | bytes 3538952 | tf_op jit(solution)/shard_map/ppermute | solution.py:404
  330.4 15.2 %collective-permute-start.35 = (bf16[384,768]{1,0:T(8,128)(2,1)S(1)}, bf16[384,768]{1,0:T(8,128)(2,1)S(1)}, u32[]{:S(2)}, u32[]{:S(2)}) collective-permute-start(bf16[384,768]{1,0:T(8,128)(2,1)S(1)} %earlier_frame.7.refs_3_), channel_id=1, source_target_pairs={{0,1},{1,0},{2,3},{3,2},{4,5},{5,4},{6,7},{7,6},{8,9},{9,8},{10,11... | collective-permute-start | bytes 1769480 | tf_op jit(solution)/shard_map/ppermute | solution.py:404
  330.6 15.6 %collective-permute-start.36 = (bf16[384,768]{1,0:T(8,128)(2,1)S(1)}, bf16[384,768]{1,0:T(8,128)(2,1)S(1)}, u32[]{:S(2)}, u32[]{:S(2)}) collective-permute-start(bf16[384,768]{1,0:T(8,128)(2,1)S(1)} %earlier_frame.7.refs_3_), channel_id=1, source_target_pairs={{0,2},{1,3},{2,0},{3,1},{4,6},{5,7},{6,4},{7,5},{8,10},{9,11},{10,... | collective-permute-start | bytes 1769480 | tf_op jit(solution)/shard_map/ppermute | solution.py:404
  340.1 14.7 %collective-permute-start.31 = (bf16[384,768]{1,0:T(8,128)(2,1)S(1)}, bf16[384,768]{1,0:T(8,128)(2,1)S(1)}, u32[]{:S(2)}, u32[]{:S(2)}) collective-permute-start(bf16[384,768]{1,0:T(8,128)(2,1)S(1)} %earlier_frame.6.refs_3_), channel_id=1, source_target_pairs={{0,1},{1,0},{2,3},{3,2},{4,5},{5,4},{6,7},{7,6},{8,9},{9,8},{10,11... | collective-permute-start | bytes 1769480 | tf_op jit(solution)/shard_map/ppermute | solution.py:404
  341.4 14.8 %collective-permute-start.32 = (bf16[384,768]{1,0:T(8,128)(2,1)S(1)}, bf16[384,768]{1,0:T(8,128)(2,1)S(1)}, u32[]{:S(2)}, u32[]{:S(2)}) collective-permute-start(bf16[384,768]{1,0:T(8,128)(2,1)S(1)} %earlier_frame.6.refs_3_), channel_id=1, source_target_pairs={{0,2},{1,3},{2,0},{3,1},{4,6},{5,7},{6,4},{7,5},{8,10},{9,11},{10,... | collective-permute-start | bytes 1769480 | tf_op jit(solution)/shard_map/ppermute | solution.py:404
  345.6 13.6 %collective-permute-start.37 = (bf16[192,768]{1,0:T(8,128)(2,1)S(1)}, bf16[192,768]{1,0:T(8,128)(2,1)S(1)}, u32[]{:S(2)}, u32[]{:S(2)}) collective-permute-start(bf16[192,768]{1,0:T(8,128)(2,1)S(1)} %slice.79), channel_id=1, source_target_pairs={{0,2},{1,3},{2,0},{3,1},{4,6},{5,7},{6,4},{7,5},{8,10},{9,11},{10,... | collective-permute-start | bytes 884744 | tf_op jit(solution)/shard_map/ppermute | solution.py:404
  346.2 13.0 %collective-permute-start.38 = (bf16[192,768]{1,0:T(8,128)(2,1)S(1)}, bf16[192,768]{1,0:T(8,128)(2,1)S(1)}, u32[]{:S(2)}, u32[]{:S(2)}) collective-permute-start(bf16[192,768]{1,0:T(8,128)(2,1)S(1)} %slice.80), channel_id=1, source_target_pairs={{0,1},{1,0},{2,3},{3,2},{4,5},{5,4},{6,7},{7,6},{8,9},{9,8},{10,11... | collective-permute-start | bytes 884744 | tf_op jit(solution)/shard_map/ppermute | solution.py:404
  354.8 19.1 %collective-permute-start.33 = (bf16[192,768]{1,0:T(8,128)(2,1)S(1)}, bf16[192,768]{1,0:T(8,128)(2,1)S(1)}, u32[]{:S(2)}, u32[]{:S(2)}) collective-permute-start(bf16[192,768]{1,0:T(8,128)(2,1)S(1)} %slice.77), channel_id=1, source_target_pairs={{0,2},{1,3},{2,0},{3,1},{4,6},{5,7},{6,4},{7,5},{8,10},{9,11},{10,... | collective-permute-start | bytes 884744 | tf_op jit(solution)/shard_map/ppermute | solution.py:404
  356.2 17.7 %collective-permute-start.34 = (bf16[192,768]{1,0:T(8,128)(2,1)S(1)}, bf16[192,768]{1,0:T(8,128)(2,1)S(1)}, u32[]{:S(2)}, u32[]{:S(2)}) collective-permute-start(bf16[192,768]{1,0:T(8,128)(2,1)S(1)} %slice.78), channel_id=1, source_target_pairs={{0,1},{1,0},{2,3},{3,2},{4,5},{5,4},{6,7},{7,6},{8,9},{9,8},{10,11... | collective-permute-start | bytes 884744 | tf_op jit(solution)/shard_map/ppermute | solution.py:404
  (42 other events, 621.7 us)

commit v3 on v2

--- a/solution.py
+++ b/solution.py
@@ -23,23 +23,49 @@
     return pltpu.CompilerParams(vmem_limit_bytes=mib * 2**20)
 
 
+def in_hbm(array):
+    return pltpu.with_memory_space_constraint(array, pltpu.HBM)
+
+
 def cost(flops, nbytes, transcendentals=0):
     return pl.CostEstimate(
         flops=int(flops), bytes_accessed=int(nbytes), transcendentals=int(transcendentals)
     )
 
 
-def qkv_kernel(*refs, tensor_size, first_row, noise_first_row, noise_step, k_blocks):
-    info_ref, scale_ref, shift_ref, w_ref, gain_ref, z_any, noise_any = refs[:7]
+def head_normalized(values, gain):
+    heads = []
+    for h in range(values.shape[1] // HD):
+        head = values[:, h * HD : (h + 1) * HD]
+        mean = jnp.mean(head * head, axis=-1, keepdims=True)
+        heads.append((head * lax.rsqrt(mean + EPS) * gain).astype(BF16))
+    return heads[0] if len(heads) == 1 else jnp.concatenate(heads, axis=1)
+
+
+def qkv_kernel(*refs, tensor_size, first_row, noise_first_row, noise_step, blocks):
+    info_ref, scale_ref, shift_ref, gain_ref, w_any, z_any, noise_any = refs[:7]
     piece_refs = refs[7 : 7 + tensor_size - 1]
-    kv_ref, query_ref, state_ref, normed_ref, acc_ref, sem = refs[6 + tensor_size :]
-    part, block = pl.program_id(0), pl.program_id(1)
+    kv_ref, query_ref, state_ref, normed_ref, w_ref, sem, w_sems = refs[6 + tensor_size :]
+    step = pl.program_id(0)
     rows, width = state_ref.shape
     piece_rows = noise_any.shape[1]
-    block_width = width // k_blocks
-
-    @pl.when(jnp.logical_and(part == 0, block == 0))
-    def _():
+    cols = query_ref.shape[1]
+    splits = w_sems.shape[1]
+    split_rows = width // splits
+
+    def weight_copies(part):
+        for i in range(splits):
+            at = pl.ds(i * split_rows, split_rows)
+            yield pltpu.make_async_copy(
+                w_any.at[part, at], w_ref.at[part, at], w_sems.at[part, i]
+            )
+
+    @pl.when(step == 0)
+    def _():
+        for part in (1, 2, 0):
+            for copy in weight_copies(part):
+                copy.start()
+
         @pl.when(info_ref[0] == 0)
         def _():
             copy = pltpu.make_async_copy(z_any.at[pl.ds(first_row, rows)], state_ref, sem.at[0])
@@ -54,12 +80,14 @@
                 away = lax.rem(row // piece_rows + tensor_size - info_ref[1], tensor_size)
                 inside = pl.ds(row % piece_rows, unit)
                 for d in range(tensor_size):
-                    source = noise_any.at[noise_step] if d == 0 else piece_refs[d - 1]
+                    source = noise_any if d == 0 else piece_refs[d - 1]
 
                     @pl.when(away == d)
                     def _():
                         copy = pltpu.make_async_copy(
-                            source.at[inside], state_ref.at[pl.ds(b * unit, unit)], sem.at[0]
+                            source.at[noise_step, inside],
+                            state_ref.at[pl.ds(b * unit, unit)],
+                            sem.at[0],
                         )
                         copy.start()
                         copy.wait()
@@ -69,53 +97,46 @@
             state = state_ref[at, :].astype(F32)
             mean = jnp.mean(state * state, axis=-1, keepdims=True)
             state = state * lax.rsqrt(mean + EPS) * scale_ref[...] + shift_ref[...]
-            state = state.astype(BF16)
-            for k in range(k_blocks):
-                normed_ref[k, at, :] = state[:, k * block_width : (k + 1) * block_width]
+            normed_ref[at, :] = state.astype(BF16)
             return carry
 
         lax.fori_loop(0, rows // 16, one, 0)
 
-    product = jnp.dot(normed_ref[block], w_ref[0], preferred_element_type=F32)
-
-    @pl.when(block == 0)
-    def _():
-        acc_ref[...] = product
-
-    @pl.when(jnp.logical_and(block > 0, block < k_blocks - 1))
-    def _():
-        acc_ref[...] += product
-
-    @pl.when(block == k_blocks - 1)
-    def _():
-        def normalized(gain):
-            for h in range(product.shape[1] // HD):
-                at = slice(h * HD, (h + 1) * HD)
-                head = acc_ref[:, at] + product[:, at]
-                mean = jnp.mean(head * head, axis=-1, keepdims=True)
-                yield at, (head * lax.rsqrt(mean + EPS) * gain).astype(BF16)
-
-        @pl.when(part == 0)
+    for order, part in enumerate((1, 2, 0)):
+
+        @pl.when(step == order * blocks)
         def _():
-            for at, head in normalized(gain_ref[1:2]):
-                kv_ref[0, :, at] = head
-
-        @pl.when(part == 1)
-        def _():
-            kv_ref[0] = (acc_ref[...] + product).astype(BF16)
-
-        @pl.when(part == 2)
-        def _():
-            for at, head in normalized(gain_ref[0:1]):
-                query_ref[:, at] = head
+            for copy in weight_copies(part):
+                copy.wait()
+
+    def project(part):
+        at = pl.ds(pl.multiple_of(lax.rem(step, blocks) * cols, HD), cols)
+        return jnp.dot(normed_ref[...], w_ref[part, :, at], preferred_element_type=F32)
+
+    @pl.when(step < blocks)
+    def _():
+        kv_ref[0] = head_normalized(project(1), gain_ref[1:2])
+
+    @pl.when(jnp.logical_and(step >= blocks, step < 2 * blocks))
+    def _():
+        kv_ref[0] = project(2).astype(BF16)
+
+    @pl.when(step >= 2 * blocks)
+    def _():
+        query_ref[...] = head_normalized(project(0), gain_ref[0:1])
 
 
 def project_qkv(info, scale1, shift, qkv_weight, gains, z, first_row, rows, noise):
     width, head_cols = qkv_weight.shape[1:]
     noise_all, noise_step, pieces, noise_first_row = noise
     tensor_size = len(pieces) + 1
-    k_blocks = 4
-    block_width = width // k_blocks
+    cols = 256 if head_cols % 256 == 0 else HD
+    blocks = head_cols // cols
+
+    def kv_block(j, i):
+        j = jnp.minimum(j, 2 * blocks - 1)
+        return j // blocks, 0, j % blocks
+
     return pl.pallas_call(
         functools.partial(
             qkv_kernel,
@@ -123,41 +144,41 @@
             first_row=first_row,
             noise_first_row=noise_first_row,
             noise_step=noise_step,
-            k_blocks=k_blocks,
+            blocks=blocks,
         ),
         grid_spec=pltpu.PrefetchScalarGridSpec(
             num_scalar_prefetch=1,
-            grid=(3, k_blocks),
+            grid=(3 * blocks,),
             in_specs=[
-                pl.BlockSpec((1, width), lambda p, k, i: (0, 0)),
-                pl.BlockSpec((1, width), lambda p, k, i: (0, 0)),
-                pl.BlockSpec((1, block_width, head_cols), lambda p, k, i: ((p + 1) % 3, k, 0)),
-                pl.BlockSpec((2, HD), lambda p, k, i: (0, 0)),
+                pl.BlockSpec((1, width), lambda j, i: (0, 0)),
+                pl.BlockSpec((1, width), lambda j, i: (0, 0)),
+                pl.BlockSpec((2, HD), lambda j, i: (0, 0)),
             ]
-            + [ANY] * (1 + tensor_size),
+            + [ANY] * (2 + tensor_size),
             out_specs=[
-                pl.BlockSpec((1, rows, head_cols), lambda p, k, i: (jnp.minimum(p, 1), 0, 0)),
-                pl.BlockSpec((rows, head_cols), lambda p, k, i: (0, 0)),
-                pl.BlockSpec((rows, width), lambda p, k, i: (0, 0)),
+                pl.BlockSpec((1, rows, cols), kv_block),
+                pl.BlockSpec((rows, cols), lambda j, i: (0, jnp.maximum(j - 2 * blocks, 0))),
+                pl.BlockSpec((rows, width), lambda j, i: (0, 0)),
             ],
             scratch_shapes=[
-                pltpu.VMEM((k_blocks, rows, block_width), BF16),
-                pltpu.VMEM((rows, head_cols), F32),
+                pltpu.VMEM((rows, width), BF16),
+                pltpu.VMEM(qkv_weight.shape, BF16),
                 pltpu.SemaphoreType.DMA((1,)),
+                pltpu.SemaphoreType.DMA((3, 4)),
             ],
         ),
         out_shape=[
             jax.ShapeDtypeStruct((2, rows, head_cols), BF16),
             jax.ShapeDtypeStruct((rows, head_cols), BF16),
-            jax.ShapeDtypeStruct((rows, width), BF16),
+            pltpu.HBM((rows, width), BF16),
         ],
-        compiler_params=compiler_params(32),
+        compiler_params=compiler_params(36),
         cost_estimate=cost(
             6 * rows * width * head_cols,
-            4 * rows * width + 6 * width * head_cols + 6 * rows * head_cols,
+            4 * rows * width + 6 * rows * head_cols + 6 * width * head_cols,
         ),
         name="norm_qkv",
-    )(info, scale1, shift, qkv_weight, gains, z, noise_all, *pieces)
+    )(info, scale1, shift, gains, *[in_hbm(a) for a in (qkv_weight, z, noise_all, *pieces)])
 
 
 def attend_parts(query, kv_refs, at):
@@ -208,7 +229,7 @@
         in_specs=[by_heads] + [pl.BlockSpec((2, key_rows, cols), lambda j: (0, 0, j))] * chunks,
         out_specs=[by_heads] * 3,
         out_shape=[jax.ShapeDtypeStruct((rows, head_cols), F32)] * 3,
-        compiler_params=compiler_params(32),
+        compiler_params=compiler_params(24),
         cost_estimate=cost(
             8 * rows * keys * head_cols,
             14 * rows * head_cols + 4 * keys * head_cols,
@@ -259,7 +280,7 @@
             out_specs=by_heads,
         ),
         out_shape=jax.ShapeDtypeStruct((rows, head_cols), BF16),
-        compiler_params=compiler_params(32),
+        compiler_params=compiler_params(24),
         cost_estimate=cost(
             8 * rows * keys * head_cols,
             16 * rows * head_cols + 4 * keys * head_cols,
@@ -269,7 +290,7 @@
     )(info, query, acc, top, total, *kvs)
 
 
-def output_kernel(*refs, piece_counts, aliased):
+def output_kernel(*refs, piece_counts, half_blocks, aliased):
     parity_ref, resid_ref, gate_ref = refs[:3]
     at = 3
     pieces = []
@@ -279,19 +300,18 @@
     size = len(piece_counts)
     own_w = refs[at]
     others = refs[at + 1 : at + 2 * size - 1]
-    at += 2 * size - 1 + aliased
-    out_ref, held_ref, w_buf, acc_ref, held_sems, w_sems = refs[at:]
+    out_ref, held_ref, w_ref, held_sems, w_sems = refs[at + 2 * size - 1 + aliased :]
     step = pl.program_id(0)
-    slots = w_buf.shape[0]
-    half_width = w_buf.shape[2]
-
-    def weight_copy(i):
-        if i % size == 0:
-            column = (parity_ref[0] ^ (i // size)) * half_width
+    cols = out_ref.shape[1]
+    head_cols, half_width = w_ref.shape[2:]
+
+    def weight_copy(half, k):
+        if k == 0:
+            column = (parity_ref[0] ^ half) * half_width
             source = own_w.at[:, pl.ds(pl.multiple_of(column, HD), half_width)]
         else:
-            source = others[i // size * (size - 1) + i % size - 1]
-        return pltpu.make_async_copy(source, w_buf.at[i % slots], w_sems.at[i % slots])
+            source = others[half * (size - 1) + k - 1]
+        return pltpu.make_async_copy(source, w_ref.at[half, k], w_sems.at[half, k])
 
     def held_copies(k):
         row = 0
@@ -304,92 +324,75 @@
 
     @pl.when(step == 0)
     def _():
-        for i in range(slots - 1):
-            weight_copy(i).start()
-            for copy in held_copies(i):
-                copy.start()
-        for k in range(slots - 1, size):
+        for k in range(size):
             for copy in held_copies(k):
                 copy.start()
-
-    for i in range(slots - 1, 2 * size):
-
-        @pl.when(step == i - (slots - 1))
-        def _():
-            weight_copy(i).start()
-
-    for k in range(size):
-
-        @pl.when(step == k)
-        def _():
+        for half in range(2):
+            for k in range(size):
+                weight_copy(half, k).start()
+        for k in range(size):
             for copy in held_copies(k):
                 copy.wait()
 
-    for i in range(2 * size):
-
-        @pl.when(step == i)
+    for half in range(2):
+
+        @pl.when(step == half * half_blocks)
         def _():
-            weight_copy(i).wait()
-
-    k = lax.rem(step, size)
-    product = jnp.dot(held_ref[k], w_buf[lax.rem(step, slots)], preferred_element_type=F32)
-
-    @pl.when(k == 0)
-    def _():
-        acc_ref[...] = product
-
-    @pl.when(jnp.logical_and(k > 0, k < size - 1))
-    def _():
-        acc_ref[...] += product
-
-    @pl.when(k == size - 1)
-    def _():
-        update = acc_ref[...] + product
-        out_ref[...] = (resid_ref[...].astype(F32) + gate_ref[...] * update).astype(BF16)
+            for k in range(size):
+                weight_copy(half, k).wait()
+
+    half = step // half_blocks
+    inside = pl.ds(pl.multiple_of(lax.rem(step, half_blocks) * cols, HD), cols)
+    update = jnp.dot(held_ref[0], w_ref[half, 0, :, inside], preferred_element_type=F32)
+    for k in range(1, size):
+        update += jnp.dot(held_ref[k], w_ref[half, k, :, inside], preferred_element_type=F32)
+    out_ref[...] = (resid_ref[...].astype(F32) + gate_ref[...] * update).astype(BF16)
 
 
 def output_projection(parity, resid, gate, pieces, own_w, mine, theirs, out_rows, chunk, into):
     head_cols, width = own_w.shape
     rows = resid.shape[0]
     size = len(pieces)
-    half_width = width // 2
+    cols = 256 if (width // 2) % 256 == 0 else HD
+    half_blocks = width // 2 // cols
     parts = max(len(p) for p in pieces)
     flat = [part for group in pieces for part in group]
     alias = [] if into is None else [into]
-    operands = [parity, resid, gate, *flat, own_w, *mine, *theirs, *alias]
+    held = [in_hbm(array) for array in [own_w, *mine, *theirs, *alias]]
+    operands = [parity, resid, gate, *flat, *held]
 
     def column(j, parity):
-        return (j // size) ^ parity[0]
+        return ((j // half_blocks) ^ parity[0]) * half_blocks + j % half_blocks
 
     return pl.pallas_call(
         functools.partial(
             output_kernel,
             piece_counts=tuple(len(p) for p in pieces),
+            half_blocks=half_blocks,
             aliased=len(alias),
         ),
         grid_spec=pltpu.PrefetchScalarGridSpec(
             num_scalar_prefetch=1,
-            grid=(2 * size,),
+            grid=(2 * half_blocks,),
             in_specs=[
-                pl.BlockSpec((rows, half_width), lambda j, p: (0, column(j, p))),
-                pl.BlockSpec((1, half_width), lambda j, p: (0, column(j, p))),
+                pl.BlockSpec((rows, cols), lambda j, p: (0, column(j, p))),
+                pl.BlockSpec((1, cols), lambda j, p: (0, column(j, p))),
             ]
             + [ANY] * (len(operands) - 3),
-            out_specs=pl.BlockSpec((rows, half_width), lambda j, p: (chunk, column(j, p))),
+            out_specs=pl.BlockSpec((rows, cols), lambda j, p: (chunk, column(j, p))),
             scratch_shapes=[
                 pltpu.VMEM((size, rows, head_cols), BF16),
-                pltpu.VMEM((3, head_cols, half_width), BF16),
-                pltpu.VMEM((rows, half_width), F32),
+                pltpu.VMEM((2, size, head_cols, width // 2), BF16),
                 pltpu.SemaphoreType.DMA((size, parts)),
-                pltpu.SemaphoreType.DMA((3,)),
+                pltpu.SemaphoreType.DMA((2, size)),
             ],
         ),
-        out_shape=jax.ShapeDtypeStruct((out_rows, width), BF16),
+        out_shape=pltpu.HBM((out_rows, width), BF16),
         input_output_aliases={} if into is None else {len(operands) - 1: 0},
         compiler_params=compiler_params(36),
         cost_estimate=cost(
             2 * rows * width * head_cols * size,
-            2 * (2 * rows * width + head_cols * width * size),
+            4 * rows * width + 2 * head_cols * width * size,
         ),
         name="output_projection",
     )(*operands)
@@ -404,7 +407,7 @@
     return lax.ppermute(block, AXES, pairs)
 
 
-def gather_pieces(block, queue_size, tensor_size, frames=None):
+def gather_pieces(block, queue_size, tensor_size, frames=None, after=None):
     half = tensor_size // 2
 
     def low(q, t):
@@ -416,6 +419,8 @@
     args = (queue_size, tensor_size, frames)
     rows = block.shape[0] // 2
     near = send(block, low, *args)
+    if after is not None:
+        block, _ = lax.optimization_barrier((block, after))
     far = [send(block, high(j), *args) for j in range(1, half)]
     pieces = [[block], [near]]
     for j in range(1, half):
@@ -449,17 +454,13 @@
         ]
 
     frame = ahead(latents[0])
+    noise = noise_pieces(fresh_noise)
     half_weight = lax.dynamic_slice(
         out_weight, (0, parity[0] * (width // 2)), (out_weight.shape[0], width // 2)
     )
-    half_weight, fresh_noise, levels = lax.optimization_barrier(
-        (half_weight, fresh_noise, levels)
-    )
-    gathered = gather_pieces(half_weight, *mesh_sizes)[1:]
+    gathered = gather_pieces(half_weight, *mesh_sizes, after=noise)[1:]
     mine = [jnp.concatenate(parts, axis=0) if len(parts) > 1 else parts[0] for parts in gathered]
     theirs = [sibling(block) for block in mine]
-
-    arriving_level = ahead(levels)[0]
 
     def modulation(level):
         row = lax.dynamic_slice(mod_table, (level, 0), (1, 3 * width)).astype(F32)
@@ -467,12 +468,10 @@
         return row[:, :width], 1.0 + row[:, width : 2 * width], rate * row[:, 2 * width :]
 
     shift, scale1, gate = modulation(levels[0])
-    arriving_gate = modulation(arriving_level)[2]
     info = jnp.stack([(queue_index == 0).astype(jnp.int32), tensor_index.astype(jnp.int32)])
     gains = jnp.stack([q_gain * SCORE_SCALE, k_gain])
 
     chunk_rows = rows // CHUNKS
-    noise = noise_pieces(fresh_noise[0])
     frames = [(frame, c * chunk_rows) for c in range(CHUNKS)]
     for step_index in range(STEPS):
         final = step_index == STEPS - 1
@@ -512,10 +511,8 @@
             pieces = [
                 gather_pieces(block, *mesh_sizes, range(1, queue_size)) for block in attended
             ]
-            later_noise, _ = lax.optimization_barrier(
-                (fresh_noise[step_index + 1], pieces[-1][1][0])
-            )
-            noise = noise_pieces(later_noise)
+            sent_level, _ = lax.optimization_barrier((levels, kvs))
+            arriving_gate = modulation(ahead(sent_level)[0])[2]
             frames = [
                 (
                     output_projection(

time: 391 us -> 398 us (1.018)
  the two profiles are of different devices: /device:TPU:1 before, /device:TPU:12 now
where the time goes in v3:
time: 398 us; the launch traced here: 397 us
  Pallas kernels  183 us (46%)
  waiting for transfers between devices  134 us (34%)
  starting transfers between devices  63.9 us (16%)
  local copies, waits for them, and re-layouts  9.3 us (2%)
    ppermute x36, waiting for transfers between devices, send(): return lax.ppermute(block, AXES, pairs)  134 us
    pallas_call x4, Pallas kernels, project_qkv(): pl.pallas_call(functools.partial(qkv_kernel, tensor_size=tensor_size, fir...  78.8 us
    pallas_call x4, Pallas kernels, output_projection(): pl.pallas_call(functools.partial(output_kernel, piece_counts=tuple((len(p...  67.2 us
    ppermute x36, starting transfers between devices, send(): return lax.ppermute(block, AXES, pairs)  63.9 us
    pallas_call x4, Pallas kernels, earlier_attention(): pl.pallas_call(functools.partial(earlier_kernel, chunks=chunks), grid_spe...  20.7 us
    pallas_call x4, Pallas kernels, own_attention(): pl.pallas_call(functools.partial(own_kernel, chunks=chunks), grid=(head_c...  16.4 us
  transfers between devices with their start and end apart: 36, of which 14 were waited for; matrix products, arithmetic and copies ran while one was open for 3% of the time, Pallas kernels for 41%

profile of v3, /device:TPU:12, one launch (start us, length us, event | category | flops | bytes accessed | tf_op | source)
XLA Modules:
  0.0 396.7 jit_solution(9796753590145051217)
XLA Ops:
  7.0 3.3 constant_dynamic-slice_fusion
  15.4 40.3 %collective-permute-done.refs_5_ = bf16[768,3072]{1,0:T(8,128)(2,1)} collective-permute-done((bf16[768,3072]{1,0:T(8,128)(2,1)}, bf16[768,3072]{1,0:T(8,128)(2,1)}, u32[]{:S(2)}, u32[]{:S(2)}) %collective-permute-start) | collective-permute-done | bytes 4718624 | tf_op jit(solution)/shard_map/ppermute | solution.py:407
  55.7 19.7 %norm_qkv.4 = (bf16[2,384,768]{2,1,0:T(8,128)(2,1)S(1)}, bf16[384,768]{1,0:T(8,128)(2,1)S(1)}, bf16[384,3072]{1,0:T(8,128)(2,1)}) custom-call(s32[2]{0:T(128)S(1)} %pad_add_fusion.refs_0_, f32[1,3072]{1,0:T(1,128)S(1)} %get-tuple-element.67.refs_1_, f32[1,3072]{1,0:T(1,128)S(1)} %get-tuple-element.66.refs_2_, f32[2,128]{1,0:T(2,128)S(1)} %pad_maximum_fusion.refs_3_, ...), custom_call_target="tpu_custom_call" | custom-call | flops 5435817984 | bytes 20643840 | tf_op jit(solution)/shard_map/norm_qkv/pallas_call | solution.py:140
  77.4 19.7 %norm_qkv.5 = (bf16[2,384,768]{2,1,0:T(8,128)(2,1)S(1)}, bf16[384,768]{1,0:T(8,128)(2,1)S(1)}, bf16[384,3072]{1,0:T(8,128)(2,1)}) custom-call(s32[2]{0:T(128)S(1)} %pad_add_fusion.refs_0_, f32[1,3072]{1,0:T(1,128)S(1)} %get-tuple-element.67.refs_1_, f32[1,3072]{1,0:T(1,128)S(1)} %get-tuple-element.66.refs_2_, f32[2,128]{1,0:T(2,128)S(1)} %pad_maximum_fusion.refs_3_, ...), custom_call_target="tpu_custom_call" | custom-call | flops 5435817984 | bytes 20643840 | tf_op jit(solution)/shard_map/norm_qkv/pallas_call | solution.py:140
  97.1 3.6 collective-permute-start.5
  104.5 4.1 %own_frame.4 = (f32[384,768]{1,0:T(8,128)S(1)}, f32[384,768]{1,0:T(8,128)S(1)}, f32[384,768]{1,0:T(8,128)S(1)}) custom-call(bf16[384,768]{1,0:T(8,128)(2,1)S(1)} %get-tuple-element.35.refs_0_.refs_1_, bf16[2,384,768]{2,1,0:T(8,128)(2,1)S(1)} %get-tuple-element.36.refs_1_, bf16[2,384,768]{2,1,0:T(8,128)(2,1)S(1)} %get-tuple-element.37.refs_2_), custom_call_target="tpu_custom_call" | custom-call | flops 1811939328 | bytes 6488064 | tf_op jit(solution)/shard_map/own_frame/pallas_call | solution.py:226
  108.6 4.1 %own_frame.5 = (f32[384,768]{1,0:T(8,128)S(1)}, f32[384,768]{1,0:T(8,128)S(1)}, f32[384,768]{1,0:T(8,128)S(1)}) custom-call(bf16[384,768]{1,0:T(8,128)(2,1)S(1)} %get-tuple-element.41.refs_0_.refs_1_, bf16[2,384,768]{2,1,0:T(8,128)(2,1)S(1)} %get-tuple-element.36.refs_1_, bf16[2,384,768]{2,1,0:T(8,128)(2,1)S(1)} %get-tuple-element.37.refs_2_), custom_call_target="tpu_custom_call" | custom-call | flops 1811939328 | bytes 6488064 | tf_op jit(solution)/shard_map/own_frame/pallas_call | solution.py:226
  114.6 5.2 %earlier_frame.4 = bf16[384,768]{1,0:T(8,128)(2,1)S(1)} custom-call(s32[2]{0:T(128)S(1)} %pad_add_fusion.refs_0_, bf16[384,768]{1,0:T(8,128)(2,1)S(1)} %get-tuple-element.35.refs_0_.refs_1_, f32[384,768]{1,0:T(8,128)S(1)} %get-tuple-element.38.refs_2_, f32[384,768]{1,0:T(8,128)S(1)} %get-tuple-element.39.refs_3_, f32[384,768]{1,0:T(8,128)S(1)} %get-tuple-element.40.refs_4_, ...), custom_call_target="tpu_custom_call" | custom-call | flops 1811939328 | bytes 7077888 | tf_op jit(solution)/shard_map/earlier_frame/pallas_call | solution.py:273
  121.7 5.2 %earlier_frame.5 = bf16[384,768]{1,0:T(8,128)(2,1)S(1)} custom-call(s32[2]{0:T(128)S(1)} %pad_add_fusion.refs_0_, bf16[384,768]{1,0:T(8,128)(2,1)S(1)} %get-tuple-element.41.refs_0_.refs_1_, f32[384,768]{1,0:T(8,128)S(1)} %get-tuple-element.42.refs_2_, f32[384,768]{1,0:T(8,128)S(1)} %get-tuple-element.43.refs_3_, f32[384,768]{1,0:T(8,128)S(1)} %get-tuple-element.44.refs_4_, ...), custom_call_target="tpu_custom_call" | custom-call | flops 1811939328 | bytes 7077888 | tf_op jit(solution)/shard_map/earlier_frame/pallas_call | solution.py:273
  126.9 3.1 collective-permute-done.16
  135.8 23.4 %collective-permute-done.6.refs_3_ = bf16[384,768]{1,0:T(8,128)(2,1)S(1)} collective-permute-done((bf16[384,768]{1,0:T(8,128)(2,1)S(1)}, bf16[384,768]{1,0:T(8,128)(2,1)S(1)}, u32[]{:S(2)}, u32[]{:S(2)}) %collective-permute-start.6) | collective-permute-done | bytes 589856 | tf_op jit(solution)/shard_map/ppermute | solution.py:407
  159.3 7.1 %collective-permute-done.7.refs_3_ = bf16[384,768]{1,0:T(8,128)(2,1)S(1)} collective-permute-done((bf16[384,768]{1,0:T(8,128)(2,1)S(1)}, bf16[384,768]{1,0:T(8,128)(2,1)S(1)}, u32[]{:S(2)}, u32[]{:S(2)}) %collective-permute-start.7) | collective-permute-done | bytes 589856 | tf_op jit(solution)/shard_map/ppermute | solution.py:407
  172.4 24.5 %collective-permute-done.9 = s32[1]{0:T(128)} collective-permute-done((s32[1]{0:T(128)}, s32[1]{0:T(128)}, u32[]{:S(2)}, u32[]{:S(2)}) %collective-permute-start.9) | collective-permute-done | bytes 36 | tf_op jit(solution)/shard_map/ppermute | solution.py:407
  196.9 3.6 collective-permute-start.23
  205.8 6.1 %collective-permute-done.23.refs_5_ = bf16[384,768]{1,0:T(8,128)(2,1)S(1)} collective-permute-done((bf16[384,768]{1,0:T(8,128)(2,1)S(1)}, bf16[384,768]{1,0:T(8,128)(2,1)S(1)}, u32[]{:S(2)}, u32[]{:S(2)}) %collective-permute-start.23) | collective-permute-done | bytes 589856 | tf_op jit(solution)/shard_map/ppermute | solution.py:407
  211.9 3.4 collective-permute-start.11
  217.9 2.7 collective-permute-start.24
  220.6 3.0 collective-permute-done.11.refs_5_
  227.3 3.9 collective-permute-start.12
  234.5 18.0 %output_projection.5.refs_5_ = bf16[384,3072]{1,0:T(8,128)(2,1)} custom-call(s32[1]{0:T(128)} %bitcast.refs_0_, bf16[384,3072]{1,0:T(8,128)(2,1)} %collective-permute-done.21.refs_1_, f32[1,3072]{1,0:T(1,128)S(1)} %fusion.refs_2_, bf16[384,768]{1,0:T(8,128)(2,1)S(1)} %copy-done.3, bf16[384,768]{1,0:T(8,128)(2,1)S(1)} %collective-permute-done.22.refs_4_, ...), custom_call_target="tpu_custom_call" | custom-call | flops 7247757312 | bytes 23592960 | tf_op jit(solution)/shard_map/output_projection/pallas_call | solution.py:367
  252.5 19.7 %norm_qkv.7 = (bf16[2,384,768]{2,1,0:T(8,128)(2,1)S(1)}, bf16[384,768]{1,0:T(8,128)(2,1)S(1)}, bf16[384,3072]{1,0:T(8,128)(2,1)}) custom-call(s32[2]{0:T(128)S(1)} %pad_add_fusion.refs_0_, f32[1,3072]{1,0:T(1,128)S(1)} %get-tuple-element.67.refs_1_, f32[1,3072]{1,0:T(1,128)S(1)} %get-tuple-element.66.refs_2_, f32[2,128]{1,0:T(2,128)S(1)} %pad_maximum_fusion.refs_3_, ...), custom_call_target="tpu_custom_call" | custom-call | flops 5435817984 | bytes 20643840 | tf_op jit(solution)/shard_map/norm_qkv/pallas_call | solution.py:140
  274.2 18.0 %output_projection.4.refs_5_ = bf16[384,3072]{1,0:T(8,128)(2,1)} custom-call(s32[1]{0:T(128)} %bitcast.refs_0_, bf16[384,3072]{1,0:T(8,128)(2,1)} %collective-permute-done.8.refs_1_, f32[1,3072]{1,0:T(1,128)S(1)} %fusion.refs_2_, bf16[384,768]{1,0:T(8,128)(2,1)S(1)} %collective-permute-done.7.refs_3_, bf16[384,768]{1,0:T(8,128)(2,1)S(1)} %collective-permute-done.10.refs_4_, ...), custom_call_target="tpu_custom_call" | custom-call | flops 7247757312 | bytes 23592960 | tf_op jit(solution)/shard_map/output_projection/pallas_call | solution.py:367
  292.2 19.7 %norm_qkv.6 = (bf16[2,384,768]{2,1,0:T(8,128)(2,1)S(1)}, bf16[384,768]{1,0:T(8,128)(2,1)S(1)}, bf16[384,3072]{1,0:T(8,128)(2,1)}) custom-call(s32[2]{0:T(128)S(1)} %pad_add_fusion.refs_0_, f32[1,3072]{1,0:T(1,128)S(1)} %get-tuple-element.67.refs_1_, f32[1,3072]{1,0:T(1,128)S(1)} %get-tuple-element.66.refs_2_, f32[2,128]{1,0:T(2,128)S(1)} %pad_maximum_fusion.refs_3_, ...), custom_call_target="tpu_custom_call" | custom-call | flops 5435817984 | bytes 20643840 | tf_op jit(solution)/shard_map/norm_qkv/pallas_call | solution.py:140
  314.1 4.1 %own_frame.7 = (f32[384,768]{1,0:T(8,128)S(1)}, f32[384,768]{1,0:T(8,128)S(1)}, f32[384,768]{1,0:T(8,128)S(1)}) custom-call(bf16[384,768]{1,0:T(8,128)(2,1)S(1)} %get-tuple-element.61.refs_0_.refs_1_, bf16[2,384,768]{2,1,0:T(8,128)(2,1)S(1)} %get-tuple-element.55.refs_1_, bf16[2,384,768]{2,1,0:T(8,128)(2,1)S(1)} %get-tuple-element.56.refs_2_), custom_call_target="tpu_custom_call" | custom-call | flops 1811939328 | bytes 6488064 | tf_op jit(solution)/shard_map/own_frame/pallas_call | solution.py:226
  318.2 11.3 %collective-permute-done.27.refs_6_ = bf16[2,384,768]{2,1,0:T(8,128)(2,1)S(1)} collective-permute-done((bf16[2,384,768]{2,1,0:T(8,128)(2,1)S(1)}, bf16[2,384,768]{2,1,0:T(8,128)(2,1)S(1)}, u32[]{:S(2)}, u32[]{:S(2)}) %collective-permute-start.27) | collective-permute-done | bytes 1179680 | tf_op jit(solution)/shard_map/ppermute | solution.py:407
  329.5 5.2 %earlier_frame.7.refs_3_ = bf16[384,768]{1,0:T(8,128)(2,1)S(1)} custom-call(s32[2]{0:T(128)S(1)} %pad_add_fusion.refs_0_, bf16[384,768]{1,0:T(8,128)(2,1)S(1)} %get-tuple-element.61.refs_0_.refs_1_, f32[384,768]{1,0:T(8,128)S(1)} %get-tuple-element.62.refs_2_, f32[384,768]{1,0:T(8,128)S(1)} %get-tuple-element.63.refs_3_, ...), custom_call_target="tpu_custom_call" | custom-call | flops 1811939328 | bytes 7077888 | tf_op jit(solution)/shard_map/earlier_frame/pallas_call | solution.py:273
  337.9 4.1 %own_frame.6 = (f32[384,768]{1,0:T(8,128)S(1)}, f32[384,768]{1,0:T(8,128)S(1)}, f32[384,768]{1,0:T(8,128)S(1)}) custom-call(bf16[384,768]{1,0:T(8,128)(2,1)S(1)} %get-tuple-element.52.refs_0_.refs_1_, bf16[2,384,768]{2,1,0:T(8,128)(2,1)S(1)} %get-tuple-element.55.refs_1_, bf16[2,384,768]{2,1,0:T(8,128)(2,1)S(1)} %get-tuple-element.56.refs_2_), custom_call_target="tpu_custom_call" | custom-call | flops 1811939328 | bytes 6488064 | tf_op jit(solution)/shard_map/own_frame/pallas_call | solution.py:226
  342.0 5.2 %earlier_frame.6.refs_3_ = bf16[384,768]{1,0:T(8,128)(2,1)S(1)} custom-call(s32[2]{0:T(128)S(1)} %pad_add_fusion.refs_0_, bf16[384,768]{1,0:T(8,128)(2,1)S(1)} %get-tuple-element.52.refs_0_.refs_1_, f32[384,768]{1,0:T(8,128)S(1)} %get-tuple-element.57.refs_2_, f32[384,768]{1,0:T(8,128)S(1)} %get-tuple-element.58.refs_3_, ...), custom_call_target="tpu_custom_call" | custom-call | flops 1811939328 | bytes 7077888 | tf_op jit(solution)/shard_map/earlier_frame/pallas_call | solution.py:273
  348.1 2.9 collective-permute-done.32.refs_4_
  354.4 7.4 %collective-permute-done.28.refs_4_ = bf16[384,768]{1,0:T(8,128)(2,1)S(1)} collective-permute-done((bf16[384,768]{1,0:T(8,128)(2,1)S(1)}, bf16[384,768]{1,0:T(8,128)(2,1)S(1)}, u32[]{:S(2)}, u32[]{:S(2)}) %collective-permute-start.28) | collective-permute-done | bytes 589856 | tf_op jit(solution)/shard_map/ppermute | solution.py:407
  365.3 15.6 %output_projection.6.refs_15_ = bf16[768,3072]{1,0:T(8,128)(2,1)} custom-call(s32[1]{0:T(128)} %bitcast.refs_0_, bf16[384,3072]{1,0:T(8,128)(2,1)S(1)} %copy-done, f32[1,3072]{1,0:T(1,128)S(1)} %get-tuple-element.65.refs_2_, bf16[384,768]{1,0:T(8,128)(2,1)S(1)} %earlier_frame.7.refs_3_, bf16[384,768]{1,0:T(8,128)(2,1)S(1)} %collective-permute-done.32.refs_4_, ...), custom_call_target="tpu_custom_call" | custom-call | flops 7247757312 | bytes 23592960 | tf_op jit(solution)/shard_map/output_projection/pallas_call | solution.py:367
  380.9 15.6 %output_projection.7 = bf16[768,3072]{1,0:T(8,128)(2,1)} custom-call(s32[1]{0:T(128)} %bitcast.refs_0_, bf16[384,3072]{1,0:T(8,128)(2,1)S(1)} %copy-done.1, f32[1,3072]{1,0:T(1,128)S(1)} %get-tuple-element.65.refs_2_, bf16[384,768]{1,0:T(8,128)(2,1)S(1)} %earlier_frame.6.refs_3_, ...), custom_call_target="tpu_custom_call", output_to_operand_aliasing={{}: (15, {})} | custom-call | flops 7247757312 | bytes 23592960 | tf_op jit(solution)/shard_map/output_projection/pallas_call | solution.py:367
  (99 shorter events, 60.9 us)
Async XLA Ops:
  0.0 55.7 %collective-permute-start = (bf16[768,3072]{1,0:T(8,128)(2,1)}, bf16[768,3072]{1,0:T(8,128)(2,1)}, u32[]{:S(2)}, u32[]{:S(2)}) collective-permute-start(bf16[768,3072]{1,0:T(8,128)(2,1)} %bitcast.16), channel_id=1, source_target_pairs={{0,4},{1,5},{2,6},{3,7},{4,8},{5,9},{6,10},{7,11},{8,12},{9,13},{1... | collective-permute-start | bytes 14155784 | tf_op jit(solution)/shard_map/ppermute | solution.py:407
  1.9 11.5 %collective-permute-start.1 = (bf16[2,192,3072]{2,1,0:T(8,128)(2,1)}, bf16[2,192,3072]{2,1,0:T(8,128)(2,1)S(1)}, u32[]{:S(2)}, u32[]{:S(2)}) collective-permute-start(bf16[2,192,3072]{2,1,0:T(8,128)(2,1)} %refs_6_.7), channel_id=1, source_target_pairs={{0,3},{1,0},{2,1},{3,2}} | collective-permute-start | bytes 7077896 | tf_op jit(solution)/shard_map/ppermute | solution.py:407
  10.2 90.4 %collective-permute-start.14 = (bf16[768,1536]{1,0:T(8,128)(2,1)}, bf16[768,1536]{1,0:T(8,128)(2,1)}, u32[]{:S(2)}, u32[]{:S(2)}) collective-permute-start(bf16[768,1536]{1,0:T(8,128)(2,1)} %constant_dynamic-slice_fusion), channel_id=1, source_target_pairs={{0,1},{1,0},{2,3},{3,2},{4,5},{5,4},{6,7},{7,6},{8,9},{9,8},{10,11... | collective-permute-start | bytes 7077896 | tf_op jit(solution)/shard_map/ppermute | solution.py:407
  13.4 89.2 %collective-permute-start.15 = (bf16[768,1536]{1,0:T(8,128)(2,1)}, bf16[768,1536]{1,0:T(8,128)(2,1)S(1)}, u32[]{:S(2)}, u32[]{:S(2)}) collective-permute-start(bf16[768,1536]{1,0:T(8,128)(2,1)} %constant_dynamic-slice_fusion), channel_id=1, source_target_pairs={{0,2},{1,3},{2,0},{3,1},{4,6},{5,7},{6,4},{7,5},{8,10},{9,11},{10,... | collective-permute-start | bytes 7077896 | tf_op jit(solution)/shard_map/ppermute | solution.py:407
  75.4 28.8 %collective-permute-start.4 = (bf16[2,384,768]{2,1,0:T(8,128)(2,1)S(1)}, bf16[2,384,768]{2,1,0:T(8,128)(2,1)S(1)}, u32[]{:S(2)}, u32[]{:S(2)}) collective-permute-start(bf16[2,384,768]{2,1,0:T(8,128)(2,1)S(1)} %get-tuple-element.36.refs_1_), channel_id=1, source_target_pairs={{0,4},{1,5},{2,6},{3,7},{4,8},{5,9},{6,10},{7,11},{8,12},{9,13},{1... | collective-permute-start | bytes 3538952 | tf_op jit(solution)/shard_map/ppermute | solution.py:407
  97.1 17.5 %collective-permute-start.5 = (bf16[2,384,768]{2,1,0:T(8,128)(2,1)S(1)}, bf16[2,384,768]{2,1,0:T(8,128)(2,1)S(1)}, u32[]{:S(2)}, u32[]{:S(2)}) collective-permute-start(bf16[2,384,768]{2,1,0:T(8,128)(2,1)S(1)} %get-tuple-element.37.refs_2_), channel_id=1, source_target_pairs={{0,4},{1,5},{2,6},{3,7},{4,8},{5,9},{6,10},{7,11},{8,12},{9,13},{1... | collective-permute-start | bytes 3538952 | tf_op jit(solution)/shard_map/ppermute | solution.py:407
  102.0 28.0 %collective-permute-start.16 = (bf16[384,1536]{1,0:T(8,128)(2,1)S(1)}, bf16[384,1536]{1,0:T(8,128)(2,1)S(1)}, u32[]{:S(2)}, u32[]{:S(2)}) collective-permute-start(bf16[384,1536]{1,0:T(8,128)(2,1)S(1)} %slice.64), channel_id=1, source_target_pairs={{0,2},{1,3},{2,0},{3,1},{4,6},{5,7},{6,4},{7,5},{8,10},{9,11},{10,... | collective-permute-start | bytes 3538952 | tf_op jit(solution)/shard_map/ppermute | solution.py:407
  102.6 67.8 %collective-permute-start.18 = (bf16[768,1536]{1,0:T(8,128)(2,1)}, bf16[768,1536]{1,0:T(8,128)(2,1)S(1)}, u32[]{:S(2)}, u32[]{:S(2)}) collective-permute-start(bf16[768,1536]{1,0:T(8,128)(2,1)} %collective-permute-done.14.refs_9_), channel_id=1, source_target_pairs={{0,4},{1,5},{2,6},{3,7},{4,0},{5,1},{6,2},{7,3},{8,12},{9,13},{10,... | collective-permute-start | bytes 7077896 | tf_op jit(solution)/shard_map/ppermute | solution.py:407
  102.7 30.4 %collective-permute-start.17 = (bf16[384,1536]{1,0:T(8,128)(2,1)S(1)}, bf16[384,1536]{1,0:T(8,128)(2,1)S(1)}, u32[]{:S(2)}, u32[]{:S(2)}) collective-permute-start(bf16[384,1536]{1,0:T(8,128)(2,1)S(1)} %slice.65), channel_id=1, source_target_pairs={{0,1},{1,0},{2,3},{3,2},{4,5},{5,4},{6,7},{7,6},{8,9},{9,8},{10,11... | collective-permute-start | bytes 3538952 | tf_op jit(solution)/shard_map/ppermute | solution.py:407
  104.3 97.1 %collective-permute-start.19 = (bf16[768,1536]{1,0:T(8,128)(2,1)S(1)}, bf16[768,1536]{1,0:T(8,128)(2,1)S(1)}, u32[]{:S(2)}, u32[]{:S(2)}) collective-permute-start(bf16[768,1536]{1,0:T(8,128)(2,1)S(1)} %collective-permute-done.15.refs_10_), channel_id=1, source_target_pairs={{0,4},{1,5},{2,6},{3,7},{4,0},{5,1},{6,2},{7,3},{8,12},{9,13},{10,... | collective-permute-start | bytes 7077896 | tf_op jit(solution)/shard_map/ppermute | solution.py:407
  119.8 39.5 %collective-permute-start.6 = (bf16[384,768]{1,0:T(8,128)(2,1)S(1)}, bf16[384,768]{1,0:T(8,128)(2,1)S(1)}, u32[]{:S(2)}, u32[]{:S(2)}) collective-permute-start(bf16[384,768]{1,0:T(8,128)(2,1)S(1)} %earlier_frame.4), channel_id=1, source_target_pairs={{0,4},{1,5},{2,6},{3,7},{4,8},{5,9},{6,10},{7,11},{8,12},{9,13},{1... | collective-permute-start | bytes 1769480 | tf_op jit(solution)/shard_map/ppermute | solution.py:407
  130.0 36.4 %collective-permute-start.7 = (bf16[384,768]{1,0:T(8,128)(2,1)S(1)}, bf16[384,768]{1,0:T(8,128)(2,1)S(1)}, u32[]{:S(2)}, u32[]{:S(2)}) collective-permute-start(bf16[384,768]{1,0:T(8,128)(2,1)S(1)} %earlier_frame.5), channel_id=1, source_target_pairs={{0,4},{1,5},{2,6},{3,7},{4,8},{5,9},{6,10},{7,11},{8,12},{9,13},{1... | collective-permute-start | bytes 1769480 | tf_op jit(solution)/shard_map/ppermute | solution.py:407
  134.2 100.3 %collective-permute-start.20 = (bf16[768,1536]{1,0:T(8,128)(2,1)}, bf16[768,1536]{1,0:T(8,128)(2,1)}, u32[]{:S(2)}, u32[]{:S(2)}) collective-permute-start(bf16[768,1536]{1,0:T(8,128)(2,1)} %constant_dynamic-update-slice_fusion.refs_11_), channel_id=1, source_target_pairs={{0,4},{1,5},{2,6},{3,7},{4,0},{5,1},{6,2},{7,3},{8,12},{9,13},{10,... | collective-permute-start | bytes 7077896 | tf_op jit(solution)/shard_map/ppermute | solution.py:407
  166.4 68.1 %collective-permute-start.21 = (bf16[384,3072]{1,0:T(8,128)(2,1)}, bf16[384,3072]{1,0:T(8,128)(2,1)}, u32[]{:S(2)}, u32[]{:S(2)}) collective-permute-start(bf16[384,3072]{1,0:T(8,128)(2,1)} %get-tuple-element.53), channel_id=1, source_target_pairs={{0,4},{1,5},{2,6},{3,7},{4,8},{5,9},{6,10},{7,11},{8,12},{9,13},{1... | collective-permute-start | bytes 7077896 | tf_op jit(solution)/shard_map/ppermute | solution.py:407
  168.3 34.9 %collective-permute-start.22 = (bf16[384,768]{1,0:T(8,128)(2,1)S(1)}, bf16[384,768]{1,0:T(8,128)(2,1)S(1)}, u32[]{:S(2)}, u32[]{:S(2)}) collective-permute-start(bf16[384,768]{1,0:T(8,128)(2,1)S(1)} %collective-permute-done.6.refs_3_), channel_id=1, source_target_pairs={{4,5},{5,4},{6,7},{7,6},{8,9},{9,8},{10,11},{11,10},{12,13},{13,12... | collective-permute-start | bytes 1769480 | tf_op jit(solution)/shard_map/ppermute | solution.py:407
  170.5 26.5 %collective-permute-start.9 = (s32[1]{0:T(128)}, s32[1]{0:T(128)}, u32[]{:S(2)}, u32[]{:S(2)}) collective-permute-start(s32[1]{0:T(128)} %param.10), channel_id=1, source_target_pairs={{0,4},{1,5},{2,6},{3,7},{4,8},{5,9},{6,10},{7,11},{8,12},{9,13},{1... | collective-permute-start | bytes 20 | tf_op jit(solution)/shard_map/ppermute | solution.py:407
  196.9 14.9 %collective-permute-start.23 = (bf16[384,768]{1,0:T(8,128)(2,1)S(1)}, bf16[384,768]{1,0:T(8,128)(2,1)S(1)}, u32[]{:S(2)}, u32[]{:S(2)}) collective-permute-start(bf16[384,768]{1,0:T(8,128)(2,1)S(1)} %collective-permute-done.6.refs_3_), channel_id=1, source_target_pairs={{4,6},{5,7},{6,4},{7,5},{8,10},{9,11},{10,8},{11,9},{12,14},{13,15... | collective-permute-start | bytes 1769480 | tf_op jit(solution)/shard_map/ppermute | solution.py:407
  201.3 72.9 %collective-permute-start.8 = (bf16[384,3072]{1,0:T(8,128)(2,1)}, bf16[384,3072]{1,0:T(8,128)(2,1)}, u32[]{:S(2)}, u32[]{:S(2)}) collective-permute-start(bf16[384,3072]{1,0:T(8,128)(2,1)} %get-tuple-element.47), channel_id=1, source_target_pairs={{0,4},{1,5},{2,6},{3,7},{4,8},{5,9},{6,10},{7,11},{8,12},{9,13},{1... | collective-permute-start | bytes 7077896 | tf_op jit(solution)/shard_map/ppermute | solution.py:407
  203.3 14.7 %collective-permute-start.10 = (bf16[384,768]{1,0:T(8,128)(2,1)S(1)}, bf16[384,768]{1,0:T(8,128)(2,1)S(1)}, u32[]{:S(2)}, u32[]{:S(2)}) collective-permute-start(bf16[384,768]{1,0:T(8,128)(2,1)S(1)} %collective-permute-done.7.refs_3_), channel_id=1, source_target_pairs={{4,5},{5,4},{6,7},{7,6},{8,9},{9,8},{10,11},{11,10},{12,13},{13,12... | collective-permute-start | bytes 1769480 | tf_op jit(solution)/shard_map/ppermute | solution.py:407
  211.9 11.8 %collective-permute-start.11 = (bf16[384,768]{1,0:T(8,128)(2,1)S(1)}, bf16[384,768]{1,0:T(8,128)(2,1)S(1)}, u32[]{:S(2)}, u32[]{:S(2)}) collective-permute-start(bf16[384,768]{1,0:T(8,128)(2,1)S(1)} %collective-permute-done.7.refs_3_), channel_id=1, source_target_pairs={{4,6},{5,7},{6,4},{7,5},{8,10},{9,11},{10,8},{11,9},{12,14},{13,15... | collective-permute-start | bytes 1769480 | tf_op jit(solution)/shard_map/ppermute | solution.py:407
  227.3 46.9 %collective-permute-start.12 = (bf16[192,768]{1,0:T(8,128)(2,1)S(1)}, bf16[192,768]{1,0:T(8,128)(2,1)S(1)}, u32[]{:S(2)}, u32[]{:S(2)}) collective-permute-start(bf16[192,768]{1,0:T(8,128)(2,1)S(1)} %slice.62), channel_id=1, source_target_pairs={{4,6},{5,7},{6,4},{7,5},{8,10},{9,11},{10,8},{11,9},{12,14},{13,15... | collective-permute-start | bytes 884744 | tf_op jit(solution)/shard_map/ppermute | solution.py:407
  232.2 42.0 %collective-permute-start.13 = (bf16[192,768]{1,0:T(8,128)(2,1)S(1)}, bf16[192,768]{1,0:T(8,128)(2,1)S(1)}, u32[]{:S(2)}, u32[]{:S(2)}) collective-permute-start(bf16[192,768]{1,0:T(8,128)(2,1)S(1)} %slice.63), channel_id=1, source_target_pairs={{4,5},{5,4},{6,7},{7,6},{8,9},{9,8},{10,11},{11,10},{12,13},{13,12... | collective-permute-start | bytes 884744 | tf_op jit(solution)/shard_map/ppermute | solution.py:407
  272.3 46.0 %collective-permute-start.26 = (bf16[2,384,768]{2,1,0:T(8,128)(2,1)S(1)}, bf16[2,384,768]{2,1,0:T(8,128)(2,1)S(1)}, u32[]{:S(2)}, u32[]{:S(2)}) collective-permute-start(bf16[2,384,768]{2,1,0:T(8,128)(2,1)S(1)} %get-tuple-element.55.refs_1_), channel_id=1, source_target_pairs={{0,4},{1,5},{2,6},{3,7},{4,8},{5,9},{6,10},{7,11},{8,12},{9,13},{1... | collective-permute-start | bytes 3538952 | tf_op jit(solution)/shard_map/ppermute | solution.py:407
  312.0 17.5 %collective-permute-start.27 = (bf16[2,384,768]{2,1,0:T(8,128)(2,1)S(1)}, bf16[2,384,768]{2,1,0:T(8,128)(2,1)S(1)}, u32[]{:S(2)}, u32[]{:S(2)}) collective-permute-start(bf16[2,384,768]{2,1,0:T(8,128)(2,1)S(1)} %get-tuple-element.56.refs_2_), channel_id=1, source_target_pairs={{0,4},{1,5},{2,6},{3,7},{4,8},{5,9},{6,10},{7,11},{8,12},{9,13},{1... | collective-permute-start | bytes 3538952 | tf_op jit(solution)/shard_map/ppermute | solution.py:407
  334.7 16.3 %collective-permute-start.32 = (bf16[384,768]{1,0:T(8,128)(2,1)S(1)}, bf16[384,768]{1,0:T(8,128)(2,1)S(1)}, u32[]{:S(2)}, u32[]{:S(2)}) collective-permute-start(bf16[384,768]{1,0:T(8,128)(2,1)S(1)} %earlier_frame.7.refs_3_), channel_id=1, source_target_pairs={{0,1},{1,0},{2,3},{3,2},{4,5},{5,4},{6,7},{7,6},{8,9},{9,8},{10,11... | collective-permute-start | bytes 1769480 | tf_op jit(solution)/shard_map/ppermute | solution.py:407
  336.4 16.5 %collective-permute-start.33 = (bf16[384,768]{1,0:T(8,128)(2,1)S(1)}, bf16[384,768]{1,0:T(8,128)(2,1)S(1)}, u32[]{:S(2)}, u32[]{:S(2)}) collective-permute-start(bf16[384,768]{1,0:T(8,128)(2,1)S(1)} %earlier_frame.7.refs_3_), channel_id=1, source_target_pairs={{0,2},{1,3},{2,0},{3,1},{4,6},{5,7},{6,4},{7,5},{8,10},{9,11},{10,... | collective-permute-start | bytes 1769480 | tf_op jit(solution)/shard_map/ppermute | solution.py:407
  347.2 14.6 %collective-permute-start.28 = (bf16[384,768]{1,0:T(8,128)(2,1)S(1)}, bf16[384,768]{1,0:T(8,128)(2,1)S(1)}, u32[]{:S(2)}, u32[]{:S(2)}) collective-permute-start(bf16[384,768]{1,0:T(8,128)(2,1)S(1)} %earlier_frame.6.refs_3_), channel_id=1, source_target_pairs={{0,1},{1,0},{2,3},{3,2},{4,5},{5,4},{6,7},{7,6},{8,9},{9,8},{10,11... | collective-permute-start | bytes 1769480 | tf_op jit(solution)/shard_map/ppermute | solution.py:407
  347.9 14.5 %collective-permute-start.29 = (bf16[384,768]{1,0:T(8,128)(2,1)S(1)}, bf16[384,768]{1,0:T(8,128)(2,1)S(1)}, u32[]{:S(2)}, u32[]{:S(2)}) collective-permute-start(bf16[384,768]{1,0:T(8,128)(2,1)S(1)} %earlier_frame.6.refs_3_), channel_id=1, source_target_pairs={{0,2},{1,3},{2,0},{3,1},{4,6},{5,7},{6,4},{7,5},{8,10},{9,11},{10,... | collective-permute-start | bytes 1769480 | tf_op jit(solution)/shard_map/ppermute | solution.py:407
  351.0 14.3 %collective-permute-start.34 = (bf16[192,768]{1,0:T(8,128)(2,1)S(1)}, bf16[192,768]{1,0:T(8,128)(2,1)S(1)}, u32[]{:S(2)}, u32[]{:S(2)}) collective-permute-start(bf16[192,768]{1,0:T(8,128)(2,1)S(1)} %slice.71), channel_id=1, source_target_pairs={{0,2},{1,3},{2,0},{3,1},{4,6},{5,7},{6,4},{7,5},{8,10},{9,11},{10,... | collective-permute-start | bytes 884744 | tf_op jit(solution)/shard_map/ppermute | solution.py:407
  352.9 12.4 %collective-permute-start.35 = (bf16[192,768]{1,0:T(8,128)(2,1)S(1)}, bf16[192,768]{1,0:T(8,128)(2,1)S(1)}, u32[]{:S(2)}, u32[]{:S(2)}) collective-permute-start(bf16[192,768]{1,0:T(8,128)(2,1)S(1)} %slice.72), channel_id=1, source_target_pairs={{0,1},{1,0},{2,3},{3,2},{4,5},{5,4},{6,7},{7,6},{8,9},{9,8},{10,11... | collective-permute-start | bytes 884744 | tf_op jit(solution)/shard_map/ppermute | solution.py:407
  361.8 19.1 %collective-permute-start.30 = (bf16[192,768]{1,0:T(8,128)(2,1)S(1)}, bf16[192,768]{1,0:T(8,128)(2,1)S(1)}, u32[]{:S(2)}, u32[]{:S(2)}) collective-permute-start(bf16[192,768]{1,0:T(8,128)(2,1)S(1)} %slice.69), channel_id=1, source_target_pairs={{0,2},{1,3},{2,0},{3,1},{4,6},{5,7},{6,4},{7,5},{8,10},{9,11},{10,... | collective-permute-start | bytes 884744 | tf_op jit(solution)/shard_map/ppermute | solution.py:407
  362.4 18.5 %collective-permute-start.31 = (bf16[192,768]{1,0:T(8,128)(2,1)S(1)}, bf16[192,768]{1,0:T(8,128)(2,1)S(1)}, u32[]{:S(2)}, u32[]{:S(2)}) collective-permute-start(bf16[192,768]{1,0:T(8,128)(2,1)S(1)} %slice.70), channel_id=1, source_target_pairs={{0,1},{1,0},{2,3},{3,2},{4,5},{5,4},{6,7},{7,6},{8,9},{9,8},{10,11... | collective-permute-start | bytes 884744 | tf_op jit(solution)/shard_map/ppermute | solution.py:407
  (15 other events, 168.3 us)

commit v4 on v3

v4 whole, which is shorter than its diff:
```python
import functools
import math

import jax
import jax.numpy as jnp
from jax import lax
from jax.experimental import pallas as pl
from jax.experimental.pallas import tpu as pltpu
from jax.sharding import PartitionSpec as P

HD = 128
STEPS = 2
CHUNKS = 2
EPS = 1e-6
AXES = ("queue", "tensor")
F32 = jnp.float32
BF16 = jnp.bfloat16
SCORE_SCALE = math.log2(math.e) / math.sqrt(HD)
ANY = pl.BlockSpec(memory_space=pl.ANY)


def compiler_params(mib):
    return pltpu.CompilerParams(vmem_limit_bytes=mib * 2**20)


def in_hbm(array):
    return pltpu.with_memory_space_constraint(array, pltpu.HBM)


def cost(flops, nbytes, transcendentals=0):
    return pl.CostEstimate(
        flops=int(flops) // 1000,
        bytes_accessed=int(nbytes) // 1000,
        transcendentals=int(transcendentals) // 1000,
    )


def head_normalized(values, gain):
    heads = []
    for h in range(values.shape[1] // HD):
        head = values[:, h * HD : (h + 1) * HD]
        mean = jnp.mean(head * head, axis=-1, keepdims=True)
        heads.append((head * lax.rsqrt(mean + EPS) * gain).astype(BF16))
    return heads[0] if len(heads) == 1 else jnp.concatenate(heads, axis=1)


def tile_cols(head_cols):
    return 256 if head_cols % 256 == 0 else HD


def weight_copies(w_any, part, w_ref, w_sems):
    splits = w_sems.shape[0]
    split_rows = w_ref.shape[0] // splits
    for i in range(splits):
        at = pl.ds(i * split_rows, split_rows)
        yield pltpu.make_async_copy(w_any.at[part, at], w_ref.at[at], w_sems.at[i])


def key_kernel(*refs, tensor_size, noise_step):
    info_ref, scale_ref, shift_ref, gain_ref, w_any, z_any, noise_any = refs[:7]
    piece_refs = refs[7 : 7 + tensor_size - 1]
    key_ref, normed_ref, state_ref, w_ref, sem, w_sems = refs[6 + tensor_size :]
    step = pl.program_id(0)
    rows = state_ref.shape[0]
    piece_rows = noise_any.shape[1]
    cols = key_ref.shape[1]

    @pl.when(step == 0)
    def _():
        for copy in weight_copies(w_any, 1, w_ref, w_sems):
            copy.start()

        @pl.when(info_ref[0] == 0)
        def _():
            copy = pltpu.make_async_copy(z_any, state_ref, sem.at[0])
            copy.start()
            copy.wait()

        @pl.when(info_ref[0] != 0)
        def _():
            for block in range(tensor_size):
                away = lax.rem(block + tensor_size - info_ref[1], tensor_size)
                for d in range(tensor_size):
                    source = noise_any if d == 0 else piece_refs[d - 1]

                    @pl.when(away == d)
                    def _():
                        copy = pltpu.make_async_copy(
                            source.at[noise_step],
                            state_ref.at[pl.ds(block * piece_rows, piece_rows)],
                            sem.at[0],
                        )
                        copy.start()
                        copy.wait()

        def one(i, carry):
            at = pl.ds(pl.multiple_of(i * 16, 16), 16)
            state = state_ref[at, :].astype(F32)
            mean = jnp.mean(state * state, axis=-1, keepdims=True)
            state = state * lax.rsqrt(mean + EPS) * scale_ref[...] + shift_ref[...]
            normed_ref[at, :] = state.astype(BF16)
            return carry

        lax.fori_loop(0, rows // 16, one, 0, unroll=4)
        for copy in weight_copies(w_any, 1, w_ref, w_sems):
            copy.wait()

    at = pl.ds(pl.multiple_of(step * cols, HD), cols)
    product = jnp.dot(normed_ref[...], w_ref[:, at], preferred_element_type=F32)
    key_ref[...] = head_normalized(product, gain_ref[1:2])


def project_keys(info, scale1, shift, gains, qkv_weight, z, noise_all, noise_step, noise_pieces):
    rows, width = z.shape
    head_cols = qkv_weight.shape[2]
    cols = tile_cols(head_cols)
    tensor_size = len(noise_pieces) + 1
    return pl.pallas_call(
        functools.partial(key_kernel, tensor_size=tensor_size, noise_step=noise_step),
        grid_spec=pltpu.PrefetchScalarGridSpec(
            num_scalar_prefetch=1,
            grid=(head_cols // cols,),
            in_specs=[
                pl.BlockSpec((1, width), lambda j, i: (0, 0)),
                pl.BlockSpec((1, width), lambda j, i: (0, 0)),
                pl.BlockSpec((2, HD), lambda j, i: (0, 0)),
            ]
            + [ANY] * (2 + tensor_size),
            out_specs=[
                pl.BlockSpec((rows, cols), lambda j, i: (0, j)),
                pl.BlockSpec((rows, width), lambda j, i: (0, 0)),
                pl.BlockSpec((rows, width), lambda j, i: (0, 0)),
            ],
            scratch_shapes=[
                pltpu.VMEM((width, head_cols), BF16),
                pltpu.SemaphoreType.DMA((1,)),
                pltpu.SemaphoreType.DMA((4,)),
            ],
        ),
        out_shape=[
            jax.ShapeDtypeStruct((rows, head_cols), BF16),
            jax.ShapeDtypeStruct((rows, width), BF16),
            pltpu.HBM((rows, width), BF16),
        ],
        compiler_params=compiler_params(26),
        cost_estimate=cost(
            2 * rows * width * head_cols,
            6 * rows * width + 2 * rows * head_cols + 2 * width * head_cols,
        ),
        name="norm_keys",
    )(
        info,
        scale1,
        shift,
        gains,
        *[in_hbm(a) for a in (qkv_weight, z, noise_all)],
        *noise_pieces,
    )


def value_kernel(normed_ref, w_any, value_ref, w_ref, w_sems):
    step = pl.program_id(0)
    cols = value_ref.shape[1]

    @pl.when(step == 0)
    def _():
        for copy in weight_copies(w_any, 2, w_ref, w_sems):
            copy.start()
        for copy in weight_copies(w_any, 2, w_ref, w_sems):
            copy.wait()

    at = pl.ds(pl.multiple_of(step * cols, HD), cols)
    product = jnp.dot(normed_ref[...], w_ref[:, at], preferred_element_type=F32)
    value_ref[...] = product.astype(BF16)


def project_values(normed, qkv_weight):
    rows, width = normed.shape
    head_cols = qkv_weight.shape[2]
    cols = tile_cols(head_cols)
    return pl.pallas_call(
        value_kernel,
        grid=(head_cols // cols,),
        in_specs=[pl.BlockSpec((rows, width), lambda j: (0, 0)), ANY],
        out_specs=pl.BlockSpec((rows, cols), lambda j: (0, j)),
        scratch_shapes=[
            pltpu.VMEM((width, head_cols), BF16),
            pltpu.SemaphoreType.DMA((4,)),
        ],
        out_shape=jax.ShapeDtypeStruct((rows, head_cols), BF16),
        compiler_params=compiler_params(20),
        cost_estimate=cost(
            2 * rows * width * head_cols,
            2 * rows * width + 2 * rows * head_cols + 2 * width * head_cols,
        ),
        name="values",
    )(normed, in_hbm(qkv_weight))


def attend(query, key):
    return lax.dot_general(query, key, (((1,), (1,)), ((), ())), preferred_element_type=F32)


def weigh(scores, top, values):
    weights = jnp.exp2(scores - top).astype(BF16)
    extended = jnp.concatenate([values, jnp.ones_like(values)], axis=1)
    total = jnp.dot(weights, extended, preferred_element_type=F32)
    return total[:, :HD], total[:, HD:]


def own_kernel(
    gain_ref, normed_ref, key_ref, value_ref, w_any,
    query_ref, acc_ref, top_ref, total_ref, w_ref, w_sems,
):
    step = pl.program_id(0)
    cols = query_ref.shape[1]

    @pl.when(step == 0)
    def _():
        for copy in weight_copies(w_any, 0, w_ref, w_sems):
            copy.start()
        for copy in weight_copies(w_any, 0, w_ref, w_sems):
            copy.wait()

    inside = pl.ds(pl.multiple_of(step * cols, HD), cols)
    product = jnp.dot(normed_ref[...], w_ref[:, inside], preferred_element_type=F32)
    query = head_normalized(product, gain_ref[0:1])
    query_ref[...] = query
    for h in range(cols // HD):
        at = slice(h * HD, (h + 1) * HD)
        scores = attend(query[:, at], key_ref[:, at])
        top = jnp.max(scores, axis=-1, keepdims=True)
        acc, total = weigh(scores, top, value_ref[:, at])
        acc_ref[:, at] = acc
        total_ref[:, at] = total
        top_ref[:, at] = jnp.broadcast_to(top, acc.shape)


def own_attention(gains, normed, qkv_weight, key, value):
    rows, width = normed.shape
    head_cols = qkv_weight.shape[2]
    cols = tile_cols(head_cols)
    by_heads = pl.BlockSpec((rows, cols), lambda j: (0, j))
    return pl.pallas_call(
        own_kernel,
        grid=(head_cols // cols,),
        in_specs=[
            pl.BlockSpec((2, HD), lambda j: (0, 0)),
            pl.BlockSpec((rows, width), lambda j: (0, 0)),
            by_heads,
            by_heads,
            ANY,
        ],
        out_specs=[by_heads] * 4,
        scratch_shapes=[
            pltpu.VMEM((width, head_cols), BF16),
            pltpu.SemaphoreType.DMA((4,)),
        ],
        out_shape=[jax.ShapeDtypeStruct((rows, head_cols), BF16)]
        + [jax.ShapeDtypeStruct((rows, head_cols), F32)] * 3,
        compiler_params=compiler_params(32),
        cost_estimate=cost(
            2 * rows * width * head_cols + 8 * rows * rows * head_cols,
            2 * rows * width + 18 * rows * head_cols + 2 * width * head_cols,
            rows * rows * head_cols // HD,
        ),
        name="queries_own_frame",
    )(gains, normed, key, value, in_hbm(qkv_weight))


def earlier_kernel(*refs, chunks):
    info_ref, query_ref, acc_ref, top_ref, total_ref, key_ref, value_ref = refs[:7]
    out_refs = refs[7:]
    rows = query_ref.shape[0] // chunks

    def store(at, result):
        for c, out_ref in enumerate(out_refs):
            out_ref[:, at] = result[c * rows : (c + 1) * rows]

    @pl.when(info_ref[0] != 0)
    def _():
        store(slice(None), (acc_ref[...] / total_ref[...]).astype(BF16))

    @pl.when(info_ref[0] == 0)
    def _():
        for h in range(query_ref.shape[1] // HD):
            at = slice(h * HD, (h + 1) * HD)
            old_top = top_ref[:, at][:, :1]
            scores = attend(query_ref[:, at], key_ref[:, at])
            top = jnp.maximum(jnp.max(scores, axis=-1, keepdims=True), old_top)
            acc, total = weigh(scores, top, value_ref[:, at])
            kept = jnp.exp2(old_top - top)
            acc = acc + acc_ref[:, at] * kept
            total = total + total_ref[:, at] * kept
            store(at, (acc / total).astype(BF16))


def earlier_attention(info, query, acc, top, total, key, value, chunks):
    rows, head_cols = query.shape
    cols = tile_cols(head_cols)
    return pl.pallas_call(
        functools.partial(earlier_kernel, chunks=chunks),
        grid_spec=pltpu.PrefetchScalarGridSpec(
            num_scalar_prefetch=1,
            grid=(head_cols // cols,),
            in_specs=[pl.BlockSpec((rows, cols), lambda j, i: (0, j))] * 6,
            out_specs=[pl.BlockSpec((rows // chunks, cols), lambda j, i: (0, j))] * chunks,
        ),
        out_shape=[jax.ShapeDtypeStruct((rows // chunks, head_cols), BF16)] * chunks,
        compiler_params=compiler_params(24),
        cost_estimate=cost(
            8 * rows * rows * head_cols,
            20 * rows * head_cols,
            rows * rows * head_cols // HD,
        ),
        name="earlier_frame",
    )(info, query, acc, top, total, key, value)


def output_kernel(*refs, part_counts, whole_weights, half_blocks, last):
    parity_ref = refs[0]
    at = 1
    acc_in = resid_ref = gate_ref = None
    if last:
        acc_in, resid_ref, gate_ref = refs[1:4]
        at = 4
    pieces = []
    for count in part_counts:
        pieces.append(refs[at : at + count])
        at += count
    size = len(part_counts)
    wholes = refs[at : at + whole_weights]
    at += whole_weights
    halves = refs[at : at + 2 * (size - whole_weights)]
    at += 2 * (size - whole_weights)
    out_ref, held_ref, w_ref, held_sems, w_sems = refs[at:]
    step = pl.program_id(0)
    cols = out_ref.shape[1]
    half_width = w_ref.shape[3]

    def weight_copy(half, k):
        if k < whole_weights:
            column = (parity_ref[0] ^ half) * half_width
            source = wholes[k].at[:, pl.ds(pl.multiple_of(column, HD), half_width)]
        else:
            source = halves[half * (size - whole_weights) + k - whole_weights]
        return pltpu.make_async_copy(source, w_ref.at[half, k], w_sems.at[half, k])

    def held_copies(k):
        row = 0
        for number, part in enumerate(pieces[k]):
            count = part.shape[0]
            yield pltpu.make_async_copy(
                part, held_ref.at[k, pl.ds(row, count)], held_sems.at[k, number]
            )
            row += count

    @pl.when(step == 0)
    def _():
        for k in range(size):
            for copy in held_copies(k):
                copy.start()
        for half in range(2):
            for k in range(size):
                weight_copy(half, k).start()
        for k in range(size):
            for copy in held_copies(k):
                copy.wait()

    for half in range(2):

        @pl.when(step == half * half_blocks)
        def _():
            for k in range(size):
                weight_copy(half, k).wait()

    half = step // half_blocks
    inside = pl.ds(pl.multiple_of(lax.rem(step, half_blocks) * cols, HD), cols)
    update = acc_in[...] if last else None
    for k in range(size):
        term = jnp.dot(held_ref[k], w_ref[half, k, :, inside], preferred_element_type=F32)
        update = term if update is None else update + term
    if last:
        update = resid_ref[...].astype(F32) + gate_ref[...] * update
    out_ref[...] = update.astype(out_ref.dtype)


def output_projection(parity, pieces, wholes, mine, theirs, finish=None):
    head_cols, half_width = mine[0].shape
    rows = sum(part.shape[0] for part in pieces[0])
    width = 2 * half_width
    size = len(pieces)
    cols = tile_cols(half_width)
    half_blocks = half_width // cols
    parts = max(len(p) for p in pieces)
    flat = [part for group in pieces for part in group]
    weights = [in_hbm(array) for array in [*wholes, *mine, *theirs]]
    last = finish is not None

    def column(j, parity):
        return 0, ((j // half_blocks) ^ parity[0]) * half_blocks + j % half_blocks

    block = pl.BlockSpec((rows, cols), column)
    return pl.pallas_call(
        functools.partial(
            output_kernel,
            part_counts=tuple(len(p) for p in pieces),
            whole_weights=len(wholes),
            half_blocks=half_blocks,
            last=last,
        ),
        grid_spec=pltpu.PrefetchScalarGridSpec(
            num_scalar_prefetch=1,
            grid=(2 * half_blocks,),
            in_specs=([block, block, pl.BlockSpec((1, cols), column)] if last else [])
            + [ANY] * (len(flat) + len(weights)),
            out_specs=block,
            scratch_shapes=[
                pltpu.VMEM((size, rows, head_cols), BF16),
                pltpu.VMEM((2, size, head_cols, half_width), BF16),
                pltpu.SemaphoreType.DMA((size, parts)),
                pltpu.SemaphoreType.DMA((2, size)),
            ],
        ),
        out_shape=(pltpu.HBM if last else jax.ShapeDtypeStruct)((rows, width), BF16 if last else F32),
        compiler_params=compiler_params(16 if last else 28),
        cost_estimate=cost(
            2 * rows * width * head_cols * size,
            (8 if last else 4) * rows * width + 2 * head_cols * width * size,
        ),
        name="projection_end" if last else "projection_start",
    )(parity, *(finish if last else ()), *flat, *weights)


def send(block, move, queue_size, tensor_size, frames=None):
    pairs = []
    for q in range(queue_size) if frames is None else frames:
        for t in range(tensor_size):
            to_q, to_t = move(q, t)
            pairs.append((q * tensor_size + t, to_q * tensor_size + to_t))
    return lax.ppermute(block, AXES, pairs)


def gather_pieces(block, queue_size, tensor_size, frames=None, after=None):
    half = tensor_size // 2

    def low(q, t):
        return q, t ^ 1

    def high(j):
        return lambda q, t: (q, (t // 2 - j) % half * 2 + t % 2)

    args = (queue_size, tensor_size, frames)
    rows = block.shape[0] // 2
    near = send(block, low, *args)
    if after is not None:
        block, _ = lax.optimization_barrier((block, after))
    far = [send(block, high(j), *args) for j in range(1, half)]
    corners = []
    for j in range(1, half):
        top = send(near[:rows], high(j), *args)
        bottom = send(far[j - 1][rows:], low, *args)
        corners.append([top, bottom])
    return [near, *far], corners


def body(
    latents, levels, mod_table, step_size, qkv_weight, q_gain, k_gain, out_weight, fresh_noise
):
    queue_size = lax.axis_size("queue")
    tensor_size = lax.axis_size("tensor")
    rows, width = latents.shape[1:]
    mesh_sizes = (queue_size, tensor_size)
    queue_index = lax.axis_index("queue")
    tensor_index = lax.axis_index("tensor")
    is_last = queue_index == queue_size - 1
    parity = (queue_index % 2).astype(jnp.int32)[None]

    def ring(block):
        return send(block, lambda q, t: ((q + 1) % queue_size, t), *mesh_sizes)

    def sibling(block):
        return send(block, lambda q, t: (q ^ 1, t), *mesh_sizes)

    worked_level = send(levels, lambda q, t: ((q - 1) % queue_size, t), *mesh_sizes)[0]
    noise_pieces = [
        send(
            fresh_noise,
            lambda q, t: (q, (t - d) % tensor_size),
            *mesh_sizes,
            [queue_size - 1],
        )
        for d in range(1, tensor_size)
    ]
    half_weight = lax.dynamic_slice(
        out_weight, (0, parity[0] * (width // 2)), (out_weight.shape[0], width // 2)
    )
    half_weight, latents = lax.optimization_barrier((half_weight, latents))
    mine, mine_corners = gather_pieces(half_weight, *mesh_sizes, after=noise_pieces)
    theirs = [sibling(block) for block in mine]
    mine_corners = [jnp.concatenate(parts, axis=0) for parts in mine_corners]
    theirs_corners = [sibling(block) for block in mine_corners]

    def modulation(level):
        row = lax.dynamic_slice(mod_table, (level, 0), (1, 3 * width)).astype(F32)
        rate = lax.dynamic_slice(step_size, (level,), (1,))[:, None]
        return row[:, :width], 1.0 + row[:, width : 2 * width], rate * row[:, 2 * width :]

    shift, scale1, _ = modulation(worked_level)
    _, _, gate = modulation(levels[0])
    info = jnp.stack([is_last.astype(jnp.int32), tensor_index.astype(jnp.int32)])
    gains = jnp.stack([q_gain * SCORE_SCALE, k_gain])

    frame = latents[0]
    for step_index in range(STEPS):
        final = step_index == STEPS - 1
        key, normed, state = project_keys(
            info, scale1, shift, gains, qkv_weight, frame, fresh_noise, step_index, noise_pieces
        )
        earlier_key = ring(key)
        value = project_values(normed, qkv_weight)
        earlier_value = ring(value)
        normed, earlier_key = lax.optimization_barrier((normed, earlier_key))
        query, *own = own_attention(gains, normed, qkv_weight, key, value)
        if not final:
            query, mine = lax.optimization_barrier((query, mine))
        attended = earlier_attention(
            info, query, *own, earlier_key, earlier_value, CHUNKS
        )
        attended = [ring(block) for block in attended]
        targets = range(queue_size) if final else range(queue_size - 1)
        gathered = [gather_pieces(block, *mesh_sizes, targets) for block in attended]
        sent_state, _ = lax.optimization_barrier((state, attended))
        resid = ring(sent_state)
        direct = [attended] + [list(p) for p in zip(*[near for near, _ in gathered])]
        corners = [
            [half for parts in p for half in parts] for p in zip(*[c for _, c in gathered])
        ]
        begun = output_projection(parity, direct, [out_weight], mine, theirs)
        frame = output_projection(
            parity, corners, [], mine_corners, theirs_corners, (begun, resid, gate)
        )
    return frame[None]


def solution(mesh):
    return jax.shard_map(
        body,
        mesh=mesh,
        in_specs=(
            P("queue", None, None),
            P("queue"),
            P(),
            P(),
            P(None, None, "tensor"),
            P(),
            P(),
            P("tensor", None),
            P(None, "tensor", None),
        ),
        out_specs=P("queue", None, None),
        check_vma=False,
    )
```

time: 398 us -> 433 us (1.088)
  the two profiles are of different devices: /device:TPU:12 before, /device:TPU:0 now
where the time goes in v4:
time: 433 us; the launch traced here: 431 us
  waiting for transfers between devices  193 us (45%)
  Pallas kernels  159 us (37%)
  starting transfers between devices  58.2 us (13%)
  local copies, waits for them, and re-layouts  14.7 us (3%)
    ppermute x37, waiting for transfers between devices, send(): return lax.ppermute(block, AXES, pairs)  193 us
    pallas_call x4, Pallas kernels, output_projection(): pl.pallas_call(functools.partial(output_kernel, part_counts=tuple((len(p)...  61.2 us
    ppermute x37, starting transfers between devices, send(): return lax.ppermute(block, AXES, pairs)  58.2 us
    pallas_call x2, Pallas kernels, own_attention(): pl.pallas_call(own_kernel, grid=(head_cols // cols,), in_specs=[pl.BlockS...  36.5 us
    pallas_call x2, Pallas kernels, project_keys(): pl.pallas_call(functools.partial(key_kernel, tensor_size=tensor_size, noi...  27.8 us
    pallas_call x2, Pallas kernels, earlier_attention(): pl.pallas_call(functools.partial(earlier_kernel, chunks=chunks), grid_spe...  20.5 us
    pallas_call x2, Pallas kernels, project_values(): pl.pallas_call(value_kernel, grid=(head_cols // cols,), in_specs=[pl.Bloc...  13.4 us
  transfers between devices with their start and end apart: 37, of which 16 were waited for; matrix products, arithmetic and copies ran while one was open for 3% of the time, Pallas kernels for 23%

profile of v4, /device:TPU:0, one launch (start us, length us, event | category | flops | bytes accessed | tf_op | source)
XLA Modules:
  0.0 431.0 jit_solution(1357836915430264521)
XLA Ops:
  5.0 8.0 %collective-permute-start = (s32[1]{0:T(128)}, s32[1]{0:T(128)}, u32[]{:S(2)}, u32[]{:S(2)}) collective-permute-start(s32[1]{0:T(128)} %param.10), channel_id=1, source_target_pairs={{0,28},{1,29},{2,30},{3,31},{4,0},{5,1},{6,2},{7,3},{8,4},{9,5},{1... | collective-permute-start | bytes 20 | tf_op jit(solution)/shard_map/ppermute | solution.py:441
  13.0 3.2 constant_dynamic-slice_fusion
  22.2 13.9 %norm_keys.2 = (bf16[768,768]{1,0:T(8,128)(2,1)S(1)}, bf16[768,3072]{1,0:T(8,128)(2,1)S(1)}, bf16[768,3072]{1,0:T(8,128)(2,1)}) custom-call(s32[2]{0:T(128)S(1)} %pad_add_fusion.refs_0_, f32[1,3072]{1,0:T(1,128)S(1)} %get-tuple-element.66.refs_1_, f32[1,3072]{1,0:T(1,128)S(1)} %get-tuple-element.65.refs_2_, f32[2,128]{1,0:T(2,128)S(1)} %pad_maximum_fusion.refs_3_.gain_ref, ...), custom_call_target="tpu_custom_call" | custom-call | flops 3623878 | bytes 20054 | tf_op jit(solution)/shard_map/norm_keys/pallas_call | solution.py:118
  36.2 6.6 %values.2.value_ref = bf16[768,768]{1,0:T(8,128)(2,1)S(1)} custom-call(bf16[768,3072]{1,0:T(8,128)(2,1)S(1)} %get-tuple-element.38.normed_ref, bf16[3,3072,768]{2,1,0:T(8,128)(2,1)} %w_any.7), custom_call_target="tpu_custom_call" | custom-call | flops 3623878 | bytes 10616 | tf_op jit(solution)/shard_map/values/pallas_call | solution.py:181
  42.9 73.9 %collective-permute-done.4.refs_5_ = bf16[768,768]{1,0:T(8,128)(2,1)S(1)} collective-permute-done((bf16[768,768]{1,0:T(8,128)(2,1)S(1)}, bf16[768,768]{1,0:T(8,128)(2,1)S(1)}, u32[]{:S(2)}, u32[]{:S(2)}) %collective-permute-start.4) | collective-permute-done | bytes 1179680 | tf_op jit(solution)/shard_map/ppermute | solution.py:441
  116.8 18.3 %queries_own_frame.2 = (bf16[768,768]{1,0:T(8,128)(2,1)S(1)}, f32[768,768]{1,0:T(8,128)S(1)}, f32[768,768]{1,0:T(8,128)S(1)}, f32[768,768]{1,0:T(8,128)S(1)}) custom-call(f32[2,128]{1,0:T(2,128)S(1)} %pad_maximum_fusion.refs_3_.gain_ref, bf16[768,3072]{1,0:T(8,128)(2,1)S(1)} %get-tuple-element.38.normed_ref, bf16[768,768]{1,0:T(8,128)(2,1)S(1)} %get-tuple-element.37.key_ref, ...), custom_call_target="tpu_custom_call" | custom-call | flops 7247757 | bytes 20054 | tf_op jit(solution)/shard_map/queries_own_frame/pallas_call | solution.py:244
  135.1 10.2 %earlier_frame.2 = (bf16[384,768]{1,0:T(8,128)(2,1)S(1)}, bf16[384,768]{1,0:T(8,128)(2,1)S(1)}) custom-call(s32[2]{0:T(128)S(1)} %pad_add_fusion.refs_0_, bf16[768,768]{1,0:T(8,128)(2,1)S(1)} %get-tuple-element.42.refs_1_, f32[768,768]{1,0:T(8,128)S(1)} %get-tuple-element.43.refs_2_, f32[768,768]{1,0:T(8,128)S(1)} %get-tuple-element.44.refs_3_, ...), custom_call_target="tpu_custom_call" | custom-call | flops 3623878 | bytes 11796 | tf_op jit(solution)/shard_map/earlier_frame/pallas_call | solution.py:301
  145.5 11.0 %collective-permute-done.8.refs_1_ = bf16[384,768]{1,0:T(8,128)(2,1)S(1)} collective-permute-done((bf16[384,768]{1,0:T(8,128)(2,1)S(1)}, bf16[384,768]{1,0:T(8,128)(2,1)S(1)}, u32[]{:S(2)}, u32[]{:S(2)}) %collective-permute-start.8) | collective-permute-done | bytes 589856 | tf_op jit(solution)/shard_map/ppermute | solution.py:441
  156.5 6.3 %collective-permute-done.9.refs_2_ = bf16[384,768]{1,0:T(8,128)(2,1)S(1)} collective-permute-done((bf16[384,768]{1,0:T(8,128)(2,1)S(1)}, bf16[384,768]{1,0:T(8,128)(2,1)S(1)}, u32[]{:S(2)}, u32[]{:S(2)}) %collective-permute-start.9) | collective-permute-done | bytes 589856 | tf_op jit(solution)/shard_map/ppermute | solution.py:441
  171.4 9.3 %collective-permute-done.21 = bf16[384,1536]{1,0:T(8,128)(2,1)S(1)} collective-permute-done((bf16[384,1536]{1,0:T(8,128)(2,1)S(1)}, bf16[384,1536]{1,0:T(8,128)(2,1)S(1)}, u32[]{:S(2)}, u32[]{:S(2)}) %collective-permute-start.21) | collective-permute-done | bytes 1179680 | tf_op jit(solution)/shard_map/ppermute | solution.py:441
  181.8 4.9 %collective-permute-done.22 = bf16[384,1536]{1,0:T(8,128)(2,1)S(1)} collective-permute-done((bf16[384,1536]{1,0:T(8,128)(2,1)S(1)}, bf16[384,1536]{1,0:T(8,128)(2,1)S(1)}, u32[]{:S(2)}, u32[]{:S(2)}) %collective-permute-start.22) | collective-permute-done | bytes 1179680 | tf_op jit(solution)/shard_map/ppermute | solution.py:441
  186.7 3.3 collective-permute-start.11
  191.2 8.1 %collective-permute-done.10.refs_3_ = bf16[384,768]{1,0:T(8,128)(2,1)S(1)} collective-permute-done((bf16[384,768]{1,0:T(8,128)(2,1)S(1)}, bf16[384,768]{1,0:T(8,128)(2,1)S(1)}, u32[]{:S(2)}, u32[]{:S(2)}) %collective-permute-start.10) | collective-permute-done | bytes 589856 | tf_op jit(solution)/shard_map/ppermute | solution.py:441
  199.2 6.4 %collective-permute-done.11.refs_4_ = bf16[384,768]{1,0:T(8,128)(2,1)S(1)} collective-permute-done((bf16[384,768]{1,0:T(8,128)(2,1)S(1)}, bf16[384,768]{1,0:T(8,128)(2,1)S(1)}, u32[]{:S(2)}, u32[]{:S(2)}) %collective-permute-start.11) | collective-permute-done | bytes 589856 | tf_op jit(solution)/shard_map/ppermute | solution.py:441
  208.1 11.5 %collective-permute-done.12.refs_5_ = bf16[384,768]{1,0:T(8,128)(2,1)} collective-permute-done((bf16[384,768]{1,0:T(8,128)(2,1)S(1)}, bf16[384,768]{1,0:T(8,128)(2,1)}, u32[]{:S(2)}, u32[]{:S(2)}) %collective-permute-start.12) | collective-permute-done | bytes 589856 | tf_op jit(solution)/shard_map/ppermute | solution.py:441
  222.4 12.1 %collective-permute-done.13.refs_6_ = bf16[384,768]{1,0:T(8,128)(2,1)} collective-permute-done((bf16[384,768]{1,0:T(8,128)(2,1)S(1)}, bf16[384,768]{1,0:T(8,128)(2,1)}, u32[]{:S(2)}, u32[]{:S(2)}) %collective-permute-start.13) | collective-permute-done | bytes 589856 | tf_op jit(solution)/shard_map/ppermute | solution.py:441
  247.7 3.3 collective-permute-start.20
  254.7 19.2 %projection_start.2.refs_1_ = f32[768,3072]{1,0:T(8,128)S(1)} custom-call(s32[1]{0:T(128)} %bitcast.refs_0_, bf16[384,768]{1,0:T(8,128)(2,1)S(1)} %copy-done.1, bf16[384,768]{1,0:T(8,128)(2,1)S(1)} %copy-done.3, bf16[384,768]{1,0:T(8,128)(2,1)S(1)} %collective-permute-done.10.refs_3_, bf16[384,768]{1,0:T(8,128)(2,1)S(1)} %collective-permute-done.11.refs_4_, ...), custom_call_target="tpu_custom_call" | custom-call | flops 10871635 | bytes 23592 | tf_op jit(solution)/shard_map/projection_start/pallas_call | solution.py:404
  274.0 13.2 %projection_end.2.refs_5_ = bf16[768,3072]{1,0:T(8,128)(2,1)} custom-call(s32[1]{0:T(128)} %bitcast.refs_0_, f32[768,3072]{1,0:T(8,128)S(1)} %projection_start.2.refs_1_, bf16[768,3072]{1,0:T(8,128)(2,1)} %collective-permute-done.16.refs_2_, f32[1,3072]{1,0:T(1,128)S(1)} %fusion.refs_3_, bf16[192,768]{1,0:T(8,128)(2,1)} %collective-permute-done.17.refs_4_, ...), custom_call_target="tpu_custom_call" | custom-call | flops 3623878 | bytes 23592 | tf_op jit(solution)/shard_map/projection_end/pallas_call | solution.py:404
  287.2 13.9 %norm_keys.3 = (bf16[768,768]{1,0:T(8,128)(2,1)S(1)}, bf16[768,3072]{1,0:T(8,128)(2,1)S(1)}, bf16[768,3072]{1,0:T(8,128)(2,1)}) custom-call(s32[2]{0:T(128)S(1)} %copy-done.7, f32[1,3072]{1,0:T(1,128)S(1)} %copy-done.5, f32[1,3072]{1,0:T(1,128)S(1)} %get-tuple-element.65.refs_2_, f32[2,128]{1,0:T(2,128)S(1)} %pad_maximum_fusion.refs_3_.gain_ref, ...), custom_call_target="tpu_custom_call" | custom-call | flops 3623878 | bytes 20054 | tf_op jit(solution)/shard_map/norm_keys/pallas_call | solution.py:118
  301.2 6.8 %values.3.value_ref = bf16[768,768]{1,0:T(8,128)(2,1)S(1)} custom-call(bf16[768,3072]{1,0:T(8,128)(2,1)S(1)} %get-tuple-element.55.normed_ref, bf16[3,3072,768]{2,1,0:T(8,128)(2,1)} %w_any.7), custom_call_target="tpu_custom_call" | custom-call | flops 3623878 | bytes 10616 | tf_op jit(solution)/shard_map/values/pallas_call | solution.py:181
  308.0 5.0 %collective-permute-start.25 = (bf16[768,768]{1,0:T(8,128)(2,1)S(1)}, bf16[768,768]{1,0:T(8,128)(2,1)S(1)}, u32[]{:S(2)}, u32[]{:S(2)}) collective-permute-start(bf16[768,768]{1,0:T(8,128)(2,1)S(1)} %values.3.value_ref), channel_id=1, source_target_pairs={{0,4},{1,5},{2,6},{3,7},{4,8},{5,9},{6,10},{7,11},{8,12},{9,13},{1... | collective-permute-start | bytes 3538952 | tf_op jit(solution)/shard_map/ppermute | solution.py:441
  313.0 5.6 %collective-permute-done.24.refs_5_ = bf16[768,768]{1,0:T(8,128)(2,1)S(1)} collective-permute-done((bf16[768,768]{1,0:T(8,128)(2,1)S(1)}, bf16[768,768]{1,0:T(8,128)(2,1)S(1)}, u32[]{:S(2)}, u32[]{:S(2)}) %collective-permute-start.24) | collective-permute-done | bytes 1179680 | tf_op jit(solution)/shard_map/ppermute | solution.py:441
  318.6 18.3 %queries_own_frame.3 = (bf16[768,768]{1,0:T(8,128)(2,1)S(1)}, f32[768,768]{1,0:T(8,128)S(1)}, f32[768,768]{1,0:T(8,128)S(1)}, f32[768,768]{1,0:T(8,128)S(1)}) custom-call(f32[2,128]{1,0:T(2,128)S(1)} %pad_maximum_fusion.refs_3_.gain_ref, bf16[768,3072]{1,0:T(8,128)(2,1)S(1)} %get-tuple-element.55.normed_ref, bf16[768,768]{1,0:T(8,128)(2,1)S(1)} %get-tuple-element.54.key_ref, ...), custom_call_target="tpu_custom_call" | custom-call | flops 7247757 | bytes 20054 | tf_op jit(solution)/shard_map/queries_own_frame/pallas_call | solution.py:244
  336.9 10.2 %earlier_frame.3 = (bf16[384,768]{1,0:T(8,128)(2,1)S(1)}, bf16[384,768]{1,0:T(8,128)(2,1)S(1)}) custom-call(s32[2]{0:T(128)S(1)} %copy-done.7, bf16[768,768]{1,0:T(8,128)(2,1)S(1)} %get-tuple-element.56.refs_1_, f32[768,768]{1,0:T(8,128)S(1)} %get-tuple-element.57.refs_2_, f32[768,768]{1,0:T(8,128)S(1)} %get-tuple-element.58.refs_3_, ...), custom_call_target="tpu_custom_call" | custom-call | flops 3623878 | bytes 11796 | tf_op jit(solution)/shard_map/earlier_frame/pallas_call | solution.py:301
  350.4 7.9 %collective-permute-done.26.refs_1_ = bf16[384,768]{1,0:T(8,128)(2,1)S(1)} collective-permute-done((bf16[384,768]{1,0:T(8,128)(2,1)S(1)}, bf16[384,768]{1,0:T(8,128)(2,1)S(1)}, u32[]{:S(2)}, u32[]{:S(2)}) %collective-permute-start.26) | collective-permute-done | bytes 589856 | tf_op jit(solution)/shard_map/ppermute | solution.py:441
  358.3 6.3 %collective-permute-done.27.refs_2_ = bf16[384,768]{1,0:T(8,128)(2,1)S(1)} collective-permute-done((bf16[384,768]{1,0:T(8,128)(2,1)S(1)}, bf16[384,768]{1,0:T(8,128)(2,1)S(1)}, u32[]{:S(2)}, u32[]{:S(2)}) %collective-permute-start.27) | collective-permute-done | bytes 589856 | tf_op jit(solution)/shard_map/ppermute | solution.py:441
  368.8 11.8 %collective-permute-done.28.refs_3_ = bf16[384,768]{1,0:T(8,128)(2,1)S(1)} collective-permute-done((bf16[384,768]{1,0:T(8,128)(2,1)S(1)}, bf16[384,768]{1,0:T(8,128)(2,1)S(1)}, u32[]{:S(2)}, u32[]{:S(2)}) %collective-permute-start.28) | collective-permute-done | bytes 589856 | tf_op jit(solution)/shard_map/ppermute | solution.py:441
  383.5 9.7 %collective-permute-done.29.refs_4_ = bf16[384,768]{1,0:T(8,128)(2,1)S(1)} collective-permute-done((bf16[384,768]{1,0:T(8,128)(2,1)S(1)}, bf16[384,768]{1,0:T(8,128)(2,1)S(1)}, u32[]{:S(2)}, u32[]{:S(2)}) %collective-permute-start.29) | collective-permute-done | bytes 589856 | tf_op jit(solution)/shard_map/ppermute | solution.py:441
  396.1 17.9 %projection_start.3.refs_1_ = f32[768,3072]{1,0:T(8,128)S(1)} custom-call(s32[1]{0:T(128)} %bitcast.refs_0_, bf16[384,768]{1,0:T(8,128)(2,1)S(1)} %collective-permute-done.26.refs_1_, bf16[384,768]{1,0:T(8,128)(2,1)S(1)} %collective-permute-done.27.refs_2_, bf16[384,768]{1,0:T(8,128)(2,1)S(1)} %collective-permute-done.28.refs_3_, ...), custom_call_target="tpu_custom_call" | custom-call | flops 10871635 | bytes 23592 | tf_op jit(solution)/shard_map/projection_start/pallas_call | solution.py:404
  414.1 5.9 %collective-permute-done.32.refs_2_ = bf16[768,3072]{1,0:T(8,128)(2,1)S(1)} collective-permute-done((bf16[768,3072]{1,0:T(8,128)(2,1)S(1)}, bf16[768,3072]{1,0:T(8,128)(2,1)S(1)}, u32[]{:S(2)}, u32[]{:S(2)}) %collective-permute-start.32) | collective-permute-done | bytes 4718624 | tf_op jit(solution)/shard_map/ppermute | solution.py:441
  420.0 10.8 %projection_end.3 = bf16[768,3072]{1,0:T(8,128)(2,1)} custom-call(s32[1]{0:T(128)} %bitcast.refs_0_, f32[768,3072]{1,0:T(8,128)S(1)} %projection_start.3.refs_1_, bf16[768,3072]{1,0:T(8,128)(2,1)S(1)} %collective-permute-done.32.refs_2_, f32[1,3072]{1,0:T(1,128)S(1)} %fusion.refs_3_, bf16[192,768]{1,0:T(8,128)(2,1)S(1)} %collective-permute-done.33.refs_4_, ...), custom_call_target="tpu_custom_call" | custom-call | flops 3623878 | bytes 23592 | tf_op jit(solution)/shard_map/projection_end/pallas_call | solution.py:404
  (99 shorter events, 54.5 us)
Async XLA Ops:
  0.0 20.6 %collective-permute-start.1 = (bf16[2,192,3072]{2,1,0:T(8,128)(2,1)}, bf16[2,192,3072]{2,1,0:T(8,128)(2,1)S(1)}, u32[]{:S(2)}, u32[]{:S(2)}) collective-permute-start(bf16[2,192,3072]{2,1,0:T(8,128)(2,1)} %refs_6_.3), channel_id=1, source_target_pairs={{28,31},{29,28},{30,29},{31,30}} | collective-permute-start | bytes 7077896 | tf_op jit(solution)/shard_map/ppermute | solution.py:441
  0.8 19.8 %collective-permute-start.2 = (bf16[2,192,3072]{2,1,0:T(8,128)(2,1)}, bf16[2,192,3072]{2,1,0:T(8,128)(2,1)}, u32[]{:S(2)}, u32[]{:S(2)}) collective-permute-start(bf16[2,192,3072]{2,1,0:T(8,128)(2,1)} %refs_6_.3), channel_id=1, source_target_pairs={{28,30},{29,31},{30,28},{31,29}} | collective-permute-start | bytes 7077896 | tf_op jit(solution)/shard_map/ppermute | solution.py:441
  2.9 17.8 %collective-permute-start.3 = (bf16[2,192,3072]{2,1,0:T(8,128)(2,1)}, bf16[2,192,3072]{2,1,0:T(8,128)(2,1)}, u32[]{:S(2)}, u32[]{:S(2)}) collective-permute-start(bf16[2,192,3072]{2,1,0:T(8,128)(2,1)} %refs_6_.3), channel_id=1, source_target_pairs={{28,29},{29,30},{30,31},{31,28}} | collective-permute-start | bytes 7077896 | tf_op jit(solution)/shard_map/ppermute | solution.py:441
  16.2 118.8 %collective-permute-start.5 = (bf16[768,1536]{1,0:T(8,128)(2,1)}, bf16[768,1536]{1,0:T(8,128)(2,1)}, u32[]{:S(2)}, u32[]{:S(2)}) collective-permute-start(bf16[768,1536]{1,0:T(8,128)(2,1)} %constant_dynamic-slice_fusion), channel_id=1, source_target_pairs={{0,1},{1,0},{2,3},{3,2},{4,5},{5,4},{6,7},{7,6},{8,9},{9,8},{10,11... | collective-permute-start | bytes 7077896 | tf_op jit(solution)/shard_map/ppermute | solution.py:441
  20.7 114.4 %collective-permute-start.6 = (bf16[768,1536]{1,0:T(8,128)(2,1)}, bf16[768,1536]{1,0:T(8,128)(2,1)}, u32[]{:S(2)}, u32[]{:S(2)}) collective-permute-start(bf16[768,1536]{1,0:T(8,128)(2,1)} %constant_dynamic-slice_fusion), channel_id=1, source_target_pairs={{0,2},{1,3},{2,0},{3,1},{4,6},{5,7},{6,4},{7,5},{8,10},{9,11},{10,... | collective-permute-start | bytes 7077896 | tf_op jit(solution)/shard_map/ppermute | solution.py:441
  36.1 80.7 %collective-permute-start.4 = (bf16[768,768]{1,0:T(8,128)(2,1)S(1)}, bf16[768,768]{1,0:T(8,128)(2,1)S(1)}, u32[]{:S(2)}, u32[]{:S(2)}) collective-permute-start(bf16[768,768]{1,0:T(8,128)(2,1)S(1)} %get-tuple-element.37.key_ref), channel_id=1, source_target_pairs={{0,4},{1,5},{2,6},{3,7},{4,8},{5,9},{6,10},{7,11},{8,12},{9,13},{1... | collective-permute-start | bytes 3538952 | tf_op jit(solution)/shard_map/ppermute | solution.py:441
  42.8 92.3 %collective-permute-start.7 = (bf16[768,768]{1,0:T(8,128)(2,1)S(1)}, bf16[768,768]{1,0:T(8,128)(2,1)S(1)}, u32[]{:S(2)}, u32[]{:S(2)}) collective-permute-start(bf16[768,768]{1,0:T(8,128)(2,1)S(1)} %values.2.value_ref), channel_id=1, source_target_pairs={{0,4},{1,5},{2,6},{3,7},{4,8},{5,9},{6,10},{7,11},{8,12},{9,13},{1... | collective-permute-start | bytes 3538952 | tf_op jit(solution)/shard_map/ppermute | solution.py:441
  145.4 17.4 %collective-permute-start.9 = (bf16[384,768]{1,0:T(8,128)(2,1)S(1)}, bf16[384,768]{1,0:T(8,128)(2,1)S(1)}, u32[]{:S(2)}, u32[]{:S(2)}) collective-permute-start(bf16[384,768]{1,0:T(8,128)(2,1)S(1)} %get-tuple-element.48), channel_id=1, source_target_pairs={{0,4},{1,5},{2,6},{3,7},{4,8},{5,9},{6,10},{7,11},{8,12},{9,13},{1... | collective-permute-start | bytes 1769480 | tf_op jit(solution)/shard_map/ppermute | solution.py:441
  162.8 111.1 %collective-permute-start.16 = (bf16[768,3072]{1,0:T(8,128)(2,1)}, bf16[768,3072]{1,0:T(8,128)(2,1)}, u32[]{:S(2)}, u32[]{:S(2)}) collective-permute-start(bf16[768,3072]{1,0:T(8,128)(2,1)} %get-tuple-element.52), channel_id=1, source_target_pairs={{0,4},{1,5},{2,6},{3,7},{4,8},{5,9},{6,10},{7,11},{8,12},{9,13},{1... | collective-permute-start | bytes 14155784 | tf_op jit(solution)/shard_map/ppermute | solution.py:441
  164.4 16.3 %collective-permute-start.21 = (bf16[384,1536]{1,0:T(8,128)(2,1)S(1)}, bf16[384,1536]{1,0:T(8,128)(2,1)S(1)}, u32[]{:S(2)}, u32[]{:S(2)}) collective-permute-start(bf16[384,1536]{1,0:T(8,128)(2,1)S(1)} %slice.62), channel_id=1, source_target_pairs={{0,2},{1,3},{2,0},{3,1},{4,6},{5,7},{6,4},{7,5},{8,10},{9,11},{10,... | collective-permute-start | bytes 3538952 | tf_op jit(solution)/shard_map/ppermute | solution.py:441
  167.3 19.4 %collective-permute-start.22 = (bf16[384,1536]{1,0:T(8,128)(2,1)S(1)}, bf16[384,1536]{1,0:T(8,128)(2,1)S(1)}, u32[]{:S(2)}, u32[]{:S(2)}) collective-permute-start(bf16[384,1536]{1,0:T(8,128)(2,1)S(1)} %slice.63), channel_id=1, source_target_pairs={{0,1},{1,0},{2,3},{3,2},{4,5},{5,4},{6,7},{7,6},{8,9},{9,8},{10,11... | collective-permute-start | bytes 3538952 | tf_op jit(solution)/shard_map/ppermute | solution.py:441
  168.8 30.4 %collective-permute-start.10 = (bf16[384,768]{1,0:T(8,128)(2,1)S(1)}, bf16[384,768]{1,0:T(8,128)(2,1)S(1)}, u32[]{:S(2)}, u32[]{:S(2)}) collective-permute-start(bf16[384,768]{1,0:T(8,128)(2,1)S(1)} %collective-permute-done.8.refs_1_), channel_id=1, source_target_pairs={{0,1},{1,0},{2,3},{3,2},{4,5},{5,4},{6,7},{7,6},{8,9},{9,8},{10,11... | collective-permute-start | bytes 1769480 | tf_op jit(solution)/shard_map/ppermute | solution.py:441
  171.3 69.2 %collective-permute-start.14 = (bf16[768,1536]{1,0:T(8,128)(2,1)}, bf16[768,1536]{1,0:T(8,128)(2,1)}, u32[]{:S(2)}, u32[]{:S(2)}) collective-permute-start(bf16[768,1536]{1,0:T(8,128)(2,1)} %collective-permute-done.5.refs_8_), channel_id=1, source_target_pairs={{0,4},{1,5},{2,6},{3,7},{4,0},{5,1},{6,2},{7,3},{8,12},{9,13},{10,... | collective-permute-start | bytes 7077896 | tf_op jit(solution)/shard_map/ppermute | solution.py:441
  180.7 67.1 %collective-permute-start.15 = (bf16[768,1536]{1,0:T(8,128)(2,1)}, bf16[768,1536]{1,0:T(8,128)(2,1)}, u32[]{:S(2)}, u32[]{:S(2)}) collective-permute-start(bf16[768,1536]{1,0:T(8,128)(2,1)} %collective-permute-done.6.refs_9_), channel_id=1, source_target_pairs={{0,4},{1,5},{2,6},{3,7},{4,0},{5,1},{6,2},{7,3},{8,12},{9,13},{10,... | collective-permute-start | bytes 7077896 | tf_op jit(solution)/shard_map/ppermute | solution.py:441
  186.7 19.0 %collective-permute-start.11 = (bf16[384,768]{1,0:T(8,128)(2,1)S(1)}, bf16[384,768]{1,0:T(8,128)(2,1)S(1)}, u32[]{:S(2)}, u32[]{:S(2)}) collective-permute-start(bf16[384,768]{1,0:T(8,128)(2,1)S(1)} %collective-permute-done.9.refs_2_), channel_id=1, source_target_pairs={{0,1},{1,0},{2,3},{3,2},{4,5},{5,4},{6,7},{7,6},{8,9},{9,8},{10,11... | collective-permute-start | bytes 1769480 | tf_op jit(solution)/shard_map/ppermute | solution.py:441
  199.2 74.7 %collective-permute-start.23 = (bf16[768,1536]{1,0:T(8,128)(2,1)}, bf16[768,1536]{1,0:T(8,128)(2,1)}, u32[]{:S(2)}, u32[]{:S(2)}) collective-permute-start(bf16[768,1536]{1,0:T(8,128)(2,1)} %constant_dynamic-update-slice_fusion.refs_8_), channel_id=1, source_target_pairs={{0,4},{1,5},{2,6},{3,7},{4,0},{5,1},{6,2},{7,3},{8,12},{9,13},{10,... | collective-permute-start | bytes 7077896 | tf_op jit(solution)/shard_map/ppermute | solution.py:441
  219.7 14.8 %collective-permute-start.13 = (bf16[384,768]{1,0:T(8,128)(2,1)S(1)}, bf16[384,768]{1,0:T(8,128)(2,1)}, u32[]{:S(2)}, u32[]{:S(2)}) collective-permute-start(bf16[384,768]{1,0:T(8,128)(2,1)S(1)} %collective-permute-done.9.refs_2_), channel_id=1, source_target_pairs={{0,2},{1,3},{2,0},{3,1},{4,6},{5,7},{6,4},{7,5},{8,10},{9,11},{10,... | collective-permute-start | bytes 1769480 | tf_op jit(solution)/shard_map/ppermute | solution.py:441
  240.6 33.4 %collective-permute-start.18 = (bf16[192,768]{1,0:T(8,128)(2,1)S(1)}, bf16[192,768]{1,0:T(8,128)(2,1)S(1)}, u32[]{:S(2)}, u32[]{:S(2)}) collective-permute-start(bf16[192,768]{1,0:T(8,128)(2,1)S(1)} %slice.59), channel_id=1, source_target_pairs={{0,1},{1,0},{2,3},{3,2},{4,5},{5,4},{6,7},{7,6},{8,9},{9,8},{10,11... | collective-permute-start | bytes 884744 | tf_op jit(solution)/shard_map/ppermute | solution.py:441
  245.5 28.4 %collective-permute-start.19 = (bf16[192,768]{1,0:T(8,128)(2,1)S(1)}, bf16[192,768]{1,0:T(8,128)(2,1)S(1)}, u32[]{:S(2)}, u32[]{:S(2)}) collective-permute-start(bf16[192,768]{1,0:T(8,128)(2,1)S(1)} %slice.60), channel_id=1, source_target_pairs={{0,2},{1,3},{2,0},{3,1},{4,6},{5,7},{6,4},{7,5},{8,10},{9,11},{10,... | collective-permute-start | bytes 884744 | tf_op jit(solution)/shard_map/ppermute | solution.py:441
  247.7 26.2 %collective-permute-start.20 = (bf16[192,768]{1,0:T(8,128)(2,1)S(1)}, bf16[192,768]{1,0:T(8,128)(2,1)S(1)}, u32[]{:S(2)}, u32[]{:S(2)}) collective-permute-start(bf16[192,768]{1,0:T(8,128)(2,1)S(1)} %slice.61), channel_id=1, source_target_pairs={{0,1},{1,0},{2,3},{3,2},{4,5},{5,4},{6,7},{7,6},{8,9},{9,8},{10,11... | collective-permute-start | bytes 884744 | tf_op jit(solution)/shard_map/ppermute | solution.py:441
  301.1 17.5 %collective-permute-start.24 = (bf16[768,768]{1,0:T(8,128)(2,1)S(1)}, bf16[768,768]{1,0:T(8,128)(2,1)S(1)}, u32[]{:S(2)}, u32[]{:S(2)}) collective-permute-start(bf16[768,768]{1,0:T(8,128)(2,1)S(1)} %get-tuple-element.54.key_ref), channel_id=1, source_target_pairs={{0,4},{1,5},{2,6},{3,7},{4,8},{5,9},{6,10},{7,11},{8,12},{9,13},{1... | collective-permute-start | bytes 3538952 | tf_op jit(solution)/shard_map/ppermute | solution.py:441
  308.0 28.9 %collective-permute-start.25 = (bf16[768,768]{1,0:T(8,128)(2,1)S(1)}, bf16[768,768]{1,0:T(8,128)(2,1)S(1)}, u32[]{:S(2)}, u32[]{:S(2)}) collective-permute-start(bf16[768,768]{1,0:T(8,128)(2,1)S(1)} %values.3.value_ref), channel_id=1, source_target_pairs={{0,4},{1,5},{2,6},{3,7},{4,8},{5,9},{6,10},{7,11},{8,12},{9,13},{1... | collective-permute-start | bytes 3538952 | tf_op jit(solution)/shard_map/ppermute | solution.py:441
  347.9 16.7 %collective-permute-start.27 = (bf16[384,768]{1,0:T(8,128)(2,1)S(1)}, bf16[384,768]{1,0:T(8,128)(2,1)S(1)}, u32[]{:S(2)}, u32[]{:S(2)}) collective-permute-start(bf16[384,768]{1,0:T(8,128)(2,1)S(1)} %get-tuple-element.62), channel_id=1, source_target_pairs={{0,4},{1,5},{2,6},{3,7},{4,8},{5,9},{6,10},{7,11},{8,12},{9,13},{1... | collective-permute-start | bytes 1769480 | tf_op jit(solution)/shard_map/ppermute | solution.py:441
  364.6 55.3 %collective-permute-start.32 = (bf16[768,3072]{1,0:T(8,128)(2,1)S(1)}, bf16[768,3072]{1,0:T(8,128)(2,1)S(1)}, u32[]{:S(2)}, u32[]{:S(2)}) collective-permute-start(bf16[768,3072]{1,0:T(8,128)(2,1)S(1)} %bitcast.17), channel_id=1, source_target_pairs={{0,4},{1,5},{2,6},{3,7},{4,8},{5,9},{6,10},{7,11},{8,12},{9,13},{1... | collective-permute-start | bytes 14155784 | tf_op jit(solution)/shard_map/ppermute | solution.py:441
  364.6 15.9 %collective-permute-start.28 = (bf16[384,768]{1,0:T(8,128)(2,1)S(1)}, bf16[384,768]{1,0:T(8,128)(2,1)S(1)}, u32[]{:S(2)}, u32[]{:S(2)}) collective-permute-start(bf16[384,768]{1,0:T(8,128)(2,1)S(1)} %collective-permute-done.26.refs_1_), channel_id=1, source_target_pairs={{0,1},{1,0},{2,3},{3,2},{4,5},{5,4},{6,7},{7,6},{8,9},{9,8},{10,11... | collective-permute-start | bytes 1769480 | tf_op jit(solution)/shard_map/ppermute | solution.py:441
  365.4 17.1 %collective-permute-start.30 = (bf16[384,768]{1,0:T(8,128)(2,1)S(1)}, bf16[384,768]{1,0:T(8,128)(2,1)S(1)}, u32[]{:S(2)}, u32[]{:S(2)}) collective-permute-start(bf16[384,768]{1,0:T(8,128)(2,1)S(1)} %collective-permute-done.26.refs_1_), channel_id=1, source_target_pairs={{0,2},{1,3},{2,0},{3,1},{4,6},{5,7},{6,4},{7,5},{8,10},{9,11},{10,... | collective-permute-start | bytes 1769480 | tf_op jit(solution)/shard_map/ppermute | solution.py:441
  367.1 26.1 %collective-permute-start.29 = (bf16[384,768]{1,0:T(8,128)(2,1)S(1)}, bf16[384,768]{1,0:T(8,128)(2,1)S(1)}, u32[]{:S(2)}, u32[]{:S(2)}) collective-permute-start(bf16[384,768]{1,0:T(8,128)(2,1)S(1)} %collective-permute-done.27.refs_2_), channel_id=1, source_target_pairs={{0,1},{1,0},{2,3},{3,2},{4,5},{5,4},{6,7},{7,6},{8,9},{9,8},{10,11... | collective-permute-start | bytes 1769480 | tf_op jit(solution)/shard_map/ppermute | solution.py:441
  368.2 26.8 %collective-permute-start.31 = (bf16[384,768]{1,0:T(8,128)(2,1)S(1)}, bf16[384,768]{1,0:T(8,128)(2,1)S(1)}, u32[]{:S(2)}, u32[]{:S(2)}) collective-permute-start(bf16[384,768]{1,0:T(8,128)(2,1)S(1)} %collective-permute-done.27.refs_2_), channel_id=1, source_target_pairs={{0,2},{1,3},{2,0},{3,1},{4,6},{5,7},{6,4},{7,5},{8,10},{9,11},{10,... | collective-permute-start | bytes 1769480 | tf_op jit(solution)/shard_map/ppermute | solution.py:441
  380.6 33.5 %collective-permute-start.33 = (bf16[192,768]{1,0:T(8,128)(2,1)S(1)}, bf16[192,768]{1,0:T(8,128)(2,1)S(1)}, u32[]{:S(2)}, u32[]{:S(2)}) collective-permute-start(bf16[192,768]{1,0:T(8,128)(2,1)S(1)} %slice.64), channel_id=1, source_target_pairs={{0,2},{1,3},{2,0},{3,1},{4,6},{5,7},{6,4},{7,5},{8,10},{9,11},{10,... | collective-permute-start | bytes 884744 | tf_op jit(solution)/shard_map/ppermute | solution.py:441
  382.4 31.6 %collective-permute-start.34 = (bf16[192,768]{1,0:T(8,128)(2,1)S(1)}, bf16[192,768]{1,0:T(8,128)(2,1)S(1)}, u32[]{:S(2)}, u32[]{:S(2)}) collective-permute-start(bf16[192,768]{1,0:T(8,128)(2,1)S(1)} %slice.65), channel_id=1, source_target_pairs={{0,1},{1,0},{2,3},{3,2},{4,5},{5,4},{6,7},{7,6},{8,9},{9,8},{10,11... | collective-permute-start | bytes 884744 | tf_op jit(solution)/shard_map/ppermute | solution.py:441
  393.3 20.8 %collective-permute-start.35 = (bf16[192,768]{1,0:T(8,128)(2,1)S(1)}, bf16[192,768]{1,0:T(8,128)(2,1)S(1)}, u32[]{:S(2)}, u32[]{:S(2)}) collective-permute-start(bf16[192,768]{1,0:T(8,128)(2,1)S(1)} %slice.66), channel_id=1, source_target_pairs={{0,2},{1,3},{2,0},{3,1},{4,6},{5,7},{6,4},{7,5},{8,10},{9,11},{10,... | collective-permute-start | bytes 884744 | tf_op jit(solution)/shard_map/ppermute | solution.py:441
  395.1 19.0 %collective-permute-start.36 = (bf16[192,768]{1,0:T(8,128)(2,1)S(1)}, bf16[192,768]{1,0:T(8,128)(2,1)S(1)}, u32[]{:S(2)}, u32[]{:S(2)}) collective-permute-start(bf16[192,768]{1,0:T(8,128)(2,1)S(1)} %slice.67), channel_id=1, source_target_pairs={{0,1},{1,0},{2,3},{3,2},{4,5},{5,4},{6,7},{7,6},{8,9},{9,8},{10,11... | collective-permute-start | bytes 884744 | tf_op jit(solution)/shard_map/ppermute | solution.py:441
  (17 other events, 457.6 us)

commit v5 on v4

--- a/solution.py
+++ b/solution.py
@@ -27,11 +27,11 @@
     return pltpu.with_memory_space_constraint(array, pltpu.HBM)
 
 
-def cost(flops, nbytes, transcendentals=0):
+def cost(flops, nbytes, transcendentals=0, share=1000):
     return pl.CostEstimate(
-        flops=int(flops) // 1000,
-        bytes_accessed=int(nbytes) // 1000,
-        transcendentals=int(transcendentals) // 1000,
+        flops=int(flops) // share,
+        bytes_accessed=int(nbytes) // share,
+        transcendentals=int(transcendentals) // share,
     )
 
 
@@ -56,28 +56,32 @@
         yield pltpu.make_async_copy(w_any.at[part, at], w_ref.at[at], w_sems.at[i])
 
 
-def key_kernel(*refs, tensor_size, noise_step):
+def key_kernel(*refs, tensor_size):
     info_ref, scale_ref, shift_ref, gain_ref, w_any, z_any, noise_any = refs[:7]
     piece_refs = refs[7 : 7 + tensor_size - 1]
-    key_ref, normed_ref, state_ref, w_ref, sem, w_sems = refs[6 + tensor_size :]
+    key_ref, normed_any, state_any = refs[6 + tensor_size : 9 + tensor_size]
+    state_ref, normed_ref, inverse_ref, w_ref, sem, out_sems, w_sems = refs[9 + tensor_size :]
     step = pl.program_id(0)
     rows = state_ref.shape[0]
-    piece_rows = noise_any.shape[1]
+    piece_rows = noise_any.shape[0]
     cols = key_ref.shape[1]
+    state_copy = pltpu.make_async_copy(state_ref, state_any, out_sems.at[0])
+    normed_copy = pltpu.make_async_copy(normed_ref, normed_any, out_sems.at[1])
 
     @pl.when(step == 0)
     def _():
-        for copy in weight_copies(w_any, 1, w_ref, w_sems):
-            copy.start()
-
         @pl.when(info_ref[0] == 0)
         def _():
             copy = pltpu.make_async_copy(z_any, state_ref, sem.at[0])
             copy.start()
+            for weight_copy in weight_copies(w_any, 1, w_ref, w_sems):
+                weight_copy.start()
             copy.wait()
 
         @pl.when(info_ref[0] != 0)
         def _():
+            for weight_copy in weight_copies(w_any, 1, w_ref, w_sems):
+                weight_copy.start()
             for block in range(tensor_size):
                 away = lax.rem(block + tensor_size - info_ref[1], tensor_size)
                 for d in range(tensor_size):
@@ -86,22 +90,32 @@
                     @pl.when(away == d)
                     def _():
                         copy = pltpu.make_async_copy(
-                            source.at[noise_step],
+                            source,
                             state_ref.at[pl.ds(block * piece_rows, piece_rows)],
                             sem.at[0],
                         )
                         copy.start()
                         copy.wait()
 
-        def one(i, carry):
+        state_copy.start()
+
+        def measure(i, carry):
             at = pl.ds(pl.multiple_of(i * 16, 16), 16)
             state = state_ref[at, :].astype(F32)
             mean = jnp.mean(state * state, axis=-1, keepdims=True)
-            state = state * lax.rsqrt(mean + EPS) * scale_ref[...] + shift_ref[...]
-            normed_ref[at, :] = state.astype(BF16)
+            inverse_ref[at, :] = jnp.broadcast_to(lax.rsqrt(mean + EPS), (16, HD))
             return carry
 
-        lax.fori_loop(0, rows // 16, one, 0, unroll=4)
+        def apply(i, carry):
+            at = pl.ds(pl.multiple_of(i * 16, 16), 16)
+            inverse = inverse_ref[at, :][:, :1]
+            state = state_ref[at, :].astype(F32) * inverse
+            normed_ref[at, :] = (state * scale_ref[...] + shift_ref[...]).astype(BF16)
+            return carry
+
+        lax.fori_loop(0, rows // 16, measure, 0, unroll=4)
+        lax.fori_loop(0, rows // 16, apply, 0, unroll=2)
+        normed_copy.start()
         for copy in weight_copies(w_any, 1, w_ref, w_sems):
             copy.wait()
 
@@ -109,14 +123,19 @@
     product = jnp.dot(normed_ref[...], w_ref[:, at], preferred_element_type=F32)
     key_ref[...] = head_normalized(product, gain_ref[1:2])
 
-
-def project_keys(info, scale1, shift, gains, qkv_weight, z, noise_all, noise_step, noise_pieces):
+    @pl.when(step == pl.num_programs(0) - 1)
+    def _():
+        state_copy.wait()
+        normed_copy.wait()
+
+
+def project_keys(info, scale1, shift, gains, qkv_weight, z, noise, noise_pieces):
     rows, width = z.shape
     head_cols = qkv_weight.shape[2]
     cols = tile_cols(head_cols)
     tensor_size = len(noise_pieces) + 1
     return pl.pallas_call(
-        functools.partial(key_kernel, tensor_size=tensor_size, noise_step=noise_step),
+        functools.partial(key_kernel, tensor_size=tensor_size),
         grid_spec=pltpu.PrefetchScalarGridSpec(
             num_scalar_prefetch=1,
             grid=(head_cols // cols,),
@@ -126,14 +145,14 @@
                 pl.BlockSpec((2, HD), lambda j, i: (0, 0)),
             ]
             + [ANY] * (2 + tensor_size),
-            out_specs=[
-                pl.BlockSpec((rows, cols), lambda j, i: (0, j)),
-                pl.BlockSpec((rows, width), lambda j, i: (0, 0)),
-                pl.BlockSpec((rows, width), lambda j, i: (0, 0)),
-            ],
+            out_specs=[pl.BlockSpec((rows, cols), lambda j, i: (0, j)), ANY, ANY],
             scratch_shapes=[
+                pltpu.VMEM((rows, width), BF16),
+                pltpu.VMEM((rows, width), BF16),
+                pltpu.VMEM((rows, HD), F32),
                 pltpu.VMEM((width, head_cols), BF16),
                 pltpu.SemaphoreType.DMA((1,)),
+                pltpu.SemaphoreType.DMA((2,)),
                 pltpu.SemaphoreType.DMA((4,)),
             ],
         ),
@@ -153,7 +172,8 @@
         scale1,
         shift,
         gains,
-        *[in_hbm(a) for a in (qkv_weight, z, noise_all)],
+        *[in_hbm(a) for a in (qkv_weight, z)],
+        noise,
         *noise_pieces,
     )
 
@@ -208,6 +228,21 @@
     return total[:, :HD], total[:, HD:]
 
 
+def attention_tiles(query, key_ref, value_ref, finish):
+    rows, cols = query.shape
+    tile = math.gcd(rows, 256)
+    waiting = None
+    for h in range(cols // HD):
+        at = slice(h * HD, (h + 1) * HD)
+        for r in range(rows // tile):
+            row = slice(r * tile, (r + 1) * tile)
+            scores = attend(query[row, at], key_ref[:, at])
+            if waiting is not None:
+                finish(*waiting)
+            waiting = (scores, row, at)
+    finish(*waiting)
+
+
 def own_kernel(
     gain_ref, normed_ref, key_ref, value_ref, w_any,
     query_ref, acc_ref, top_ref, total_ref, w_ref, w_sems,
@@ -226,14 +261,15 @@
     product = jnp.dot(normed_ref[...], w_ref[:, inside], preferred_element_type=F32)
     query = head_normalized(product, gain_ref[0:1])
     query_ref[...] = query
-    for h in range(cols // HD):
-        at = slice(h * HD, (h + 1) * HD)
-        scores = attend(query[:, at], key_ref[:, at])
+
+    def finish(scores, row, at):
         top = jnp.max(scores, axis=-1, keepdims=True)
         acc, total = weigh(scores, top, value_ref[:, at])
-        acc_ref[:, at] = acc
-        total_ref[:, at] = total
-        top_ref[:, at] = jnp.broadcast_to(top, acc.shape)
+        acc_ref[row, at] = acc
+        total_ref[row, at] = total
+        top_ref[row, at] = jnp.broadcast_to(top, acc.shape)
+
+    attention_tiles(query, key_ref, value_ref, finish)
 
 
 def own_attention(gains, normed, qkv_weight, key, value):
@@ -273,26 +309,30 @@
     out_refs = refs[7:]
     rows = query_ref.shape[0] // chunks
 
-    def store(at, result):
+    def store(row, at, result):
         for c, out_ref in enumerate(out_refs):
-            out_ref[:, at] = result[c * rows : (c + 1) * rows]
+            first, end = max(row.start, c * rows), min(row.stop, (c + 1) * rows)
+            if first < end:
+                inside = slice(first - c * rows, end - c * rows)
+                out_ref[inside, at] = result[first - row.start : end - row.start]
 
     @pl.when(info_ref[0] != 0)
     def _():
-        store(slice(None), (acc_ref[...] / total_ref[...]).astype(BF16))
+        every = slice(0, query_ref.shape[0])
+        store(every, slice(None), (acc_ref[...] / total_ref[...]).astype(BF16))
 
     @pl.when(info_ref[0] == 0)
     def _():
-        for h in range(query_ref.shape[1] // HD):
-            at = slice(h * HD, (h + 1) * HD)
-            old_top = top_ref[:, at][:, :1]
-            scores = attend(query_ref[:, at], key_ref[:, at])
+        def finish(scores, row, at):
+            old_top = top_ref[row, at][:, :1]
             top = jnp.maximum(jnp.max(scores, axis=-1, keepdims=True), old_top)
             acc, total = weigh(scores, top, value_ref[:, at])
             kept = jnp.exp2(old_top - top)
-            acc = acc + acc_ref[:, at] * kept
-            total = total + total_ref[:, at] * kept
-            store(at, (acc / total).astype(BF16))
+            acc = acc + acc_ref[row, at] * kept
+            total = total + total_ref[row, at] * kept
+            store(row, at, (acc / total).astype(BF16))
+
+        attention_tiles(query_ref[...], key_ref, value_ref, finish)
 
 
 def earlier_attention(info, query, acc, top, total, key, value, chunks):
@@ -375,14 +415,18 @@
                 weight_copy(half, k).wait()
 
     half = step // half_blocks
-    inside = pl.ds(pl.multiple_of(lax.rem(step, half_blocks) * cols, HD), cols)
-    update = acc_in[...] if last else None
-    for k in range(size):
-        term = jnp.dot(held_ref[k], w_ref[half, k, :, inside], preferred_element_type=F32)
-        update = term if update is None else update + term
-    if last:
-        update = resid_ref[...].astype(F32) + gate_ref[...] * update
-    out_ref[...] = update.astype(out_ref.dtype)
+    tile = tile_cols(cols)
+    for t in range(cols // tile):
+        at = slice(t * tile, (t + 1) * tile)
+        first = lax.rem(step, half_blocks) * cols + t * tile
+        inside = pl.ds(pl.multiple_of(first, HD), tile)
+        update = acc_in[:, at].astype(F32) if last else None
+        for k in range(size):
+            term = jnp.dot(held_ref[k], w_ref[half, k, :, inside], preferred_element_type=F32)
+            update = term if update is None else update + term
+        if last:
+            update = resid_ref[:, at].astype(F32) + gate_ref[:, at] * update
+        out_ref[:, at] = update.astype(BF16)
 
 
 def output_projection(parity, pieces, wholes, mine, theirs, finish=None):
@@ -390,7 +434,7 @@
     rows = sum(part.shape[0] for part in pieces[0])
     width = 2 * half_width
     size = len(pieces)
-    cols = tile_cols(half_width)
+    cols = half_width // 2 if half_width % 512 == 0 else half_width
     half_blocks = half_width // cols
     parts = max(len(p) for p in pieces)
     flat = [part for group in pieces for part in group]
@@ -422,11 +466,11 @@
                 pltpu.SemaphoreType.DMA((2, size)),
             ],
         ),
-        out_shape=(pltpu.HBM if last else jax.ShapeDtypeStruct)((rows, width), BF16 if last else F32),
-        compiler_params=compiler_params(16 if last else 28),
+        out_shape=(pltpu.HBM if last else jax.ShapeDtypeStruct)((rows, width), BF16),
+        compiler_params=compiler_params(24 if last else 32),
         cost_estimate=cost(
             2 * rows * width * head_cols * size,
-            (8 if last else 4) * rows * width + 2 * head_cols * width * size,
+            (6 if last else 2) * rows * width + 2 * head_cols * width * size,
         ),
         name="projection_end" if last else "projection_start",
     )(parity, *(finish if last else ()), *flat, *weights)
@@ -441,27 +485,28 @@
     return lax.ppermute(block, AXES, pairs)
 
 
-def gather_pieces(block, queue_size, tensor_size, frames=None, after=None):
+def one_hop(block, queue_size, tensor_size, frames=None):
     half = tensor_size // 2
-
-    def low(q, t):
-        return q, t ^ 1
-
-    def high(j):
-        return lambda q, t: (q, (t // 2 - j) % half * 2 + t % 2)
-
     args = (queue_size, tensor_size, frames)
-    rows = block.shape[0] // 2
-    near = send(block, low, *args)
-    if after is not None:
-        block, _ = lax.optimization_barrier((block, after))
-    far = [send(block, high(j), *args) for j in range(1, half)]
+    near = send(block, lambda q, t: (q, t ^ 1), *args)
+    return [near] + [send(block, away(j, half), *args) for j in range(1, half)]
+
+
+def two_hops(blocks, queue_size, tensor_size, frames=None):
+    half = tensor_size // 2
+    args = (queue_size, tensor_size, frames)
+    near, far = blocks[0], blocks[1:]
+    rows = near.shape[0] // 2
     corners = []
     for j in range(1, half):
-        top = send(near[:rows], high(j), *args)
-        bottom = send(far[j - 1][rows:], low, *args)
+        top = send(near[:rows], away(j, half), *args)
+        bottom = send(far[j - 1][rows:], lambda q, t: (q, t ^ 1), *args)
         corners.append([top, bottom])
-    return [near, *far], corners
+    return corners
+
+
+def away(j, half):
+    return lambda q, t: (q, (t // 2 - j) % half * 2 + t % 2)
 
 
 def body(
@@ -483,23 +528,22 @@
         return send(block, lambda q, t: (q ^ 1, t), *mesh_sizes)
 
     worked_level = send(levels, lambda q, t: ((q - 1) % queue_size, t), *mesh_sizes)[0]
-    noise_pieces = [
-        send(
-            fresh_noise,
-            lambda q, t: (q, (t - d) % tensor_size),
-            *mesh_sizes,
-            [queue_size - 1],
-        )
-        for d in range(1, tensor_size)
-    ]
+
+    def gather_noise(noise):
+        return [
+            send(noise, lambda q, t: (q, (t - d) % tensor_size), *mesh_sizes, [queue_size - 1])
+            for d in range(1, tensor_size)
+        ]
+
+    noise = fresh_noise[0]
+    noise_pieces = gather_noise(noise)
     half_weight = lax.dynamic_slice(
         out_weight, (0, parity[0] * (width // 2)), (out_weight.shape[0], width // 2)
     )
-    half_weight, latents = lax.optimization_barrier((half_weight, latents))
-    mine, mine_corners = gather_pieces(half_weight, *mesh_sizes, after=noise_pieces)
-    theirs = [sibling(block) for block in mine]
-    mine_corners = [jnp.concatenate(parts, axis=0) for parts in mine_corners]
-    theirs_corners = [sibling(block) for block in mine_corners]
+    half_weight, latents, noise_pieces = lax.optimization_barrier(
+        (half_weight, latents, noise_pieces)
+    )
+    mine = one_hop(half_weight, *mesh_sizes)
 
     def modulation(level):
         row = lax.dynamic_slice(mod_table, (level, 0), (1, 3 * width)).astype(F32)
@@ -515,27 +559,39 @@
     for step_index in range(STEPS):
         final = step_index == STEPS - 1
         key, normed, state = project_keys(
-            info, scale1, shift, gains, qkv_weight, frame, fresh_noise, step_index, noise_pieces
+            info, scale1, shift, gains, qkv_weight, frame, noise, noise_pieces
         )
         earlier_key = ring(key)
         value = project_values(normed, qkv_weight)
         earlier_value = ring(value)
         normed, earlier_key = lax.optimization_barrier((normed, earlier_key))
         query, *own = own_attention(gains, normed, qkv_weight, key, value)
+        sent_state, query, earlier_value = lax.optimization_barrier(
+            (state, query, earlier_value)
+        )
+        resid = ring(sent_state)
         if not final:
             query, mine = lax.optimization_barrier((query, mine))
+            mine_corners = [
+                jnp.concatenate(parts, axis=0) for parts in two_hops(mine, *mesh_sizes)
+            ]
+            theirs = [sibling(block) for block in mine]
+            query, theirs = lax.optimization_barrier((query, theirs))
         attended = earlier_attention(
-            info, query, *own, earlier_key, earlier_value, CHUNKS
+            info, query, *own, earlier_key, earlier_value, CHUNKS if final else 1
         )
         attended = [ring(block) for block in attended]
+        if not final:
+            attended, mine_corners = lax.optimization_barrier((attended, mine_corners))
+            theirs_corners = [sibling(block) for block in mine_corners]
         targets = range(queue_size) if final else range(queue_size - 1)
-        gathered = [gather_pieces(block, *mesh_sizes, targets) for block in attended]
-        sent_state, _ = lax.optimization_barrier((state, attended))
-        resid = ring(sent_state)
-        direct = [attended] + [list(p) for p in zip(*[near for near, _ in gathered])]
-        corners = [
-            [half for parts in p for half in parts] for p in zip(*[c for _, c in gathered])
-        ]
+        near = [one_hop(block, *mesh_sizes, targets) for block in attended]
+        beyond = [two_hops(blocks, *mesh_sizes, targets) for blocks in near]
+        direct = [attended] + [list(parts) for parts in zip(*near)]
+        corners = [[half for parts in p for half in parts] for p in zip(*beyond)]
+        if not final:
+            noise, corners = lax.optimization_barrier((fresh_noise[step_index + 1], corners))
+            noise_pieces = gather_noise(noise)
         begun = output_projection(parity, direct, [out_weight], mine, theirs)
         frame = output_projection(
             parity, corners, [], mine_corners, theirs_corners, (begun, resid, gate)

time: 433 us -> 419 us (0.968)
  Pallas kernels: 159 us -> 143 us
  waiting for transfers between devices: 193 us -> 199 us
    pallas_call x4, Pallas kernels: 61.2 us -> 50.4 us  [output_projection(): pl.pallas_call(functools.partial(output_kernel, part_counts=tuple((len(p)...]
    pallas_call x2, Pallas kernels: 20.5 us -> 13.8 us  [earlier_attention(): pl.pallas_call(functools.partial(earlier_kernel, chunks=chunks), grid_spe...]
    ppermute x37 -> x35, waiting for transfers between devices: 193 us -> 199 us  [send(): return lax.ppermute(block, AXES, pairs)]
    slice x10 -> x8, local copies, waits for them, and re-layouts: 5.72 us -> 0.31 us  [the longest x4 0.16 us: two_hops(): top = send(near[:rows], away(j, half), *args)]
    ppermute x37 -> x35, starting transfers between devices: 58.2 us -> 54.6 us  [send(): return lax.ppermute(block, AXES, pairs)]
  transfers between devices with their start and end apart: 37 -> 35, of which waited for: 16 -> 15; matrix products, arithmetic and copies ran while one was open for 3% -> 2% of each run, Pallas kernels for 23% -> 29%
where the time goes in v5:
time: 419 us; the launch traced here: 416 us
  waiting for transfers between devices  199 us (47%)
  Pallas kernels  143 us (34%)
  starting transfers between devices  54.6 us (13%)
  local copies, waits for them, and re-layouts  11.7 us (3%)
  other arithmetic  4.7 us (1%)
    ppermute x35, waiting for transfers between devices, send(): return lax.ppermute(block, AXES, pairs)  199 us
    ppermute x35, starting transfers between devices, send(): return lax.ppermute(block, AXES, pairs)  54.6 us
    pallas_call x4, Pallas kernels, output_projection(): pl.pallas_call(functools.partial(output_kernel, part_counts=tuple((len(p)...  50.4 us
    pallas_call x2, Pallas kernels, own_attention(): pl.pallas_call(own_kernel, grid=(head_cols // cols,), in_specs=[pl.BlockS...  36.4 us
    pallas_call x2, Pallas kernels, project_keys(): pl.pallas_call(functools.partial(key_kernel, tensor_size=tensor_size), gr...  28.5 us
    pallas_call x2, Pallas kernels, earlier_attention(): pl.pallas_call(functools.partial(earlier_kernel, chunks=chunks), grid_spe...  13.8 us
    pallas_call x2, Pallas kernels, project_values(): pl.pallas_call(value_kernel, grid=(head_cols // cols,), in_specs=[pl.Bloc...  13.4 us
  transfers between devices with their start and end apart: 35, of which 15 were waited for; matrix products, arithmetic and copies ran while one was open for 2% of the time, Pallas kernels for 29%

profile of v5, /device:TPU:0, one launch (start us, length us, event | category | flops | bytes accessed | tf_op | source)
XLA Modules:
  0.0 415.9 jit_solution(14405164481846193778)
XLA Ops:
  6.0 8.9 %collective-permute-start = (s32[1]{0:T(128)}, s32[1]{0:T(128)}, u32[]{:S(2)}, u32[]{:S(2)}) collective-permute-start(s32[1]{0:T(128)} %param.10), channel_id=1, source_target_pairs={{0,28},{1,29},{2,30},{3,31},{4,0},{5,1},{6,2},{7,3},{8,4},{9,5},{1... | collective-permute-start | bytes 20 | tf_op jit(solution)/shard_map/ppermute | solution.py:485
  15.5 3.2 constant_dynamic-slice_fusion
  20.6 2.5 collective-permute-start.6
  25.2 14.2 %norm_keys.2 = (bf16[768,768]{1,0:T(8,128)(2,1)S(1)}, bf16[768,3072]{1,0:T(8,128)(2,1)S(1)}, bf16[768,3072]{1,0:T(8,128)(2,1)}) custom-call(s32[2]{0:T(128)S(1)} %copy-done.8, f32[1,3072]{1,0:T(1,128)S(1)} %get-tuple-element.92.refs_1_, f32[1,3072]{1,0:T(1,128)S(1)} %get-tuple-element.91.refs_2_, f32[2,128]{1,0:T(2,128)S(1)} %pad_maximum_fusion.1.refs_3_.gain_ref, ...), custom_call_target="tpu_custom_call" | custom-call | flops 3623878 | bytes 20054 | tf_op jit(solution)/shard_map/norm_keys/pallas_call | solution.py:137
  39.5 6.6 %values.2.value_ref = bf16[768,768]{1,0:T(8,128)(2,1)S(1)} custom-call(bf16[768,3072]{1,0:T(8,128)(2,1)S(1)} %get-tuple-element.54.normed_ref, bf16[3,3072,768]{2,1,0:T(8,128)(2,1)} %w_any.7), custom_call_target="tpu_custom_call" | custom-call | flops 3623878 | bytes 10616 | tf_op jit(solution)/shard_map/values/pallas_call | solution.py:201
  46.2 37.8 %collective-permute-done.4.refs_5_ = bf16[768,768]{1,0:T(8,128)(2,1)S(1)} collective-permute-done((bf16[768,768]{1,0:T(8,128)(2,1)S(1)}, bf16[768,768]{1,0:T(8,128)(2,1)S(1)}, u32[]{:S(2)}, u32[]{:S(2)}) %collective-permute-start.4) | collective-permute-done | bytes 1179680 | tf_op jit(solution)/shard_map/ppermute | solution.py:485
  84.0 18.2 %queries_own_frame.2 = (bf16[768,768]{1,0:T(8,128)(2,1)S(1)}, f32[768,768]{1,0:T(8,128)S(1)}, f32[768,768]{1,0:T(8,128)S(1)}, f32[768,768]{1,0:T(8,128)S(1)}) custom-call(f32[2,128]{1,0:T(2,128)S(1)} %pad_maximum_fusion.1.refs_3_.gain_ref, bf16[768,3072]{1,0:T(8,128)(2,1)S(1)} %get-tuple-element.54.normed_ref, ...), custom_call_target="tpu_custom_call" | custom-call | flops 7247757 | bytes 20054 | tf_op jit(solution)/shard_map/queries_own_frame/pallas_call | solution.py:280
  106.9 6.4 %collective-permute-done.9.refs_8_.refs_11_ = bf16[768,1536]{1,0:T(8,128)(2,1)S(1)} collective-permute-done((bf16[768,1536]{1,0:T(8,128)(2,1)S(1)}, bf16[768,1536]{1,0:T(8,128)(2,1)S(1)}, u32[]{:S(2)}, u32[]{:S(2)}) %collective-permute-start.9) | collective-permute-done | bytes 2359328 | tf_op jit(solution)/shard_map/ppermute | solution.py:485
  113.2 6.9 %earlier_frame.2 = bf16[768,768]{1,0:T(8,128)(2,1)S(1)} custom-call(s32[2]{0:T(128)S(1)} %copy-done.9, bf16[768,768]{1,0:T(8,128)(2,1)S(1)} %get-tuple-element.61.refs_1_, f32[768,768]{1,0:T(8,128)S(1)} %get-tuple-element.62.refs_2_, f32[768,768]{1,0:T(8,128)S(1)} %get-tuple-element.63.refs_3_, f32[768,768]{1,0:T(8,128)S(1)} %get-tuple-element.64.refs_4_, ...), custom_call_target="tpu_custom_call" | custom-call | flops 3623878 | bytes 11796 | tf_op jit(solution)/shard_map/earlier_frame/pallas_call | solution.py:341
  120.6 10.4 %collective-permute-done.12 = bf16[384,1536]{1,0:T(8,128)(2,1)S(1)} collective-permute-done((bf16[384,1536]{1,0:T(8,128)(2,1)S(1)}, bf16[384,1536]{1,0:T(8,128)(2,1)S(1)}, u32[]{:S(2)}, u32[]{:S(2)}) %collective-permute-start.12) | collective-permute-done | bytes 1179680 | tf_op jit(solution)/shard_map/ppermute | solution.py:485
  133.0 38.0 %collective-permute-done.10.refs_1_ = bf16[768,768]{1,0:T(8,128)(2,1)S(1)} collective-permute-done((bf16[768,768]{1,0:T(8,128)(2,1)S(1)}, bf16[768,768]{1,0:T(8,128)(2,1)S(1)}, u32[]{:S(2)}, u32[]{:S(2)}) %collective-permute-start.10) | collective-permute-done | bytes 1179680 | tf_op jit(solution)/shard_map/ppermute | solution.py:485
  171.0 2.6 collective-permute-start.13
  173.6 3.4 collective-permute-start.14
  177.1 19.4 %collective-permute-done.13.refs_2_ = bf16[768,768]{1,0:T(8,128)(2,1)S(1)} collective-permute-done((bf16[768,768]{1,0:T(8,128)(2,1)S(1)}, bf16[768,768]{1,0:T(8,128)(2,1)S(1)}, u32[]{:S(2)}, u32[]{:S(2)}) %collective-permute-start.13) | collective-permute-done | bytes 1179680 | tf_op jit(solution)/shard_map/ppermute | solution.py:485
  196.6 3.8 collective-permute-start.16
  201.6 4.4 %collective-permute-start.17 = (bf16[384,768]{1,0:T(8,128)(2,1)S(1)}, bf16[384,768]{1,0:T(8,128)(2,1)S(1)}, u32[]{:S(2)}, u32[]{:S(2)}) collective-permute-start(bf16[384,768]{1,0:T(8,128)(2,1)S(1)} %slice.59), channel_id=1, source_target_pairs={{0,1},{1,0},{2,3},{3,2},{4,5},{5,4},{6,7},{7,6},{8,9},{9,8},{10,11... | collective-permute-start | bytes 1769480 | tf_op jit(solution)/shard_map/ppermute | solution.py:485
  206.1 5.5 %collective-permute-done.16.refs_4_ = bf16[384,768]{1,0:T(8,128)(2,1)S(1)} collective-permute-done((bf16[384,768]{1,0:T(8,128)(2,1)S(1)}, bf16[384,768]{1,0:T(8,128)(2,1)S(1)}, u32[]{:S(2)}, u32[]{:S(2)}) %collective-permute-start.16) | collective-permute-done | bytes 589856 | tf_op jit(solution)/shard_map/ppermute | solution.py:485
  224.6 16.0 %projection_start.2.refs_1_ = bf16[768,3072]{1,0:T(8,128)(2,1)S(1)} custom-call(s32[1]{0:T(128)} %bitcast.refs_0_, bf16[768,768]{1,0:T(8,128)(2,1)S(1)} %copy-done.1, bf16[768,768]{1,0:T(8,128)(2,1)S(1)} %collective-permute-done.13.refs_2_, bf16[768,768]{1,0:T(8,128)(2,1)S(1)} %collective-permute-done.14.refs_3_, bf16[768,3072]{1,0:T(8,128)(2,1)} %refs_7_.1, ...), custom_call_target="tpu_custom_call" | custom-call | flops 10871635 | bytes 18874 | tf_op jit(solution)/shard_map/projection_start/pallas_call | solution.py:448
  240.7 9.8 %projection_end.2.refs_5_ = bf16[768,3072]{1,0:T(8,128)(2,1)} custom-call(s32[1]{0:T(128)} %bitcast.refs_0_, bf16[768,3072]{1,0:T(8,128)(2,1)S(1)} %projection_start.2.refs_1_, bf16[768,3072]{1,0:T(8,128)(2,1)} %collective-permute-done.15.refs_2_, f32[1,3072]{1,0:T(1,128)S(1)} %fusion.refs_3_, bf16[384,768]{1,0:T(8,128)(2,1)S(1)} %copy-done.3, ...), custom_call_target="tpu_custom_call" | custom-call | flops 3623878 | bytes 18874 | tf_op jit(solution)/shard_map/projection_end/pallas_call | solution.py:448
  250.6 14.2 %norm_keys.3 = (bf16[768,768]{1,0:T(8,128)(2,1)S(1)}, bf16[768,3072]{1,0:T(8,128)(2,1)S(1)}, bf16[768,3072]{1,0:T(8,128)(2,1)}) custom-call(s32[2]{0:T(128)S(1)} %copy-done.10, f32[1,3072]{1,0:T(1,128)S(1)} %copy-done.7, f32[1,3072]{1,0:T(1,128)S(1)} %get-tuple-element.91.refs_2_, f32[2,128]{1,0:T(2,128)S(1)} %pad_maximum_fusion.1.refs_3_.gain_ref, ...), custom_call_target="tpu_custom_call" | custom-call | flops 3623878 | bytes 20054 | tf_op jit(solution)/shard_map/norm_keys/pallas_call | solution.py:137
  264.9 6.8 %values.3.value_ref = bf16[768,768]{1,0:T(8,128)(2,1)S(1)} custom-call(bf16[768,3072]{1,0:T(8,128)(2,1)S(1)} %get-tuple-element.78.normed_ref, bf16[3,3072,768]{2,1,0:T(8,128)(2,1)} %w_any.7), custom_call_target="tpu_custom_call" | custom-call | flops 3623878 | bytes 10616 | tf_op jit(solution)/shard_map/values/pallas_call | solution.py:201
  271.8 10.5 %collective-permute-done.22.refs_5_ = bf16[768,768]{1,0:T(8,128)(2,1)S(1)} collective-permute-done((bf16[768,768]{1,0:T(8,128)(2,1)S(1)}, bf16[768,768]{1,0:T(8,128)(2,1)S(1)}, u32[]{:S(2)}, u32[]{:S(2)}) %collective-permute-start.22) | collective-permute-done | bytes 1179680 | tf_op jit(solution)/shard_map/ppermute | solution.py:485
  282.3 18.2 %queries_own_frame.3 = (bf16[768,768]{1,0:T(8,128)(2,1)S(1)}, f32[768,768]{1,0:T(8,128)S(1)}, f32[768,768]{1,0:T(8,128)S(1)}, f32[768,768]{1,0:T(8,128)S(1)}) custom-call(f32[2,128]{1,0:T(2,128)S(1)} %pad_maximum_fusion.1.refs_3_.gain_ref, bf16[768,3072]{1,0:T(8,128)(2,1)S(1)} %get-tuple-element.78.normed_ref, ...), custom_call_target="tpu_custom_call" | custom-call | flops 7247757 | bytes 20054 | tf_op jit(solution)/shard_map/queries_own_frame/pallas_call | solution.py:280
  300.6 6.9 %earlier_frame.3 = (bf16[384,768]{1,0:T(8,128)(2,1)S(1)}, bf16[384,768]{1,0:T(8,128)(2,1)S(1)}) custom-call(s32[2]{0:T(128)S(1)} %copy-done.10, bf16[768,768]{1,0:T(8,128)(2,1)S(1)} %get-tuple-element.80.refs_1_, f32[768,768]{1,0:T(8,128)S(1)} %get-tuple-element.81.refs_2_, f32[768,768]{1,0:T(8,128)S(1)} %get-tuple-element.82.refs_3_, ...), custom_call_target="tpu_custom_call" | custom-call | flops 3623878 | bytes 11796 | tf_op jit(solution)/shard_map/earlier_frame/pallas_call | solution.py:341
  307.9 54.4 %collective-permute-done.24.refs_1_ = bf16[384,768]{1,0:T(8,128)(2,1)S(1)} collective-permute-done((bf16[384,768]{1,0:T(8,128)(2,1)S(1)}, bf16[384,768]{1,0:T(8,128)(2,1)S(1)}, u32[]{:S(2)}, u32[]{:S(2)}) %collective-permute-start.24) | collective-permute-done | bytes 589856 | tf_op jit(solution)/shard_map/ppermute | solution.py:485
  362.3 2.0 collective-permute-start.26
  366.2 2.4 collective-permute-done.25.refs_2_
  372.5 6.0 %collective-permute-done.26.refs_3_ = bf16[384,768]{1,0:T(8,128)(2,1)S(1)} collective-permute-done((bf16[384,768]{1,0:T(8,128)(2,1)S(1)}, bf16[384,768]{1,0:T(8,128)(2,1)S(1)}, u32[]{:S(2)}, u32[]{:S(2)}) %collective-permute-start.26) | collective-permute-done | bytes 589856 | tf_op jit(solution)/shard_map/ppermute | solution.py:485
  380.6 2.1 collective-permute-start.32
  382.7 5.0 %collective-permute-done.27.refs_4_ = bf16[384,768]{1,0:T(8,128)(2,1)S(1)} collective-permute-done((bf16[384,768]{1,0:T(8,128)(2,1)S(1)}, bf16[384,768]{1,0:T(8,128)(2,1)S(1)}, u32[]{:S(2)}, u32[]{:S(2)}) %collective-permute-start.27) | collective-permute-done | bytes 589856 | tf_op jit(solution)/shard_map/ppermute | solution.py:485
  391.1 16.0 %projection_start.3.refs_1_ = bf16[768,3072]{1,0:T(8,128)(2,1)S(1)} custom-call(s32[1]{0:T(128)} %bitcast.refs_0_, bf16[384,768]{1,0:T(8,128)(2,1)S(1)} %collective-permute-done.24.refs_1_, bf16[384,768]{1,0:T(8,128)(2,1)S(1)} %collective-permute-done.25.refs_2_, bf16[384,768]{1,0:T(8,128)(2,1)S(1)} %collective-permute-done.26.refs_3_, ...), custom_call_target="tpu_custom_call" | custom-call | flops 10871635 | bytes 18874 | tf_op jit(solution)/shard_map/projection_start/pallas_call | solution.py:448
  407.2 8.6 %projection_end.3 = bf16[768,3072]{1,0:T(8,128)(2,1)} custom-call(s32[1]{0:T(128)} %bitcast.refs_0_, bf16[768,3072]{1,0:T(8,128)(2,1)S(1)} %projection_start.3.refs_1_, bf16[768,3072]{1,0:T(8,128)(2,1)S(1)} %collective-permute-done.30.refs_2_, f32[1,3072]{1,0:T(1,128)S(1)} %fusion.refs_3_, bf16[192,768]{1,0:T(8,128)(2,1)S(1)} %collective-permute-done.31.refs_4_, ...), custom_call_target="tpu_custom_call" | custom-call | flops 3623878 | bytes 18874 | tf_op jit(solution)/shard_map/projection_end/pallas_call | solution.py:448
  (107 shorter events, 41.4 us)
Async XLA Ops:
  1.8 18.7 %collective-permute-start.1 = (bf16[192,3072]{1,0:T(8,128)(2,1)S(1)}, bf16[192,3072]{1,0:T(8,128)(2,1)S(1)}, u32[]{:S(2)}, u32[]{:S(2)}) collective-permute-start(bf16[192,3072]{1,0:T(8,128)(2,1)S(1)} %get-tuple-element.90.refs_6_), channel_id=1, source_target_pairs={{28,31},{29,28},{30,29},{31,30}} | collective-permute-start | bytes 3538952 | tf_op jit(solution)/shard_map/ppermute | solution.py:485
  2.6 18.0 %collective-permute-start.2 = (bf16[192,3072]{1,0:T(8,128)(2,1)S(1)}, bf16[192,3072]{1,0:T(8,128)(2,1)}, u32[]{:S(2)}, u32[]{:S(2)}) collective-permute-start(bf16[192,3072]{1,0:T(8,128)(2,1)S(1)} %get-tuple-element.90.refs_6_), channel_id=1, source_target_pairs={{28,30},{29,31},{30,28},{31,29}} | collective-permute-start | bytes 3538952 | tf_op jit(solution)/shard_map/ppermute | solution.py:485
  4.2 16.3 %collective-permute-start.3 = (bf16[192,3072]{1,0:T(8,128)(2,1)S(1)}, bf16[192,3072]{1,0:T(8,128)(2,1)}, u32[]{:S(2)}, u32[]{:S(2)}) collective-permute-start(bf16[192,3072]{1,0:T(8,128)(2,1)S(1)} %get-tuple-element.90.refs_6_), channel_id=1, source_target_pairs={{28,29},{29,30},{30,31},{31,28}} | collective-permute-start | bytes 3538952 | tf_op jit(solution)/shard_map/ppermute | solution.py:485
  6.0 12.8 %collective-permute-start = (s32[1]{0:T(128)}, s32[1]{0:T(128)}, u32[]{:S(2)}, u32[]{:S(2)}) collective-permute-start(s32[1]{0:T(128)} %param.10), channel_id=1, source_target_pairs={{0,28},{1,29},{2,30},{3,31},{4,0},{5,1},{6,2},{7,3},{8,4},{9,5},{1... | collective-permute-start | bytes 20 | tf_op jit(solution)/shard_map/ppermute | solution.py:485
  20.6 81.7 %collective-permute-start.6 = (bf16[768,1536]{1,0:T(8,128)(2,1)}, bf16[768,1536]{1,0:T(8,128)(2,1)S(1)}, u32[]{:S(2)}, u32[]{:S(2)}) collective-permute-start(bf16[768,1536]{1,0:T(8,128)(2,1)} %constant_dynamic-slice_fusion), channel_id=1, source_target_pairs={{0,1},{1,0},{2,3},{3,2},{4,5},{5,4},{6,7},{7,6},{8,9},{9,8},{10,11... | collective-permute-start | bytes 7077896 | tf_op jit(solution)/shard_map/ppermute | solution.py:485
  23.0 79.2 %collective-permute-start.7 = (bf16[768,1536]{1,0:T(8,128)(2,1)}, bf16[768,1536]{1,0:T(8,128)(2,1)S(1)}, u32[]{:S(2)}, u32[]{:S(2)}) collective-permute-start(bf16[768,1536]{1,0:T(8,128)(2,1)} %constant_dynamic-slice_fusion), channel_id=1, source_target_pairs={{0,2},{1,3},{2,0},{3,1},{4,6},{5,7},{6,4},{7,5},{8,10},{9,11},{10,... | collective-permute-start | bytes 7077896 | tf_op jit(solution)/shard_map/ppermute | solution.py:485
  39.4 44.6 %collective-permute-start.4 = (bf16[768,768]{1,0:T(8,128)(2,1)S(1)}, bf16[768,768]{1,0:T(8,128)(2,1)S(1)}, u32[]{:S(2)}, u32[]{:S(2)}) collective-permute-start(bf16[768,768]{1,0:T(8,128)(2,1)S(1)} %get-tuple-element.53.key_ref), channel_id=1, source_target_pairs={{0,4},{1,5},{2,6},{3,7},{4,8},{5,9},{6,10},{7,11},{8,12},{9,13},{1... | collective-permute-start | bytes 3538952 | tf_op jit(solution)/shard_map/ppermute | solution.py:485
  46.1 56.1 %collective-permute-start.5 = (bf16[768,768]{1,0:T(8,128)(2,1)S(1)}, bf16[768,768]{1,0:T(8,128)(2,1)S(1)}, u32[]{:S(2)}, u32[]{:S(2)}) collective-permute-start(bf16[768,768]{1,0:T(8,128)(2,1)S(1)} %values.2.value_ref), channel_id=1, source_target_pairs={{0,4},{1,5},{2,6},{3,7},{4,8},{5,9},{6,10},{7,11},{8,12},{9,13},{1... | collective-permute-start | bytes 3538952 | tf_op jit(solution)/shard_map/ppermute | solution.py:485
  102.8 137.8 %collective-permute-start.15 = (bf16[768,3072]{1,0:T(8,128)(2,1)}, bf16[768,3072]{1,0:T(8,128)(2,1)}, u32[]{:S(2)}, u32[]{:S(2)}) collective-permute-start(bf16[768,3072]{1,0:T(8,128)(2,1)} %get-tuple-element.70), channel_id=1, source_target_pairs={{0,4},{1,5},{2,6},{3,7},{4,8},{5,9},{6,10},{7,11},{8,12},{9,13},{1... | collective-permute-start | bytes 14155784 | tf_op jit(solution)/shard_map/ppermute | solution.py:485
  104.4 26.6 %collective-permute-start.12 = (bf16[384,1536]{1,0:T(8,128)(2,1)S(1)}, bf16[384,1536]{1,0:T(8,128)(2,1)S(1)}, u32[]{:S(2)}, u32[]{:S(2)}) collective-permute-start(bf16[384,1536]{1,0:T(8,128)(2,1)S(1)} %slice.46), channel_id=1, source_target_pairs={{0,1},{1,0},{2,3},{3,2},{4,5},{5,4},{6,7},{7,6},{8,9},{9,8},{10,11... | collective-permute-start | bytes 3538952 | tf_op jit(solution)/shard_map/ppermute | solution.py:485
  105.1 26.3 %collective-permute-start.11 = (bf16[384,1536]{1,0:T(8,128)(2,1)S(1)}, bf16[384,1536]{1,0:T(8,128)(2,1)S(1)}, u32[]{:S(2)}, u32[]{:S(2)}) collective-permute-start(bf16[384,1536]{1,0:T(8,128)(2,1)S(1)} %slice.45), channel_id=1, source_target_pairs={{0,2},{1,3},{2,0},{3,1},{4,6},{5,7},{6,4},{7,5},{8,10},{9,11},{10,... | collective-permute-start | bytes 3538952 | tf_op jit(solution)/shard_map/ppermute | solution.py:485
  120.2 50.9 %collective-permute-start.10 = (bf16[768,768]{1,0:T(8,128)(2,1)S(1)}, bf16[768,768]{1,0:T(8,128)(2,1)S(1)}, u32[]{:S(2)}, u32[]{:S(2)}) collective-permute-start(bf16[768,768]{1,0:T(8,128)(2,1)S(1)} %earlier_frame.2), channel_id=1, source_target_pairs={{0,4},{1,5},{2,6},{3,7},{4,8},{5,9},{6,10},{7,11},{8,12},{9,13},{1... | collective-permute-start | bytes 3538952 | tf_op jit(solution)/shard_map/ppermute | solution.py:485
  171.0 25.6 %collective-permute-start.13 = (bf16[768,768]{1,0:T(8,128)(2,1)S(1)}, bf16[768,768]{1,0:T(8,128)(2,1)S(1)}, u32[]{:S(2)}, u32[]{:S(2)}) collective-permute-start(bf16[768,768]{1,0:T(8,128)(2,1)S(1)} %collective-permute-done.10.refs_1_), channel_id=1, source_target_pairs={{0,1},{1,0},{2,3},{3,2},{4,5},{5,4},{6,7},{7,6},{8,9},{9,8},{10,11... | collective-permute-start | bytes 3538952 | tf_op jit(solution)/shard_map/ppermute | solution.py:485
  173.6 28.0 %collective-permute-start.14 = (bf16[768,768]{1,0:T(8,128)(2,1)S(1)}, bf16[768,768]{1,0:T(8,128)(2,1)S(1)}, u32[]{:S(2)}, u32[]{:S(2)}) collective-permute-start(bf16[768,768]{1,0:T(8,128)(2,1)S(1)} %collective-permute-done.10.refs_1_), channel_id=1, source_target_pairs={{0,2},{1,3},{2,0},{3,1},{4,6},{5,7},{6,4},{7,5},{8,10},{9,11},{10,... | collective-permute-start | bytes 3538952 | tf_op jit(solution)/shard_map/ppermute | solution.py:485
  177.1 63.6 %collective-permute-start.18 = (bf16[768,1536]{1,0:T(8,128)(2,1)}, bf16[768,1536]{1,0:T(8,128)(2,1)}, u32[]{:S(2)}, u32[]{:S(2)}) collective-permute-start(bf16[768,1536]{1,0:T(8,128)(2,1)} %pad_maximum_fusion.refs_6_.refs_8_), channel_id=1, source_target_pairs={{0,4},{1,5},{2,6},{3,7},{4,0},{5,1},{6,2},{7,3},{8,12},{9,13},{10,... | collective-permute-start | bytes 7077896 | tf_op jit(solution)/shard_map/ppermute | solution.py:485
  196.6 14.9 %collective-permute-start.16 = (bf16[384,768]{1,0:T(8,128)(2,1)S(1)}, bf16[384,768]{1,0:T(8,128)(2,1)S(1)}, u32[]{:S(2)}, u32[]{:S(2)}) collective-permute-start(bf16[384,768]{1,0:T(8,128)(2,1)S(1)} %slice.58), channel_id=1, source_target_pairs={{0,2},{1,3},{2,0},{3,1},{4,6},{5,7},{6,4},{7,5},{8,10},{9,11},{10,... | collective-permute-start | bytes 1769480 | tf_op jit(solution)/shard_map/ppermute | solution.py:485
  214.8 35.7 %collective-permute-start.19 = (bf16[192,3072]{1,0:T(8,128)(2,1)S(1)}, bf16[192,3072]{1,0:T(8,128)(2,1)}, u32[]{:S(2)}, u32[]{:S(2)}) collective-permute-start(bf16[192,3072]{1,0:T(8,128)(2,1)S(1)} %get-tuple-element.74.refs_6_), channel_id=1, source_target_pairs={{28,31},{29,28},{30,29},{31,30}} | collective-permute-start | bytes 3538952 | tf_op jit(solution)/shard_map/ppermute | solution.py:485
  216.5 34.1 %collective-permute-start.20 = (bf16[192,3072]{1,0:T(8,128)(2,1)S(1)}, bf16[192,3072]{1,0:T(8,128)(2,1)}, u32[]{:S(2)}, u32[]{:S(2)}) collective-permute-start(bf16[192,3072]{1,0:T(8,128)(2,1)S(1)} %get-tuple-element.74.refs_6_), channel_id=1, source_target_pairs={{28,30},{29,31},{30,28},{31,29}} | collective-permute-start | bytes 3538952 | tf_op jit(solution)/shard_map/ppermute | solution.py:485
  218.1 32.4 %collective-permute-start.21 = (bf16[192,3072]{1,0:T(8,128)(2,1)S(1)}, bf16[192,3072]{1,0:T(8,128)(2,1)}, u32[]{:S(2)}, u32[]{:S(2)}) collective-permute-start(bf16[192,3072]{1,0:T(8,128)(2,1)S(1)} %get-tuple-element.74.refs_6_), channel_id=1, source_target_pairs={{28,29},{29,30},{30,31},{31,28}} | collective-permute-start | bytes 3538952 | tf_op jit(solution)/shard_map/ppermute | solution.py:485
  264.8 17.5 %collective-permute-start.22 = (bf16[768,768]{1,0:T(8,128)(2,1)S(1)}, bf16[768,768]{1,0:T(8,128)(2,1)S(1)}, u32[]{:S(2)}, u32[]{:S(2)}) collective-permute-start(bf16[768,768]{1,0:T(8,128)(2,1)S(1)} %get-tuple-element.77.key_ref), channel_id=1, source_target_pairs={{0,4},{1,5},{2,6},{3,7},{4,8},{5,9},{6,10},{7,11},{8,12},{9,13},{1... | collective-permute-start | bytes 3538952 | tf_op jit(solution)/shard_map/ppermute | solution.py:485
  271.7 28.8 %collective-permute-start.23 = (bf16[768,768]{1,0:T(8,128)(2,1)S(1)}, bf16[768,768]{1,0:T(8,128)(2,1)S(1)}, u32[]{:S(2)}, u32[]{:S(2)}) collective-permute-start(bf16[768,768]{1,0:T(8,128)(2,1)S(1)} %values.3.value_ref), channel_id=1, source_target_pairs={{0,4},{1,5},{2,6},{3,7},{4,8},{5,9},{6,10},{7,11},{8,12},{9,13},{1... | collective-permute-start | bytes 3538952 | tf_op jit(solution)/shard_map/ppermute | solution.py:485
  300.5 106.6 %collective-permute-start.30 = (bf16[768,3072]{1,0:T(8,128)(2,1)S(1)}, bf16[768,3072]{1,0:T(8,128)(2,1)S(1)}, u32[]{:S(2)}, u32[]{:S(2)}) collective-permute-start(bf16[768,3072]{1,0:T(8,128)(2,1)S(1)} %bitcast.21), channel_id=1, source_target_pairs={{0,4},{1,5},{2,6},{3,7},{4,8},{5,9},{6,10},{7,11},{8,12},{9,13},{1... | collective-permute-start | bytes 14155784 | tf_op jit(solution)/shard_map/ppermute | solution.py:485
  307.5 54.7 %collective-permute-start.24 = (bf16[384,768]{1,0:T(8,128)(2,1)S(1)}, bf16[384,768]{1,0:T(8,128)(2,1)S(1)}, u32[]{:S(2)}, u32[]{:S(2)}) collective-permute-start(bf16[384,768]{1,0:T(8,128)(2,1)S(1)} %get-tuple-element.86), channel_id=1, source_target_pairs={{0,4},{1,5},{2,6},{3,7},{4,8},{5,9},{6,10},{7,11},{8,12},{9,13},{1... | collective-permute-start | bytes 1769480 | tf_op jit(solution)/shard_map/ppermute | solution.py:485
  307.6 61.0 %collective-permute-start.25 = (bf16[384,768]{1,0:T(8,128)(2,1)S(1)}, bf16[384,768]{1,0:T(8,128)(2,1)S(1)}, u32[]{:S(2)}, u32[]{:S(2)}) collective-permute-start(bf16[384,768]{1,0:T(8,128)(2,1)S(1)} %get-tuple-element.87), channel_id=1, source_target_pairs={{0,4},{1,5},{2,6},{3,7},{4,8},{5,9},{6,10},{7,11},{8,12},{9,13},{1... | collective-permute-start | bytes 1769480 | tf_op jit(solution)/shard_map/ppermute | solution.py:485
  362.3 16.3 %collective-permute-start.26 = (bf16[384,768]{1,0:T(8,128)(2,1)S(1)}, bf16[384,768]{1,0:T(8,128)(2,1)S(1)}, u32[]{:S(2)}, u32[]{:S(2)}) collective-permute-start(bf16[384,768]{1,0:T(8,128)(2,1)S(1)} %collective-permute-done.24.refs_1_), channel_id=1, source_target_pairs={{0,1},{1,0},{2,3},{3,2},{4,5},{5,4},{6,7},{7,6},{8,9},{9,8},{10,11... | collective-permute-start | bytes 1769480 | tf_op jit(solution)/shard_map/ppermute | solution.py:485
  364.3 16.3 %collective-permute-start.28 = (bf16[384,768]{1,0:T(8,128)(2,1)S(1)}, bf16[384,768]{1,0:T(8,128)(2,1)S(1)}, u32[]{:S(2)}, u32[]{:S(2)}) collective-permute-start(bf16[384,768]{1,0:T(8,128)(2,1)S(1)} %collective-permute-done.24.refs_1_), channel_id=1, source_target_pairs={{0,2},{1,3},{2,0},{3,1},{4,6},{5,7},{6,4},{7,5},{8,10},{9,11},{10,... | collective-permute-start | bytes 1769480 | tf_op jit(solution)/shard_map/ppermute | solution.py:485
  368.6 19.1 %collective-permute-start.27 = (bf16[384,768]{1,0:T(8,128)(2,1)S(1)}, bf16[384,768]{1,0:T(8,128)(2,1)S(1)}, u32[]{:S(2)}, u32[]{:S(2)}) collective-permute-start(bf16[384,768]{1,0:T(8,128)(2,1)S(1)} %collective-permute-done.25.refs_2_), channel_id=1, source_target_pairs={{0,1},{1,0},{2,3},{3,2},{4,5},{5,4},{6,7},{7,6},{8,9},{9,8},{10,11... | collective-permute-start | bytes 1769480 | tf_op jit(solution)/shard_map/ppermute | solution.py:485
  370.6 18.7 %collective-permute-start.29 = (bf16[384,768]{1,0:T(8,128)(2,1)S(1)}, bf16[384,768]{1,0:T(8,128)(2,1)S(1)}, u32[]{:S(2)}, u32[]{:S(2)}) collective-permute-start(bf16[384,768]{1,0:T(8,128)(2,1)S(1)} %collective-permute-done.25.refs_2_), channel_id=1, source_target_pairs={{0,2},{1,3},{2,0},{3,1},{4,6},{5,7},{6,4},{7,5},{8,10},{9,11},{10,... | collective-permute-start | bytes 1769480 | tf_op jit(solution)/shard_map/ppermute | solution.py:485
  378.6 28.6 %collective-permute-start.31 = (bf16[192,768]{1,0:T(8,128)(2,1)S(1)}, bf16[192,768]{1,0:T(8,128)(2,1)S(1)}, u32[]{:S(2)}, u32[]{:S(2)}) collective-permute-start(bf16[192,768]{1,0:T(8,128)(2,1)S(1)} %slice.60), channel_id=1, source_target_pairs={{0,2},{1,3},{2,0},{3,1},{4,6},{5,7},{6,4},{7,5},{8,10},{9,11},{10,... | collective-permute-start | bytes 884744 | tf_op jit(solution)/shard_map/ppermute | solution.py:485
  380.6 26.6 %collective-permute-start.32 = (bf16[192,768]{1,0:T(8,128)(2,1)S(1)}, bf16[192,768]{1,0:T(8,128)(2,1)S(1)}, u32[]{:S(2)}, u32[]{:S(2)}) collective-permute-start(bf16[192,768]{1,0:T(8,128)(2,1)S(1)} %slice.61), channel_id=1, source_target_pairs={{0,1},{1,0},{2,3},{3,2},{4,5},{5,4},{6,7},{7,6},{8,9},{9,8},{10,11... | collective-permute-start | bytes 884744 | tf_op jit(solution)/shard_map/ppermute | solution.py:485
  387.7 19.5 %collective-permute-start.33 = (bf16[192,768]{1,0:T(8,128)(2,1)S(1)}, bf16[192,768]{1,0:T(8,128)(2,1)S(1)}, u32[]{:S(2)}, u32[]{:S(2)}) collective-permute-start(bf16[192,768]{1,0:T(8,128)(2,1)S(1)} %slice.62), channel_id=1, source_target_pairs={{0,2},{1,3},{2,0},{3,1},{4,6},{5,7},{6,4},{7,5},{8,10},{9,11},{10,... | collective-permute-start | bytes 884744 | tf_op jit(solution)/shard_map/ppermute | solution.py:485
  389.3 17.8 %collective-permute-start.34 = (bf16[192,768]{1,0:T(8,128)(2,1)S(1)}, bf16[192,768]{1,0:T(8,128)(2,1)S(1)}, u32[]{:S(2)}, u32[]{:S(2)}) collective-permute-start(bf16[192,768]{1,0:T(8,128)(2,1)S(1)} %slice.63), channel_id=1, source_target_pairs={{0,1},{1,0},{2,3},{3,2},{4,5},{5,4},{6,7},{7,6},{8,9},{9,8},{10,11... | collective-permute-start | bytes 884744 | tf_op jit(solution)/shard_map/ppermute | solution.py:485
  (22 other events, 274.0 us)

commit v6 on v5

--- a/solution.py
+++ b/solution.py
@@ -56,14 +56,20 @@
         yield pltpu.make_async_copy(w_any.at[part, at], w_ref.at[at], w_sems.at[i])
 
 
-def key_kernel(*refs, tensor_size):
-    info_ref, scale_ref, shift_ref, gain_ref, w_any, z_any, noise_any = refs[:7]
-    piece_refs = refs[7 : 7 + tensor_size - 1]
-    key_ref, normed_any, state_any = refs[6 + tensor_size : 9 + tensor_size]
-    state_ref, normed_ref, inverse_ref, w_ref, sem, out_sems, w_sems = refs[9 + tensor_size :]
+def key_kernel(*refs, half):
+    info_ref, scale_ref, shift_ref, gain_ref, w_any, z_any, noise_any, near_any = refs[:8]
+    pair_refs = refs[8 : 7 + half]
+    key_ref, normed_any, state_any = refs[7 + half : 10 + half]
+    state_ref, normed_ref, inverse_ref, w_ref, sem, out_sems, w_sems = refs[10 + half :]
     step = pl.program_id(0)
     rows = state_ref.shape[0]
     piece_rows = noise_any.shape[0]
+
+    def piece_at(j, f):
+        if j > 0:
+            return pair_refs[j - 1], f * piece_rows
+        return (noise_any, near_any)[f], 0
+
     cols = key_ref.shape[1]
     state_copy = pltpu.make_async_copy(state_ref, state_any, out_sems.at[0])
     normed_copy = pltpu.make_async_copy(normed_ref, normed_any, out_sems.at[1])
@@ -82,20 +88,23 @@
         def _():
             for weight_copy in weight_copies(w_any, 1, w_ref, w_sems):
                 weight_copy.start()
-            for block in range(tensor_size):
-                away = lax.rem(block + tensor_size - info_ref[1], tensor_size)
-                for d in range(tensor_size):
-                    source = noise_any if d == 0 else piece_refs[d - 1]
-
-                    @pl.when(away == d)
-                    def _():
-                        copy = pltpu.make_async_copy(
-                            source,
-                            state_ref.at[pl.ds(block * piece_rows, piece_rows)],
-                            sem.at[0],
-                        )
-                        copy.start()
-                        copy.wait()
+            for block in range(2 * half):
+                high, low = block // 2, block % 2
+                steps = lax.rem(high + half - info_ref[1], half)
+                other = jnp.abs(low - info_ref[2])
+                for j in range(half):
+                    for f in range(2):
+                        source, row = piece_at(j, f)
+
+                        @pl.when(jnp.logical_and(steps == j, other == f))
+                        def _():
+                            copy = pltpu.make_async_copy(
+                                source.at[pl.ds(row, piece_rows)],
+                                state_ref.at[pl.ds(block * piece_rows, piece_rows)],
+                                sem.at[0],
+                            )
+                            copy.start()
+                            copy.wait()
 
         state_copy.start()
 
@@ -133,9 +142,9 @@
     rows, width = z.shape
     head_cols = qkv_weight.shape[2]
     cols = tile_cols(head_cols)
-    tensor_size = len(noise_pieces) + 1
+    half = len(noise_pieces)
     return pl.pallas_call(
-        functools.partial(key_kernel, tensor_size=tensor_size),
+        functools.partial(key_kernel, half=half),
         grid_spec=pltpu.PrefetchScalarGridSpec(
             num_scalar_prefetch=1,
             grid=(head_cols // cols,),
@@ -144,7 +153,7 @@
                 pl.BlockSpec((1, width), lambda j, i: (0, 0)),
                 pl.BlockSpec((2, HD), lambda j, i: (0, 0)),
             ]
-            + [ANY] * (2 + tensor_size),
+            + [ANY] * (3 + half),
             out_specs=[pl.BlockSpec((rows, cols), lambda j, i: (0, j)), ANY, ANY],
             scratch_shapes=[
                 pltpu.VMEM((rows, width), BF16),
@@ -228,7 +237,7 @@
     return total[:, :HD], total[:, HD:]
 
 
-def attention_tiles(query, key_ref, value_ref, finish):
+def attention_tiles(query, key, finish):
     rows, cols = query.shape
     tile = math.gcd(rows, 256)
     waiting = None
@@ -236,7 +245,7 @@
         at = slice(h * HD, (h + 1) * HD)
         for r in range(rows // tile):
             row = slice(r * tile, (r + 1) * tile)
-            scores = attend(query[row, at], key_ref[:, at])
+            scores = attend(query[row, at], key[:, at])
             if waiting is not None:
                 finish(*waiting)
             waiting = (scores, row, at)
@@ -269,7 +278,7 @@
         total_ref[row, at] = total
         top_ref[row, at] = jnp.broadcast_to(top, acc.shape)
 
-    attention_tiles(query, key_ref, value_ref, finish)
+    attention_tiles(query, key_ref, finish)
 
 
 def own_attention(gains, normed, qkv_weight, key, value):
@@ -305,8 +314,9 @@
 
 
 def earlier_kernel(*refs, chunks):
-    info_ref, query_ref, acc_ref, top_ref, total_ref, key_ref, value_ref = refs[:7]
-    out_refs = refs[7:]
+    info_ref, query_ref, acc_ref, top_ref, total_ref = refs[:5]
+    key_ref, first_key_ref, value_ref, first_value_ref = refs[5:9]
+    out_refs = refs[9:]
     rows = query_ref.shape[0] // chunks
 
     def store(row, at, result):
@@ -323,19 +333,24 @@
 
     @pl.when(info_ref[0] == 0)
     def _():
+        keys = jnp.where(info_ref[3] != 0, first_key_ref[...], key_ref[...])
+        values = jnp.where(info_ref[3] != 0, first_value_ref[...], value_ref[...])
+
         def finish(scores, row, at):
             old_top = top_ref[row, at][:, :1]
             top = jnp.maximum(jnp.max(scores, axis=-1, keepdims=True), old_top)
-            acc, total = weigh(scores, top, value_ref[:, at])
+            acc, total = weigh(scores, top, values[:, at])
             kept = jnp.exp2(old_top - top)
             acc = acc + acc_ref[row, at] * kept
             total = total + total_ref[row, at] * kept
             store(row, at, (acc / total).astype(BF16))
 
-        attention_tiles(query_ref[...], key_ref, value_ref, finish)
-
-
-def earlier_attention(info, query, acc, top, total, key, value, chunks):
+        attention_tiles(query_ref[...], keys, finish)
+
+
+def earlier_attention(
+    info, query, acc, top, total, key, first_key, value, first_value, chunks
+):
     rows, head_cols = query.shape
     cols = tile_cols(head_cols)
     return pl.pallas_call(
@@ -343,18 +358,18 @@
         grid_spec=pltpu.PrefetchScalarGridSpec(
             num_scalar_prefetch=1,
             grid=(head_cols // cols,),
-            in_specs=[pl.BlockSpec((rows, cols), lambda j, i: (0, j))] * 6,
+            in_specs=[pl.BlockSpec((rows, cols), lambda j, i: (0, j))] * 8,
             out_specs=[pl.BlockSpec((rows // chunks, cols), lambda j, i: (0, j))] * chunks,
         ),
         out_shape=[jax.ShapeDtypeStruct((rows // chunks, head_cols), BF16)] * chunks,
         compiler_params=compiler_params(24),
         cost_estimate=cost(
             8 * rows * rows * head_cols,
-            20 * rows * head_cols,
+            22 * rows * head_cols,
             rows * rows * head_cols // HD,
         ),
         name="earlier_frame",
-    )(info, query, acc, top, total, key, value)
+    )(info, query, acc, top, total, key, first_key, value, first_value)
 
 
 def output_kernel(*refs, part_counts, whole_weights, half_blocks, last):
@@ -521,22 +536,31 @@
     is_last = queue_index == queue_size - 1
     parity = (queue_index % 2).astype(jnp.int32)[None]
 
-    def ring(block):
-        return send(block, lambda q, t: ((q + 1) % queue_size, t), *mesh_sizes)
+    def ring(block, frames=None):
+        return send(block, lambda q, t: ((q + 1) % queue_size, t), *mesh_sizes, frames)
 
     def sibling(block):
         return send(block, lambda q, t: (q ^ 1, t), *mesh_sizes)
 
     worked_level = send(levels, lambda q, t: ((q - 1) % queue_size, t), *mesh_sizes)[0]
 
-    def gather_noise(noise):
-        return [
-            send(noise, lambda q, t: (q, (t - d) % tensor_size), *mesh_sizes, [queue_size - 1])
-            for d in range(1, tensor_size)
-        ]
+    def gather_noise(noise, at_once):
+        args = (*mesh_sizes, [queue_size - 1])
+        half = tensor_size // 2
+        near = send(noise, lambda q, t: (q, t ^ 1), *args)
+        pairs = []
+        if at_once:
+            for j in range(1, half):
+                straight = send(noise, away(j, half), *args)
+                across = send(noise, lambda q, t: away(j, half)(q, t ^ 1), *args)
+                pairs.append(jnp.concatenate([straight, across], axis=0))
+        else:
+            pair = jnp.concatenate([noise, near], axis=0)
+            pairs = [send(pair, away(j, half), *args) for j in range(1, half)]
+        return [near, *pairs]
 
     noise = fresh_noise[0]
-    noise_pieces = gather_noise(noise)
+    noise_pieces = gather_noise(noise, True)
     half_weight = lax.dynamic_slice(
         out_weight, (0, parity[0] * (width // 2)), (out_weight.shape[0], width // 2)
     )
@@ -552,7 +576,8 @@
 
     shift, scale1, _ = modulation(worked_level)
     _, _, gate = modulation(levels[0])
-    info = jnp.stack([is_last.astype(jnp.int32), tensor_index.astype(jnp.int32)])
+    info = jnp.stack([is_last, tensor_index // 2, tensor_index % 2, queue_index == 0])
+    info = info.astype(jnp.int32)
     gains = jnp.stack([q_gain * SCORE_SCALE, k_gain])
 
     frame = latents[0]
@@ -561,37 +586,47 @@
         key, normed, state = project_keys(
             info, scale1, shift, gains, qkv_weight, frame, noise, noise_pieces
         )
-        earlier_key = ring(key)
+        earlier_key = ring(key, range(queue_size - 2))
+        first_key = ring(key, [queue_size - 1])
         value = project_values(normed, qkv_weight)
-        earlier_value = ring(value)
+        earlier_value = ring(value, range(queue_size - 2))
+        first_value = ring(value, [queue_size - 1])
         normed, earlier_key = lax.optimization_barrier((normed, earlier_key))
         query, *own = own_attention(gains, normed, qkv_weight, key, value)
-        sent_state, query, earlier_value = lax.optimization_barrier(
-            (state, query, earlier_value)
-        )
-        resid = ring(sent_state)
         if not final:
-            query, mine = lax.optimization_barrier((query, mine))
+            query, mine, earlier_value, first_key, first_value = lax.optimization_barrier(
+                (query, mine, earlier_value, first_key, first_value)
+            )
             mine_corners = [
                 jnp.concatenate(parts, axis=0) for parts in two_hops(mine, *mesh_sizes)
             ]
             theirs = [sibling(block) for block in mine]
             query, theirs = lax.optimization_barrier((query, theirs))
         attended = earlier_attention(
-            info, query, *own, earlier_key, earlier_value, CHUNKS if final else 1
+            info,
+            query,
+            *own,
+            earlier_key,
+            first_key,
+            earlier_value,
+            first_value,
+            CHUNKS if final else 1,
         )
-        attended = [ring(block) for block in attended]
+        senders = [q for q in range(queue_size) if final or q != queue_size - 2]
+        targets = range(queue_size if final else queue_size - 1)
+        attended = [ring(block, senders) for block in attended]
         if not final:
             attended, mine_corners = lax.optimization_barrier((attended, mine_corners))
             theirs_corners = [sibling(block) for block in mine_corners]
-        targets = range(queue_size) if final else range(queue_size - 1)
+        sent_state, _ = lax.optimization_barrier((state, attended))
+        resid = ring(sent_state, senders)
         near = [one_hop(block, *mesh_sizes, targets) for block in attended]
         beyond = [two_hops(blocks, *mesh_sizes, targets) for blocks in near]
         direct = [attended] + [list(parts) for parts in zip(*near)]
         corners = [[half for parts in p for half in parts] for p in zip(*beyond)]
         if not final:
-            noise, corners = lax.optimization_barrier((fresh_noise[step_index + 1], corners))
-            noise_pieces = gather_noise(noise)
+            noise, _ = lax.optimization_barrier((fresh_noise[step_index + 1], attended))
+            noise_pieces = gather_noise(noise, False)
         begun = output_projection(parity, direct, [out_weight], mine, theirs)
         frame = output_projection(
             parity, corners, [], mine_corners, theirs_corners, (begun, resid, gate)

time: 419 us -> 348 us (0.83)
  waiting for transfers between devices: 199 us -> 124 us
    ppermute x35 -> x38, waiting for transfers between devices: 199 us -> 124 us  [send(): return lax.ppermute(block, AXES, pairs)]
    ppermute x35 -> x38, starting transfers between devices: 54.6 us -> 54.9 us  [send(): return lax.ppermute(block, AXES, pairs)]
  transfers between devices with their start and end apart: 35 -> 38, of which waited for: 15 -> 16; matrix products, arithmetic and copies ran while one was open for 2% -> 4% of each run, Pallas kernels for 29% -> 29%
where the time goes in v6:
time: 348 us; the launch traced here: 347 us
  Pallas kernels  143 us (41%)
  waiting for transfers between devices  124 us (36%)
  starting transfers between devices  54.9 us (16%)
  local copies, waits for them, and re-layouts  13.3 us (4%)
  other arithmetic  8.04 us (2%)
  between operations  3.52 us (1%)
    ppermute x38, waiting for transfers between devices, send(): return lax.ppermute(block, AXES, pairs)  124 us
    ppermute x38, starting transfers between devices, send(): return lax.ppermute(block, AXES, pairs)  54.9 us
    pallas_call x4, Pallas kernels, output_projection(): pl.pallas_call(functools.partial(output_kernel, part_counts=tuple((len(p)...  50.5 us
    pallas_call x2, Pallas kernels, own_attention(): pl.pallas_call(own_kernel, grid=(head_cols // cols,), in_specs=[pl.BlockS...  36.4 us
    pallas_call x2, Pallas kernels, project_keys(): pl.pallas_call(functools.partial(key_kernel, half=half), grid_spec=pltpu....  28.6 us
    pallas_call x2, Pallas kernels, earlier_attention(): pl.pallas_call(functools.partial(earlier_kernel, chunks=chunks), grid_spe...  14.2 us
    pallas_call x2, Pallas kernels, project_values(): pl.pallas_call(value_kernel, grid=(head_cols // cols,), in_specs=[pl.Bloc...  13.4 us
  transfers between devices with their start and end apart: 38, of which 16 were waited for; matrix products, arithmetic and copies ran while one was open for 4% of the time, Pallas kernels for 29%

profile of v6, /device:TPU:0, one launch (start us, length us, event | category | flops | bytes accessed | tf_op | source)
XLA Modules:
  0.0 346.9 jit_solution(10105269855383729157)
XLA Ops:
  5.9 8.8 %collective-permute-start = (s32[1]{0:T(128)}, s32[1]{0:T(128)}, u32[]{:S(2)}, u32[]{:S(2)}) collective-permute-start(s32[1]{0:T(128)} %param.10), channel_id=1, source_target_pairs={{0,28},{1,29},{2,30},{3,31},{4,0},{5,1},{6,2},{7,3},{8,4},{9,5},{1... | collective-permute-start | bytes 20 | tf_op jit(solution)/shard_map/ppermute | solution.py:500
  14.7 3.2 constant_dynamic-slice_fusion
  23.6 14.3 %norm_keys.2 = (bf16[768,768]{1,0:T(8,128)(2,1)S(1)}, bf16[768,3072]{1,0:T(8,128)(2,1)S(1)}, bf16[768,3072]{1,0:T(8,128)(2,1)}) custom-call(s32[4]{0:T(128)S(1)} %copy-done.6, f32[1,3072]{1,0:T(1,128)S(1)} %get-tuple-element.84.refs_1_, f32[1,3072]{1,0:T(1,128)S(1)} %get-tuple-element.83.refs_2_, f32[2,128]{1,0:T(2,128)S(1)} %pad_maximum_fusion.3.refs_3_.gain_ref, ...), custom_call_target="tpu_custom_call" | custom-call | flops 3623878 | bytes 20054 | tf_op jit(solution)/shard_map/norm_keys/pallas_call | solution.py:146
  42.4 6.6 %values.2.value_ref = bf16[768,768]{1,0:T(8,128)(2,1)S(1)} custom-call(bf16[768,3072]{1,0:T(8,128)(2,1)S(1)} %get-tuple-element.48.normed_ref, bf16[3,3072,768]{2,1,0:T(8,128)(2,1)} %w_any.7), custom_call_target="tpu_custom_call" | custom-call | flops 3623878 | bytes 10616 | tf_op jit(solution)/shard_map/values/pallas_call | solution.py:210
  53.0 18.2 %queries_own_frame.2 = (bf16[768,768]{1,0:T(8,128)(2,1)S(1)}, f32[768,768]{1,0:T(8,128)S(1)}, f32[768,768]{1,0:T(8,128)S(1)}, f32[768,768]{1,0:T(8,128)S(1)}) custom-call(f32[2,128]{1,0:T(2,128)S(1)} %pad_maximum_fusion.3.refs_3_.gain_ref, bf16[768,3072]{1,0:T(8,128)(2,1)S(1)} %get-tuple-element.48.normed_ref, ...), custom_call_target="tpu_custom_call" | custom-call | flops 7247757 | bytes 20054 | tf_op jit(solution)/shard_map/queries_own_frame/pallas_call | solution.py:289
  71.2 5.5 %collective-permute-done.9.refs_8_ = bf16[768,768]{1,0:T(8,128)(2,1)S(1)} collective-permute-done((bf16[768,768]{1,0:T(8,128)(2,1)S(1)}, bf16[768,768]{1,0:T(8,128)(2,1)S(1)}, u32[]{:S(2)}, u32[]{:S(2)}) %collective-permute-start.9) | collective-permute-done | bytes 1179680 | tf_op jit(solution)/shard_map/ppermute | solution.py:500
  76.7 12.6 %collective-permute-done.8.refs_6_ = bf16[768,768]{1,0:T(8,128)(2,1)S(1)} collective-permute-done((bf16[768,768]{1,0:T(8,128)(2,1)S(1)}, bf16[768,768]{1,0:T(8,128)(2,1)S(1)}, u32[]{:S(2)}, u32[]{:S(2)}) %collective-permute-start.8) | collective-permute-done | bytes 1179680 | tf_op jit(solution)/shard_map/ppermute | solution.py:500
  94.0 3.4 collective-permute-done.11.refs_8_.refs_11_
  97.4 7.1 %earlier_frame.2 = bf16[768,768]{1,0:T(8,128)(2,1)S(1)} custom-call(s32[4]{0:T(128)S(1)} %copy-done.6, bf16[768,768]{1,0:T(8,128)(2,1)S(1)} %get-tuple-element.54.refs_1_, f32[768,768]{1,0:T(8,128)S(1)} %get-tuple-element.55.refs_2_, f32[768,768]{1,0:T(8,128)S(1)} %get-tuple-element.56.refs_3_, f32[768,768]{1,0:T(8,128)S(1)} %get-tuple-element.57.refs_4_, ...), custom_call_target="tpu_custom_call" | custom-call | flops 3623878 | bytes 12976 | tf_op jit(solution)/shard_map/earlier_frame/pallas_call | solution.py:356
  106.5 11.6 %collective-permute-done.13 = bf16[384,1536]{1,0:T(8,128)(2,1)S(1)} collective-permute-done((bf16[384,1536]{1,0:T(8,128)(2,1)S(1)}, bf16[384,1536]{1,0:T(8,128)(2,1)S(1)}, u32[]{:S(2)}, u32[]{:S(2)}) %collective-permute-start.13) | collective-permute-done | bytes 1179680 | tf_op jit(solution)/shard_map/ppermute | solution.py:500
  120.2 3.7 %collective-permute-done.12.refs_1_ = bf16[768,768]{1,0:T(8,128)(2,1)S(1)} collective-permute-done((bf16[768,768]{1,0:T(8,128)(2,1)S(1)}, bf16[768,768]{1,0:T(8,128)(2,1)S(1)}, u32[]{:S(2)}, u32[]{:S(2)}) %collective-permute-start.12) | collective-permute-done | bytes 1179680 | tf_op jit(solution)/shard_map/ppermute | solution.py:500
  128.3 2.1 collective-permute-start.22
  130.4 2.4 collective-permute-start.15
  132.9 2.7 collective-permute-start.16
  135.6 25.1 %collective-permute-done.15.refs_2_ = bf16[768,768]{1,0:T(8,128)(2,1)S(1)} collective-permute-done((bf16[768,768]{1,0:T(8,128)(2,1)S(1)}, bf16[768,768]{1,0:T(8,128)(2,1)S(1)}, u32[]{:S(2)}, u32[]{:S(2)}) %collective-permute-start.15) | collective-permute-done | bytes 1179680 | tf_op jit(solution)/shard_map/ppermute | solution.py:500
  161.5 2.7 collective-permute-start.18
  166.2 2.4 collective-permute-start.19
  174.6 16.0 %projection_start.2.refs_1_ = bf16[768,3072]{1,0:T(8,128)(2,1)S(1)} custom-call(s32[1]{0:T(128)} %bitcast.refs_0_, bf16[768,768]{1,0:T(8,128)(2,1)S(1)} %copy-done.3, bf16[768,768]{1,0:T(8,128)(2,1)S(1)} %collective-permute-done.15.refs_2_, bf16[768,768]{1,0:T(8,128)(2,1)S(1)} %copy-done.1, bf16[768,3072]{1,0:T(8,128)(2,1)} %refs_7_.1, ...), custom_call_target="tpu_custom_call" | custom-call | flops 10871635 | bytes 18874 | tf_op jit(solution)/shard_map/projection_start/pallas_call | solution.py:463
  190.7 9.9 %projection_end.2.refs_5_ = bf16[768,3072]{1,0:T(8,128)(2,1)} custom-call(s32[1]{0:T(128)} %bitcast.refs_0_, bf16[768,3072]{1,0:T(8,128)(2,1)S(1)} %projection_start.2.refs_1_, bf16[768,3072]{1,0:T(8,128)(2,1)} %collective-permute-done.17.refs_2_, f32[1,3072]{1,0:T(1,128)S(1)} %fusion.refs_3_, bf16[384,768]{1,0:T(8,128)(2,1)} %collective-permute-done.18.refs_4_, ...), custom_call_target="tpu_custom_call" | custom-call | flops 3623878 | bytes 18874 | tf_op jit(solution)/shard_map/projection_end/pallas_call | solution.py:463
  200.6 14.2 %norm_keys.3 = (bf16[768,768]{1,0:T(8,128)(2,1)S(1)}, bf16[768,3072]{1,0:T(8,128)(2,1)S(1)}, bf16[768,3072]{1,0:T(8,128)(2,1)}) custom-call(s32[4]{0:T(128)S(1)} %copy-done.7, f32[1,3072]{1,0:T(1,128)S(1)} %copy-done.5, f32[1,3072]{1,0:T(1,128)S(1)} %get-tuple-element.83.refs_2_, f32[2,128]{1,0:T(2,128)S(1)} %pad_maximum_fusion.3.refs_3_.gain_ref, ...), custom_call_target="tpu_custom_call" | custom-call | flops 3623878 | bytes 20054 | tf_op jit(solution)/shard_map/norm_keys/pallas_call | solution.py:146
  216.2 6.8 %values.3.value_ref = bf16[768,768]{1,0:T(8,128)(2,1)S(1)} custom-call(bf16[768,3072]{1,0:T(8,128)(2,1)S(1)} %get-tuple-element.71.normed_ref, bf16[3,3072,768]{2,1,0:T(8,128)(2,1)} %w_any.7), custom_call_target="tpu_custom_call" | custom-call | flops 3623878 | bytes 10616 | tf_op jit(solution)/shard_map/values/pallas_call | solution.py:210
  223.0 3.2 collective-permute-start.25
  229.1 18.2 %queries_own_frame.3 = (bf16[768,768]{1,0:T(8,128)(2,1)S(1)}, f32[768,768]{1,0:T(8,128)S(1)}, f32[768,768]{1,0:T(8,128)S(1)}, f32[768,768]{1,0:T(8,128)S(1)}) custom-call(f32[2,128]{1,0:T(2,128)S(1)} %pad_maximum_fusion.3.refs_3_.gain_ref, bf16[768,3072]{1,0:T(8,128)(2,1)S(1)} %get-tuple-element.71.normed_ref, ...), custom_call_target="tpu_custom_call" | custom-call | flops 7247757 | bytes 20054 | tf_op jit(solution)/shard_map/queries_own_frame/pallas_call | solution.py:289
  247.3 10.9 %collective-permute-done.24.refs_6_ = bf16[768,768]{1,0:T(8,128)(2,1)S(1)} collective-permute-done((bf16[768,768]{1,0:T(8,128)(2,1)S(1)}, bf16[768,768]{1,0:T(8,128)(2,1)S(1)}, u32[]{:S(2)}, u32[]{:S(2)}) %collective-permute-start.24) | collective-permute-done | bytes 1179680 | tf_op jit(solution)/shard_map/ppermute | solution.py:500
  258.2 7.1 %earlier_frame.3 = (bf16[384,768]{1,0:T(8,128)(2,1)S(1)}, bf16[384,768]{1,0:T(8,128)(2,1)S(1)}) custom-call(s32[4]{0:T(128)S(1)} %copy-done.7, bf16[768,768]{1,0:T(8,128)(2,1)S(1)} %get-tuple-element.72.refs_1_, f32[768,768]{1,0:T(8,128)S(1)} %get-tuple-element.73.refs_2_, f32[768,768]{1,0:T(8,128)S(1)} %get-tuple-element.74.refs_3_, ...), custom_call_target="tpu_custom_call" | custom-call | flops 3623878 | bytes 12976 | tf_op jit(solution)/shard_map/earlier_frame/pallas_call | solution.py:356
  265.4 11.0 %collective-permute-done.27.refs_1_ = bf16[384,768]{1,0:T(8,128)(2,1)S(1)} collective-permute-done((bf16[384,768]{1,0:T(8,128)(2,1)S(1)}, bf16[384,768]{1,0:T(8,128)(2,1)S(1)}, u32[]{:S(2)}, u32[]{:S(2)}) %collective-permute-start.27) | collective-permute-done | bytes 589856 | tf_op jit(solution)/shard_map/ppermute | solution.py:500
  276.5 6.3 %collective-permute-done.28.refs_2_ = bf16[384,768]{1,0:T(8,128)(2,1)S(1)} collective-permute-done((bf16[384,768]{1,0:T(8,128)(2,1)S(1)}, bf16[384,768]{1,0:T(8,128)(2,1)S(1)}, u32[]{:S(2)}, u32[]{:S(2)}) %collective-permute-start.28) | collective-permute-done | bytes 589856 | tf_op jit(solution)/shard_map/ppermute | solution.py:500
  286.9 12.2 %collective-permute-done.29.refs_3_ = bf16[384,768]{1,0:T(8,128)(2,1)S(1)} collective-permute-done((bf16[384,768]{1,0:T(8,128)(2,1)S(1)}, bf16[384,768]{1,0:T(8,128)(2,1)S(1)}, u32[]{:S(2)}, u32[]{:S(2)}) %collective-permute-start.29) | collective-permute-done | bytes 589856 | tf_op jit(solution)/shard_map/ppermute | solution.py:500
  301.3 6.8 %collective-permute-done.30.refs_4_ = bf16[384,768]{1,0:T(8,128)(2,1)S(1)} collective-permute-done((bf16[384,768]{1,0:T(8,128)(2,1)S(1)}, bf16[384,768]{1,0:T(8,128)(2,1)S(1)}, u32[]{:S(2)}, u32[]{:S(2)}) %collective-permute-start.30) | collective-permute-done | bytes 589856 | tf_op jit(solution)/shard_map/ppermute | solution.py:500
  310.3 16.0 %projection_start.3.refs_1_ = bf16[768,3072]{1,0:T(8,128)(2,1)S(1)} custom-call(s32[1]{0:T(128)} %bitcast.refs_0_, bf16[384,768]{1,0:T(8,128)(2,1)S(1)} %collective-permute-done.27.refs_1_, bf16[384,768]{1,0:T(8,128)(2,1)S(1)} %collective-permute-done.28.refs_2_, bf16[384,768]{1,0:T(8,128)(2,1)S(1)} %collective-permute-done.29.refs_3_, ...), custom_call_target="tpu_custom_call" | custom-call | flops 10871635 | bytes 18874 | tf_op jit(solution)/shard_map/projection_start/pallas_call | solution.py:463
  326.4 11.7 %collective-permute-done.33.refs_2_ = bf16[768,3072]{1,0:T(8,128)(2,1)S(1)} collective-permute-done((bf16[768,3072]{1,0:T(8,128)(2,1)S(1)}, bf16[768,3072]{1,0:T(8,128)(2,1)S(1)}, u32[]{:S(2)}, u32[]{:S(2)}) %collective-permute-start.33) | collective-permute-done | bytes 4718624 | tf_op jit(solution)/shard_map/ppermute | solution.py:500
  338.1 8.5 %projection_end.3 = bf16[768,3072]{1,0:T(8,128)(2,1)} custom-call(s32[1]{0:T(128)} %bitcast.refs_0_, bf16[768,3072]{1,0:T(8,128)(2,1)S(1)} %projection_start.3.refs_1_, bf16[768,3072]{1,0:T(8,128)(2,1)S(1)} %collective-permute-done.33.refs_2_, f32[1,3072]{1,0:T(1,128)S(1)} %fusion.refs_3_, bf16[192,768]{1,0:T(8,128)(2,1)S(1)} %collective-permute-done.34.refs_4_, ...), custom_call_target="tpu_custom_call" | custom-call | flops 3623878 | bytes 18874 | tf_op jit(solution)/shard_map/projection_end/pallas_call | solution.py:463
  (111 shorter events, 51.8 us)
Async XLA Ops:
  1.8 19.9 %collective-permute-start.2 = (bf16[192,3072]{1,0:T(8,128)(2,1)S(1)}, bf16[192,3072]{1,0:T(8,128)(2,1)}, u32[]{:S(2)}, u32[]{:S(2)}) collective-permute-start(bf16[192,3072]{1,0:T(8,128)(2,1)S(1)} %get-tuple-element.82.refs_6_), channel_id=1, source_target_pairs={{28,30},{29,31},{30,28},{31,29}} | collective-permute-start | bytes 3538952 | tf_op jit(solution)/shard_map/ppermute | solution.py:500
  3.5 18.2 %collective-permute-start.3 = (bf16[192,3072]{1,0:T(8,128)(2,1)S(1)}, bf16[192,3072]{1,0:T(8,128)(2,1)}, u32[]{:S(2)}, u32[]{:S(2)}) collective-permute-start(bf16[192,3072]{1,0:T(8,128)(2,1)S(1)} %get-tuple-element.82.refs_6_), channel_id=1, source_target_pairs={{28,31},{29,30},{30,29},{31,28}} | collective-permute-start | bytes 3538952 | tf_op jit(solution)/shard_map/ppermute | solution.py:500
  5.2 18.3 %collective-permute-start.1 = (bf16[192,3072]{1,0:T(8,128)(2,1)S(1)}, bf16[192,3072]{1,0:T(8,128)(2,1)S(1)}, u32[]{:S(2)}, u32[]{:S(2)}) collective-permute-start(bf16[192,3072]{1,0:T(8,128)(2,1)S(1)} %get-tuple-element.82.refs_6_), channel_id=1, source_target_pairs={{28,29},{29,28},{30,31},{31,30}} | collective-permute-start | bytes 3538952 | tf_op jit(solution)/shard_map/ppermute | solution.py:500
  39.3 50.1 %collective-permute-start.5 = (bf16[768,1536]{1,0:T(8,128)(2,1)S(1)}, bf16[768,1536]{1,0:T(8,128)(2,1)S(1)}, u32[]{:S(2)}, u32[]{:S(2)}) collective-permute-start(bf16[768,1536]{1,0:T(8,128)(2,1)S(1)} %copy-done.12), channel_id=1, source_target_pairs={{0,1},{1,0},{2,3},{3,2},{4,5},{5,4},{6,7},{7,6},{8,9},{9,8},{10,11... | collective-permute-start | bytes 7077896 | tf_op jit(solution)/shard_map/ppermute | solution.py:500
  40.9 48.5 %collective-permute-start.6 = (bf16[768,1536]{1,0:T(8,128)(2,1)S(1)}, bf16[768,1536]{1,0:T(8,128)(2,1)S(1)}, u32[]{:S(2)}, u32[]{:S(2)}) collective-permute-start(bf16[768,1536]{1,0:T(8,128)(2,1)S(1)} %copy-done.12), channel_id=1, source_target_pairs={{0,2},{1,3},{2,0},{3,1},{4,6},{5,7},{6,4},{7,5},{8,10},{9,11},{10,... | collective-permute-start | bytes 7077896 | tf_op jit(solution)/shard_map/ppermute | solution.py:500
  49.0 22.2 %collective-permute-start.7 = (bf16[768,768]{1,0:T(8,128)(2,1)S(1)}, bf16[768,768]{1,0:T(8,128)(2,1)S(1)}, u32[]{:S(2)}, u32[]{:S(2)}) collective-permute-start(bf16[768,768]{1,0:T(8,128)(2,1)S(1)} %values.2.value_ref), channel_id=1, source_target_pairs={{0,4},{1,5},{2,6},{3,7},{4,8},{5,9},{6,10},{7,11},{8,12},{9,13},{1... | collective-permute-start | bytes 3538952 | tf_op jit(solution)/shard_map/ppermute | solution.py:500
  50.4 26.4 %collective-permute-start.9 = (bf16[768,768]{1,0:T(8,128)(2,1)S(1)}, bf16[768,768]{1,0:T(8,128)(2,1)S(1)}, u32[]{:S(2)}, u32[]{:S(2)}) collective-permute-start(bf16[768,768]{1,0:T(8,128)(2,1)S(1)} %values.2.value_ref), channel_id=1, source_target_pairs={{28,0},{29,1},{30,2},{31,3}} | collective-permute-start | bytes 3538952 | tf_op jit(solution)/shard_map/ppermute | solution.py:500
  51.7 37.7 %collective-permute-start.8 = (bf16[768,768]{1,0:T(8,128)(2,1)S(1)}, bf16[768,768]{1,0:T(8,128)(2,1)S(1)}, u32[]{:S(2)}, u32[]{:S(2)}) collective-permute-start(bf16[768,768]{1,0:T(8,128)(2,1)S(1)} %get-tuple-element.47.key_ref), channel_id=1, source_target_pairs={{28,0},{29,1},{30,2},{31,3}} | collective-permute-start | bytes 3538952 | tf_op jit(solution)/shard_map/ppermute | solution.py:500
  91.5 26.7 %collective-permute-start.13 = (bf16[384,1536]{1,0:T(8,128)(2,1)S(1)}, bf16[384,1536]{1,0:T(8,128)(2,1)S(1)}, u32[]{:S(2)}, u32[]{:S(2)}) collective-permute-start(bf16[384,1536]{1,0:T(8,128)(2,1)S(1)} %slice.45), channel_id=1, source_target_pairs={{0,2},{1,3},{2,0},{3,1},{4,6},{5,7},{6,4},{7,5},{8,10},{9,11},{10,... | collective-permute-start | bytes 3538952 | tf_op jit(solution)/shard_map/ppermute | solution.py:500
  92.0 26.6 %collective-permute-start.14 = (bf16[384,1536]{1,0:T(8,128)(2,1)S(1)}, bf16[384,1536]{1,0:T(8,128)(2,1)S(1)}, u32[]{:S(2)}, u32[]{:S(2)}) collective-permute-start(bf16[384,1536]{1,0:T(8,128)(2,1)S(1)} %slice.46), channel_id=1, source_target_pairs={{0,1},{1,0},{2,3},{3,2},{4,5},{5,4},{6,7},{7,6},{8,9},{9,8},{10,11... | collective-permute-start | bytes 3538952 | tf_op jit(solution)/shard_map/ppermute | solution.py:500
  104.5 19.3 %collective-permute-start.12 = (bf16[768,768]{1,0:T(8,128)(2,1)S(1)}, bf16[768,768]{1,0:T(8,128)(2,1)S(1)}, u32[]{:S(2)}, u32[]{:S(2)}) collective-permute-start(bf16[768,768]{1,0:T(8,128)(2,1)S(1)} %earlier_frame.2), channel_id=1, source_target_pairs={{0,4},{1,5},{2,6},{3,7},{4,8},{5,9},{6,10},{7,11},{8,12},{9,13},{1... | collective-permute-start | bytes 3538952 | tf_op jit(solution)/shard_map/ppermute | solution.py:500
  123.8 66.8 %collective-permute-start.17 = (bf16[768,3072]{1,0:T(8,128)(2,1)}, bf16[768,3072]{1,0:T(8,128)(2,1)}, u32[]{:S(2)}, u32[]{:S(2)}) collective-permute-start(bf16[768,3072]{1,0:T(8,128)(2,1)} %get-tuple-element.66), channel_id=1, source_target_pairs={{0,4},{1,5},{2,6},{3,7},{4,8},{5,9},{6,10},{7,11},{8,12},{9,13},{1... | collective-permute-start | bytes 14155784 | tf_op jit(solution)/shard_map/ppermute | solution.py:500
  126.7 64.0 %collective-permute-start.20 = (bf16[768,1536]{1,0:T(8,128)(2,1)}, bf16[768,1536]{1,0:T(8,128)(2,1)}, u32[]{:S(2)}, u32[]{:S(2)}) collective-permute-start(bf16[768,1536]{1,0:T(8,128)(2,1)} %pad_maximum_fusion.1.refs_6_.refs_8_), channel_id=1, source_target_pairs={{0,4},{1,5},{2,6},{3,7},{4,0},{5,1},{6,2},{7,3},{8,12},{9,13},{10,... | collective-permute-start | bytes 7077896 | tf_op jit(solution)/shard_map/ppermute | solution.py:500
  128.3 72.3 %collective-permute-start.22 = (bf16[384,3072]{1,0:T(8,128)(2,1)}, bf16[384,3072]{1,0:T(8,128)(2,1)}, u32[]{:S(2)}, u32[]{:S(2)}) collective-permute-start(bf16[384,3072]{1,0:T(8,128)(2,1)} %pad_maximum_fusion.2), channel_id=1, source_target_pairs={{28,30},{29,31},{30,28},{31,29}} | collective-permute-start | bytes 7077896 | tf_op jit(solution)/shard_map/ppermute | solution.py:500
  130.4 30.2 %collective-permute-start.15 = (bf16[768,768]{1,0:T(8,128)(2,1)S(1)}, bf16[768,768]{1,0:T(8,128)(2,1)S(1)}, u32[]{:S(2)}, u32[]{:S(2)}) collective-permute-start(bf16[768,768]{1,0:T(8,128)(2,1)S(1)} %collective-permute-done.12.refs_1_), channel_id=1, source_target_pairs={{0,1},{1,0},{2,3},{3,2},{4,5},{5,4},{6,7},{7,6},{8,9},{9,8},{10,11... | collective-permute-start | bytes 3538952 | tf_op jit(solution)/shard_map/ppermute | solution.py:500
  132.9 31.4 %collective-permute-start.16 = (bf16[768,768]{1,0:T(8,128)(2,1)S(1)}, bf16[768,768]{1,0:T(8,128)(2,1)S(1)}, u32[]{:S(2)}, u32[]{:S(2)}) collective-permute-start(bf16[768,768]{1,0:T(8,128)(2,1)S(1)} %collective-permute-done.12.refs_1_), channel_id=1, source_target_pairs={{0,2},{1,3},{2,0},{3,1},{4,6},{5,7},{6,4},{7,5},{8,10},{9,11},{10,... | collective-permute-start | bytes 3538952 | tf_op jit(solution)/shard_map/ppermute | solution.py:500
  161.5 29.1 %collective-permute-start.18 = (bf16[384,768]{1,0:T(8,128)(2,1)}, bf16[384,768]{1,0:T(8,128)(2,1)}, u32[]{:S(2)}, u32[]{:S(2)}) collective-permute-start(bf16[384,768]{1,0:T(8,128)(2,1)} %slice.58), channel_id=1, source_target_pairs={{0,2},{1,3},{2,0},{3,1},{4,6},{5,7},{6,4},{7,5},{8,10},{9,11},{10,... | collective-permute-start | bytes 1769480 | tf_op jit(solution)/shard_map/ppermute | solution.py:500
  166.2 24.5 %collective-permute-start.19 = (bf16[384,768]{1,0:T(8,128)(2,1)}, bf16[384,768]{1,0:T(8,128)(2,1)}, u32[]{:S(2)}, u32[]{:S(2)}) collective-permute-start(bf16[384,768]{1,0:T(8,128)(2,1)} %slice.59), channel_id=1, source_target_pairs={{0,1},{1,0},{2,3},{3,2},{4,5},{5,4},{6,7},{7,6},{8,9},{9,8},{10,11... | collective-permute-start | bytes 1769480 | tf_op jit(solution)/shard_map/ppermute | solution.py:500
  214.9 14.2 %collective-permute-start.23 = (bf16[768,768]{1,0:T(8,128)(2,1)S(1)}, bf16[768,768]{1,0:T(8,128)(2,1)S(1)}, u32[]{:S(2)}, u32[]{:S(2)}) collective-permute-start(bf16[768,768]{1,0:T(8,128)(2,1)S(1)} %get-tuple-element.70.key_ref), channel_id=1, source_target_pairs={{0,4},{1,5},{2,6},{3,7},{4,8},{5,9},{6,10},{7,11},{8,12},{9,13},{1... | collective-permute-start | bytes 3538952 | tf_op jit(solution)/shard_map/ppermute | solution.py:500
  223.0 24.2 %collective-permute-start.25 = (bf16[768,768]{1,0:T(8,128)(2,1)S(1)}, bf16[768,768]{1,0:T(8,128)(2,1)S(1)}, u32[]{:S(2)}, u32[]{:S(2)}) collective-permute-start(bf16[768,768]{1,0:T(8,128)(2,1)S(1)} %values.3.value_ref), channel_id=1, source_target_pairs={{0,4},{1,5},{2,6},{3,7},{4,8},{5,9},{6,10},{7,11},{8,12},{9,13},{1... | collective-permute-start | bytes 3538952 | tf_op jit(solution)/shard_map/ppermute | solution.py:500
  226.2 21.1 %collective-permute-start.26 = (bf16[768,768]{1,0:T(8,128)(2,1)S(1)}, bf16[768,768]{1,0:T(8,128)(2,1)S(1)}, u32[]{:S(2)}, u32[]{:S(2)}) collective-permute-start(bf16[768,768]{1,0:T(8,128)(2,1)S(1)} %values.3.value_ref), channel_id=1, source_target_pairs={{28,0},{29,1},{30,2},{31,3}} | collective-permute-start | bytes 3538952 | tf_op jit(solution)/shard_map/ppermute | solution.py:500
  227.5 30.7 %collective-permute-start.24 = (bf16[768,768]{1,0:T(8,128)(2,1)S(1)}, bf16[768,768]{1,0:T(8,128)(2,1)S(1)}, u32[]{:S(2)}, u32[]{:S(2)}) collective-permute-start(bf16[768,768]{1,0:T(8,128)(2,1)S(1)} %get-tuple-element.70.key_ref), channel_id=1, source_target_pairs={{28,0},{29,1},{30,2},{31,3}} | collective-permute-start | bytes 3538952 | tf_op jit(solution)/shard_map/ppermute | solution.py:500
  265.4 17.4 %collective-permute-start.28 = (bf16[384,768]{1,0:T(8,128)(2,1)S(1)}, bf16[384,768]{1,0:T(8,128)(2,1)S(1)}, u32[]{:S(2)}, u32[]{:S(2)}) collective-permute-start(bf16[384,768]{1,0:T(8,128)(2,1)S(1)} %get-tuple-element.78), channel_id=1, source_target_pairs={{0,4},{1,5},{2,6},{3,7},{4,8},{5,9},{6,10},{7,11},{8,12},{9,13},{1... | collective-permute-start | bytes 1769480 | tf_op jit(solution)/shard_map/ppermute | solution.py:500
  282.8 55.3 %collective-permute-start.33 = (bf16[768,3072]{1,0:T(8,128)(2,1)S(1)}, bf16[768,3072]{1,0:T(8,128)(2,1)S(1)}, u32[]{:S(2)}, u32[]{:S(2)}) collective-permute-start(bf16[768,3072]{1,0:T(8,128)(2,1)S(1)} %bitcast.23), channel_id=1, source_target_pairs={{0,4},{1,5},{2,6},{3,7},{4,8},{5,9},{6,10},{7,11},{8,12},{9,13},{1... | collective-permute-start | bytes 14155784 | tf_op jit(solution)/shard_map/ppermute | solution.py:500
  282.8 16.3 %collective-permute-start.29 = (bf16[384,768]{1,0:T(8,128)(2,1)S(1)}, bf16[384,768]{1,0:T(8,128)(2,1)S(1)}, u32[]{:S(2)}, u32[]{:S(2)}) collective-permute-start(bf16[384,768]{1,0:T(8,128)(2,1)S(1)} %collective-permute-done.27.refs_1_), channel_id=1, source_target_pairs={{0,1},{1,0},{2,3},{3,2},{4,5},{5,4},{6,7},{7,6},{8,9},{9,8},{10,11... | collective-permute-start | bytes 1769480 | tf_op jit(solution)/shard_map/ppermute | solution.py:500
  284.4 16.3 %collective-permute-start.31 = (bf16[384,768]{1,0:T(8,128)(2,1)S(1)}, bf16[384,768]{1,0:T(8,128)(2,1)S(1)}, u32[]{:S(2)}, u32[]{:S(2)}) collective-permute-start(bf16[384,768]{1,0:T(8,128)(2,1)S(1)} %collective-permute-done.27.refs_1_), channel_id=1, source_target_pairs={{0,2},{1,3},{2,0},{3,1},{4,6},{5,7},{6,4},{7,5},{8,10},{9,11},{10,... | collective-permute-start | bytes 1769480 | tf_op jit(solution)/shard_map/ppermute | solution.py:500
  284.9 23.3 %collective-permute-start.30 = (bf16[384,768]{1,0:T(8,128)(2,1)S(1)}, bf16[384,768]{1,0:T(8,128)(2,1)S(1)}, u32[]{:S(2)}, u32[]{:S(2)}) collective-permute-start(bf16[384,768]{1,0:T(8,128)(2,1)S(1)} %collective-permute-done.28.refs_2_), channel_id=1, source_target_pairs={{0,1},{1,0},{2,3},{3,2},{4,5},{5,4},{6,7},{7,6},{8,9},{9,8},{10,11... | collective-permute-start | bytes 1769480 | tf_op jit(solution)/shard_map/ppermute | solution.py:500
  285.5 23.9 %collective-permute-start.32 = (bf16[384,768]{1,0:T(8,128)(2,1)S(1)}, bf16[384,768]{1,0:T(8,128)(2,1)S(1)}, u32[]{:S(2)}, u32[]{:S(2)}) collective-permute-start(bf16[384,768]{1,0:T(8,128)(2,1)S(1)} %collective-permute-done.28.refs_2_), channel_id=1, source_target_pairs={{0,2},{1,3},{2,0},{3,1},{4,6},{5,7},{6,4},{7,5},{8,10},{9,11},{10,... | collective-permute-start | bytes 1769480 | tf_op jit(solution)/shard_map/ppermute | solution.py:500
  299.2 27.2 %collective-permute-start.34 = (bf16[192,768]{1,0:T(8,128)(2,1)S(1)}, bf16[192,768]{1,0:T(8,128)(2,1)S(1)}, u32[]{:S(2)}, u32[]{:S(2)}) collective-permute-start(bf16[192,768]{1,0:T(8,128)(2,1)S(1)} %slice.60), channel_id=1, source_target_pairs={{0,2},{1,3},{2,0},{3,1},{4,6},{5,7},{6,4},{7,5},{8,10},{9,11},{10,... | collective-permute-start | bytes 884744 | tf_op jit(solution)/shard_map/ppermute | solution.py:500
  300.6 25.7 %collective-permute-start.35 = (bf16[192,768]{1,0:T(8,128)(2,1)S(1)}, bf16[192,768]{1,0:T(8,128)(2,1)S(1)}, u32[]{:S(2)}, u32[]{:S(2)}) collective-permute-start(bf16[192,768]{1,0:T(8,128)(2,1)S(1)} %slice.61), channel_id=1, source_target_pairs={{0,1},{1,0},{2,3},{3,2},{4,5},{5,4},{6,7},{7,6},{8,9},{9,8},{10,11... | collective-permute-start | bytes 884744 | tf_op jit(solution)/shard_map/ppermute | solution.py:500
  308.2 18.2 %collective-permute-start.36 = (bf16[192,768]{1,0:T(8,128)(2,1)S(1)}, bf16[192,768]{1,0:T(8,128)(2,1)S(1)}, u32[]{:S(2)}, u32[]{:S(2)}) collective-permute-start(bf16[192,768]{1,0:T(8,128)(2,1)S(1)} %slice.62), channel_id=1, source_target_pairs={{0,2},{1,3},{2,0},{3,1},{4,6},{5,7},{6,4},{7,5},{8,10},{9,11},{10,... | collective-permute-start | bytes 884744 | tf_op jit(solution)/shard_map/ppermute | solution.py:500
  309.4 17.0 %collective-permute-start.37 = (bf16[192,768]{1,0:T(8,128)(2,1)S(1)}, bf16[192,768]{1,0:T(8,128)(2,1)S(1)}, u32[]{:S(2)}, u32[]{:S(2)}) collective-permute-start(bf16[192,768]{1,0:T(8,128)(2,1)S(1)} %slice.63), channel_id=1, source_target_pairs={{0,1},{1,0},{2,3},{3,2},{4,5},{5,4},{6,7},{7,6},{8,9},{9,8},{10,11... | collective-permute-start | bytes 884744 | tf_op jit(solution)/shard_map/ppermute | solution.py:500
  (23 other events, 268.7 us)

commit v7 on v6

--- a/solution.py
+++ b/solution.py
@@ -314,9 +314,8 @@
 
 
 def earlier_kernel(*refs, chunks):
-    info_ref, query_ref, acc_ref, top_ref, total_ref = refs[:5]
-    key_ref, first_key_ref, value_ref, first_value_ref = refs[5:9]
-    out_refs = refs[9:]
+    info_ref, query_ref, acc_ref, top_ref, total_ref, key_ref, value_ref = refs[:7]
+    out_refs = refs[7:]
     rows = query_ref.shape[0] // chunks
 
     def store(row, at, result):
@@ -333,24 +332,19 @@
 
     @pl.when(info_ref[0] == 0)
     def _():
-        keys = jnp.where(info_ref[3] != 0, first_key_ref[...], key_ref[...])
-        values = jnp.where(info_ref[3] != 0, first_value_ref[...], value_ref[...])
-
         def finish(scores, row, at):
             old_top = top_ref[row, at][:, :1]
             top = jnp.maximum(jnp.max(scores, axis=-1, keepdims=True), old_top)
-            acc, total = weigh(scores, top, values[:, at])
+            acc, total = weigh(scores, top, value_ref[:, at])
             kept = jnp.exp2(old_top - top)
             acc = acc + acc_ref[row, at] * kept
             total = total + total_ref[row, at] * kept
             store(row, at, (acc / total).astype(BF16))
 
-        attention_tiles(query_ref[...], keys, finish)
-
-
-def earlier_attention(
-    info, query, acc, top, total, key, first_key, value, first_value, chunks
-):
+        attention_tiles(query_ref[...], key_ref, finish)
+
+
+def earlier_attention(info, query, acc, top, total, key, value, chunks):
     rows, head_cols = query.shape
     cols = tile_cols(head_cols)
     return pl.pallas_call(
@@ -358,7 +352,7 @@
         grid_spec=pltpu.PrefetchScalarGridSpec(
             num_scalar_prefetch=1,
             grid=(head_cols // cols,),
-            in_specs=[pl.BlockSpec((rows, cols), lambda j, i: (0, j))] * 8,
+            in_specs=[pl.BlockSpec((rows, cols), lambda j, i: (0, j))] * 6,
             out_specs=[pl.BlockSpec((rows // chunks, cols), lambda j, i: (0, j))] * chunks,
         ),
         out_shape=[jax.ShapeDtypeStruct((rows // chunks, head_cols), BF16)] * chunks,
@@ -369,7 +363,7 @@
             rows * rows * head_cols // HD,
         ),
         name="earlier_frame",
-    )(info, query, acc, top, total, key, first_key, value, first_value)
+    )(info, query, acc, top, total, key, value)
 
 
 def output_kernel(*refs, part_counts, whole_weights, half_blocks, last):
@@ -576,7 +570,7 @@
 
     shift, scale1, _ = modulation(worked_level)
     _, _, gate = modulation(levels[0])
-    info = jnp.stack([is_last, tensor_index // 2, tensor_index % 2, queue_index == 0])
+    info = jnp.stack([is_last, tensor_index // 2, tensor_index % 2])
     info = info.astype(jnp.int32)
     gains = jnp.stack([q_gain * SCORE_SCALE, k_gain])
 
@@ -586,16 +580,15 @@
         key, normed, state = project_keys(
             info, scale1, shift, gains, qkv_weight, frame, noise, noise_pieces
         )
-        earlier_key = ring(key, range(queue_size - 2))
-        first_key = ring(key, [queue_size - 1])
+        to_next = [q for q in range(queue_size) if q != queue_size - 2]
+        earlier_key = ring(key, to_next)
         value = project_values(normed, qkv_weight)
-        earlier_value = ring(value, range(queue_size - 2))
-        first_value = ring(value, [queue_size - 1])
+        earlier_value = ring(value, to_next)
         normed, earlier_key = lax.optimization_barrier((normed, earlier_key))
         query, *own = own_attention(gains, normed, qkv_weight, key, value)
         if not final:
-            query, mine, earlier_value, first_key, first_value = lax.optimization_barrier(
-                (query, mine, earlier_value, first_key, first_value)
+            query, mine, earlier_value = lax.optimization_barrier(
+                (query, mine, earlier_value)
             )
             mine_corners = [
                 jnp.concatenate(parts, axis=0) for parts in two_hops(mine, *mesh_sizes)
@@ -603,30 +596,25 @@
             theirs = [sibling(block) for block in mine]
             query, theirs = lax.optimization_barrier((query, theirs))
         attended = earlier_attention(
-            info,
-            query,
-            *own,
-            earlier_key,
-            first_key,
-            earlier_value,
-            first_value,
-            CHUNKS if final else 1,
+            info, query, *own, earlier_key, earlier_value, CHUNKS if final else 1
         )
-        senders = [q for q in range(queue_size) if final or q != queue_size - 2]
+        senders = range(queue_size) if final else to_next
         targets = range(queue_size if final else queue_size - 1)
         attended = [ring(block, senders) for block in attended]
         if not final:
             attended, mine_corners = lax.optimization_barrier((attended, mine_corners))
-            theirs_corners = [sibling(block) for block in mine_corners]
         sent_state, _ = lax.optimization_barrier((state, attended))
         resid = ring(sent_state, senders)
         near = [one_hop(block, *mesh_sizes, targets) for block in attended]
+        if not final:
+            noise, mine_corners, near = lax.optimization_barrier(
+                (fresh_noise[step_index + 1], mine_corners, near)
+            )
+            theirs_corners = [sibling(block) for block in mine_corners]
+            noise_pieces = gather_noise(noise, False)
         beyond = [two_hops(blocks, *mesh_sizes, targets) for blocks in near]
         direct = [attended] + [list(parts) for parts in zip(*near)]
         corners = [[half for parts in p for half in parts] for p in zip(*beyond)]
-        if not final:
-            noise, _ = lax.optimization_barrier((fresh_noise[step_index + 1], attended))
-            noise_pieces = gather_noise(noise, False)
         begun = output_projection(parity, direct, [out_weight], mine, theirs)
         frame = output_projection(
             parity, corners, [], mine_corners, theirs_corners, (begun, resid, gate)

time: 348 us -> 353 us (1.014)
  waiting for transfers between devices: 124 us -> 131 us
    ppermute x38 -> x34, waiting for transfers between devices: 124 us -> 131 us  [send(): return lax.ppermute(block, AXES, pairs)]
    ppermute x38 -> x34, starting transfers between devices: 54.9 us -> 53 us  [send(): return lax.ppermute(block, AXES, pairs)]
  transfers between devices with their start and end apart: 38 -> 34, of which waited for: 16 -> 15; matrix products, arithmetic and copies ran while one was open for 4% -> 4% of each run, Pallas kernels for 29% -> 32%
where the time goes in v7:
time: 353 us; the launch traced here: 352 us
  Pallas kernels  143 us (41%)
  waiting for transfers between devices  131 us (37%)
  starting transfers between devices  53 us (15%)
  local copies, waits for them, and re-layouts  13.7 us (4%)
  other arithmetic  8.26 us (2%)
    ppermute x34, waiting for transfers between devices, send(): return lax.ppermute(block, AXES, pairs)  131 us
    ppermute x34, starting transfers between devices, send(): return lax.ppermute(block, AXES, pairs)  53 us
    pallas_call x4, Pallas kernels, output_projection(): pl.pallas_call(functools.partial(output_kernel, part_counts=tuple((len(p)...  50.4 us
    pallas_call x2, Pallas kernels, own_attention(): pl.pallas_call(own_kernel, grid=(head_cols // cols,), in_specs=[pl.BlockS...  36.4 us
    pallas_call x2, Pallas kernels, project_keys(): pl.pallas_call(functools.partial(key_kernel, half=half), grid_spec=pltpu....  28.5 us
    pallas_call x2, Pallas kernels, earlier_attention(): pl.pallas_call(functools.partial(earlier_kernel, chunks=chunks), grid_spe...  13.8 us
    pallas_call x2, Pallas kernels, project_values(): pl.pallas_call(value_kernel, grid=(head_cols // cols,), in_specs=[pl.Bloc...  13.4 us
  transfers between devices with their start and end apart: 34, of which 15 were waited for; matrix products, arithmetic and copies ran while one was open for 4% of the time, Pallas kernels for 32%

profile of v7, /device:TPU:0, one launch (start us, length us, event | category | flops | bytes accessed | tf_op | source)
XLA Modules:
  0.0 351.8 jit_solution(11883009638171052580)
XLA Ops:
  6.0 8.8 %collective-permute-start = (s32[1]{0:T(128)}, s32[1]{0:T(128)}, u32[]{:S(2)}, u32[]{:S(2)}) collective-permute-start(s32[1]{0:T(128)} %param.10), channel_id=1, source_target_pairs={{0,28},{1,29},{2,30},{3,31},{4,0},{5,1},{6,2},{7,3},{8,4},{9,5},{1... | collective-permute-start | bytes 20 | tf_op jit(solution)/shard_map/ppermute | solution.py:494
  15.4 3.2 constant_dynamic-slice_fusion
  26.9 14.2 %norm_keys.2 = (bf16[768,768]{1,0:T(8,128)(2,1)S(1)}, bf16[768,3072]{1,0:T(8,128)(2,1)S(1)}, bf16[768,3072]{1,0:T(8,128)(2,1)}) custom-call(s32[3]{0:T(128)S(1)} %copy-done.6, f32[1,3072]{1,0:T(1,128)S(1)} %get-tuple-element.86.refs_1_, f32[1,3072]{1,0:T(1,128)S(1)} %get-tuple-element.85.refs_2_, f32[2,128]{1,0:T(2,128)S(1)} %pad_maximum_fusion.3.refs_3_.gain_ref, ...), custom_call_target="tpu_custom_call" | custom-call | flops 3623878 | bytes 20054 | tf_op jit(solution)/shard_map/norm_keys/pallas_call | solution.py:146
  43.1 6.6 %values.2.value_ref = bf16[768,768]{1,0:T(8,128)(2,1)S(1)} custom-call(bf16[768,3072]{1,0:T(8,128)(2,1)S(1)} %get-tuple-element.49.normed_ref, bf16[3,3072,768]{2,1,0:T(8,128)(2,1)} %w_any.7), custom_call_target="tpu_custom_call" | custom-call | flops 3623878 | bytes 10616 | tf_op jit(solution)/shard_map/values/pallas_call | solution.py:210
  51.7 34.0 %collective-permute-done.4.refs_5_ = bf16[768,768]{1,0:T(8,128)(2,1)S(1)} collective-permute-done((bf16[768,768]{1,0:T(8,128)(2,1)S(1)}, bf16[768,768]{1,0:T(8,128)(2,1)S(1)}, u32[]{:S(2)}, u32[]{:S(2)}) %collective-permute-start.4) | collective-permute-done | bytes 1179680 | tf_op jit(solution)/shard_map/ppermute | solution.py:494
  85.7 18.2 %queries_own_frame.2 = (bf16[768,768]{1,0:T(8,128)(2,1)S(1)}, f32[768,768]{1,0:T(8,128)S(1)}, f32[768,768]{1,0:T(8,128)S(1)}, f32[768,768]{1,0:T(8,128)S(1)}) custom-call(f32[2,128]{1,0:T(2,128)S(1)} %pad_maximum_fusion.3.refs_3_.gain_ref, bf16[768,3072]{1,0:T(8,128)(2,1)S(1)} %get-tuple-element.49.normed_ref, ...), custom_call_target="tpu_custom_call" | custom-call | flops 7247757 | bytes 20054 | tf_op jit(solution)/shard_map/queries_own_frame/pallas_call | solution.py:289
  108.5 3.4 collective-permute-done.9.refs_8_.refs_11_
  111.9 6.9 %earlier_frame.2 = bf16[768,768]{1,0:T(8,128)(2,1)S(1)} custom-call(s32[3]{0:T(128)S(1)} %copy-done.6, bf16[768,768]{1,0:T(8,128)(2,1)S(1)} %get-tuple-element.55.refs_1_, f32[768,768]{1,0:T(8,128)S(1)} %get-tuple-element.56.refs_2_, f32[768,768]{1,0:T(8,128)S(1)} %get-tuple-element.57.refs_3_, f32[768,768]{1,0:T(8,128)S(1)} %get-tuple-element.58.refs_4_, ...), custom_call_target="tpu_custom_call" | custom-call | flops 3623878 | bytes 12976 | tf_op jit(solution)/shard_map/earlier_frame/pallas_call | solution.py:350
  120.9 11.8 %collective-permute-done.11 = bf16[384,1536]{1,0:T(8,128)(2,1)S(1)} collective-permute-done((bf16[384,1536]{1,0:T(8,128)(2,1)S(1)}, bf16[384,1536]{1,0:T(8,128)(2,1)S(1)}, u32[]{:S(2)}, u32[]{:S(2)}) %collective-permute-start.11) | collective-permute-done | bytes 1179680 | tf_op jit(solution)/shard_map/ppermute | solution.py:494
  134.5 3.7 %collective-permute-done.10.refs_1_ = bf16[768,768]{1,0:T(8,128)(2,1)S(1)} collective-permute-done((bf16[768,768]{1,0:T(8,128)(2,1)S(1)}, bf16[768,768]{1,0:T(8,128)(2,1)S(1)}, u32[]{:S(2)}, u32[]{:S(2)}) %collective-permute-start.10) | collective-permute-done | bytes 1179680 | tf_op jit(solution)/shard_map/ppermute | solution.py:494
  138.2 2.4 collective-permute-start.13
  140.6 2.4 collective-permute-start.14
  146.0 17.7 %collective-permute-done.13.refs_2_ = bf16[768,768]{1,0:T(8,128)(2,1)S(1)} collective-permute-done((bf16[768,768]{1,0:T(8,128)(2,1)S(1)}, bf16[768,768]{1,0:T(8,128)(2,1)S(1)}, u32[]{:S(2)}, u32[]{:S(2)}) %collective-permute-start.13) | collective-permute-done | bytes 1179680 | tf_op jit(solution)/shard_map/ppermute | solution.py:494
  163.8 2.2 collective-permute-done.14.refs_3_
  168.5 2.1 collective-permute-start.20
  171.5 2.4 collective-permute-start.16
  174.7 3.4 collective-permute-start.17
  184.2 16.0 %projection_start.2.refs_1_ = bf16[768,3072]{1,0:T(8,128)(2,1)S(1)} custom-call(s32[1]{0:T(128)} %bitcast.refs_0_, bf16[768,768]{1,0:T(8,128)(2,1)S(1)} %copy-done.3, bf16[768,768]{1,0:T(8,128)(2,1)S(1)} %collective-permute-done.13.refs_2_, bf16[768,768]{1,0:T(8,128)(2,1)S(1)} %copy-done.1, bf16[768,3072]{1,0:T(8,128)(2,1)} %refs_7_.1, ...), custom_call_target="tpu_custom_call" | custom-call | flops 10871635 | bytes 18874 | tf_op jit(solution)/shard_map/projection_start/pallas_call | solution.py:457
  201.7 9.9 %projection_end.2.refs_5_ = bf16[768,3072]{1,0:T(8,128)(2,1)} custom-call(s32[1]{0:T(128)} %bitcast.refs_0_, bf16[768,3072]{1,0:T(8,128)(2,1)S(1)} %projection_start.2.refs_1_, bf16[768,3072]{1,0:T(8,128)(2,1)} %collective-permute-done.15.refs_2_, f32[1,3072]{1,0:T(1,128)S(1)} %fusion.refs_3_, bf16[384,768]{1,0:T(8,128)(2,1)} %collective-permute-done.16.refs_4_, ...), custom_call_target="tpu_custom_call" | custom-call | flops 3623878 | bytes 18874 | tf_op jit(solution)/shard_map/projection_end/pallas_call | solution.py:457
  211.6 14.2 %norm_keys.3 = (bf16[768,768]{1,0:T(8,128)(2,1)S(1)}, bf16[768,3072]{1,0:T(8,128)(2,1)S(1)}, bf16[768,3072]{1,0:T(8,128)(2,1)}) custom-call(s32[3]{0:T(128)S(1)} %copy-done.7, f32[1,3072]{1,0:T(1,128)S(1)} %copy-done.5, f32[1,3072]{1,0:T(1,128)S(1)} %get-tuple-element.85.refs_2_, f32[2,128]{1,0:T(2,128)S(1)} %pad_maximum_fusion.3.refs_3_.gain_ref, ...), custom_call_target="tpu_custom_call" | custom-call | flops 3623878 | bytes 20054 | tf_op jit(solution)/shard_map/norm_keys/pallas_call | solution.py:146
  227.8 6.8 %values.3.value_ref = bf16[768,768]{1,0:T(8,128)(2,1)S(1)} custom-call(bf16[768,3072]{1,0:T(8,128)(2,1)S(1)} %get-tuple-element.73.normed_ref, bf16[3,3072,768]{2,1,0:T(8,128)(2,1)} %w_any.7), custom_call_target="tpu_custom_call" | custom-call | flops 3623878 | bytes 10616 | tf_op jit(solution)/shard_map/values/pallas_call | solution.py:210
  234.5 2.3 collective-permute-start.22
  236.8 8.3 %collective-permute-done.21.refs_5_ = bf16[768,768]{1,0:T(8,128)(2,1)S(1)} collective-permute-done((bf16[768,768]{1,0:T(8,128)(2,1)S(1)}, bf16[768,768]{1,0:T(8,128)(2,1)S(1)}, u32[]{:S(2)}, u32[]{:S(2)}) %collective-permute-start.21) | collective-permute-done | bytes 1179680 | tf_op jit(solution)/shard_map/ppermute | solution.py:494
  245.1 18.2 %queries_own_frame.3 = (bf16[768,768]{1,0:T(8,128)(2,1)S(1)}, f32[768,768]{1,0:T(8,128)S(1)}, f32[768,768]{1,0:T(8,128)S(1)}, f32[768,768]{1,0:T(8,128)S(1)}) custom-call(f32[2,128]{1,0:T(2,128)S(1)} %pad_maximum_fusion.3.refs_3_.gain_ref, bf16[768,3072]{1,0:T(8,128)(2,1)S(1)} %get-tuple-element.73.normed_ref, ...), custom_call_target="tpu_custom_call" | custom-call | flops 7247757 | bytes 20054 | tf_op jit(solution)/shard_map/queries_own_frame/pallas_call | solution.py:289
  263.4 6.9 %earlier_frame.3 = (bf16[384,768]{1,0:T(8,128)(2,1)S(1)}, bf16[384,768]{1,0:T(8,128)(2,1)S(1)}) custom-call(s32[3]{0:T(128)S(1)} %copy-done.7, bf16[768,768]{1,0:T(8,128)(2,1)S(1)} %get-tuple-element.74.refs_1_, f32[768,768]{1,0:T(8,128)S(1)} %get-tuple-element.75.refs_2_, f32[768,768]{1,0:T(8,128)S(1)} %get-tuple-element.76.refs_3_, ...), custom_call_target="tpu_custom_call" | custom-call | flops 3623878 | bytes 12976 | tf_op jit(solution)/shard_map/earlier_frame/pallas_call | solution.py:350
  270.4 11.0 %collective-permute-done.23.refs_1_ = bf16[384,768]{1,0:T(8,128)(2,1)S(1)} collective-permute-done((bf16[384,768]{1,0:T(8,128)(2,1)S(1)}, bf16[384,768]{1,0:T(8,128)(2,1)S(1)}, u32[]{:S(2)}, u32[]{:S(2)}) %collective-permute-start.23) | collective-permute-done | bytes 589856 | tf_op jit(solution)/shard_map/ppermute | solution.py:494
  281.4 6.3 %collective-permute-done.24.refs_2_ = bf16[384,768]{1,0:T(8,128)(2,1)S(1)} collective-permute-done((bf16[384,768]{1,0:T(8,128)(2,1)S(1)}, bf16[384,768]{1,0:T(8,128)(2,1)S(1)}, u32[]{:S(2)}, u32[]{:S(2)}) %collective-permute-start.24) | collective-permute-done | bytes 589856 | tf_op jit(solution)/shard_map/ppermute | solution.py:494
  291.9 12.2 %collective-permute-done.25.refs_3_ = bf16[384,768]{1,0:T(8,128)(2,1)S(1)} collective-permute-done((bf16[384,768]{1,0:T(8,128)(2,1)S(1)}, bf16[384,768]{1,0:T(8,128)(2,1)S(1)}, u32[]{:S(2)}, u32[]{:S(2)}) %collective-permute-start.25) | collective-permute-done | bytes 589856 | tf_op jit(solution)/shard_map/ppermute | solution.py:494
  307.3 9.4 %collective-permute-done.26.refs_4_ = bf16[384,768]{1,0:T(8,128)(2,1)S(1)} collective-permute-done((bf16[384,768]{1,0:T(8,128)(2,1)S(1)}, bf16[384,768]{1,0:T(8,128)(2,1)S(1)}, u32[]{:S(2)}, u32[]{:S(2)}) %collective-permute-start.26) | collective-permute-done | bytes 589856 | tf_op jit(solution)/shard_map/ppermute | solution.py:494
  319.2 16.0 %projection_start.3.refs_1_ = bf16[768,3072]{1,0:T(8,128)(2,1)S(1)} custom-call(s32[1]{0:T(128)} %bitcast.refs_0_, bf16[384,768]{1,0:T(8,128)(2,1)S(1)} %collective-permute-done.23.refs_1_, bf16[384,768]{1,0:T(8,128)(2,1)S(1)} %collective-permute-done.24.refs_2_, bf16[384,768]{1,0:T(8,128)(2,1)S(1)} %collective-permute-done.25.refs_3_, ...), custom_call_target="tpu_custom_call" | custom-call | flops 10871635 | bytes 18874 | tf_op jit(solution)/shard_map/projection_start/pallas_call | solution.py:457
  335.3 7.8 %collective-permute-done.29.refs_2_ = bf16[768,3072]{1,0:T(8,128)(2,1)S(1)} collective-permute-done((bf16[768,3072]{1,0:T(8,128)(2,1)S(1)}, bf16[768,3072]{1,0:T(8,128)(2,1)S(1)}, u32[]{:S(2)}, u32[]{:S(2)}) %collective-permute-start.29) | collective-permute-done | bytes 4718624 | tf_op jit(solution)/shard_map/ppermute | solution.py:494
  343.1 8.5 %projection_end.3 = bf16[768,3072]{1,0:T(8,128)(2,1)} custom-call(s32[1]{0:T(128)} %bitcast.refs_0_, bf16[768,3072]{1,0:T(8,128)(2,1)S(1)} %projection_start.3.refs_1_, bf16[768,3072]{1,0:T(8,128)(2,1)S(1)} %collective-permute-done.29.refs_2_, f32[1,3072]{1,0:T(1,128)S(1)} %fusion.refs_3_, bf16[192,768]{1,0:T(8,128)(2,1)S(1)} %collective-permute-done.30.refs_4_, ...), custom_call_target="tpu_custom_call" | custom-call | flops 3623878 | bytes 18874 | tf_op jit(solution)/shard_map/projection_end/pallas_call | solution.py:457
  (103 shorter events, 51.1 us)
Async XLA Ops:
  1.8 18.8 %collective-permute-start.2 = (bf16[192,3072]{1,0:T(8,128)(2,1)S(1)}, bf16[192,3072]{1,0:T(8,128)(2,1)}, u32[]{:S(2)}, u32[]{:S(2)}) collective-permute-start(bf16[192,3072]{1,0:T(8,128)(2,1)S(1)} %get-tuple-element.84.refs_6_), channel_id=1, source_target_pairs={{28,30},{29,31},{30,28},{31,29}} | collective-permute-start | bytes 3538952 | tf_op jit(solution)/shard_map/ppermute | solution.py:494
  3.5 17.1 %collective-permute-start.3 = (bf16[192,3072]{1,0:T(8,128)(2,1)S(1)}, bf16[192,3072]{1,0:T(8,128)(2,1)}, u32[]{:S(2)}, u32[]{:S(2)}) collective-permute-start(bf16[192,3072]{1,0:T(8,128)(2,1)S(1)} %get-tuple-element.84.refs_6_), channel_id=1, source_target_pairs={{28,31},{29,30},{30,29},{31,28}} | collective-permute-start | bytes 3538952 | tf_op jit(solution)/shard_map/ppermute | solution.py:494
  5.2 17.3 %collective-permute-start.1 = (bf16[192,3072]{1,0:T(8,128)(2,1)S(1)}, bf16[192,3072]{1,0:T(8,128)(2,1)S(1)}, u32[]{:S(2)}, u32[]{:S(2)}) collective-permute-start(bf16[192,3072]{1,0:T(8,128)(2,1)S(1)} %get-tuple-element.84.refs_6_), channel_id=1, source_target_pairs={{28,29},{29,28},{30,31},{31,30}} | collective-permute-start | bytes 3538952 | tf_op jit(solution)/shard_map/ppermute | solution.py:494
  6.0 12.7 %collective-permute-start = (s32[1]{0:T(128)}, s32[1]{0:T(128)}, u32[]{:S(2)}, u32[]{:S(2)}) collective-permute-start(s32[1]{0:T(128)} %param.10), channel_id=1, source_target_pairs={{0,28},{1,29},{2,30},{3,31},{4,0},{5,1},{6,2},{7,3},{8,4},{9,5},{1... | collective-permute-start | bytes 20 | tf_op jit(solution)/shard_map/ppermute | solution.py:494
  22.9 81.0 %collective-permute-start.5 = (bf16[768,1536]{1,0:T(8,128)(2,1)S(1)}, bf16[768,1536]{1,0:T(8,128)(2,1)S(1)}, u32[]{:S(2)}, u32[]{:S(2)}) collective-permute-start(bf16[768,1536]{1,0:T(8,128)(2,1)S(1)} %copy-done.12), channel_id=1, source_target_pairs={{0,1},{1,0},{2,3},{3,2},{4,5},{5,4},{6,7},{7,6},{8,9},{9,8},{10,11... | collective-permute-start | bytes 7077896 | tf_op jit(solution)/shard_map/ppermute | solution.py:494
  24.4 79.5 %collective-permute-start.6 = (bf16[768,1536]{1,0:T(8,128)(2,1)S(1)}, bf16[768,1536]{1,0:T(8,128)(2,1)S(1)}, u32[]{:S(2)}, u32[]{:S(2)}) collective-permute-start(bf16[768,1536]{1,0:T(8,128)(2,1)S(1)} %copy-done.12), channel_id=1, source_target_pairs={{0,2},{1,3},{2,0},{3,1},{4,6},{5,7},{6,4},{7,5},{8,10},{9,11},{10,... | collective-permute-start | bytes 7077896 | tf_op jit(solution)/shard_map/ppermute | solution.py:494
  41.2 44.5 %collective-permute-start.4 = (bf16[768,768]{1,0:T(8,128)(2,1)S(1)}, bf16[768,768]{1,0:T(8,128)(2,1)S(1)}, u32[]{:S(2)}, u32[]{:S(2)}) collective-permute-start(bf16[768,768]{1,0:T(8,128)(2,1)S(1)} %get-tuple-element.48.key_ref), channel_id=1, source_target_pairs={{0,4},{1,5},{2,6},{3,7},{4,8},{5,9},{6,10},{7,11},{8,12},{9,13},{1... | collective-permute-start | bytes 3538952 | tf_op jit(solution)/shard_map/ppermute | solution.py:494
  49.7 54.1 %collective-permute-start.7 = (bf16[768,768]{1,0:T(8,128)(2,1)S(1)}, bf16[768,768]{1,0:T(8,128)(2,1)S(1)}, u32[]{:S(2)}, u32[]{:S(2)}) collective-permute-start(bf16[768,768]{1,0:T(8,128)(2,1)S(1)} %values.2.value_ref), channel_id=1, source_target_pairs={{0,4},{1,5},{2,6},{3,7},{4,8},{5,9},{6,10},{7,11},{8,12},{9,13},{1... | collective-permute-start | bytes 3538952 | tf_op jit(solution)/shard_map/ppermute | solution.py:494
  104.0 7.9 %collective-permute-start.9 = (bf16[768,1536]{1,0:T(8,128)(2,1)S(1)}, bf16[768,1536]{1,0:T(8,128)(2,1)S(1)}, u32[]{:S(2)}, u32[]{:S(2)}) collective-permute-start(bf16[768,1536]{1,0:T(8,128)(2,1)S(1)} %collective-permute-done.6.refs_6_.refs_9_), channel_id=1, source_target_pairs={{0,4},{1,5},{2,6},{3,7},{4,0},{5,1},{6,2},{7,3},{8,12},{9,13},{10,... | collective-permute-start | bytes 7077896 | tf_op jit(solution)/shard_map/ppermute | solution.py:494
  106.0 26.7 %collective-permute-start.11 = (bf16[384,1536]{1,0:T(8,128)(2,1)S(1)}, bf16[384,1536]{1,0:T(8,128)(2,1)S(1)}, u32[]{:S(2)}, u32[]{:S(2)}) collective-permute-start(bf16[384,1536]{1,0:T(8,128)(2,1)S(1)} %slice.45), channel_id=1, source_target_pairs={{0,2},{1,3},{2,0},{3,1},{4,6},{5,7},{6,4},{7,5},{8,10},{9,11},{10,... | collective-permute-start | bytes 3538952 | tf_op jit(solution)/shard_map/ppermute | solution.py:494
  106.5 26.4 %collective-permute-start.12 = (bf16[384,1536]{1,0:T(8,128)(2,1)S(1)}, bf16[384,1536]{1,0:T(8,128)(2,1)S(1)}, u32[]{:S(2)}, u32[]{:S(2)}) collective-permute-start(bf16[384,1536]{1,0:T(8,128)(2,1)S(1)} %slice.46), channel_id=1, source_target_pairs={{0,1},{1,0},{2,3},{3,2},{4,5},{5,4},{6,7},{7,6},{8,9},{9,8},{10,11... | collective-permute-start | bytes 3538952 | tf_op jit(solution)/shard_map/ppermute | solution.py:494
  118.8 19.3 %collective-permute-start.10 = (bf16[768,768]{1,0:T(8,128)(2,1)S(1)}, bf16[768,768]{1,0:T(8,128)(2,1)S(1)}, u32[]{:S(2)}, u32[]{:S(2)}) collective-permute-start(bf16[768,768]{1,0:T(8,128)(2,1)S(1)} %earlier_frame.2), channel_id=1, source_target_pairs={{0,4},{1,5},{2,6},{3,7},{4,8},{5,9},{6,10},{7,11},{8,12},{9,13},{1... | collective-permute-start | bytes 3538952 | tf_op jit(solution)/shard_map/ppermute | solution.py:494
  138.2 25.6 %collective-permute-start.13 = (bf16[768,768]{1,0:T(8,128)(2,1)S(1)}, bf16[768,768]{1,0:T(8,128)(2,1)S(1)}, u32[]{:S(2)}, u32[]{:S(2)}) collective-permute-start(bf16[768,768]{1,0:T(8,128)(2,1)S(1)} %collective-permute-done.10.refs_1_), channel_id=1, source_target_pairs={{0,1},{1,0},{2,3},{3,2},{4,5},{5,4},{6,7},{7,6},{8,9},{9,8},{10,11... | collective-permute-start | bytes 3538952 | tf_op jit(solution)/shard_map/ppermute | solution.py:494
  140.6 25.4 %collective-permute-start.14 = (bf16[768,768]{1,0:T(8,128)(2,1)S(1)}, bf16[768,768]{1,0:T(8,128)(2,1)S(1)}, u32[]{:S(2)}, u32[]{:S(2)}) collective-permute-start(bf16[768,768]{1,0:T(8,128)(2,1)S(1)} %collective-permute-done.10.refs_1_), channel_id=1, source_target_pairs={{0,2},{1,3},{2,0},{3,1},{4,6},{5,7},{6,4},{7,5},{8,10},{9,11},{10,... | collective-permute-start | bytes 3538952 | tf_op jit(solution)/shard_map/ppermute | solution.py:494
  144.1 57.5 %collective-permute-start.15 = (bf16[768,3072]{1,0:T(8,128)(2,1)}, bf16[768,3072]{1,0:T(8,128)(2,1)}, u32[]{:S(2)}, u32[]{:S(2)}) collective-permute-start(bf16[768,3072]{1,0:T(8,128)(2,1)} %get-tuple-element.68), channel_id=1, source_target_pairs={{0,4},{1,5},{2,6},{3,7},{4,8},{5,9},{6,10},{7,11},{8,12},{9,13},{1... | collective-permute-start | bytes 14155784 | tf_op jit(solution)/shard_map/ppermute | solution.py:494
  166.9 33.4 %collective-permute-start.18 = (bf16[768,1536]{1,0:T(8,128)(2,1)}, bf16[768,1536]{1,0:T(8,128)(2,1)}, u32[]{:S(2)}, u32[]{:S(2)}) collective-permute-start(bf16[768,1536]{1,0:T(8,128)(2,1)} %pad_maximum_fusion.1.refs_6_.refs_8_), channel_id=1, source_target_pairs={{0,4},{1,5},{2,6},{3,7},{4,0},{5,1},{6,2},{7,3},{8,12},{9,13},{10,... | collective-permute-start | bytes 7077896 | tf_op jit(solution)/shard_map/ppermute | solution.py:494
  168.5 43.0 %collective-permute-start.20 = (bf16[384,3072]{1,0:T(8,128)(2,1)}, bf16[384,3072]{1,0:T(8,128)(2,1)}, u32[]{:S(2)}, u32[]{:S(2)}) collective-permute-start(bf16[384,3072]{1,0:T(8,128)(2,1)} %pad_maximum_fusion.2), channel_id=1, source_target_pairs={{28,30},{29,31},{30,28},{31,29}} | collective-permute-start | bytes 7077896 | tf_op jit(solution)/shard_map/ppermute | solution.py:494
  171.5 28.8 %collective-permute-start.16 = (bf16[384,768]{1,0:T(8,128)(2,1)}, bf16[384,768]{1,0:T(8,128)(2,1)}, u32[]{:S(2)}, u32[]{:S(2)}) collective-permute-start(bf16[384,768]{1,0:T(8,128)(2,1)} %slice.50), channel_id=1, source_target_pairs={{0,2},{1,3},{2,0},{3,1},{4,6},{5,7},{6,4},{7,5},{8,10},{9,11},{10,... | collective-permute-start | bytes 1769480 | tf_op jit(solution)/shard_map/ppermute | solution.py:494
  174.7 25.5 %collective-permute-start.17 = (bf16[384,768]{1,0:T(8,128)(2,1)}, bf16[384,768]{1,0:T(8,128)(2,1)}, u32[]{:S(2)}, u32[]{:S(2)}) collective-permute-start(bf16[384,768]{1,0:T(8,128)(2,1)} %slice.51), channel_id=1, source_target_pairs={{0,1},{1,0},{2,3},{3,2},{4,5},{5,4},{6,7},{7,6},{8,9},{9,8},{10,11... | collective-permute-start | bytes 1769480 | tf_op jit(solution)/shard_map/ppermute | solution.py:494
  225.8 19.3 %collective-permute-start.21 = (bf16[768,768]{1,0:T(8,128)(2,1)S(1)}, bf16[768,768]{1,0:T(8,128)(2,1)S(1)}, u32[]{:S(2)}, u32[]{:S(2)}) collective-permute-start(bf16[768,768]{1,0:T(8,128)(2,1)S(1)} %get-tuple-element.72.key_ref), channel_id=1, source_target_pairs={{0,4},{1,5},{2,6},{3,7},{4,8},{5,9},{6,10},{7,11},{8,12},{9,13},{1... | collective-permute-start | bytes 3538952 | tf_op jit(solution)/shard_map/ppermute | solution.py:494
  234.5 28.8 %collective-permute-start.22 = (bf16[768,768]{1,0:T(8,128)(2,1)S(1)}, bf16[768,768]{1,0:T(8,128)(2,1)S(1)}, u32[]{:S(2)}, u32[]{:S(2)}) collective-permute-start(bf16[768,768]{1,0:T(8,128)(2,1)S(1)} %values.3.value_ref), channel_id=1, source_target_pairs={{0,4},{1,5},{2,6},{3,7},{4,8},{5,9},{6,10},{7,11},{8,12},{9,13},{1... | collective-permute-start | bytes 3538952 | tf_op jit(solution)/shard_map/ppermute | solution.py:494
  270.3 11.2 %collective-permute-start.23 = (bf16[384,768]{1,0:T(8,128)(2,1)S(1)}, bf16[384,768]{1,0:T(8,128)(2,1)S(1)}, u32[]{:S(2)}, u32[]{:S(2)}) collective-permute-start(bf16[384,768]{1,0:T(8,128)(2,1)S(1)} %get-tuple-element.79), channel_id=1, source_target_pairs={{0,4},{1,5},{2,6},{3,7},{4,8},{5,9},{6,10},{7,11},{8,12},{9,13},{1... | collective-permute-start | bytes 1769480 | tf_op jit(solution)/shard_map/ppermute | solution.py:494
  270.3 17.4 %collective-permute-start.24 = (bf16[384,768]{1,0:T(8,128)(2,1)S(1)}, bf16[384,768]{1,0:T(8,128)(2,1)S(1)}, u32[]{:S(2)}, u32[]{:S(2)}) collective-permute-start(bf16[384,768]{1,0:T(8,128)(2,1)S(1)} %get-tuple-element.80), channel_id=1, source_target_pairs={{0,4},{1,5},{2,6},{3,7},{4,8},{5,9},{6,10},{7,11},{8,12},{9,13},{1... | collective-permute-start | bytes 1769480 | tf_op jit(solution)/shard_map/ppermute | solution.py:494
  287.8 55.3 %collective-permute-start.29 = (bf16[768,3072]{1,0:T(8,128)(2,1)S(1)}, bf16[768,3072]{1,0:T(8,128)(2,1)S(1)}, u32[]{:S(2)}, u32[]{:S(2)}) collective-permute-start(bf16[768,3072]{1,0:T(8,128)(2,1)S(1)} %bitcast.22), channel_id=1, source_target_pairs={{0,4},{1,5},{2,6},{3,7},{4,8},{5,9},{6,10},{7,11},{8,12},{9,13},{1... | collective-permute-start | bytes 14155784 | tf_op jit(solution)/shard_map/ppermute | solution.py:494
  287.8 16.3 %collective-permute-start.25 = (bf16[384,768]{1,0:T(8,128)(2,1)S(1)}, bf16[384,768]{1,0:T(8,128)(2,1)S(1)}, u32[]{:S(2)}, u32[]{:S(2)}) collective-permute-start(bf16[384,768]{1,0:T(8,128)(2,1)S(1)} %collective-permute-done.23.refs_1_), channel_id=1, source_target_pairs={{0,1},{1,0},{2,3},{3,2},{4,5},{5,4},{6,7},{7,6},{8,9},{9,8},{10,11... | collective-permute-start | bytes 1769480 | tf_op jit(solution)/shard_map/ppermute | solution.py:494
  289.3 16.4 %collective-permute-start.27 = (bf16[384,768]{1,0:T(8,128)(2,1)S(1)}, bf16[384,768]{1,0:T(8,128)(2,1)S(1)}, u32[]{:S(2)}, u32[]{:S(2)}) collective-permute-start(bf16[384,768]{1,0:T(8,128)(2,1)S(1)} %collective-permute-done.23.refs_1_), channel_id=1, source_target_pairs={{0,2},{1,3},{2,0},{3,1},{4,6},{5,7},{6,4},{7,5},{8,10},{9,11},{10,... | collective-permute-start | bytes 1769480 | tf_op jit(solution)/shard_map/ppermute | solution.py:494
  290.8 25.9 %collective-permute-start.26 = (bf16[384,768]{1,0:T(8,128)(2,1)S(1)}, bf16[384,768]{1,0:T(8,128)(2,1)S(1)}, u32[]{:S(2)}, u32[]{:S(2)}) collective-permute-start(bf16[384,768]{1,0:T(8,128)(2,1)S(1)} %collective-permute-done.24.refs_2_), channel_id=1, source_target_pairs={{0,1},{1,0},{2,3},{3,2},{4,5},{5,4},{6,7},{7,6},{8,9},{9,8},{10,11... | collective-permute-start | bytes 1769480 | tf_op jit(solution)/shard_map/ppermute | solution.py:494
  291.4 27.0 %collective-permute-start.28 = (bf16[384,768]{1,0:T(8,128)(2,1)S(1)}, bf16[384,768]{1,0:T(8,128)(2,1)S(1)}, u32[]{:S(2)}, u32[]{:S(2)}) collective-permute-start(bf16[384,768]{1,0:T(8,128)(2,1)S(1)} %collective-permute-done.24.refs_2_), channel_id=1, source_target_pairs={{0,2},{1,3},{2,0},{3,1},{4,6},{5,7},{6,4},{7,5},{8,10},{9,11},{10,... | collective-permute-start | bytes 1769480 | tf_op jit(solution)/shard_map/ppermute | solution.py:494
  304.1 31.1 %collective-permute-start.30 = (bf16[192,768]{1,0:T(8,128)(2,1)S(1)}, bf16[192,768]{1,0:T(8,128)(2,1)S(1)}, u32[]{:S(2)}, u32[]{:S(2)}) collective-permute-start(bf16[192,768]{1,0:T(8,128)(2,1)S(1)} %slice.58), channel_id=1, source_target_pairs={{0,2},{1,3},{2,0},{3,1},{4,6},{5,7},{6,4},{7,5},{8,10},{9,11},{10,... | collective-permute-start | bytes 884744 | tf_op jit(solution)/shard_map/ppermute | solution.py:494
  305.7 29.5 %collective-permute-start.31 = (bf16[192,768]{1,0:T(8,128)(2,1)S(1)}, bf16[192,768]{1,0:T(8,128)(2,1)S(1)}, u32[]{:S(2)}, u32[]{:S(2)}) collective-permute-start(bf16[192,768]{1,0:T(8,128)(2,1)S(1)} %slice.59), channel_id=1, source_target_pairs={{0,1},{1,0},{2,3},{3,2},{4,5},{5,4},{6,7},{7,6},{8,9},{9,8},{10,11... | collective-permute-start | bytes 884744 | tf_op jit(solution)/shard_map/ppermute | solution.py:494
  316.8 18.5 %collective-permute-start.32 = (bf16[192,768]{1,0:T(8,128)(2,1)S(1)}, bf16[192,768]{1,0:T(8,128)(2,1)S(1)}, u32[]{:S(2)}, u32[]{:S(2)}) collective-permute-start(bf16[192,768]{1,0:T(8,128)(2,1)S(1)} %slice.60), channel_id=1, source_target_pairs={{0,2},{1,3},{2,0},{3,1},{4,6},{5,7},{6,4},{7,5},{8,10},{9,11},{10,... | collective-permute-start | bytes 884744 | tf_op jit(solution)/shard_map/ppermute | solution.py:494
  318.4 16.9 %collective-permute-start.33 = (bf16[192,768]{1,0:T(8,128)(2,1)S(1)}, bf16[192,768]{1,0:T(8,128)(2,1)S(1)}, u32[]{:S(2)}, u32[]{:S(2)}) collective-permute-start(bf16[192,768]{1,0:T(8,128)(2,1)S(1)} %slice.61), channel_id=1, source_target_pairs={{0,1},{1,0},{2,3},{3,2},{4,5},{5,4},{6,7},{7,6},{8,9},{9,8},{10,11... | collective-permute-start | bytes 884744 | tf_op jit(solution)/shard_map/ppermute | solution.py:494
  (19 other events, 220.7 us)

commit v8 on v7

--- a/solution.py
+++ b/solution.py
@@ -44,6 +44,11 @@
     return heads[0] if len(heads) == 1 else jnp.concatenate(heads, axis=1)
 
 
+def over_lanes(values, fold, reduce):
+    parts = [values[:, i : i + HD] for i in range(0, values.shape[1], HD)]
+    return reduce(functools.reduce(fold, parts), axis=-1, keepdims=True)
+
+
 def tile_cols(head_cols):
     return 256 if head_cols % 256 == 0 else HD
 
@@ -56,14 +61,22 @@
         yield pltpu.make_async_copy(w_any.at[part, at], w_ref.at[at], w_sems.at[i])
 
 
-def key_kernel(*refs, half):
+def key_value_kernel(*refs, half):
     info_ref, scale_ref, shift_ref, gain_ref, w_any, z_any, noise_any, near_any = refs[:8]
     pair_refs = refs[8 : 7 + half]
-    key_ref, normed_any, state_any = refs[7 + half : 10 + half]
-    state_ref, normed_ref, inverse_ref, w_ref, sem, out_sems, w_sems = refs[10 + half :]
+    key_ref, value_ref, normed_any, state_any = refs[7 + half : 11 + half]
+    state_ref, normed_ref, inverse_ref, w_ref, sem, out_sems, w_sems = refs[11 + half :]
     step = pl.program_id(0)
     rows = state_ref.shape[0]
     piece_rows = noise_any.shape[0]
+
+    def weights_of(part):
+        return weight_copies(w_any, part + 1, w_ref.at[part], w_sems.at[part])
+
+    def start_weights():
+        for part in range(2):
+            for weight_copy in weights_of(part):
+                weight_copy.start()
 
     def piece_at(j, f):
         if j > 0:
@@ -71,6 +84,7 @@
         return (noise_any, near_any)[f], 0
 
     cols = key_ref.shape[1]
+    blocks = pl.num_programs(0) // 2
     state_copy = pltpu.make_async_copy(state_ref, state_any, out_sems.at[0])
     normed_copy = pltpu.make_async_copy(normed_ref, normed_any, out_sems.at[1])
 
@@ -80,14 +94,12 @@
         def _():
             copy = pltpu.make_async_copy(z_any, state_ref, sem.at[0])
             copy.start()
-            for weight_copy in weight_copies(w_any, 1, w_ref, w_sems):
-                weight_copy.start()
+            start_weights()
             copy.wait()
 
         @pl.when(info_ref[0] != 0)
         def _():
-            for weight_copy in weight_copies(w_any, 1, w_ref, w_sems):
-                weight_copy.start()
+            start_weights()
             for block in range(2 * half):
                 high, low = block // 2, block % 2
                 steps = lax.rem(high + half - info_ref[1], half)
@@ -111,7 +123,7 @@
         def measure(i, carry):
             at = pl.ds(pl.multiple_of(i * 16, 16), 16)
             state = state_ref[at, :].astype(F32)
-            mean = jnp.mean(state * state, axis=-1, keepdims=True)
+            mean = over_lanes(state * state, jnp.add, jnp.sum) * (1.0 / state.shape[1])
             inverse_ref[at, :] = jnp.broadcast_to(lax.rsqrt(mean + EPS), (16, HD))
             return carry
 
@@ -125,12 +137,25 @@
         lax.fori_loop(0, rows // 16, measure, 0, unroll=4)
         lax.fori_loop(0, rows // 16, apply, 0, unroll=2)
         normed_copy.start()
-        for copy in weight_copies(w_any, 1, w_ref, w_sems):
-            copy.wait()
-
-    at = pl.ds(pl.multiple_of(step * cols, HD), cols)
-    product = jnp.dot(normed_ref[...], w_ref[:, at], preferred_element_type=F32)
-    key_ref[...] = head_normalized(product, gain_ref[1:2])
+
+    for part in range(2):
+
+        @pl.when(step == part * blocks)
+        def _():
+            for copy in weights_of(part):
+                copy.wait()
+
+    at = pl.ds(pl.multiple_of(lax.rem(step, blocks) * cols, HD), cols)
+
+    @pl.when(step < blocks)
+    def _():
+        product = jnp.dot(normed_ref[...], w_ref[0, :, at], preferred_element_type=F32)
+        key_ref[...] = head_normalized(product, gain_ref[1:2])
+
+    @pl.when(step >= blocks)
+    def _():
+        product = jnp.dot(normed_ref[...], w_ref[1, :, at], preferred_element_type=F32)
+        value_ref[...] = product.astype(BF16)
 
     @pl.when(step == pl.num_programs(0) - 1)
     def _():
@@ -138,44 +163,51 @@
         normed_copy.wait()
 
 
-def project_keys(info, scale1, shift, gains, qkv_weight, z, noise, noise_pieces):
+def project_keys_values(info, scale1, shift, gains, qkv_weight, z, noise, noise_pieces):
     rows, width = z.shape
     head_cols = qkv_weight.shape[2]
     cols = tile_cols(head_cols)
     half = len(noise_pieces)
+    blocks = head_cols // cols
     return pl.pallas_call(
-        functools.partial(key_kernel, half=half),
+        functools.partial(key_value_kernel, half=half),
         grid_spec=pltpu.PrefetchScalarGridSpec(
             num_scalar_prefetch=1,
-            grid=(head_cols // cols,),
+            grid=(2 * blocks,),
             in_specs=[
                 pl.BlockSpec((1, width), lambda j, i: (0, 0)),
                 pl.BlockSpec((1, width), lambda j, i: (0, 0)),
                 pl.BlockSpec((2, HD), lambda j, i: (0, 0)),
             ]
             + [ANY] * (3 + half),
-            out_specs=[pl.BlockSpec((rows, cols), lambda j, i: (0, j)), ANY, ANY],
+            out_specs=[
+                pl.BlockSpec((rows, cols), lambda j, i: (0, jnp.minimum(j, blocks - 1))),
+                pl.BlockSpec((rows, cols), lambda j, i: (0, jnp.maximum(j - blocks, 0))),
+                ANY,
+                ANY,
+            ],
             scratch_shapes=[
                 pltpu.VMEM((rows, width), BF16),
                 pltpu.VMEM((rows, width), BF16),
                 pltpu.VMEM((rows, HD), F32),
-                pltpu.VMEM((width, head_cols), BF16),
+                pltpu.VMEM((2, width, head_cols), BF16),
                 pltpu.SemaphoreType.DMA((1,)),
                 pltpu.SemaphoreType.DMA((2,)),
-                pltpu.SemaphoreType.DMA((4,)),
+                pltpu.SemaphoreType.DMA((2, 4)),
             ],
         ),
         out_shape=[
+            jax.ShapeDtypeStruct((rows, head_cols), BF16),
             jax.ShapeDtypeStruct((rows, head_cols), BF16),
             jax.ShapeDtypeStruct((rows, width), BF16),
             pltpu.HBM((rows, width), BF16),
         ],
-        compiler_params=compiler_params(26),
+        compiler_params=compiler_params(32),
         cost_estimate=cost(
-            2 * rows * width * head_cols,
-            6 * rows * width + 2 * rows * head_cols + 2 * width * head_cols,
-        ),
-        name="norm_keys",
+            4 * rows * width * head_cols,
+            6 * rows * width + 4 * rows * head_cols + 4 * width * head_cols,
+        ),
+        name="norm_keys_values",
     )(
         info,
         scale1,
@@ -185,45 +217,6 @@
         noise,
         *noise_pieces,
     )
-
-
-def value_kernel(normed_ref, w_any, value_ref, w_ref, w_sems):
-    step = pl.program_id(0)
-    cols = value_ref.shape[1]
-
-    @pl.when(step == 0)
-    def _():
-        for copy in weight_copies(w_any, 2, w_ref, w_sems):
-            copy.start()
-        for copy in weight_copies(w_any, 2, w_ref, w_sems):
-            copy.wait()
-
-    at = pl.ds(pl.multiple_of(step * cols, HD), cols)
-    product = jnp.dot(normed_ref[...], w_ref[:, at], preferred_element_type=F32)
-    value_ref[...] = product.astype(BF16)
-
-
-def project_values(normed, qkv_weight):
-    rows, width = normed.shape
-    head_cols = qkv_weight.shape[2]
-    cols = tile_cols(head_cols)
-    return pl.pallas_call(
-        value_kernel,
-        grid=(head_cols // cols,),
-        in_specs=[pl.BlockSpec((rows, width), lambda j: (0, 0)), ANY],
-        out_specs=pl.BlockSpec((rows, cols), lambda j: (0, j)),
-        scratch_shapes=[
-            pltpu.VMEM((width, head_cols), BF16),
-            pltpu.SemaphoreType.DMA((4,)),
-        ],
-        out_shape=jax.ShapeDtypeStruct((rows, head_cols), BF16),
-        compiler_params=compiler_params(20),
-        cost_estimate=cost(
-            2 * rows * width * head_cols,
-            2 * rows * width + 2 * rows * head_cols + 2 * width * head_cols,
-        ),
-        name="values",
-    )(normed, in_hbm(qkv_weight))
 
 
 def attend(query, key):
@@ -272,7 +265,7 @@
     query_ref[...] = query
 
     def finish(scores, row, at):
-        top = jnp.max(scores, axis=-1, keepdims=True)
+        top = over_lanes(scores, jnp.maximum, jnp.max)
         acc, total = weigh(scores, top, value_ref[:, at])
         acc_ref[row, at] = acc
         total_ref[row, at] = total
@@ -334,7 +327,7 @@
     def _():
         def finish(scores, row, at):
             old_top = top_ref[row, at][:, :1]
-            top = jnp.maximum(jnp.max(scores, axis=-1, keepdims=True), old_top)
+            top = jnp.maximum(over_lanes(scores, jnp.maximum, jnp.max), old_top)
             acc, total = weigh(scores, top, value_ref[:, at])
             kept = jnp.exp2(old_top - top)
             acc = acc + acc_ref[row, at] * kept
@@ -558,8 +551,10 @@
     half_weight = lax.dynamic_slice(
         out_weight, (0, parity[0] * (width // 2)), (out_weight.shape[0], width // 2)
     )
-    half_weight, latents, noise_pieces = lax.optimization_barrier(
-        (half_weight, latents, noise_pieces)
+    word, noise_pieces = lax.optimization_barrier((levels, noise_pieces))
+    word = send(word, lambda q, t: (q - 1, t), *mesh_sizes, [queue_size - 1])
+    half_weight, latents, noise_pieces, word = lax.optimization_barrier(
+        (half_weight, latents, noise_pieces, word)
     )
     mine = one_hop(half_weight, *mesh_sizes)
 
@@ -570,41 +565,37 @@
 
     shift, scale1, _ = modulation(worked_level)
     _, _, gate = modulation(levels[0])
-    info = jnp.stack([is_last, tensor_index // 2, tensor_index % 2])
+    info = jnp.stack([is_last, tensor_index // 2, tensor_index % 2, word[0]])
     info = info.astype(jnp.int32)
     gains = jnp.stack([q_gain * SCORE_SCALE, k_gain])
 
     frame = latents[0]
     for step_index in range(STEPS):
         final = step_index == STEPS - 1
-        key, normed, state = project_keys(
+        key, value, normed, state = project_keys_values(
             info, scale1, shift, gains, qkv_weight, frame, noise, noise_pieces
         )
         to_next = [q for q in range(queue_size) if q != queue_size - 2]
-        earlier_key = ring(key, to_next)
-        value = project_values(normed, qkv_weight)
-        earlier_value = ring(value, to_next)
-        normed, earlier_key = lax.optimization_barrier((normed, earlier_key))
+        earlier = [ring(block, to_next) for block in (key, value)]
         query, *own = own_attention(gains, normed, qkv_weight, key, value)
         if not final:
-            query, mine, earlier_value = lax.optimization_barrier(
-                (query, mine, earlier_value)
-            )
+            query, mine = lax.optimization_barrier((query, mine))
             mine_corners = [
                 jnp.concatenate(parts, axis=0) for parts in two_hops(mine, *mesh_sizes)
             ]
+            mine, earlier = lax.optimization_barrier((mine, earlier))
             theirs = [sibling(block) for block in mine]
             query, theirs = lax.optimization_barrier((query, theirs))
         attended = earlier_attention(
-            info, query, *own, earlier_key, earlier_value, CHUNKS if final else 1
+            info, query, *own, *earlier, CHUNKS if final else 1
         )
         senders = range(queue_size) if final else to_next
         targets = range(queue_size if final else queue_size - 1)
         attended = [ring(block, senders) for block in attended]
+        sent_state, _ = lax.optimization_barrier((state, attended))
+        resid = ring(sent_state, senders)
         if not final:
             attended, mine_corners = lax.optimization_barrier((attended, mine_corners))
-        sent_state, _ = lax.optimization_barrier((state, attended))
-        resid = ring(sent_state, senders)
         near = [one_hop(block, *mesh_sizes, targets) for block in attended]
         if not final:
             noise, mine_corners, near = lax.optimization_barrier(

time: 353 us -> 339 us (0.960)
  waiting for transfers between devices: 131 us -> 116 us
  starting transfers between devices: 53 us -> 57.6 us
    ppermute x34 -> x35, waiting for transfers between devices: 131 us -> 116 us  [send(): return lax.ppermute(block, AXES, pairs)]
    ppermute x34 -> x35, starting transfers between devices: 53 us -> 57.6 us  [send(): return lax.ppermute(block, AXES, pairs)]
    pallas_call x4 -> x2, Pallas kernels: 41.9 us -> 40.9 us  [project_keys_values(): pl.pallas_call(functools.partial(key_value_kernel, half=half), grid_spec=...]
  transfers between devices with their start and end apart: 34 -> 35, of which waited for: 15 -> 17; matrix products, arithmetic and copies ran while one was open for 4% -> 4% of each run, Pallas kernels for 32% -> 31%
where the time goes in v8:
time: 339 us; the launch traced here: 338 us
  Pallas kernels  142 us (42%)
  waiting for transfers between devices  116 us (34%)
  starting transfers between devices  57.6 us (17%)
  local copies, waits for them, and re-layouts  11.9 us (4%)
  other arithmetic  8.18 us (2%)
    ppermute x35, waiting for transfers between devices, send(): return lax.ppermute(block, AXES, pairs)  116 us
    ppermute x35, starting transfers between devices, send(): return lax.ppermute(block, AXES, pairs)  57.6 us
    pallas_call x4, Pallas kernels, output_projection(): pl.pallas_call(functools.partial(output_kernel, part_counts=tuple((len(p)...  50.4 us
    pallas_call x2, Pallas kernels, project_keys_values(): pl.pallas_call(functools.partial(key_value_kernel, half=half), grid_spec=...  40.9 us
    pallas_call x2, Pallas kernels, own_attention(): pl.pallas_call(own_kernel, grid=(head_cols // cols,), in_specs=[pl.BlockS...  36.4 us
    pallas_call x2, Pallas kernels, earlier_attention(): pl.pallas_call(functools.partial(earlier_kernel, chunks=chunks), grid_spe...  13.9 us
  transfers between devices with their start and end apart: 35, of which 17 were waited for; matrix products, arithmetic and copies ran while one was open for 4% of the time, Pallas kernels for 31%

profile of v8, /device:TPU:0, one launch (start us, length us, event | category | flops | bytes accessed | tf_op | source)
XLA Modules:
  0.0 338.2 jit_solution(16574543488166547964)
XLA Ops:
  6.0 8.8 %collective-permute-start.4 = (s32[1]{0:T(128)}, s32[1]{0:T(128)}, u32[]{:S(2)}, u32[]{:S(2)}) collective-permute-start(s32[1]{0:T(128)} %param.10), channel_id=1, source_target_pairs={{0,28},{1,29},{2,30},{3,31},{4,0},{5,1},{6,2},{7,3},{8,4},{9,5},{1... | collective-permute-start | bytes 20 | tf_op jit(solution)/shard_map/ppermute | solution.py:487
  14.8 3.2 constant_dynamic-slice_fusion
  27.8 20.4 %norm_keys_values.2 = (bf16[768,768]{1,0:T(8,128)(2,1)S(1)}, bf16[768,768]{1,0:T(8,128)(2,1)S(1)}, bf16[768,3072]{1,0:T(8,128)(2,1)S(1)}, bf16[768,3072]{1,0:T(8,128)(2,1)}) custom-call(s32[4]{0:T(128)S(1)} %pad_add_fusion.refs_0_, f32[1,3072]{1,0:T(1,128)S(1)} %get-tuple-element.96.refs_1_, f32[1,3072]{1,0:T(1,128)S(1)} %get-tuple-element.95.refs_2_, ...), custom_call_target="tpu_custom_call" | custom-call | flops 7247757 | bytes 25952 | tf_op jit(solution)/shard_map/norm_keys_values/pallas_call | solution.py:172
  52.1 18.2 %queries_own_frame.2 = (bf16[768,768]{1,0:T(8,128)(2,1)S(1)}, f32[768,768]{1,0:T(8,128)S(1)}, f32[768,768]{1,0:T(8,128)S(1)}, f32[768,768]{1,0:T(8,128)S(1)}) custom-call(f32[2,128]{1,0:T(2,128)S(1)} %pad_maximum_fusion.3.refs_3_.gain_ref, bf16[768,3072]{1,0:T(8,128)(2,1)S(1)} %get-tuple-element.56.normed_ref, ...), custom_call_target="tpu_custom_call" | custom-call | flops 7247757 | bytes 20054 | tf_op jit(solution)/shard_map/queries_own_frame/pallas_call | solution.py:282
  70.7 6.3 %collective-permute-done.7.refs_5_ = bf16[768,768]{1,0:T(8,128)(2,1)S(1)} collective-permute-done((bf16[768,768]{1,0:T(8,128)(2,1)S(1)}, bf16[768,768]{1,0:T(8,128)(2,1)S(1)}, u32[]{:S(2)}, u32[]{:S(2)}) %collective-permute-start.7) | collective-permute-done | bytes 1179680 | tf_op jit(solution)/shard_map/ppermute | solution.py:487
  77.0 12.6 %collective-permute-done.8.refs_6_ = bf16[768,768]{1,0:T(8,128)(2,1)S(1)} collective-permute-done((bf16[768,768]{1,0:T(8,128)(2,1)S(1)}, bf16[768,768]{1,0:T(8,128)(2,1)S(1)}, u32[]{:S(2)}, u32[]{:S(2)}) %collective-permute-start.8) | collective-permute-done | bytes 1179680 | tf_op jit(solution)/shard_map/ppermute | solution.py:487
  91.4 2.7 collective-permute-done.10.refs_8_.refs_11_
  94.2 3.4 collective-permute-done.9.refs_7_.refs_10_
  97.5 6.9 %earlier_frame.2 = bf16[768,768]{1,0:T(8,128)(2,1)S(1)} custom-call(s32[4]{0:T(128)S(1)} %pad_add_fusion.refs_0_, bf16[768,768]{1,0:T(8,128)(2,1)S(1)} %get-tuple-element.66.refs_1_, f32[768,768]{1,0:T(8,128)S(1)} %get-tuple-element.67.refs_2_, f32[768,768]{1,0:T(8,128)S(1)} %get-tuple-element.68.refs_3_, f32[768,768]{1,0:T(8,128)S(1)} %get-tuple-element.69.refs_4_, ...), custom_call_target="tpu_custom_call" | custom-call | flops 3623878 | bytes 12976 | tf_op jit(solution)/shard_map/earlier_frame/pallas_call | solution.py:343
  106.5 11.7 %collective-permute-done.12 = bf16[384,1536]{1,0:T(8,128)(2,1)S(1)} collective-permute-done((bf16[384,1536]{1,0:T(8,128)(2,1)S(1)}, bf16[384,1536]{1,0:T(8,128)(2,1)S(1)}, u32[]{:S(2)}, u32[]{:S(2)}) %collective-permute-start.12) | collective-permute-done | bytes 1179680 | tf_op jit(solution)/shard_map/ppermute | solution.py:487
  120.0 3.8 %collective-permute-done.11.refs_1_ = bf16[768,768]{1,0:T(8,128)(2,1)S(1)} collective-permute-done((bf16[768,768]{1,0:T(8,128)(2,1)S(1)}, bf16[768,768]{1,0:T(8,128)(2,1)S(1)}, u32[]{:S(2)}, u32[]{:S(2)}) %collective-permute-start.11) | collective-permute-done | bytes 1179680 | tf_op jit(solution)/shard_map/ppermute | solution.py:487
  123.8 2.4 collective-permute-start.14
  126.3 2.4 collective-permute-start.15
  131.7 17.7 %collective-permute-done.14.refs_2_ = bf16[768,768]{1,0:T(8,128)(2,1)S(1)} collective-permute-done((bf16[768,768]{1,0:T(8,128)(2,1)S(1)}, bf16[768,768]{1,0:T(8,128)(2,1)S(1)}, u32[]{:S(2)}, u32[]{:S(2)}) %collective-permute-start.14) | collective-permute-done | bytes 1179680 | tf_op jit(solution)/shard_map/ppermute | solution.py:487
  149.4 2.2 collective-permute-done.15.refs_3_
  154.2 2.1 collective-permute-start.21
  157.1 2.6 collective-permute-start.17
  160.6 3.4 %collective-permute-start.18 = (bf16[384,768]{1,0:T(8,128)(2,1)}, bf16[384,768]{1,0:T(8,128)(2,1)}, u32[]{:S(2)}, u32[]{:S(2)}) collective-permute-start(bf16[384,768]{1,0:T(8,128)(2,1)} %slice.51), channel_id=1, source_target_pairs={{0,1},{1,0},{2,3},{3,2},{4,5},{5,4},{6,7},{7,6},{8,9},{9,8},{10,11... | collective-permute-start | bytes 1769480 | tf_op jit(solution)/shard_map/ppermute | solution.py:487
  169.9 16.0 %projection_start.2.refs_1_ = bf16[768,3072]{1,0:T(8,128)(2,1)S(1)} custom-call(s32[1]{0:T(128)} %bitcast.refs_0_, bf16[768,768]{1,0:T(8,128)(2,1)S(1)} %copy-done.3, bf16[768,768]{1,0:T(8,128)(2,1)S(1)} %collective-permute-done.14.refs_2_, bf16[768,768]{1,0:T(8,128)(2,1)S(1)} %copy-done.1, bf16[768,3072]{1,0:T(8,128)(2,1)} %refs_7_.1, ...), custom_call_target="tpu_custom_call" | custom-call | flops 10871635 | bytes 18874 | tf_op jit(solution)/shard_map/projection_start/pallas_call | solution.py:450
  187.4 9.9 %projection_end.2.refs_5_ = bf16[768,3072]{1,0:T(8,128)(2,1)} custom-call(s32[1]{0:T(128)} %bitcast.refs_0_, bf16[768,3072]{1,0:T(8,128)(2,1)S(1)} %projection_start.2.refs_1_, bf16[768,3072]{1,0:T(8,128)(2,1)} %collective-permute-done.16.refs_2_, f32[1,3072]{1,0:T(1,128)S(1)} %fusion.refs_3_, bf16[384,768]{1,0:T(8,128)(2,1)} %collective-permute-done.17.refs_4_, ...), custom_call_target="tpu_custom_call" | custom-call | flops 3623878 | bytes 18874 | tf_op jit(solution)/shard_map/projection_end/pallas_call | solution.py:450
  197.3 20.4 %norm_keys_values.3 = (bf16[768,768]{1,0:T(8,128)(2,1)S(1)}, bf16[768,768]{1,0:T(8,128)(2,1)S(1)}, bf16[768,3072]{1,0:T(8,128)(2,1)S(1)}, bf16[768,3072]{1,0:T(8,128)(2,1)}) custom-call(s32[4]{0:T(128)S(1)} %copy-done.7, f32[1,3072]{1,0:T(1,128)S(1)} %copy-done.5, f32[1,3072]{1,0:T(1,128)S(1)} %get-tuple-element.95.refs_2_, ...), custom_call_target="tpu_custom_call" | custom-call | flops 7247757 | bytes 25952 | tf_op jit(solution)/shard_map/norm_keys_values/pallas_call | solution.py:172
  219.7 4.2 %collective-permute-start.23 = (bf16[768,768]{1,0:T(8,128)(2,1)S(1)}, bf16[768,768]{1,0:T(8,128)(2,1)S(1)}, u32[]{:S(2)}, u32[]{:S(2)}) collective-permute-start(bf16[768,768]{1,0:T(8,128)(2,1)S(1)} %get-tuple-element.84.value_ref), channel_id=1, source_target_pairs={{0,4},{1,5},{2,6},{3,7},{4,8},{5,9},{6,10},{7,11},{8,12},{9,13},{1... | collective-permute-start | bytes 3538952 | tf_op jit(solution)/shard_map/ppermute | solution.py:487
  223.9 18.2 %queries_own_frame.3 = (bf16[768,768]{1,0:T(8,128)(2,1)S(1)}, f32[768,768]{1,0:T(8,128)S(1)}, f32[768,768]{1,0:T(8,128)S(1)}, f32[768,768]{1,0:T(8,128)S(1)}) custom-call(f32[2,128]{1,0:T(2,128)S(1)} %pad_maximum_fusion.3.refs_3_.gain_ref, bf16[768,3072]{1,0:T(8,128)(2,1)S(1)} %get-tuple-element.82.normed_ref, ...), custom_call_target="tpu_custom_call" | custom-call | flops 7247757 | bytes 20054 | tf_op jit(solution)/shard_map/queries_own_frame/pallas_call | solution.py:282
  242.1 7.5 %collective-permute-done.23.refs_6_ = bf16[768,768]{1,0:T(8,128)(2,1)S(1)} collective-permute-done((bf16[768,768]{1,0:T(8,128)(2,1)S(1)}, bf16[768,768]{1,0:T(8,128)(2,1)S(1)}, u32[]{:S(2)}, u32[]{:S(2)}) %collective-permute-start.23) | collective-permute-done | bytes 1179680 | tf_op jit(solution)/shard_map/ppermute | solution.py:487
  249.7 6.9 %earlier_frame.3 = (bf16[384,768]{1,0:T(8,128)(2,1)S(1)}, bf16[384,768]{1,0:T(8,128)(2,1)S(1)}) custom-call(s32[4]{0:T(128)S(1)} %copy-done.7, bf16[768,768]{1,0:T(8,128)(2,1)S(1)} %get-tuple-element.85.refs_1_, f32[768,768]{1,0:T(8,128)S(1)} %get-tuple-element.86.refs_2_, f32[768,768]{1,0:T(8,128)S(1)} %get-tuple-element.87.refs_3_, ...), custom_call_target="tpu_custom_call" | custom-call | flops 3623878 | bytes 12976 | tf_op jit(solution)/shard_map/earlier_frame/pallas_call | solution.py:343
  257.2 10.6 %collective-permute-done.24.refs_1_ = bf16[384,768]{1,0:T(8,128)(2,1)S(1)} collective-permute-done((bf16[384,768]{1,0:T(8,128)(2,1)S(1)}, bf16[384,768]{1,0:T(8,128)(2,1)S(1)}, u32[]{:S(2)}, u32[]{:S(2)}) %collective-permute-start.24) | collective-permute-done | bytes 589856 | tf_op jit(solution)/shard_map/ppermute | solution.py:487
  267.8 6.3 %collective-permute-done.25.refs_2_ = bf16[384,768]{1,0:T(8,128)(2,1)S(1)} collective-permute-done((bf16[384,768]{1,0:T(8,128)(2,1)S(1)}, bf16[384,768]{1,0:T(8,128)(2,1)S(1)}, u32[]{:S(2)}, u32[]{:S(2)}) %collective-permute-start.25) | collective-permute-done | bytes 589856 | tf_op jit(solution)/shard_map/ppermute | solution.py:487
  278.2 12.2 %collective-permute-done.26.refs_3_ = bf16[384,768]{1,0:T(8,128)(2,1)S(1)} collective-permute-done((bf16[384,768]{1,0:T(8,128)(2,1)S(1)}, bf16[384,768]{1,0:T(8,128)(2,1)S(1)}, u32[]{:S(2)}, u32[]{:S(2)}) %collective-permute-start.26) | collective-permute-done | bytes 589856 | tf_op jit(solution)/shard_map/ppermute | solution.py:487
  293.6 9.5 %collective-permute-done.27.refs_4_ = bf16[384,768]{1,0:T(8,128)(2,1)S(1)} collective-permute-done((bf16[384,768]{1,0:T(8,128)(2,1)S(1)}, bf16[384,768]{1,0:T(8,128)(2,1)S(1)}, u32[]{:S(2)}, u32[]{:S(2)}) %collective-permute-start.27) | collective-permute-done | bytes 589856 | tf_op jit(solution)/shard_map/ppermute | solution.py:487
  306.2 16.0 %projection_start.3.refs_1_ = bf16[768,3072]{1,0:T(8,128)(2,1)S(1)} custom-call(s32[1]{0:T(128)} %bitcast.refs_0_, bf16[384,768]{1,0:T(8,128)(2,1)S(1)} %collective-permute-done.24.refs_1_, bf16[384,768]{1,0:T(8,128)(2,1)S(1)} %collective-permute-done.25.refs_2_, bf16[384,768]{1,0:T(8,128)(2,1)S(1)} %collective-permute-done.26.refs_3_, ...), custom_call_target="tpu_custom_call" | custom-call | flops 10871635 | bytes 18874 | tf_op jit(solution)/shard_map/projection_start/pallas_call | solution.py:450
  322.3 7.2 %collective-permute-done.30.refs_2_ = bf16[768,3072]{1,0:T(8,128)(2,1)S(1)} collective-permute-done((bf16[768,3072]{1,0:T(8,128)(2,1)S(1)}, bf16[768,3072]{1,0:T(8,128)(2,1)S(1)}, u32[]{:S(2)}, u32[]{:S(2)}) %collective-permute-start.30) | collective-permute-done | bytes 4718624 | tf_op jit(solution)/shard_map/ppermute | solution.py:487
  329.5 8.5 %projection_end.3 = bf16[768,3072]{1,0:T(8,128)(2,1)} custom-call(s32[1]{0:T(128)} %bitcast.refs_0_, bf16[768,3072]{1,0:T(8,128)(2,1)S(1)} %projection_start.3.refs_1_, bf16[768,3072]{1,0:T(8,128)(2,1)S(1)} %collective-permute-done.30.refs_2_, f32[1,3072]{1,0:T(1,128)S(1)} %fusion.refs_3_, bf16[192,768]{1,0:T(8,128)(2,1)S(1)} %collective-permute-done.31.refs_4_, ...), custom_call_target="tpu_custom_call" | custom-call | flops 3623878 | bytes 18874 | tf_op jit(solution)/shard_map/projection_end/pallas_call | solution.py:450
  (100 shorter events, 50.5 us)
Async XLA Ops:
  1.8 18.1 %collective-permute-start.1 = (bf16[192,3072]{1,0:T(8,128)(2,1)S(1)}, bf16[192,3072]{1,0:T(8,128)(2,1)}, u32[]{:S(2)}, u32[]{:S(2)}) collective-permute-start(bf16[192,3072]{1,0:T(8,128)(2,1)S(1)} %get-tuple-element.94.refs_6_), channel_id=1, source_target_pairs={{28,30},{29,31},{30,28},{31,29}} | collective-permute-start | bytes 3538952 | tf_op jit(solution)/shard_map/ppermute | solution.py:487
  3.5 16.4 %collective-permute-start.2 = (bf16[192,3072]{1,0:T(8,128)(2,1)S(1)}, bf16[192,3072]{1,0:T(8,128)(2,1)}, u32[]{:S(2)}, u32[]{:S(2)}) collective-permute-start(bf16[192,3072]{1,0:T(8,128)(2,1)S(1)} %get-tuple-element.94.refs_6_), channel_id=1, source_target_pairs={{28,31},{29,30},{30,29},{31,28}} | collective-permute-start | bytes 3538952 | tf_op jit(solution)/shard_map/ppermute | solution.py:487
  5.2 16.6 %collective-permute-start = (bf16[192,3072]{1,0:T(8,128)(2,1)S(1)}, bf16[192,3072]{1,0:T(8,128)(2,1)S(1)}, u32[]{:S(2)}, u32[]{:S(2)}) collective-permute-start(bf16[192,3072]{1,0:T(8,128)(2,1)S(1)} %get-tuple-element.94.refs_6_), channel_id=1, source_target_pairs={{28,29},{29,28},{30,31},{31,30}} | collective-permute-start | bytes 3538952 | tf_op jit(solution)/shard_map/ppermute | solution.py:487
  6.0 12.0 %collective-permute-start.4 = (s32[1]{0:T(128)}, s32[1]{0:T(128)}, u32[]{:S(2)}, u32[]{:S(2)}) collective-permute-start(s32[1]{0:T(128)} %param.10), channel_id=1, source_target_pairs={{0,28},{1,29},{2,30},{3,31},{4,0},{5,1},{6,2},{7,3},{8,4},{9,5},{1... | collective-permute-start | bytes 20 | tf_op jit(solution)/shard_map/ppermute | solution.py:487
  23.1 47.2 %collective-permute-start.5 = (bf16[768,1536]{1,0:T(8,128)(2,1)S(1)}, bf16[768,1536]{1,0:T(8,128)(2,1)S(1)}, u32[]{:S(2)}, u32[]{:S(2)}) collective-permute-start(bf16[768,1536]{1,0:T(8,128)(2,1)S(1)} %copy-done.12), channel_id=1, source_target_pairs={{0,1},{1,0},{2,3},{3,2},{4,5},{5,4},{6,7},{7,6},{8,9},{9,8},{10,11... | collective-permute-start | bytes 7077896 | tf_op jit(solution)/shard_map/ppermute | solution.py:487
  24.6 46.1 %collective-permute-start.6 = (bf16[768,1536]{1,0:T(8,128)(2,1)S(1)}, bf16[768,1536]{1,0:T(8,128)(2,1)S(1)}, u32[]{:S(2)}, u32[]{:S(2)}) collective-permute-start(bf16[768,1536]{1,0:T(8,128)(2,1)S(1)} %copy-done.12), channel_id=1, source_target_pairs={{0,2},{1,3},{2,0},{3,1},{4,6},{5,7},{6,4},{7,5},{8,10},{9,11},{10,... | collective-permute-start | bytes 7077896 | tf_op jit(solution)/shard_map/ppermute | solution.py:487
  48.3 28.7 %collective-permute-start.7 = (bf16[768,768]{1,0:T(8,128)(2,1)S(1)}, bf16[768,768]{1,0:T(8,128)(2,1)S(1)}, u32[]{:S(2)}, u32[]{:S(2)}) collective-permute-start(bf16[768,768]{1,0:T(8,128)(2,1)S(1)} %get-tuple-element.57.key_ref), channel_id=1, source_target_pairs={{0,4},{1,5},{2,6},{3,7},{4,8},{5,9},{6,10},{7,11},{8,12},{9,13},{1... | collective-permute-start | bytes 3538952 | tf_op jit(solution)/shard_map/ppermute | solution.py:487
  50.2 39.4 %collective-permute-start.8 = (bf16[768,768]{1,0:T(8,128)(2,1)S(1)}, bf16[768,768]{1,0:T(8,128)(2,1)S(1)}, u32[]{:S(2)}, u32[]{:S(2)}) collective-permute-start(bf16[768,768]{1,0:T(8,128)(2,1)S(1)} %get-tuple-element.58.value_ref), channel_id=1, source_target_pairs={{0,4},{1,5},{2,6},{3,7},{4,8},{5,9},{6,10},{7,11},{8,12},{9,13},{1... | collective-permute-start | bytes 3538952 | tf_op jit(solution)/shard_map/ppermute | solution.py:487
  89.6 7.9 %collective-permute-start.9 = (bf16[768,1536]{1,0:T(8,128)(2,1)S(1)}, bf16[768,1536]{1,0:T(8,128)(2,1)S(1)}, u32[]{:S(2)}, u32[]{:S(2)}) collective-permute-start(bf16[768,1536]{1,0:T(8,128)(2,1)S(1)} %collective-permute-done.5.refs_5_.refs_8_), channel_id=1, source_target_pairs={{0,4},{1,5},{2,6},{3,7},{4,0},{5,1},{6,2},{7,3},{8,12},{9,13},{10,... | collective-permute-start | bytes 7077896 | tf_op jit(solution)/shard_map/ppermute | solution.py:487
  90.3 27.9 %collective-permute-start.12 = (bf16[384,1536]{1,0:T(8,128)(2,1)S(1)}, bf16[384,1536]{1,0:T(8,128)(2,1)S(1)}, u32[]{:S(2)}, u32[]{:S(2)}) collective-permute-start(bf16[384,1536]{1,0:T(8,128)(2,1)S(1)} %slice.45), channel_id=1, source_target_pairs={{0,2},{1,3},{2,0},{3,1},{4,6},{5,7},{6,4},{7,5},{8,10},{9,11},{10,... | collective-permute-start | bytes 3538952 | tf_op jit(solution)/shard_map/ppermute | solution.py:487
  90.9 27.6 %collective-permute-start.13 = (bf16[384,1536]{1,0:T(8,128)(2,1)S(1)}, bf16[384,1536]{1,0:T(8,128)(2,1)S(1)}, u32[]{:S(2)}, u32[]{:S(2)}) collective-permute-start(bf16[384,1536]{1,0:T(8,128)(2,1)S(1)} %slice.46), channel_id=1, source_target_pairs={{0,1},{1,0},{2,3},{3,2},{4,5},{5,4},{6,7},{7,6},{8,9},{9,8},{10,11... | collective-permute-start | bytes 3538952 | tf_op jit(solution)/shard_map/ppermute | solution.py:487
  104.5 19.3 %collective-permute-start.11 = (bf16[768,768]{1,0:T(8,128)(2,1)S(1)}, bf16[768,768]{1,0:T(8,128)(2,1)S(1)}, u32[]{:S(2)}, u32[]{:S(2)}) collective-permute-start(bf16[768,768]{1,0:T(8,128)(2,1)S(1)} %earlier_frame.2), channel_id=1, source_target_pairs={{0,4},{1,5},{2,6},{3,7},{4,8},{5,9},{6,10},{7,11},{8,12},{9,13},{1... | collective-permute-start | bytes 3538952 | tf_op jit(solution)/shard_map/ppermute | solution.py:487
  123.8 25.6 %collective-permute-start.14 = (bf16[768,768]{1,0:T(8,128)(2,1)S(1)}, bf16[768,768]{1,0:T(8,128)(2,1)S(1)}, u32[]{:S(2)}, u32[]{:S(2)}) collective-permute-start(bf16[768,768]{1,0:T(8,128)(2,1)S(1)} %collective-permute-done.11.refs_1_), channel_id=1, source_target_pairs={{0,1},{1,0},{2,3},{3,2},{4,5},{5,4},{6,7},{7,6},{8,9},{9,8},{10,11... | collective-permute-start | bytes 3538952 | tf_op jit(solution)/shard_map/ppermute | solution.py:487
  126.3 25.4 %collective-permute-start.15 = (bf16[768,768]{1,0:T(8,128)(2,1)S(1)}, bf16[768,768]{1,0:T(8,128)(2,1)S(1)}, u32[]{:S(2)}, u32[]{:S(2)}) collective-permute-start(bf16[768,768]{1,0:T(8,128)(2,1)S(1)} %collective-permute-done.11.refs_1_), channel_id=1, source_target_pairs={{0,2},{1,3},{2,0},{3,1},{4,6},{5,7},{6,4},{7,5},{8,10},{9,11},{10,... | collective-permute-start | bytes 3538952 | tf_op jit(solution)/shard_map/ppermute | solution.py:487
  129.8 57.5 %collective-permute-start.16 = (bf16[768,3072]{1,0:T(8,128)(2,1)}, bf16[768,3072]{1,0:T(8,128)(2,1)}, u32[]{:S(2)}, u32[]{:S(2)}) collective-permute-start(bf16[768,3072]{1,0:T(8,128)(2,1)} %get-tuple-element.79), channel_id=1, source_target_pairs={{0,4},{1,5},{2,6},{3,7},{4,8},{5,9},{6,10},{7,11},{8,12},{9,13},{1... | collective-permute-start | bytes 14155784 | tf_op jit(solution)/shard_map/ppermute | solution.py:487
  152.5 33.4 %collective-permute-start.19 = (bf16[768,1536]{1,0:T(8,128)(2,1)}, bf16[768,1536]{1,0:T(8,128)(2,1)}, u32[]{:S(2)}, u32[]{:S(2)}) collective-permute-start(bf16[768,1536]{1,0:T(8,128)(2,1)} %pad_maximum_fusion.1.refs_6_.refs_8_), channel_id=1, source_target_pairs={{0,4},{1,5},{2,6},{3,7},{4,0},{5,1},{6,2},{7,3},{8,12},{9,13},{10,... | collective-permute-start | bytes 7077896 | tf_op jit(solution)/shard_map/ppermute | solution.py:487
  154.2 43.0 %collective-permute-start.21 = (bf16[384,3072]{1,0:T(8,128)(2,1)}, bf16[384,3072]{1,0:T(8,128)(2,1)}, u32[]{:S(2)}, u32[]{:S(2)}) collective-permute-start(bf16[384,3072]{1,0:T(8,128)(2,1)} %pad_maximum_fusion.2), channel_id=1, source_target_pairs={{28,30},{29,31},{30,28},{31,29}} | collective-permute-start | bytes 7077896 | tf_op jit(solution)/shard_map/ppermute | solution.py:487
  157.1 28.8 %collective-permute-start.17 = (bf16[384,768]{1,0:T(8,128)(2,1)}, bf16[384,768]{1,0:T(8,128)(2,1)}, u32[]{:S(2)}, u32[]{:S(2)}) collective-permute-start(bf16[384,768]{1,0:T(8,128)(2,1)} %slice.50), channel_id=1, source_target_pairs={{0,2},{1,3},{2,0},{3,1},{4,6},{5,7},{6,4},{7,5},{8,10},{9,11},{10,... | collective-permute-start | bytes 1769480 | tf_op jit(solution)/shard_map/ppermute | solution.py:487
  160.6 25.3 %collective-permute-start.18 = (bf16[384,768]{1,0:T(8,128)(2,1)}, bf16[384,768]{1,0:T(8,128)(2,1)}, u32[]{:S(2)}, u32[]{:S(2)}) collective-permute-start(bf16[384,768]{1,0:T(8,128)(2,1)} %slice.51), channel_id=1, source_target_pairs={{0,1},{1,0},{2,3},{3,2},{4,5},{5,4},{6,7},{7,6},{8,9},{9,8},{10,11... | collective-permute-start | bytes 1769480 | tf_op jit(solution)/shard_map/ppermute | solution.py:487
  217.7 24.4 %collective-permute-start.22 = (bf16[768,768]{1,0:T(8,128)(2,1)S(1)}, bf16[768,768]{1,0:T(8,128)(2,1)S(1)}, u32[]{:S(2)}, u32[]{:S(2)}) collective-permute-start(bf16[768,768]{1,0:T(8,128)(2,1)S(1)} %get-tuple-element.83.key_ref), channel_id=1, source_target_pairs={{0,4},{1,5},{2,6},{3,7},{4,8},{5,9},{6,10},{7,11},{8,12},{9,13},{1... | collective-permute-start | bytes 3538952 | tf_op jit(solution)/shard_map/ppermute | solution.py:487
  219.7 30.0 %collective-permute-start.23 = (bf16[768,768]{1,0:T(8,128)(2,1)S(1)}, bf16[768,768]{1,0:T(8,128)(2,1)S(1)}, u32[]{:S(2)}, u32[]{:S(2)}) collective-permute-start(bf16[768,768]{1,0:T(8,128)(2,1)S(1)} %get-tuple-element.84.value_ref), channel_id=1, source_target_pairs={{0,4},{1,5},{2,6},{3,7},{4,8},{5,9},{6,10},{7,11},{8,12},{9,13},{1... | collective-permute-start | bytes 3538952 | tf_op jit(solution)/shard_map/ppermute | solution.py:487
  256.6 11.2 %collective-permute-start.24 = (bf16[384,768]{1,0:T(8,128)(2,1)S(1)}, bf16[384,768]{1,0:T(8,128)(2,1)S(1)}, u32[]{:S(2)}, u32[]{:S(2)}) collective-permute-start(bf16[384,768]{1,0:T(8,128)(2,1)S(1)} %get-tuple-element.89), channel_id=1, source_target_pairs={{0,4},{1,5},{2,6},{3,7},{4,8},{5,9},{6,10},{7,11},{8,12},{9,13},{1... | collective-permute-start | bytes 1769480 | tf_op jit(solution)/shard_map/ppermute | solution.py:487
  256.7 17.4 %collective-permute-start.25 = (bf16[384,768]{1,0:T(8,128)(2,1)S(1)}, bf16[384,768]{1,0:T(8,128)(2,1)S(1)}, u32[]{:S(2)}, u32[]{:S(2)}) collective-permute-start(bf16[384,768]{1,0:T(8,128)(2,1)S(1)} %get-tuple-element.90), channel_id=1, source_target_pairs={{0,4},{1,5},{2,6},{3,7},{4,8},{5,9},{6,10},{7,11},{8,12},{9,13},{1... | collective-permute-start | bytes 1769480 | tf_op jit(solution)/shard_map/ppermute | solution.py:487
  274.1 55.3 %collective-permute-start.30 = (bf16[768,3072]{1,0:T(8,128)(2,1)S(1)}, bf16[768,3072]{1,0:T(8,128)(2,1)S(1)}, u32[]{:S(2)}, u32[]{:S(2)}) collective-permute-start(bf16[768,3072]{1,0:T(8,128)(2,1)S(1)} %copy-done.14), channel_id=1, source_target_pairs={{0,4},{1,5},{2,6},{3,7},{4,8},{5,9},{6,10},{7,11},{8,12},{9,13},{1... | collective-permute-start | bytes 14155784 | tf_op jit(solution)/shard_map/ppermute | solution.py:487
  274.1 16.3 %collective-permute-start.26 = (bf16[384,768]{1,0:T(8,128)(2,1)S(1)}, bf16[384,768]{1,0:T(8,128)(2,1)S(1)}, u32[]{:S(2)}, u32[]{:S(2)}) collective-permute-start(bf16[384,768]{1,0:T(8,128)(2,1)S(1)} %collective-permute-done.24.refs_1_), channel_id=1, source_target_pairs={{0,1},{1,0},{2,3},{3,2},{4,5},{5,4},{6,7},{7,6},{8,9},{9,8},{10,11... | collective-permute-start | bytes 1769480 | tf_op jit(solution)/shard_map/ppermute | solution.py:487
  275.6 16.4 %collective-permute-start.28 = (bf16[384,768]{1,0:T(8,128)(2,1)S(1)}, bf16[384,768]{1,0:T(8,128)(2,1)S(1)}, u32[]{:S(2)}, u32[]{:S(2)}) collective-permute-start(bf16[384,768]{1,0:T(8,128)(2,1)S(1)} %collective-permute-done.24.refs_1_), channel_id=1, source_target_pairs={{0,2},{1,3},{2,0},{3,1},{4,6},{5,7},{6,4},{7,5},{8,10},{9,11},{10,... | collective-permute-start | bytes 1769480 | tf_op jit(solution)/shard_map/ppermute | solution.py:487
  277.1 25.9 %collective-permute-start.27 = (bf16[384,768]{1,0:T(8,128)(2,1)S(1)}, bf16[384,768]{1,0:T(8,128)(2,1)S(1)}, u32[]{:S(2)}, u32[]{:S(2)}) collective-permute-start(bf16[384,768]{1,0:T(8,128)(2,1)S(1)} %collective-permute-done.25.refs_2_), channel_id=1, source_target_pairs={{0,1},{1,0},{2,3},{3,2},{4,5},{5,4},{6,7},{7,6},{8,9},{9,8},{10,11... | collective-permute-start | bytes 1769480 | tf_op jit(solution)/shard_map/ppermute | solution.py:487
  277.6 27.0 %collective-permute-start.29 = (bf16[384,768]{1,0:T(8,128)(2,1)S(1)}, bf16[384,768]{1,0:T(8,128)(2,1)S(1)}, u32[]{:S(2)}, u32[]{:S(2)}) collective-permute-start(bf16[384,768]{1,0:T(8,128)(2,1)S(1)} %collective-permute-done.25.refs_2_), channel_id=1, source_target_pairs={{0,2},{1,3},{2,0},{3,1},{4,6},{5,7},{6,4},{7,5},{8,10},{9,11},{10,... | collective-permute-start | bytes 1769480 | tf_op jit(solution)/shard_map/ppermute | solution.py:487
  290.4 31.8 %collective-permute-start.31 = (bf16[192,768]{1,0:T(8,128)(2,1)S(1)}, bf16[192,768]{1,0:T(8,128)(2,1)S(1)}, u32[]{:S(2)}, u32[]{:S(2)}) collective-permute-start(bf16[192,768]{1,0:T(8,128)(2,1)S(1)} %slice.58), channel_id=1, source_target_pairs={{0,2},{1,3},{2,0},{3,1},{4,6},{5,7},{6,4},{7,5},{8,10},{9,11},{10,... | collective-permute-start | bytes 884744 | tf_op jit(solution)/shard_map/ppermute | solution.py:487
  292.0 30.3 %collective-permute-start.32 = (bf16[192,768]{1,0:T(8,128)(2,1)S(1)}, bf16[192,768]{1,0:T(8,128)(2,1)S(1)}, u32[]{:S(2)}, u32[]{:S(2)}) collective-permute-start(bf16[192,768]{1,0:T(8,128)(2,1)S(1)} %slice.59), channel_id=1, source_target_pairs={{0,1},{1,0},{2,3},{3,2},{4,5},{5,4},{6,7},{7,6},{8,9},{9,8},{10,11... | collective-permute-start | bytes 884744 | tf_op jit(solution)/shard_map/ppermute | solution.py:487
  303.0 19.2 %collective-permute-start.33 = (bf16[192,768]{1,0:T(8,128)(2,1)S(1)}, bf16[192,768]{1,0:T(8,128)(2,1)S(1)}, u32[]{:S(2)}, u32[]{:S(2)}) collective-permute-start(bf16[192,768]{1,0:T(8,128)(2,1)S(1)} %slice.60), channel_id=1, source_target_pairs={{0,2},{1,3},{2,0},{3,1},{4,6},{5,7},{6,4},{7,5},{8,10},{9,11},{10,... | collective-permute-start | bytes 884744 | tf_op jit(solution)/shard_map/ppermute | solution.py:487
  304.6 17.6 %collective-permute-start.34 = (bf16[192,768]{1,0:T(8,128)(2,1)S(1)}, bf16[192,768]{1,0:T(8,128)(2,1)S(1)}, u32[]{:S(2)}, u32[]{:S(2)}) collective-permute-start(bf16[192,768]{1,0:T(8,128)(2,1)S(1)} %slice.61), channel_id=1, source_target_pairs={{0,1},{1,0},{2,3},{3,2},{4,5},{5,4},{6,7},{7,6},{8,9},{9,8},{10,11... | collective-permute-start | bytes 884744 | tf_op jit(solution)/shard_map/ppermute | solution.py:487
  (19 other events, 239.2 us)

commit v9 on v8

--- a/solution.py
+++ b/solution.py
@@ -67,7 +67,7 @@
     key_ref, value_ref, normed_any, state_any = refs[7 + half : 11 + half]
     state_ref, normed_ref, inverse_ref, w_ref, sem, out_sems, w_sems = refs[11 + half :]
     step = pl.program_id(0)
-    rows = state_ref.shape[0]
+    rows, width = state_ref.shape
     piece_rows = noise_any.shape[0]
 
     def weights_of(part):
@@ -120,22 +120,26 @@
 
         state_copy.start()
 
+        block_rows = math.gcd(rows, 64)
+
         def measure(i, carry):
-            at = pl.ds(pl.multiple_of(i * 16, 16), 16)
-            state = state_ref[at, :].astype(F32)
-            mean = over_lanes(state * state, jnp.add, jnp.sum) * (1.0 / state.shape[1])
-            inverse_ref[at, :] = jnp.broadcast_to(lax.rsqrt(mean + EPS), (16, HD))
+            at = pl.ds(pl.multiple_of(i * block_rows, block_rows), block_rows)
+            squares = None
+            for k in range(0, width, HD):
+                part = state_ref[at, k : k + HD].astype(F32)
+                squares = part * part if squares is None else squares + part * part
+            mean = jnp.sum(squares, axis=-1, keepdims=True) * (1.0 / width)
+            inverse_ref[at, :] = jnp.broadcast_to(lax.rsqrt(mean + EPS), (block_rows, HD))
             return carry
 
-        def apply(i, carry):
-            at = pl.ds(pl.multiple_of(i * 16, 16), 16)
-            inverse = inverse_ref[at, :][:, :1]
-            state = state_ref[at, :].astype(F32) * inverse
-            normed_ref[at, :] = (state * scale_ref[...] + shift_ref[...]).astype(BF16)
+        def apply(k, carry):
+            at = pl.ds(pl.multiple_of(k * HD, HD), HD)
+            state = state_ref[:, at].astype(F32) * inverse_ref[...]
+            normed_ref[:, at] = (state * scale_ref[:, at] + shift_ref[:, at]).astype(BF16)
             return carry
 
-        lax.fori_loop(0, rows // 16, measure, 0, unroll=4)
-        lax.fori_loop(0, rows // 16, apply, 0, unroll=2)
+        lax.fori_loop(0, rows // block_rows, measure, 0)
+        lax.fori_loop(0, width // HD, apply, 0)
         normed_copy.start()
 
     for part in range(2):
@@ -539,7 +543,12 @@
         if at_once:
             for j in range(1, half):
                 straight = send(noise, away(j, half), *args)
-                across = send(noise, lambda q, t: away(j, half)(q, t ^ 1), *args)
+                across = send(
+                    noise,
+                    lambda q, t: away(j, half)(queue_size - 1, t ^ 1),
+                    *mesh_sizes,
+                    [max(queue_size - 3, 0)],
+                )
                 pairs.append(jnp.concatenate([straight, across], axis=0))
         else:
             pair = jnp.concatenate([noise, near], axis=0)
@@ -551,10 +560,8 @@
     half_weight = lax.dynamic_slice(
         out_weight, (0, parity[0] * (width // 2)), (out_weight.shape[0], width // 2)
     )
-    word, noise_pieces = lax.optimization_barrier((levels, noise_pieces))
-    word = send(word, lambda q, t: (q - 1, t), *mesh_sizes, [queue_size - 1])
-    half_weight, latents, noise_pieces, word = lax.optimization_barrier(
-        (half_weight, latents, noise_pieces, word)
+    half_weight, latents, noise_pieces = lax.optimization_barrier(
+        (half_weight, latents, noise_pieces)
     )
     mine = one_hop(half_weight, *mesh_sizes)
 
@@ -565,7 +572,7 @@
 
     shift, scale1, _ = modulation(worked_level)
     _, _, gate = modulation(levels[0])
-    info = jnp.stack([is_last, tensor_index // 2, tensor_index % 2, word[0]])
+    info = jnp.stack([is_last, tensor_index // 2, tensor_index % 2])
     info = info.astype(jnp.int32)
     gains = jnp.stack([q_gain * SCORE_SCALE, k_gain])
 

time: 339 us -> 347 us (1.024)
  waiting for transfers between devices: 116 us -> 133 us
  starting transfers between devices: 57.6 us -> 50.4 us
    ppermute x35 -> x34, waiting for transfers between devices: 116 us -> 133 us  [send(): return lax.ppermute(block, AXES, pairs)]
    ppermute x35 -> x34, starting transfers between devices: 57.6 us -> 50.4 us  [send(): return lax.ppermute(block, AXES, pairs)]
  transfers between devices with their start and end apart: 35 -> 34, of which waited for: 17 -> 19; matrix products, arithmetic and copies ran while one was open for 4% -> 4% of each run, Pallas kernels for 31% -> 30%
where the time goes in v9:
time: 347 us
  Pallas kernels  139 us (40%)
  waiting for transfers between devices  133 us (38%)
  starting transfers between devices  50.4 us (15%)
  local copies, waits for them, and re-layouts  12.3 us (4%)
  other arithmetic  8.15 us (2%)
    ppermute x34, waiting for transfers between devices, send(): return lax.ppermute(block, AXES, pairs)  133 us
    pallas_call x4, Pallas kernels, output_projection(): pl.pallas_call(functools.partial(output_kernel, part_counts=tuple((len(p)...  50.4 us
    ppermute x34, starting transfers between devices, send(): return lax.ppermute(block, AXES, pairs)  50.4 us
    pallas_call x2, Pallas kernels, project_keys_values(): pl.pallas_call(functools.partial(key_value_kernel, half=half), grid_spec=...  38.6 us
    pallas_call x2, Pallas kernels, own_attention(): pl.pallas_call(own_kernel, grid=(head_cols // cols,), in_specs=[pl.BlockS...  36.4 us
    pallas_call x2, Pallas kernels, earlier_attention(): pl.pallas_call(functools.partial(earlier_kernel, chunks=chunks), grid_spe...  13.9 us
  transfers between devices with their start and end apart: 34, of which 19 were waited for; matrix products, arithmetic and copies ran while one was open for 4% of the time, Pallas kernels for 30%

profile of v9, /device:TPU:0, one launch (start us, length us, event | category | flops | bytes accessed | tf_op | source)
XLA Modules:
  0.0 346.7 jit_solution(9167545737386172343)
XLA Ops:
  6.0 8.0 %collective-permute-start = (s32[1]{0:T(128)}, s32[1]{0:T(128)}, u32[]{:S(2)}, u32[]{:S(2)}) collective-permute-start(s32[1]{0:T(128)} %param.10), channel_id=1, source_target_pairs={{0,28},{1,29},{2,30},{3,31},{4,0},{5,1},{6,2},{7,3},{8,4},{9,5},{1... | collective-permute-start | bytes 20 | tf_op jit(solution)/shard_map/ppermute | solution.py:491
  14.6 3.2 constant_dynamic-slice_fusion
  24.1 19.3 %norm_keys_values.2 = (bf16[768,768]{1,0:T(8,128)(2,1)S(1)}, bf16[768,768]{1,0:T(8,128)(2,1)S(1)}, bf16[768,3072]{1,0:T(8,128)(2,1)S(1)}, bf16[768,3072]{1,0:T(8,128)(2,1)}) custom-call(s32[3]{0:T(128)S(1)} %copy-done.6, f32[1,3072]{1,0:T(1,128)S(1)} %get-tuple-element.88.refs_1_, f32[1,3072]{1,0:T(1,128)S(1)} %get-tuple-element.87.refs_2_, ...), custom_call_target="tpu_custom_call" | custom-call | flops 7247757 | bytes 25952 | tf_op jit(solution)/shard_map/norm_keys_values/pallas_call | solution.py:176
  47.3 18.2 %queries_own_frame.2 = (bf16[768,768]{1,0:T(8,128)(2,1)S(1)}, f32[768,768]{1,0:T(8,128)S(1)}, f32[768,768]{1,0:T(8,128)S(1)}, f32[768,768]{1,0:T(8,128)S(1)}) custom-call(f32[2,128]{1,0:T(2,128)S(1)} %pad_maximum_fusion.3.refs_3_.gain_ref, bf16[768,3072]{1,0:T(8,128)(2,1)S(1)} %get-tuple-element.48.normed_ref, ...), custom_call_target="tpu_custom_call" | custom-call | flops 7247757 | bytes 20054 | tf_op jit(solution)/shard_map/queries_own_frame/pallas_call | solution.py:286
  65.5 3.5 %collective-permute-done.4.refs_5_.refs_8_ = bf16[768,1536]{1,0:T(8,128)(2,1)S(1)} collective-permute-done((bf16[768,1536]{1,0:T(8,128)(2,1)S(1)}, bf16[768,1536]{1,0:T(8,128)(2,1)S(1)}, u32[]{:S(2)}, u32[]{:S(2)}) %collective-permute-start.4) | collective-permute-done | bytes 2359328 | tf_op jit(solution)/shard_map/ppermute | solution.py:491
  70.5 14.9 %collective-permute-done.6.refs_5_ = bf16[768,768]{1,0:T(8,128)(2,1)S(1)} collective-permute-done((bf16[768,768]{1,0:T(8,128)(2,1)S(1)}, bf16[768,768]{1,0:T(8,128)(2,1)S(1)}, u32[]{:S(2)}, u32[]{:S(2)}) %collective-permute-start.6) | collective-permute-done | bytes 1179680 | tf_op jit(solution)/shard_map/ppermute | solution.py:491
  85.4 12.6 %collective-permute-done.7.refs_6_ = bf16[768,768]{1,0:T(8,128)(2,1)S(1)} collective-permute-done((bf16[768,768]{1,0:T(8,128)(2,1)S(1)}, bf16[768,768]{1,0:T(8,128)(2,1)S(1)}, u32[]{:S(2)}, u32[]{:S(2)}) %collective-permute-start.7) | collective-permute-done | bytes 1179680 | tf_op jit(solution)/shard_map/ppermute | solution.py:491
  102.6 3.4 collective-permute-done.9.refs_8_.refs_11_
  106.0 6.9 %earlier_frame.2 = bf16[768,768]{1,0:T(8,128)(2,1)S(1)} custom-call(s32[3]{0:T(128)S(1)} %copy-done.6, bf16[768,768]{1,0:T(8,128)(2,1)S(1)} %get-tuple-element.58.refs_1_, f32[768,768]{1,0:T(8,128)S(1)} %get-tuple-element.59.refs_2_, f32[768,768]{1,0:T(8,128)S(1)} %get-tuple-element.60.refs_3_, f32[768,768]{1,0:T(8,128)S(1)} %get-tuple-element.61.refs_4_, ...), custom_call_target="tpu_custom_call" | custom-call | flops 3623878 | bytes 12976 | tf_op jit(solution)/shard_map/earlier_frame/pallas_call | solution.py:347
  113.0 2.0 collective-permute-start.10
  115.0 11.7 %collective-permute-done.11 = bf16[384,1536]{1,0:T(8,128)(2,1)S(1)} collective-permute-done((bf16[384,1536]{1,0:T(8,128)(2,1)S(1)}, bf16[384,1536]{1,0:T(8,128)(2,1)S(1)}, u32[]{:S(2)}, u32[]{:S(2)}) %collective-permute-start.11) | collective-permute-done | bytes 1179680 | tf_op jit(solution)/shard_map/ppermute | solution.py:491
  129.7 2.6 collective-permute-done.10.refs_1_
  132.3 2.4 collective-permute-start.13
  134.7 3.6 %collective-permute-start.14 = (bf16[768,768]{1,0:T(8,128)(2,1)S(1)}, bf16[768,768]{1,0:T(8,128)(2,1)S(1)}, u32[]{:S(2)}, u32[]{:S(2)}) collective-permute-start(bf16[768,768]{1,0:T(8,128)(2,1)S(1)} %collective-permute-done.10.refs_1_), channel_id=1, source_target_pairs={{0,2},{1,3},{2,0},{3,1},{4,6},{5,7},{6,4},{7,5},{8,10},{9,11},{10,... | collective-permute-start | bytes 3538952 | tf_op jit(solution)/shard_map/ppermute | solution.py:491
  141.3 16.9 %collective-permute-done.13.refs_2_ = bf16[768,768]{1,0:T(8,128)(2,1)S(1)} collective-permute-done((bf16[768,768]{1,0:T(8,128)(2,1)S(1)}, bf16[768,768]{1,0:T(8,128)(2,1)S(1)}, u32[]{:S(2)}, u32[]{:S(2)}) %collective-permute-start.13) | collective-permute-done | bytes 1179680 | tf_op jit(solution)/shard_map/ppermute | solution.py:491
  158.3 2.2 collective-permute-done.14.refs_3_
  163.0 2.1 collective-permute-start.20
  166.0 3.2 collective-permute-start.16
  170.1 3.4 collective-permute-start.17
  179.5 16.0 %projection_start.2.refs_1_ = bf16[768,3072]{1,0:T(8,128)(2,1)S(1)} custom-call(s32[1]{0:T(128)} %bitcast.refs_0_, bf16[768,768]{1,0:T(8,128)(2,1)S(1)} %copy-done.3, bf16[768,768]{1,0:T(8,128)(2,1)S(1)} %collective-permute-done.13.refs_2_, bf16[768,768]{1,0:T(8,128)(2,1)S(1)} %copy-done.1, bf16[768,3072]{1,0:T(8,128)(2,1)} %refs_7_.1, ...), custom_call_target="tpu_custom_call" | custom-call | flops 10871635 | bytes 18874 | tf_op jit(solution)/shard_map/projection_start/pallas_call | solution.py:454
  197.0 9.9 %projection_end.2.refs_5_ = bf16[768,3072]{1,0:T(8,128)(2,1)} custom-call(s32[1]{0:T(128)} %bitcast.refs_0_, bf16[768,3072]{1,0:T(8,128)(2,1)S(1)} %projection_start.2.refs_1_, bf16[768,3072]{1,0:T(8,128)(2,1)} %collective-permute-done.15.refs_2_, f32[1,3072]{1,0:T(1,128)S(1)} %fusion.refs_3_, bf16[384,768]{1,0:T(8,128)(2,1)} %collective-permute-done.16.refs_4_, ...), custom_call_target="tpu_custom_call" | custom-call | flops 3623878 | bytes 18874 | tf_op jit(solution)/shard_map/projection_end/pallas_call | solution.py:454
  206.9 19.3 %norm_keys_values.3 = (bf16[768,768]{1,0:T(8,128)(2,1)S(1)}, bf16[768,768]{1,0:T(8,128)(2,1)S(1)}, bf16[768,3072]{1,0:T(8,128)(2,1)S(1)}, bf16[768,3072]{1,0:T(8,128)(2,1)}) custom-call(s32[3]{0:T(128)S(1)} %copy-done.7, f32[1,3072]{1,0:T(1,128)S(1)} %copy-done.5, f32[1,3072]{1,0:T(1,128)S(1)} %get-tuple-element.87.refs_2_, ...), custom_call_target="tpu_custom_call" | custom-call | flops 7247757 | bytes 25952 | tf_op jit(solution)/shard_map/norm_keys_values/pallas_call | solution.py:176
  230.1 18.2 %queries_own_frame.3 = (bf16[768,768]{1,0:T(8,128)(2,1)S(1)}, f32[768,768]{1,0:T(8,128)S(1)}, f32[768,768]{1,0:T(8,128)S(1)}, f32[768,768]{1,0:T(8,128)S(1)}) custom-call(f32[2,128]{1,0:T(2,128)S(1)} %pad_maximum_fusion.3.refs_3_.gain_ref, bf16[768,3072]{1,0:T(8,128)(2,1)S(1)} %get-tuple-element.74.normed_ref, ...), custom_call_target="tpu_custom_call" | custom-call | flops 7247757 | bytes 20054 | tf_op jit(solution)/shard_map/queries_own_frame/pallas_call | solution.py:286
  248.3 9.9 %collective-permute-done.22.refs_6_ = bf16[768,768]{1,0:T(8,128)(2,1)S(1)} collective-permute-done((bf16[768,768]{1,0:T(8,128)(2,1)S(1)}, bf16[768,768]{1,0:T(8,128)(2,1)S(1)}, u32[]{:S(2)}, u32[]{:S(2)}) %collective-permute-start.22) | collective-permute-done | bytes 1179680 | tf_op jit(solution)/shard_map/ppermute | solution.py:491
  258.2 6.9 %earlier_frame.3 = (bf16[384,768]{1,0:T(8,128)(2,1)S(1)}, bf16[384,768]{1,0:T(8,128)(2,1)S(1)}) custom-call(s32[3]{0:T(128)S(1)} %copy-done.7, bf16[768,768]{1,0:T(8,128)(2,1)S(1)} %get-tuple-element.77.refs_1_, f32[768,768]{1,0:T(8,128)S(1)} %get-tuple-element.78.refs_2_, f32[768,768]{1,0:T(8,128)S(1)} %get-tuple-element.79.refs_3_, ...), custom_call_target="tpu_custom_call" | custom-call | flops 3623878 | bytes 12976 | tf_op jit(solution)/shard_map/earlier_frame/pallas_call | solution.py:347
  265.3 11.0 %collective-permute-done.23.refs_1_ = bf16[384,768]{1,0:T(8,128)(2,1)S(1)} collective-permute-done((bf16[384,768]{1,0:T(8,128)(2,1)S(1)}, bf16[384,768]{1,0:T(8,128)(2,1)S(1)}, u32[]{:S(2)}, u32[]{:S(2)}) %collective-permute-start.23) | collective-permute-done | bytes 589856 | tf_op jit(solution)/shard_map/ppermute | solution.py:491
  276.3 6.3 %collective-permute-done.24.refs_2_ = bf16[384,768]{1,0:T(8,128)(2,1)S(1)} collective-permute-done((bf16[384,768]{1,0:T(8,128)(2,1)S(1)}, bf16[384,768]{1,0:T(8,128)(2,1)S(1)}, u32[]{:S(2)}, u32[]{:S(2)}) %collective-permute-start.24) | collective-permute-done | bytes 589856 | tf_op jit(solution)/shard_map/ppermute | solution.py:491
  286.7 12.2 %collective-permute-done.25.refs_3_ = bf16[384,768]{1,0:T(8,128)(2,1)S(1)} collective-permute-done((bf16[384,768]{1,0:T(8,128)(2,1)S(1)}, bf16[384,768]{1,0:T(8,128)(2,1)S(1)}, u32[]{:S(2)}, u32[]{:S(2)}) %collective-permute-start.25) | collective-permute-done | bytes 589856 | tf_op jit(solution)/shard_map/ppermute | solution.py:491
  301.0 10.5 %collective-permute-done.26.refs_4_ = bf16[384,768]{1,0:T(8,128)(2,1)S(1)} collective-permute-done((bf16[384,768]{1,0:T(8,128)(2,1)S(1)}, bf16[384,768]{1,0:T(8,128)(2,1)S(1)}, u32[]{:S(2)}, u32[]{:S(2)}) %collective-permute-start.26) | collective-permute-done | bytes 589856 | tf_op jit(solution)/shard_map/ppermute | solution.py:491
  313.6 16.0 %projection_start.3.refs_1_ = bf16[768,3072]{1,0:T(8,128)(2,1)S(1)} custom-call(s32[1]{0:T(128)} %bitcast.refs_0_, bf16[384,768]{1,0:T(8,128)(2,1)S(1)} %collective-permute-done.23.refs_1_, bf16[384,768]{1,0:T(8,128)(2,1)S(1)} %collective-permute-done.24.refs_2_, bf16[384,768]{1,0:T(8,128)(2,1)S(1)} %collective-permute-done.25.refs_3_, ...), custom_call_target="tpu_custom_call" | custom-call | flops 10871635 | bytes 18874 | tf_op jit(solution)/shard_map/projection_start/pallas_call | solution.py:454
  329.6 8.3 %collective-permute-done.29.refs_2_ = bf16[768,3072]{1,0:T(8,128)(2,1)S(1)} collective-permute-done((bf16[768,3072]{1,0:T(8,128)(2,1)S(1)}, bf16[768,3072]{1,0:T(8,128)(2,1)S(1)}, u32[]{:S(2)}, u32[]{:S(2)}) %collective-permute-start.29) | collective-permute-done | bytes 4718624 | tf_op jit(solution)/shard_map/ppermute | solution.py:491
  337.9 8.5 %projection_end.3 = bf16[768,3072]{1,0:T(8,128)(2,1)} custom-call(s32[1]{0:T(128)} %bitcast.refs_0_, bf16[768,3072]{1,0:T(8,128)(2,1)S(1)} %projection_start.3.refs_1_, bf16[768,3072]{1,0:T(8,128)(2,1)S(1)} %collective-permute-done.29.refs_2_, f32[1,3072]{1,0:T(1,128)S(1)} %fusion.refs_3_, bf16[192,768]{1,0:T(8,128)(2,1)S(1)} %collective-permute-done.30.refs_4_, ...), custom_call_target="tpu_custom_call" | custom-call | flops 3623878 | bytes 18874 | tf_op jit(solution)/shard_map/projection_end/pallas_call | solution.py:454
  (98 shorter events, 50.0 us)
Async XLA Ops:
  1.8 17.9 %collective-permute-start.2 = (bf16[192,3072]{1,0:T(8,128)(2,1)S(1)}, bf16[192,3072]{1,0:T(8,128)(2,1)}, u32[]{:S(2)}, u32[]{:S(2)}) collective-permute-start(bf16[192,3072]{1,0:T(8,128)(2,1)S(1)} %get-tuple-element.86.refs_6_), channel_id=1, source_target_pairs={{28,30},{29,31},{30,28},{31,29}} | collective-permute-start | bytes 3538952 | tf_op jit(solution)/shard_map/ppermute | solution.py:491
  3.5 16.2 %collective-permute-start.3 = (bf16[192,3072]{1,0:T(8,128)(2,1)S(1)}, bf16[192,3072]{1,0:T(8,128)(2,1)}, u32[]{:S(2)}, u32[]{:S(2)}) collective-permute-start(bf16[192,3072]{1,0:T(8,128)(2,1)S(1)} %get-tuple-element.86.refs_6_), channel_id=1, source_target_pairs={{20,31},{21,30},{22,29},{23,28}} | collective-permute-start | bytes 3538952 | tf_op jit(solution)/shard_map/ppermute | solution.py:491
  5.3 16.4 %collective-permute-start.1 = (bf16[192,3072]{1,0:T(8,128)(2,1)S(1)}, bf16[192,3072]{1,0:T(8,128)(2,1)S(1)}, u32[]{:S(2)}, u32[]{:S(2)}) collective-permute-start(bf16[192,3072]{1,0:T(8,128)(2,1)S(1)} %get-tuple-element.86.refs_6_), channel_id=1, source_target_pairs={{28,29},{29,28},{30,31},{31,30}} | collective-permute-start | bytes 3538952 | tf_op jit(solution)/shard_map/ppermute | solution.py:491
  6.0 11.8 %collective-permute-start = (s32[1]{0:T(128)}, s32[1]{0:T(128)}, u32[]{:S(2)}, u32[]{:S(2)}) collective-permute-start(s32[1]{0:T(128)} %param.10), channel_id=1, source_target_pairs={{0,28},{1,29},{2,30},{3,31},{4,0},{5,1},{6,2},{7,3},{8,4},{9,5},{1... | collective-permute-start | bytes 20 | tf_op jit(solution)/shard_map/ppermute | solution.py:491
  22.1 47.0 %collective-permute-start.4 = (bf16[768,1536]{1,0:T(8,128)(2,1)S(1)}, bf16[768,1536]{1,0:T(8,128)(2,1)S(1)}, u32[]{:S(2)}, u32[]{:S(2)}) collective-permute-start(bf16[768,1536]{1,0:T(8,128)(2,1)S(1)} %copy-done.12), channel_id=1, source_target_pairs={{0,1},{1,0},{2,3},{3,2},{4,5},{5,4},{6,7},{7,6},{8,9},{9,8},{10,11... | collective-permute-start | bytes 7077896 | tf_op jit(solution)/shard_map/ppermute | solution.py:491
  22.6 47.9 %collective-permute-start.5 = (bf16[768,1536]{1,0:T(8,128)(2,1)S(1)}, bf16[768,1536]{1,0:T(8,128)(2,1)S(1)}, u32[]{:S(2)}, u32[]{:S(2)}) collective-permute-start(bf16[768,1536]{1,0:T(8,128)(2,1)S(1)} %copy-done.12), channel_id=1, source_target_pairs={{0,2},{1,3},{2,0},{3,1},{4,6},{5,7},{6,4},{7,5},{8,10},{9,11},{10,... | collective-permute-start | bytes 7077896 | tf_op jit(solution)/shard_map/ppermute | solution.py:491
  43.4 42.0 %collective-permute-start.6 = (bf16[768,768]{1,0:T(8,128)(2,1)S(1)}, bf16[768,768]{1,0:T(8,128)(2,1)S(1)}, u32[]{:S(2)}, u32[]{:S(2)}) collective-permute-start(bf16[768,768]{1,0:T(8,128)(2,1)S(1)} %get-tuple-element.49.key_ref), channel_id=1, source_target_pairs={{0,4},{1,5},{2,6},{3,7},{4,8},{5,9},{6,10},{7,11},{8,12},{9,13},{1... | collective-permute-start | bytes 3538952 | tf_op jit(solution)/shard_map/ppermute | solution.py:491
  45.4 52.7 %collective-permute-start.7 = (bf16[768,768]{1,0:T(8,128)(2,1)S(1)}, bf16[768,768]{1,0:T(8,128)(2,1)S(1)}, u32[]{:S(2)}, u32[]{:S(2)}) collective-permute-start(bf16[768,768]{1,0:T(8,128)(2,1)S(1)} %get-tuple-element.50.value_ref), channel_id=1, source_target_pairs={{0,4},{1,5},{2,6},{3,7},{4,8},{5,9},{6,10},{7,11},{8,12},{9,13},{1... | collective-permute-start | bytes 3538952 | tf_op jit(solution)/shard_map/ppermute | solution.py:491
  98.1 7.9 %collective-permute-start.9 = (bf16[768,1536]{1,0:T(8,128)(2,1)S(1)}, bf16[768,1536]{1,0:T(8,128)(2,1)S(1)}, u32[]{:S(2)}, u32[]{:S(2)}) collective-permute-start(bf16[768,1536]{1,0:T(8,128)(2,1)S(1)} %collective-permute-done.5.refs_6_.refs_9_), channel_id=1, source_target_pairs={{0,4},{1,5},{2,6},{3,7},{4,0},{5,1},{6,2},{7,3},{8,12},{9,13},{10,... | collective-permute-start | bytes 7077896 | tf_op jit(solution)/shard_map/ppermute | solution.py:491
  98.8 27.9 %collective-permute-start.11 = (bf16[384,1536]{1,0:T(8,128)(2,1)S(1)}, bf16[384,1536]{1,0:T(8,128)(2,1)S(1)}, u32[]{:S(2)}, u32[]{:S(2)}) collective-permute-start(bf16[384,1536]{1,0:T(8,128)(2,1)S(1)} %slice.45), channel_id=1, source_target_pairs={{0,2},{1,3},{2,0},{3,1},{4,6},{5,7},{6,4},{7,5},{8,10},{9,11},{10,... | collective-permute-start | bytes 3538952 | tf_op jit(solution)/shard_map/ppermute | solution.py:491
  100.5 27.6 %collective-permute-start.12 = (bf16[384,1536]{1,0:T(8,128)(2,1)S(1)}, bf16[384,1536]{1,0:T(8,128)(2,1)S(1)}, u32[]{:S(2)}, u32[]{:S(2)}) collective-permute-start(bf16[384,1536]{1,0:T(8,128)(2,1)S(1)} %slice.46), channel_id=1, source_target_pairs={{0,1},{1,0},{2,3},{3,2},{4,5},{5,4},{6,7},{7,6},{8,9},{9,8},{10,11... | collective-permute-start | bytes 3538952 | tf_op jit(solution)/shard_map/ppermute | solution.py:491
  113.0 19.3 %collective-permute-start.10 = (bf16[768,768]{1,0:T(8,128)(2,1)S(1)}, bf16[768,768]{1,0:T(8,128)(2,1)S(1)}, u32[]{:S(2)}, u32[]{:S(2)}) collective-permute-start(bf16[768,768]{1,0:T(8,128)(2,1)S(1)} %earlier_frame.2), channel_id=1, source_target_pairs={{0,4},{1,5},{2,6},{3,7},{4,8},{5,9},{6,10},{7,11},{8,12},{9,13},{1... | collective-permute-start | bytes 3538952 | tf_op jit(solution)/shard_map/ppermute | solution.py:491
  132.3 26.0 %collective-permute-start.13 = (bf16[768,768]{1,0:T(8,128)(2,1)S(1)}, bf16[768,768]{1,0:T(8,128)(2,1)S(1)}, u32[]{:S(2)}, u32[]{:S(2)}) collective-permute-start(bf16[768,768]{1,0:T(8,128)(2,1)S(1)} %collective-permute-done.10.refs_1_), channel_id=1, source_target_pairs={{0,1},{1,0},{2,3},{3,2},{4,5},{5,4},{6,7},{7,6},{8,9},{9,8},{10,11... | collective-permute-start | bytes 3538952 | tf_op jit(solution)/shard_map/ppermute | solution.py:491
  134.7 25.7 %collective-permute-start.14 = (bf16[768,768]{1,0:T(8,128)(2,1)S(1)}, bf16[768,768]{1,0:T(8,128)(2,1)S(1)}, u32[]{:S(2)}, u32[]{:S(2)}) collective-permute-start(bf16[768,768]{1,0:T(8,128)(2,1)S(1)} %collective-permute-done.10.refs_1_), channel_id=1, source_target_pairs={{0,2},{1,3},{2,0},{3,1},{4,6},{5,7},{6,4},{7,5},{8,10},{9,11},{10,... | collective-permute-start | bytes 3538952 | tf_op jit(solution)/shard_map/ppermute | solution.py:491
  139.4 57.5 %collective-permute-start.15 = (bf16[768,3072]{1,0:T(8,128)(2,1)}, bf16[768,3072]{1,0:T(8,128)(2,1)}, u32[]{:S(2)}, u32[]{:S(2)}) collective-permute-start(bf16[768,3072]{1,0:T(8,128)(2,1)} %get-tuple-element.71), channel_id=1, source_target_pairs={{0,4},{1,5},{2,6},{3,7},{4,8},{5,9},{6,10},{7,11},{8,12},{9,13},{1... | collective-permute-start | bytes 14155784 | tf_op jit(solution)/shard_map/ppermute | solution.py:491
  161.3 34.2 %collective-permute-start.18 = (bf16[768,1536]{1,0:T(8,128)(2,1)}, bf16[768,1536]{1,0:T(8,128)(2,1)}, u32[]{:S(2)}, u32[]{:S(2)}) collective-permute-start(bf16[768,1536]{1,0:T(8,128)(2,1)} %pad_maximum_fusion.1.refs_6_.refs_8_), channel_id=1, source_target_pairs={{0,4},{1,5},{2,6},{3,7},{4,0},{5,1},{6,2},{7,3},{8,12},{9,13},{10,... | collective-permute-start | bytes 7077896 | tf_op jit(solution)/shard_map/ppermute | solution.py:491
  163.0 43.8 %collective-permute-start.20 = (bf16[384,3072]{1,0:T(8,128)(2,1)}, bf16[384,3072]{1,0:T(8,128)(2,1)}, u32[]{:S(2)}, u32[]{:S(2)}) collective-permute-start(bf16[384,3072]{1,0:T(8,128)(2,1)} %pad_maximum_fusion.2), channel_id=1, source_target_pairs={{28,30},{29,31},{30,28},{31,29}} | collective-permute-start | bytes 7077896 | tf_op jit(solution)/shard_map/ppermute | solution.py:491
  166.0 29.5 %collective-permute-start.16 = (bf16[384,768]{1,0:T(8,128)(2,1)}, bf16[384,768]{1,0:T(8,128)(2,1)}, u32[]{:S(2)}, u32[]{:S(2)}) collective-permute-start(bf16[384,768]{1,0:T(8,128)(2,1)} %slice.50), channel_id=1, source_target_pairs={{0,2},{1,3},{2,0},{3,1},{4,6},{5,7},{6,4},{7,5},{8,10},{9,11},{10,... | collective-permute-start | bytes 1769480 | tf_op jit(solution)/shard_map/ppermute | solution.py:491
  170.1 25.4 %collective-permute-start.17 = (bf16[384,768]{1,0:T(8,128)(2,1)}, bf16[384,768]{1,0:T(8,128)(2,1)}, u32[]{:S(2)}, u32[]{:S(2)}) collective-permute-start(bf16[384,768]{1,0:T(8,128)(2,1)} %slice.51), channel_id=1, source_target_pairs={{0,1},{1,0},{2,3},{3,2},{4,5},{5,4},{6,7},{7,6},{8,9},{9,8},{10,11... | collective-permute-start | bytes 1769480 | tf_op jit(solution)/shard_map/ppermute | solution.py:491
  226.2 22.1 %collective-permute-start.21 = (bf16[768,768]{1,0:T(8,128)(2,1)S(1)}, bf16[768,768]{1,0:T(8,128)(2,1)S(1)}, u32[]{:S(2)}, u32[]{:S(2)}) collective-permute-start(bf16[768,768]{1,0:T(8,128)(2,1)S(1)} %get-tuple-element.75.key_ref), channel_id=1, source_target_pairs={{0,4},{1,5},{2,6},{3,7},{4,8},{5,9},{6,10},{7,11},{8,12},{9,13},{1... | collective-permute-start | bytes 3538952 | tf_op jit(solution)/shard_map/ppermute | solution.py:491
  228.1 30.0 %collective-permute-start.22 = (bf16[768,768]{1,0:T(8,128)(2,1)S(1)}, bf16[768,768]{1,0:T(8,128)(2,1)S(1)}, u32[]{:S(2)}, u32[]{:S(2)}) collective-permute-start(bf16[768,768]{1,0:T(8,128)(2,1)S(1)} %get-tuple-element.76.value_ref), channel_id=1, source_target_pairs={{0,4},{1,5},{2,6},{3,7},{4,8},{5,9},{6,10},{7,11},{8,12},{9,13},{1... | collective-permute-start | bytes 3538952 | tf_op jit(solution)/shard_map/ppermute | solution.py:491
  265.1 11.2 %collective-permute-start.23 = (bf16[384,768]{1,0:T(8,128)(2,1)S(1)}, bf16[384,768]{1,0:T(8,128)(2,1)S(1)}, u32[]{:S(2)}, u32[]{:S(2)}) collective-permute-start(bf16[384,768]{1,0:T(8,128)(2,1)S(1)} %get-tuple-element.81), channel_id=1, source_target_pairs={{0,4},{1,5},{2,6},{3,7},{4,8},{5,9},{6,10},{7,11},{8,12},{9,13},{1... | collective-permute-start | bytes 1769480 | tf_op jit(solution)/shard_map/ppermute | solution.py:491
  265.2 17.4 %collective-permute-start.24 = (bf16[384,768]{1,0:T(8,128)(2,1)S(1)}, bf16[384,768]{1,0:T(8,128)(2,1)S(1)}, u32[]{:S(2)}, u32[]{:S(2)}) collective-permute-start(bf16[384,768]{1,0:T(8,128)(2,1)S(1)} %get-tuple-element.82), channel_id=1, source_target_pairs={{0,4},{1,5},{2,6},{3,7},{4,8},{5,9},{6,10},{7,11},{8,12},{9,13},{1... | collective-permute-start | bytes 1769480 | tf_op jit(solution)/shard_map/ppermute | solution.py:491
  282.6 55.3 %collective-permute-start.29 = (bf16[768,3072]{1,0:T(8,128)(2,1)S(1)}, bf16[768,3072]{1,0:T(8,128)(2,1)S(1)}, u32[]{:S(2)}, u32[]{:S(2)}) collective-permute-start(bf16[768,3072]{1,0:T(8,128)(2,1)S(1)} %copy-done.14), channel_id=1, source_target_pairs={{0,4},{1,5},{2,6},{3,7},{4,8},{5,9},{6,10},{7,11},{8,12},{9,13},{1... | collective-permute-start | bytes 14155784 | tf_op jit(solution)/shard_map/ppermute | solution.py:491
  282.6 16.3 %collective-permute-start.25 = (bf16[384,768]{1,0:T(8,128)(2,1)S(1)}, bf16[384,768]{1,0:T(8,128)(2,1)S(1)}, u32[]{:S(2)}, u32[]{:S(2)}) collective-permute-start(bf16[384,768]{1,0:T(8,128)(2,1)S(1)} %collective-permute-done.23.refs_1_), channel_id=1, source_target_pairs={{0,1},{1,0},{2,3},{3,2},{4,5},{5,4},{6,7},{7,6},{8,9},{9,8},{10,11... | collective-permute-start | bytes 1769480 | tf_op jit(solution)/shard_map/ppermute | solution.py:491
  284.1 16.3 %collective-permute-start.27 = (bf16[384,768]{1,0:T(8,128)(2,1)S(1)}, bf16[384,768]{1,0:T(8,128)(2,1)S(1)}, u32[]{:S(2)}, u32[]{:S(2)}) collective-permute-start(bf16[384,768]{1,0:T(8,128)(2,1)S(1)} %collective-permute-done.23.refs_1_), channel_id=1, source_target_pairs={{0,2},{1,3},{2,0},{3,1},{4,6},{5,7},{6,4},{7,5},{8,10},{9,11},{10,... | collective-permute-start | bytes 1769480 | tf_op jit(solution)/shard_map/ppermute | solution.py:491
  284.4 27.1 %collective-permute-start.26 = (bf16[384,768]{1,0:T(8,128)(2,1)S(1)}, bf16[384,768]{1,0:T(8,128)(2,1)S(1)}, u32[]{:S(2)}, u32[]{:S(2)}) collective-permute-start(bf16[384,768]{1,0:T(8,128)(2,1)S(1)} %collective-permute-done.24.refs_2_), channel_id=1, source_target_pairs={{0,1},{1,0},{2,3},{3,2},{4,5},{5,4},{6,7},{7,6},{8,9},{9,8},{10,11... | collective-permute-start | bytes 1769480 | tf_op jit(solution)/shard_map/ppermute | solution.py:491
  285.0 27.0 %collective-permute-start.28 = (bf16[384,768]{1,0:T(8,128)(2,1)S(1)}, bf16[384,768]{1,0:T(8,128)(2,1)S(1)}, u32[]{:S(2)}, u32[]{:S(2)}) collective-permute-start(bf16[384,768]{1,0:T(8,128)(2,1)S(1)} %collective-permute-done.24.refs_2_), channel_id=1, source_target_pairs={{0,2},{1,3},{2,0},{3,1},{4,6},{5,7},{6,4},{7,5},{8,10},{9,11},{10,... | collective-permute-start | bytes 1769480 | tf_op jit(solution)/shard_map/ppermute | solution.py:491
  298.9 30.7 %collective-permute-start.30 = (bf16[192,768]{1,0:T(8,128)(2,1)S(1)}, bf16[192,768]{1,0:T(8,128)(2,1)S(1)}, u32[]{:S(2)}, u32[]{:S(2)}) collective-permute-start(bf16[192,768]{1,0:T(8,128)(2,1)S(1)} %slice.58), channel_id=1, source_target_pairs={{0,2},{1,3},{2,0},{3,1},{4,6},{5,7},{6,4},{7,5},{8,10},{9,11},{10,... | collective-permute-start | bytes 884744 | tf_op jit(solution)/shard_map/ppermute | solution.py:491
  300.4 29.2 %collective-permute-start.31 = (bf16[192,768]{1,0:T(8,128)(2,1)S(1)}, bf16[192,768]{1,0:T(8,128)(2,1)S(1)}, u32[]{:S(2)}, u32[]{:S(2)}) collective-permute-start(bf16[192,768]{1,0:T(8,128)(2,1)S(1)} %slice.59), channel_id=1, source_target_pairs={{0,1},{1,0},{2,3},{3,2},{4,5},{5,4},{6,7},{7,6},{8,9},{9,8},{10,11... | collective-permute-start | bytes 884744 | tf_op jit(solution)/shard_map/ppermute | solution.py:491
  311.5 18.1 %collective-permute-start.32 = (bf16[192,768]{1,0:T(8,128)(2,1)S(1)}, bf16[192,768]{1,0:T(8,128)(2,1)S(1)}, u32[]{:S(2)}, u32[]{:S(2)}) collective-permute-start(bf16[192,768]{1,0:T(8,128)(2,1)S(1)} %slice.60), channel_id=1, source_target_pairs={{0,2},{1,3},{2,0},{3,1},{4,6},{5,7},{6,4},{7,5},{8,10},{9,11},{10,... | collective-permute-start | bytes 884744 | tf_op jit(solution)/shard_map/ppermute | solution.py:491
  312.0 17.6 %collective-permute-start.33 = (bf16[192,768]{1,0:T(8,128)(2,1)S(1)}, bf16[192,768]{1,0:T(8,128)(2,1)S(1)}, u32[]{:S(2)}, u32[]{:S(2)}) collective-permute-start(bf16[192,768]{1,0:T(8,128)(2,1)S(1)} %slice.61), channel_id=1, source_target_pairs={{0,1},{1,0},{2,3},{3,2},{4,5},{5,4},{6,7},{7,6},{8,9},{9,8},{10,11... | collective-permute-start | bytes 884744 | tf_op jit(solution)/shard_map/ppermute | solution.py:491
  (18 other events, 188.7 us)

commit v10 on v9

--- a/solution.py
+++ b/solution.py
@@ -94,8 +94,8 @@
         def _():
             copy = pltpu.make_async_copy(z_any, state_ref, sem.at[0])
             copy.start()
+            copy.wait()
             start_weights()
-            copy.wait()
 
         @pl.when(info_ref[0] != 0)
         def _():
@@ -587,28 +587,29 @@
         query, *own = own_attention(gains, normed, qkv_weight, key, value)
         if not final:
             query, mine = lax.optimization_barrier((query, mine))
+            theirs = [sibling(block) for block in mine]
+        attended = earlier_attention(
+            info, query, *own, *earlier, CHUNKS if final else 1
+        )
+        if not final:
             mine_corners = [
                 jnp.concatenate(parts, axis=0) for parts in two_hops(mine, *mesh_sizes)
             ]
-            mine, earlier = lax.optimization_barrier((mine, earlier))
-            theirs = [sibling(block) for block in mine]
-            query, theirs = lax.optimization_barrier((query, theirs))
-        attended = earlier_attention(
-            info, query, *own, *earlier, CHUNKS if final else 1
-        )
         senders = range(queue_size) if final else to_next
         targets = range(queue_size if final else queue_size - 1)
         attended = [ring(block, senders) for block in attended]
-        sent_state, _ = lax.optimization_barrier((state, attended))
+        sent_state, attended = lax.optimization_barrier((state, attended))
         resid = ring(sent_state, senders)
         if not final:
-            attended, mine_corners = lax.optimization_barrier((attended, mine_corners))
+            attended, mine_corners, theirs = lax.optimization_barrier(
+                (attended, mine_corners, theirs)
+            )
+            theirs_corners = [sibling(block) for block in mine_corners]
         near = [one_hop(block, *mesh_sizes, targets) for block in attended]
         if not final:
-            noise, mine_corners, near = lax.optimization_barrier(
-                (fresh_noise[step_index + 1], mine_corners, near)
+            near, theirs_corners, noise = lax.optimization_barrier(
+                (near, theirs_corners, fresh_noise[step_index + 1])
             )
-            theirs_corners = [sibling(block) for block in mine_corners]
             noise_pieces = gather_noise(noise, False)
         beyond = [two_hops(blocks, *mesh_sizes, targets) for blocks in near]
         direct = [attended] + [list(parts) for parts in zip(*near)]

time: 347 us -> 351 us (1.012)
  waiting for transfers between devices: 133 us -> 141 us
  Pallas kernels: 139 us -> 134 us
  local copies, waits for them, and re-layouts: 12.3 us -> 16 us
    ppermute x34, waiting for transfers between devices: 133 us -> 141 us  [send(): return lax.ppermute(block, AXES, pairs)]
    pallas_call x2, Pallas kernels: 38.6 us -> 33 us  [project_keys_values(): pl.pallas_call(functools.partial(key_value_kernel, half=half), grid_spec=...]
  transfers between devices with their start and end apart: 34 -> 34, of which waited for: 19 -> 17; matrix products, arithmetic and copies ran while one was open for 4% -> 4% of each run, Pallas kernels for 30% -> 29%
where the time goes in v10:
time: 351 us; the launch traced here: 350 us
  waiting for transfers between devices  141 us (40%)
  Pallas kernels  134 us (38%)
  starting transfers between devices  49.9 us (14%)
  local copies, waits for them, and re-layouts  16 us (5%)
  other arithmetic  6.77 us (2%)
    ppermute x34, waiting for transfers between devices, send(): return lax.ppermute(block, AXES, pairs)  141 us
    pallas_call x4, Pallas kernels, output_projection(): pl.pallas_call(functools.partial(output_kernel, part_counts=tuple((len(p)...  50.5 us
    ppermute x34, starting transfers between devices, send(): return lax.ppermute(block, AXES, pairs)  49.9 us
    pallas_call x2, Pallas kernels, own_attention(): pl.pallas_call(own_kernel, grid=(head_cols // cols,), in_specs=[pl.BlockS...  36.4 us
    pallas_call x2, Pallas kernels, project_keys_values(): pl.pallas_call(functools.partial(key_value_kernel, half=half), grid_spec=...  33 us
    pallas_call x2, Pallas kernels, earlier_attention(): pl.pallas_call(functools.partial(earlier_kernel, chunks=chunks), grid_spe...  13.9 us
  transfers between devices with their start and end apart: 34, of which 17 were waited for; matrix products, arithmetic and copies ran while one was open for 4% of the time, Pallas kernels for 29%

profile of v10, /device:TPU:0, one launch (start us, length us, event | category | flops | bytes accessed | tf_op | source)
XLA Modules:
  0.0 350.3 jit_solution(17123508314446815322)
XLA Ops:
  0.0 2.8 slice_bitcast_fusion
  7.0 7.9 %collective-permute-start = (s32[1]{0:T(128)}, s32[1]{0:T(128)}, u32[]{:S(2)}, u32[]{:S(2)}) collective-permute-start(s32[1]{0:T(128)} %param.10), channel_id=1, source_target_pairs={{0,28},{1,29},{2,30},{3,31},{4,0},{5,1},{6,2},{7,3},{8,4},{9,5},{1... | collective-permute-start | bytes 20 | tf_op jit(solution)/shard_map/ppermute | solution.py:491
  14.9 3.2 constant_dynamic-slice_fusion
  26.0 16.5 %norm_keys_values.2 = (bf16[768,768]{1,0:T(8,128)(2,1)S(1)}, bf16[768,768]{1,0:T(8,128)(2,1)S(1)}, bf16[768,3072]{1,0:T(8,128)(2,1)S(1)}, bf16[768,3072]{1,0:T(8,128)(2,1)}) custom-call(s32[3]{0:T(128)S(1)} %copy-done.6, f32[1,3072]{1,0:T(1,128)S(1)} %get-tuple-element.84.refs_1_, f32[1,3072]{1,0:T(1,128)S(1)} %get-tuple-element.83.refs_2_, ...), custom_call_target="tpu_custom_call" | custom-call | flops 7247757 | bytes 25952 | tf_op jit(solution)/shard_map/norm_keys_values/pallas_call | solution.py:176
  46.4 18.2 %queries_own_frame.2 = (bf16[768,768]{1,0:T(8,128)(2,1)S(1)}, f32[768,768]{1,0:T(8,128)S(1)}, f32[768,768]{1,0:T(8,128)S(1)}, f32[768,768]{1,0:T(8,128)S(1)}) custom-call(f32[2,128]{1,0:T(2,128)S(1)} %pad_maximum_fusion.3.refs_3_.gain_ref, bf16[768,3072]{1,0:T(8,128)(2,1)S(1)} %get-tuple-element.47.normed_ref, ...), custom_call_target="tpu_custom_call" | custom-call | flops 7247757 | bytes 20054 | tf_op jit(solution)/shard_map/queries_own_frame/pallas_call | solution.py:286
  64.6 3.7 %collective-permute-done.4.refs_5_.refs_8_ = bf16[768,1536]{1,0:T(8,128)(2,1)} collective-permute-done((bf16[768,1536]{1,0:T(8,128)(2,1)}, bf16[768,1536]{1,0:T(8,128)(2,1)}, u32[]{:S(2)}, u32[]{:S(2)}) %collective-permute-start.4) | collective-permute-done | bytes 2359328 | tf_op jit(solution)/shard_map/ppermute | solution.py:491
  70.2 24.2 %collective-permute-done.6.refs_5_ = bf16[768,768]{1,0:T(8,128)(2,1)S(1)} collective-permute-done((bf16[768,768]{1,0:T(8,128)(2,1)S(1)}, bf16[768,768]{1,0:T(8,128)(2,1)S(1)}, u32[]{:S(2)}, u32[]{:S(2)}) %collective-permute-start.6) | collective-permute-done | bytes 1179680 | tf_op jit(solution)/shard_map/ppermute | solution.py:491
  94.4 12.6 %collective-permute-done.7.refs_6_ = bf16[768,768]{1,0:T(8,128)(2,1)S(1)} collective-permute-done((bf16[768,768]{1,0:T(8,128)(2,1)S(1)}, bf16[768,768]{1,0:T(8,128)(2,1)S(1)}, u32[]{:S(2)}, u32[]{:S(2)}) %collective-permute-start.7) | collective-permute-done | bytes 1179680 | tf_op jit(solution)/shard_map/ppermute | solution.py:491
  107.1 6.9 %earlier_frame.2 = bf16[768,768]{1,0:T(8,128)(2,1)S(1)} custom-call(s32[3]{0:T(128)S(1)} %copy-done.6, bf16[768,768]{1,0:T(8,128)(2,1)S(1)} %get-tuple-element.52.refs_1_, f32[768,768]{1,0:T(8,128)S(1)} %get-tuple-element.53.refs_2_, f32[768,768]{1,0:T(8,128)S(1)} %get-tuple-element.54.refs_3_, f32[768,768]{1,0:T(8,128)S(1)} %get-tuple-element.55.refs_4_, ...), custom_call_target="tpu_custom_call" | custom-call | flops 3623878 | bytes 12976 | tf_op jit(solution)/shard_map/earlier_frame/pallas_call | solution.py:347
  120.5 12.8 %collective-permute-done.8.refs_1_ = bf16[768,768]{1,0:T(8,128)(2,1)S(1)} collective-permute-done((bf16[768,768]{1,0:T(8,128)(2,1)S(1)}, bf16[768,768]{1,0:T(8,128)(2,1)S(1)}, u32[]{:S(2)}, u32[]{:S(2)}) %collective-permute-start.8) | collective-permute-done | bytes 1179680 | tf_op jit(solution)/shard_map/ppermute | solution.py:491
  135.7 3.4 collective-permute-start.13
  139.1 3.2 collective-permute-start.14
  142.4 1.9 collective-permute-start.16
  144.3 21.6 %collective-permute-done.13.refs_2_ = bf16[768,768]{1,0:T(8,128)(2,1)S(1)} collective-permute-done((bf16[768,768]{1,0:T(8,128)(2,1)S(1)}, bf16[768,768]{1,0:T(8,128)(2,1)S(1)}, u32[]{:S(2)}, u32[]{:S(2)}) %collective-permute-start.13) | collective-permute-done | bytes 1179680 | tf_op jit(solution)/shard_map/ppermute | solution.py:491
  166.0 3.1 collective-permute-done.14.refs_3_
  171.6 2.3 collective-permute-start.20
  174.7 3.2 collective-permute-start.17
  178.9 2.4 collective-permute-start.18
  187.3 16.0 %projection_start.2.refs_1_ = bf16[768,3072]{1,0:T(8,128)(2,1)S(1)} custom-call(s32[1]{0:T(128)} %bitcast.refs_0_, bf16[768,768]{1,0:T(8,128)(2,1)S(1)} %copy-done.3, bf16[768,768]{1,0:T(8,128)(2,1)S(1)} %collective-permute-done.13.refs_2_, bf16[768,768]{1,0:T(8,128)(2,1)S(1)} %copy-done.1, bf16[768,3072]{1,0:T(8,128)(2,1)} %refs_7_.1, ...), custom_call_target="tpu_custom_call" | custom-call | flops 10871635 | bytes 18874 | tf_op jit(solution)/shard_map/projection_start/pallas_call | solution.py:454
  203.3 9.9 %projection_end.2.refs_5_ = bf16[768,3072]{1,0:T(8,128)(2,1)} custom-call(s32[1]{0:T(128)} %bitcast.refs_0_, bf16[768,3072]{1,0:T(8,128)(2,1)S(1)} %projection_start.2.refs_1_, bf16[768,3072]{1,0:T(8,128)(2,1)} %collective-permute-done.16.refs_2_, f32[1,3072]{1,0:T(1,128)S(1)} %fusion.refs_3_, bf16[384,768]{1,0:T(8,128)(2,1)} %collective-permute-done.17.refs_4_, ...), custom_call_target="tpu_custom_call" | custom-call | flops 3623878 | bytes 18874 | tf_op jit(solution)/shard_map/projection_end/pallas_call | solution.py:454
  213.3 16.5 %norm_keys_values.3 = (bf16[768,768]{1,0:T(8,128)(2,1)S(1)}, bf16[768,768]{1,0:T(8,128)(2,1)S(1)}, bf16[768,3072]{1,0:T(8,128)(2,1)S(1)}, bf16[768,3072]{1,0:T(8,128)(2,1)}) custom-call(s32[3]{0:T(128)S(1)} %copy-done.7, f32[1,3072]{1,0:T(1,128)S(1)} %copy-done.5, f32[1,3072]{1,0:T(1,128)S(1)} %get-tuple-element.83.refs_2_, ...), custom_call_target="tpu_custom_call" | custom-call | flops 7247757 | bytes 25952 | tf_op jit(solution)/shard_map/norm_keys_values/pallas_call | solution.py:176
  229.8 1.9 collective-permute-start.21
  233.7 18.2 %queries_own_frame.3 = (bf16[768,768]{1,0:T(8,128)(2,1)S(1)}, f32[768,768]{1,0:T(8,128)S(1)}, f32[768,768]{1,0:T(8,128)S(1)}, f32[768,768]{1,0:T(8,128)S(1)}) custom-call(f32[2,128]{1,0:T(2,128)S(1)} %pad_maximum_fusion.3.refs_3_.gain_ref, bf16[768,3072]{1,0:T(8,128)(2,1)S(1)} %get-tuple-element.69.normed_ref, ...), custom_call_target="tpu_custom_call" | custom-call | flops 7247757 | bytes 20054 | tf_op jit(solution)/shard_map/queries_own_frame/pallas_call | solution.py:286
  251.9 9.9 %collective-permute-done.22.refs_6_ = bf16[768,768]{1,0:T(8,128)(2,1)S(1)} collective-permute-done((bf16[768,768]{1,0:T(8,128)(2,1)S(1)}, bf16[768,768]{1,0:T(8,128)(2,1)S(1)}, u32[]{:S(2)}, u32[]{:S(2)}) %collective-permute-start.22) | collective-permute-done | bytes 1179680 | tf_op jit(solution)/shard_map/ppermute | solution.py:491
  261.8 6.9 %earlier_frame.3 = (bf16[384,768]{1,0:T(8,128)(2,1)S(1)}, bf16[384,768]{1,0:T(8,128)(2,1)S(1)}) custom-call(s32[3]{0:T(128)S(1)} %copy-done.7, bf16[768,768]{1,0:T(8,128)(2,1)S(1)} %get-tuple-element.72.refs_1_, f32[768,768]{1,0:T(8,128)S(1)} %get-tuple-element.73.refs_2_, f32[768,768]{1,0:T(8,128)S(1)} %get-tuple-element.74.refs_3_, ...), custom_call_target="tpu_custom_call" | custom-call | flops 3623878 | bytes 12976 | tf_op jit(solution)/shard_map/earlier_frame/pallas_call | solution.py:347
  268.9 11.0 %collective-permute-done.23.refs_1_ = bf16[384,768]{1,0:T(8,128)(2,1)S(1)} collective-permute-done((bf16[384,768]{1,0:T(8,128)(2,1)S(1)}, bf16[384,768]{1,0:T(8,128)(2,1)S(1)}, u32[]{:S(2)}, u32[]{:S(2)}) %collective-permute-start.23) | collective-permute-done | bytes 589856 | tf_op jit(solution)/shard_map/ppermute | solution.py:491
  279.9 6.3 %collective-permute-done.24.refs_2_ = bf16[384,768]{1,0:T(8,128)(2,1)S(1)} collective-permute-done((bf16[384,768]{1,0:T(8,128)(2,1)S(1)}, bf16[384,768]{1,0:T(8,128)(2,1)S(1)}, u32[]{:S(2)}, u32[]{:S(2)}) %collective-permute-start.24) | collective-permute-done | bytes 589856 | tf_op jit(solution)/shard_map/ppermute | solution.py:491
  290.3 12.2 %collective-permute-done.25.refs_3_ = bf16[384,768]{1,0:T(8,128)(2,1)S(1)} collective-permute-done((bf16[384,768]{1,0:T(8,128)(2,1)S(1)}, bf16[384,768]{1,0:T(8,128)(2,1)S(1)}, u32[]{:S(2)}, u32[]{:S(2)}) %collective-permute-start.25) | collective-permute-done | bytes 589856 | tf_op jit(solution)/shard_map/ppermute | solution.py:491
  304.9 10.3 %collective-permute-done.26.refs_4_ = bf16[384,768]{1,0:T(8,128)(2,1)S(1)} collective-permute-done((bf16[384,768]{1,0:T(8,128)(2,1)S(1)}, bf16[384,768]{1,0:T(8,128)(2,1)S(1)}, u32[]{:S(2)}, u32[]{:S(2)}) %collective-permute-start.26) | collective-permute-done | bytes 589856 | tf_op jit(solution)/shard_map/ppermute | solution.py:491
  317.5 16.0 %projection_start.3.refs_1_ = bf16[768,3072]{1,0:T(8,128)(2,1)S(1)} custom-call(s32[1]{0:T(128)} %bitcast.refs_0_, bf16[384,768]{1,0:T(8,128)(2,1)S(1)} %collective-permute-done.23.refs_1_, bf16[384,768]{1,0:T(8,128)(2,1)S(1)} %collective-permute-done.24.refs_2_, bf16[384,768]{1,0:T(8,128)(2,1)S(1)} %collective-permute-done.25.refs_3_, ...), custom_call_target="tpu_custom_call" | custom-call | flops 10871635 | bytes 18874 | tf_op jit(solution)/shard_map/projection_start/pallas_call | solution.py:454
  333.6 8.0 %collective-permute-done.29.refs_2_ = bf16[768,3072]{1,0:T(8,128)(2,1)S(1)} collective-permute-done((bf16[768,3072]{1,0:T(8,128)(2,1)S(1)}, bf16[768,3072]{1,0:T(8,128)(2,1)S(1)}, u32[]{:S(2)}, u32[]{:S(2)}) %collective-permute-start.29) | collective-permute-done | bytes 4718624 | tf_op jit(solution)/shard_map/ppermute | solution.py:491
  341.6 8.6 %projection_end.3 = bf16[768,3072]{1,0:T(8,128)(2,1)} custom-call(s32[1]{0:T(128)} %bitcast.refs_0_, bf16[768,3072]{1,0:T(8,128)(2,1)S(1)} %projection_start.3.refs_1_, bf16[768,3072]{1,0:T(8,128)(2,1)S(1)} %collective-permute-done.29.refs_2_, f32[1,3072]{1,0:T(1,128)S(1)} %fusion.refs_3_, bf16[192,768]{1,0:T(8,128)(2,1)S(1)} %collective-permute-done.30.refs_4_, ...), custom_call_target="tpu_custom_call" | custom-call | flops 3623878 | bytes 18874 | tf_op jit(solution)/shard_map/projection_end/pallas_call | solution.py:454
  (98 shorter events, 45.3 us)
Async XLA Ops:
  2.8 15.3 %collective-permute-start.2 = (bf16[192,3072]{1,0:T(8,128)(2,1)}, bf16[192,3072]{1,0:T(8,128)(2,1)S(1)}, u32[]{:S(2)}, u32[]{:S(2)}) collective-permute-start(bf16[192,3072]{1,0:T(8,128)(2,1)} %get-tuple-element.82.refs_6_), channel_id=1, source_target_pairs={{28,30},{29,31},{30,28},{31,29}} | collective-permute-start | bytes 3538952 | tf_op jit(solution)/shard_map/ppermute | solution.py:491
  3.6 15.6 %collective-permute-start.3 = (bf16[192,3072]{1,0:T(8,128)(2,1)}, bf16[192,3072]{1,0:T(8,128)(2,1)}, u32[]{:S(2)}, u32[]{:S(2)}) collective-permute-start(bf16[192,3072]{1,0:T(8,128)(2,1)} %get-tuple-element.82.refs_6_), channel_id=1, source_target_pairs={{20,31},{21,30},{22,29},{23,28}} | collective-permute-start | bytes 3538952 | tf_op jit(solution)/shard_map/ppermute | solution.py:491
  5.3 15.7 %collective-permute-start.1 = (bf16[192,3072]{1,0:T(8,128)(2,1)}, bf16[192,3072]{1,0:T(8,128)(2,1)}, u32[]{:S(2)}, u32[]{:S(2)}) collective-permute-start(bf16[192,3072]{1,0:T(8,128)(2,1)} %get-tuple-element.82.refs_6_), channel_id=1, source_target_pairs={{28,29},{29,28},{30,31},{31,30}} | collective-permute-start | bytes 3538952 | tf_op jit(solution)/shard_map/ppermute | solution.py:491
  7.0 15.7 %collective-permute-start = (s32[1]{0:T(128)}, s32[1]{0:T(128)}, u32[]{:S(2)}, u32[]{:S(2)}) collective-permute-start(s32[1]{0:T(128)} %param.10), channel_id=1, source_target_pairs={{0,28},{1,29},{2,30},{3,31},{4,0},{5,1},{6,2},{7,3},{8,4},{9,5},{1... | collective-permute-start | bytes 20 | tf_op jit(solution)/shard_map/ppermute | solution.py:491
  21.0 47.3 %collective-permute-start.4 = (bf16[768,1536]{1,0:T(8,128)(2,1)}, bf16[768,1536]{1,0:T(8,128)(2,1)}, u32[]{:S(2)}, u32[]{:S(2)}) collective-permute-start(bf16[768,1536]{1,0:T(8,128)(2,1)} %constant_dynamic-slice_fusion), channel_id=1, source_target_pairs={{0,1},{1,0},{2,3},{3,2},{4,5},{5,4},{6,7},{7,6},{8,9},{9,8},{10,11... | collective-permute-start | bytes 7077896 | tf_op jit(solution)/shard_map/ppermute | solution.py:491
  21.6 48.2 %collective-permute-start.5 = (bf16[768,1536]{1,0:T(8,128)(2,1)}, bf16[768,1536]{1,0:T(8,128)(2,1)}, u32[]{:S(2)}, u32[]{:S(2)}) collective-permute-start(bf16[768,1536]{1,0:T(8,128)(2,1)} %constant_dynamic-slice_fusion), channel_id=1, source_target_pairs={{0,2},{1,3},{2,0},{3,1},{4,6},{5,7},{6,4},{7,5},{8,10},{9,11},{10,... | collective-permute-start | bytes 7077896 | tf_op jit(solution)/shard_map/ppermute | solution.py:491
  42.5 51.9 %collective-permute-start.6 = (bf16[768,768]{1,0:T(8,128)(2,1)S(1)}, bf16[768,768]{1,0:T(8,128)(2,1)S(1)}, u32[]{:S(2)}, u32[]{:S(2)}) collective-permute-start(bf16[768,768]{1,0:T(8,128)(2,1)S(1)} %get-tuple-element.48.key_ref), channel_id=1, source_target_pairs={{0,4},{1,5},{2,6},{3,7},{4,8},{5,9},{6,10},{7,11},{8,12},{9,13},{1... | collective-permute-start | bytes 3538952 | tf_op jit(solution)/shard_map/ppermute | solution.py:491
  44.5 62.6 %collective-permute-start.7 = (bf16[768,768]{1,0:T(8,128)(2,1)S(1)}, bf16[768,768]{1,0:T(8,128)(2,1)S(1)}, u32[]{:S(2)}, u32[]{:S(2)}) collective-permute-start(bf16[768,768]{1,0:T(8,128)(2,1)S(1)} %get-tuple-element.49.value_ref), channel_id=1, source_target_pairs={{0,4},{1,5},{2,6},{3,7},{4,8},{5,9},{6,10},{7,11},{8,12},{9,13},{1... | collective-permute-start | bytes 3538952 | tf_op jit(solution)/shard_map/ppermute | solution.py:491
  69.7 65.9 %collective-permute-start.11 = (bf16[768,1536]{1,0:T(8,128)(2,1)}, bf16[768,1536]{1,0:T(8,128)(2,1)S(1)}, u32[]{:S(2)}, u32[]{:S(2)}) collective-permute-start(bf16[768,1536]{1,0:T(8,128)(2,1)} %collective-permute-done.4.refs_5_.refs_8_), channel_id=1, source_target_pairs={{0,4},{1,5},{2,6},{3,7},{4,0},{5,1},{6,2},{7,3},{8,12},{9,13},{10,... | collective-permute-start | bytes 7077896 | tf_op jit(solution)/shard_map/ppermute | solution.py:491
  69.7 65.9 %collective-permute-start.12 = (bf16[768,1536]{1,0:T(8,128)(2,1)}, bf16[768,1536]{1,0:T(8,128)(2,1)S(1)}, u32[]{:S(2)}, u32[]{:S(2)}) collective-permute-start(bf16[768,1536]{1,0:T(8,128)(2,1)} %collective-permute-done.5.refs_6_.refs_9_), channel_id=1, source_target_pairs={{0,4},{1,5},{2,6},{3,7},{4,0},{5,1},{6,2},{7,3},{8,12},{9,13},{10,... | collective-permute-start | bytes 7077896 | tf_op jit(solution)/shard_map/ppermute | solution.py:491
  114.0 19.3 %collective-permute-start.8 = (bf16[768,768]{1,0:T(8,128)(2,1)S(1)}, bf16[768,768]{1,0:T(8,128)(2,1)S(1)}, u32[]{:S(2)}, u32[]{:S(2)}) collective-permute-start(bf16[768,768]{1,0:T(8,128)(2,1)S(1)} %earlier_frame.2), channel_id=1, source_target_pairs={{0,4},{1,5},{2,6},{3,7},{4,8},{5,9},{6,10},{7,11},{8,12},{9,13},{1... | collective-permute-start | bytes 3538952 | tf_op jit(solution)/shard_map/ppermute | solution.py:491
  118.6 16.3 %collective-permute-start.10 = (bf16[384,1536]{1,0:T(8,128)(2,1)S(1)}, bf16[384,1536]{1,0:T(8,128)(2,1)S(1)}, u32[]{:S(2)}, u32[]{:S(2)}) collective-permute-start(bf16[384,1536]{1,0:T(8,128)(2,1)S(1)} %slice.46), channel_id=1, source_target_pairs={{0,1},{1,0},{2,3},{3,2},{4,5},{5,4},{6,7},{7,6},{8,9},{9,8},{10,11... | collective-permute-start | bytes 3538952 | tf_op jit(solution)/shard_map/ppermute | solution.py:491
  119.2 16.2 %collective-permute-start.9 = (bf16[384,1536]{1,0:T(8,128)(2,1)S(1)}, bf16[384,1536]{1,0:T(8,128)(2,1)S(1)}, u32[]{:S(2)}, u32[]{:S(2)}) collective-permute-start(bf16[384,1536]{1,0:T(8,128)(2,1)S(1)} %slice.45), channel_id=1, source_target_pairs={{0,2},{1,3},{2,0},{3,1},{4,6},{5,7},{6,4},{7,5},{8,10},{9,11},{10,... | collective-permute-start | bytes 3538952 | tf_op jit(solution)/shard_map/ppermute | solution.py:491
  135.6 33.5 %collective-permute-start.15 = (bf16[768,1536]{1,0:T(8,128)(2,1)S(1)}, bf16[768,1536]{1,0:T(8,128)(2,1)S(1)}, u32[]{:S(2)}, u32[]{:S(2)}) collective-permute-start(bf16[768,1536]{1,0:T(8,128)(2,1)S(1)} %pad_maximum_fusion.1.refs_6_.refs_8_), channel_id=1, source_target_pairs={{0,4},{1,5},{2,6},{3,7},{4,0},{5,1},{6,2},{7,3},{8,12},{9,13},{10,... | collective-permute-start | bytes 7077896 | tf_op jit(solution)/shard_map/ppermute | solution.py:491
  135.7 30.3 %collective-permute-start.13 = (bf16[768,768]{1,0:T(8,128)(2,1)S(1)}, bf16[768,768]{1,0:T(8,128)(2,1)S(1)}, u32[]{:S(2)}, u32[]{:S(2)}) collective-permute-start(bf16[768,768]{1,0:T(8,128)(2,1)S(1)} %collective-permute-done.8.refs_1_), channel_id=1, source_target_pairs={{0,1},{1,0},{2,3},{3,2},{4,5},{5,4},{6,7},{7,6},{8,9},{9,8},{10,11... | collective-permute-start | bytes 3538952 | tf_op jit(solution)/shard_map/ppermute | solution.py:491
  139.1 30.0 %collective-permute-start.14 = (bf16[768,768]{1,0:T(8,128)(2,1)S(1)}, bf16[768,768]{1,0:T(8,128)(2,1)S(1)}, u32[]{:S(2)}, u32[]{:S(2)}) collective-permute-start(bf16[768,768]{1,0:T(8,128)(2,1)S(1)} %collective-permute-done.8.refs_1_), channel_id=1, source_target_pairs={{0,2},{1,3},{2,0},{3,1},{4,6},{5,7},{6,4},{7,5},{8,10},{9,11},{10,... | collective-permute-start | bytes 3538952 | tf_op jit(solution)/shard_map/ppermute | solution.py:491
  142.4 60.9 %collective-permute-start.16 = (bf16[768,3072]{1,0:T(8,128)(2,1)}, bf16[768,3072]{1,0:T(8,128)(2,1)}, u32[]{:S(2)}, u32[]{:S(2)}) collective-permute-start(bf16[768,3072]{1,0:T(8,128)(2,1)} %get-tuple-element.65), channel_id=1, source_target_pairs={{0,4},{1,5},{2,6},{3,7},{4,8},{5,9},{6,10},{7,11},{8,12},{9,13},{1... | collective-permute-start | bytes 14155784 | tf_op jit(solution)/shard_map/ppermute | solution.py:491
  171.6 41.6 %collective-permute-start.20 = (bf16[384,3072]{1,0:T(8,128)(2,1)}, bf16[384,3072]{1,0:T(8,128)(2,1)}, u32[]{:S(2)}, u32[]{:S(2)}) collective-permute-start(bf16[384,3072]{1,0:T(8,128)(2,1)} %pad_maximum_fusion.2), channel_id=1, source_target_pairs={{28,30},{29,31},{30,28},{31,29}} | collective-permute-start | bytes 7077896 | tf_op jit(solution)/shard_map/ppermute | solution.py:491
  174.7 28.6 %collective-permute-start.17 = (bf16[384,768]{1,0:T(8,128)(2,1)}, bf16[384,768]{1,0:T(8,128)(2,1)}, u32[]{:S(2)}, u32[]{:S(2)}) collective-permute-start(bf16[384,768]{1,0:T(8,128)(2,1)} %slice.50), channel_id=1, source_target_pairs={{0,2},{1,3},{2,0},{3,1},{4,6},{5,7},{6,4},{7,5},{8,10},{9,11},{10,... | collective-permute-start | bytes 1769480 | tf_op jit(solution)/shard_map/ppermute | solution.py:491
  178.9 24.5 %collective-permute-start.18 = (bf16[384,768]{1,0:T(8,128)(2,1)}, bf16[384,768]{1,0:T(8,128)(2,1)}, u32[]{:S(2)}, u32[]{:S(2)}) collective-permute-start(bf16[384,768]{1,0:T(8,128)(2,1)} %slice.51), channel_id=1, source_target_pairs={{0,1},{1,0},{2,3},{3,2},{4,5},{5,4},{6,7},{7,6},{8,9},{9,8},{10,11... | collective-permute-start | bytes 1769480 | tf_op jit(solution)/shard_map/ppermute | solution.py:491
  229.8 22.1 %collective-permute-start.21 = (bf16[768,768]{1,0:T(8,128)(2,1)S(1)}, bf16[768,768]{1,0:T(8,128)(2,1)S(1)}, u32[]{:S(2)}, u32[]{:S(2)}) collective-permute-start(bf16[768,768]{1,0:T(8,128)(2,1)S(1)} %get-tuple-element.70.key_ref), channel_id=1, source_target_pairs={{0,4},{1,5},{2,6},{3,7},{4,8},{5,9},{6,10},{7,11},{8,12},{9,13},{1... | collective-permute-start | bytes 3538952 | tf_op jit(solution)/shard_map/ppermute | solution.py:491
  231.8 30.0 %collective-permute-start.22 = (bf16[768,768]{1,0:T(8,128)(2,1)S(1)}, bf16[768,768]{1,0:T(8,128)(2,1)S(1)}, u32[]{:S(2)}, u32[]{:S(2)}) collective-permute-start(bf16[768,768]{1,0:T(8,128)(2,1)S(1)} %get-tuple-element.71.value_ref), channel_id=1, source_target_pairs={{0,4},{1,5},{2,6},{3,7},{4,8},{5,9},{6,10},{7,11},{8,12},{9,13},{1... | collective-permute-start | bytes 3538952 | tf_op jit(solution)/shard_map/ppermute | solution.py:491
  268.8 17.4 %collective-permute-start.24 = (bf16[384,768]{1,0:T(8,128)(2,1)S(1)}, bf16[384,768]{1,0:T(8,128)(2,1)S(1)}, u32[]{:S(2)}, u32[]{:S(2)}) collective-permute-start(bf16[384,768]{1,0:T(8,128)(2,1)S(1)} %get-tuple-element.77), channel_id=1, source_target_pairs={{0,4},{1,5},{2,6},{3,7},{4,8},{5,9},{6,10},{7,11},{8,12},{9,13},{1... | collective-permute-start | bytes 1769480 | tf_op jit(solution)/shard_map/ppermute | solution.py:491
  286.2 55.3 %collective-permute-start.29 = (bf16[768,3072]{1,0:T(8,128)(2,1)S(1)}, bf16[768,3072]{1,0:T(8,128)(2,1)S(1)}, u32[]{:S(2)}, u32[]{:S(2)}) collective-permute-start(bf16[768,3072]{1,0:T(8,128)(2,1)S(1)} %copy-done.14), channel_id=1, source_target_pairs={{0,4},{1,5},{2,6},{3,7},{4,8},{5,9},{6,10},{7,11},{8,12},{9,13},{1... | collective-permute-start | bytes 14155784 | tf_op jit(solution)/shard_map/ppermute | solution.py:491
  286.2 16.3 %collective-permute-start.25 = (bf16[384,768]{1,0:T(8,128)(2,1)S(1)}, bf16[384,768]{1,0:T(8,128)(2,1)S(1)}, u32[]{:S(2)}, u32[]{:S(2)}) collective-permute-start(bf16[384,768]{1,0:T(8,128)(2,1)S(1)} %collective-permute-done.23.refs_1_), channel_id=1, source_target_pairs={{0,1},{1,0},{2,3},{3,2},{4,5},{5,4},{6,7},{7,6},{8,9},{9,8},{10,11... | collective-permute-start | bytes 1769480 | tf_op jit(solution)/shard_map/ppermute | solution.py:491
  287.7 16.3 %collective-permute-start.27 = (bf16[384,768]{1,0:T(8,128)(2,1)S(1)}, bf16[384,768]{1,0:T(8,128)(2,1)S(1)}, u32[]{:S(2)}, u32[]{:S(2)}) collective-permute-start(bf16[384,768]{1,0:T(8,128)(2,1)S(1)} %collective-permute-done.23.refs_1_), channel_id=1, source_target_pairs={{0,2},{1,3},{2,0},{3,1},{4,6},{5,7},{6,4},{7,5},{8,10},{9,11},{10,... | collective-permute-start | bytes 1769480 | tf_op jit(solution)/shard_map/ppermute | solution.py:491
  288.4 26.7 %collective-permute-start.26 = (bf16[384,768]{1,0:T(8,128)(2,1)S(1)}, bf16[384,768]{1,0:T(8,128)(2,1)S(1)}, u32[]{:S(2)}, u32[]{:S(2)}) collective-permute-start(bf16[384,768]{1,0:T(8,128)(2,1)S(1)} %collective-permute-done.24.refs_2_), channel_id=1, source_target_pairs={{0,1},{1,0},{2,3},{3,2},{4,5},{5,4},{6,7},{7,6},{8,9},{9,8},{10,11... | collective-permute-start | bytes 1769480 | tf_op jit(solution)/shard_map/ppermute | solution.py:491
  288.9 27.7 %collective-permute-start.28 = (bf16[384,768]{1,0:T(8,128)(2,1)S(1)}, bf16[384,768]{1,0:T(8,128)(2,1)S(1)}, u32[]{:S(2)}, u32[]{:S(2)}) collective-permute-start(bf16[384,768]{1,0:T(8,128)(2,1)S(1)} %collective-permute-done.24.refs_2_), channel_id=1, source_target_pairs={{0,2},{1,3},{2,0},{3,1},{4,6},{5,7},{6,4},{7,5},{8,10},{9,11},{10,... | collective-permute-start | bytes 1769480 | tf_op jit(solution)/shard_map/ppermute | solution.py:491
  302.5 31.0 %collective-permute-start.30 = (bf16[192,768]{1,0:T(8,128)(2,1)S(1)}, bf16[192,768]{1,0:T(8,128)(2,1)S(1)}, u32[]{:S(2)}, u32[]{:S(2)}) collective-permute-start(bf16[192,768]{1,0:T(8,128)(2,1)S(1)} %slice.58), channel_id=1, source_target_pairs={{0,2},{1,3},{2,0},{3,1},{4,6},{5,7},{6,4},{7,5},{8,10},{9,11},{10,... | collective-permute-start | bytes 884744 | tf_op jit(solution)/shard_map/ppermute | solution.py:491
  304.0 29.5 %collective-permute-start.31 = (bf16[192,768]{1,0:T(8,128)(2,1)S(1)}, bf16[192,768]{1,0:T(8,128)(2,1)S(1)}, u32[]{:S(2)}, u32[]{:S(2)}) collective-permute-start(bf16[192,768]{1,0:T(8,128)(2,1)S(1)} %slice.59), channel_id=1, source_target_pairs={{0,1},{1,0},{2,3},{3,2},{4,5},{5,4},{6,7},{7,6},{8,9},{9,8},{10,11... | collective-permute-start | bytes 884744 | tf_op jit(solution)/shard_map/ppermute | solution.py:491
  315.1 18.4 %collective-permute-start.32 = (bf16[192,768]{1,0:T(8,128)(2,1)S(1)}, bf16[192,768]{1,0:T(8,128)(2,1)S(1)}, u32[]{:S(2)}, u32[]{:S(2)}) collective-permute-start(bf16[192,768]{1,0:T(8,128)(2,1)S(1)} %slice.60), channel_id=1, source_target_pairs={{0,2},{1,3},{2,0},{3,1},{4,6},{5,7},{6,4},{7,5},{8,10},{9,11},{10,... | collective-permute-start | bytes 884744 | tf_op jit(solution)/shard_map/ppermute | solution.py:491
  316.7 16.9 %collective-permute-start.33 = (bf16[192,768]{1,0:T(8,128)(2,1)S(1)}, bf16[192,768]{1,0:T(8,128)(2,1)S(1)}, u32[]{:S(2)}, u32[]{:S(2)}) collective-permute-start(bf16[192,768]{1,0:T(8,128)(2,1)S(1)} %slice.61), channel_id=1, source_target_pairs={{0,1},{1,0},{2,3},{3,2},{4,5},{5,4},{6,7},{7,6},{8,9},{9,8},{10,11... | collective-permute-start | bytes 884744 | tf_op jit(solution)/shard_map/ppermute | solution.py:491
  (18 other events, 228.8 us)

commit v11 on v10

--- a/solution.py
+++ b/solution.py
@@ -524,7 +524,6 @@
     mesh_sizes = (queue_size, tensor_size)
     queue_index = lax.axis_index("queue")
     tensor_index = lax.axis_index("tensor")
-    is_last = queue_index == queue_size - 1
     parity = (queue_index % 2).astype(jnp.int32)[None]
 
     def ring(block, frames=None):
@@ -533,35 +532,19 @@
     def sibling(block):
         return send(block, lambda q, t: (q ^ 1, t), *mesh_sizes)
 
-    worked_level = send(levels, lambda q, t: ((q - 1) % queue_size, t), *mesh_sizes)[0]
-
-    def gather_noise(noise, at_once):
-        args = (*mesh_sizes, [queue_size - 1])
+    def gather_noise(noise):
+        args = (*mesh_sizes, [0])
         half = tensor_size // 2
         near = send(noise, lambda q, t: (q, t ^ 1), *args)
-        pairs = []
-        if at_once:
-            for j in range(1, half):
-                straight = send(noise, away(j, half), *args)
-                across = send(
-                    noise,
-                    lambda q, t: away(j, half)(queue_size - 1, t ^ 1),
-                    *mesh_sizes,
-                    [max(queue_size - 3, 0)],
-                )
-                pairs.append(jnp.concatenate([straight, across], axis=0))
-        else:
-            pair = jnp.concatenate([noise, near], axis=0)
-            pairs = [send(pair, away(j, half), *args) for j in range(1, half)]
-        return [near, *pairs]
-
+        pair = jnp.concatenate([noise, near], axis=0)
+        return [near, *[send(pair, away(j, half), *args) for j in range(1, half)]]
+
+    to_next = range(queue_size - 1)
+    frame = ring(latents[0], to_next)
     noise = fresh_noise[0]
-    noise_pieces = gather_noise(noise, True)
+    noise_pieces = gather_noise(noise)
     half_weight = lax.dynamic_slice(
         out_weight, (0, parity[0] * (width // 2)), (out_weight.shape[0], width // 2)
-    )
-    half_weight, latents, noise_pieces = lax.optimization_barrier(
-        (half_weight, latents, noise_pieces)
     )
     mine = one_hop(half_weight, *mesh_sizes)
 
@@ -570,47 +553,46 @@
         rate = lax.dynamic_slice(step_size, (level,), (1,))[:, None]
         return row[:, :width], 1.0 + row[:, width : 2 * width], rate * row[:, 2 * width :]
 
-    shift, scale1, _ = modulation(worked_level)
-    _, _, gate = modulation(levels[0])
-    info = jnp.stack([is_last, tensor_index // 2, tensor_index % 2])
+    shift, scale1, own_gate = modulation(levels[0])
+    arriving_gate = modulation(ring(levels, to_next)[0])[2]
+    info = jnp.stack([queue_index == 0, tensor_index // 2, tensor_index % 2])
     info = info.astype(jnp.int32)
     gains = jnp.stack([q_gain * SCORE_SCALE, k_gain])
 
-    frame = latents[0]
     for step_index in range(STEPS):
         final = step_index == STEPS - 1
         key, value, normed, state = project_keys_values(
             info, scale1, shift, gains, qkv_weight, frame, noise, noise_pieces
         )
-        to_next = [q for q in range(queue_size) if q != queue_size - 2]
+        if not final:
+            value, mine = lax.optimization_barrier((value, mine))
         earlier = [ring(block, to_next) for block in (key, value)]
         query, *own = own_attention(gains, normed, qkv_weight, key, value)
         if not final:
-            query, mine = lax.optimization_barrier((query, mine))
-            theirs = [sibling(block) for block in mine]
+            mine_corners = two_hops(mine, *mesh_sizes)
+            earlier, mine_corners = lax.optimization_barrier((earlier, mine_corners))
         attended = earlier_attention(
             info, query, *own, *earlier, CHUNKS if final else 1
         )
+        targets = range(queue_size) if final else range(1, queue_size)
+        resid, gate = state, own_gate
         if not final:
-            mine_corners = [
-                jnp.concatenate(parts, axis=0) for parts in two_hops(mine, *mesh_sizes)
-            ]
-        senders = range(queue_size) if final else to_next
-        targets = range(queue_size if final else queue_size - 1)
-        attended = [ring(block, senders) for block in attended]
-        sent_state, attended = lax.optimization_barrier((state, attended))
-        resid = ring(sent_state, senders)
-        if not final:
-            attended, mine_corners, theirs = lax.optimization_barrier(
-                (attended, mine_corners, theirs)
+            attended, mine, mine_corners = lax.optimization_barrier(
+                (attended, mine, mine_corners)
             )
+            mine_corners = [jnp.concatenate(parts, axis=0) for parts in mine_corners]
+            theirs = [sibling(block) for block in mine]
             theirs_corners = [sibling(block) for block in mine_corners]
+            attended = [ring(block, to_next) for block in attended]
+            sent_state, attended = lax.optimization_barrier((state, attended))
+            resid, gate = ring(sent_state, to_next), arriving_gate
+            attended, theirs, theirs_corners = lax.optimization_barrier(
+                (attended, theirs, theirs_corners)
+            )
         near = [one_hop(block, *mesh_sizes, targets) for block in attended]
         if not final:
-            near, theirs_corners, noise = lax.optimization_barrier(
-                (near, theirs_corners, fresh_noise[step_index + 1])
-            )
-            noise_pieces = gather_noise(noise, False)
+            near, noise = lax.optimization_barrier((near, fresh_noise[step_index + 1]))
+            noise_pieces = gather_noise(noise)
         beyond = [two_hops(blocks, *mesh_sizes, targets) for blocks in near]
         direct = [attended] + [list(parts) for parts in zip(*near)]
         corners = [[half for parts in p for half in parts] for p in zip(*beyond)]

time: 351 us -> 327 us (0.932)
  the two profiles are of different devices: /device:TPU:0 before, /device:TPU:8 now
where the time goes in v11:
time: 327 us; the launch traced here: 326 us
  Pallas kernels  134 us (41%)
  waiting for transfers between devices  117 us (36%)
  starting transfers between devices  50.9 us (16%)
  local copies, waits for them, and re-layouts  13 us (4%)
  other arithmetic  8.85 us (3%)
    ppermute x31, waiting for transfers between devices, send(): return lax.ppermute(block, AXES, pairs)  117 us
    ppermute x31, starting transfers between devices, send(): return lax.ppermute(block, AXES, pairs)  50.9 us
    pallas_call x4, Pallas kernels, output_projection(): pl.pallas_call(functools.partial(output_kernel, part_counts=tuple((len(p)...  50.5 us
    pallas_call x2, Pallas kernels, own_attention(): pl.pallas_call(own_kernel, grid=(head_cols // cols,), in_specs=[pl.BlockS...  36.4 us
    pallas_call x2, Pallas kernels, project_keys_values(): pl.pallas_call(functools.partial(key_value_kernel, half=half), grid_spec=...  33 us
    pallas_call x2, Pallas kernels, earlier_attention(): pl.pallas_call(functools.partial(earlier_kernel, chunks=chunks), grid_spe...  13.9 us
  transfers between devices with their start and end apart: 31, of which 10 were waited for; matrix products, arithmetic and copies ran while one was open for 5% of the time, Pallas kernels for 29%

profile of v11, /device:TPU:8, one launch (start us, length us, event | category | flops | bytes accessed | tf_op | source)
XLA Modules:
  0.0 326.4 jit_solution(8443348933555592141)
XLA Ops:
  6.1 2.2 collective-permute-start.2
  12.8 3.0 collective-permute-start.16
  18.8 37.0 %collective-permute-done.16 = s32[1]{0:T(128)} collective-permute-done((s32[1]{0:T(128)}, s32[1]{0:T(128)}, u32[]{:S(2)}, u32[]{:S(2)}) %collective-permute-start.16) | collective-permute-done | bytes 36 | tf_op jit(solution)/shard_map/ppermute | solution.py:491
  58.2 1.9 slice_multiply_fusion
  60.9 16.5 %norm_keys_values.2 = (bf16[768,768]{1,0:T(8,128)(2,1)S(1)}, bf16[768,768]{1,0:T(8,128)(2,1)S(1)}, bf16[768,3072]{1,0:T(8,128)(2,1)S(1)}, bf16[768,3072]{1,0:T(8,128)(2,1)}) custom-call(s32[3]{0:T(128)S(1)} %copy-done.7, f32[1,3072]{1,0:T(1,128)S(1)} %get-tuple-element.87.refs_1_, f32[1,3072]{1,0:T(1,128)S(1)} %get-tuple-element.86.refs_2_, ...), custom_call_target="tpu_custom_call" | custom-call | flops 7247757 | bytes 25952 | tf_op jit(solution)/shard_map/norm_keys_values/pallas_call | solution.py:176
  85.2 3.6 %collective-permute-start.5 = (bf16[768,768]{1,0:T(8,128)(2,1)S(1)}, bf16[768,768]{1,0:T(8,128)(2,1)S(1)}, u32[]{:S(2)}, u32[]{:S(2)}) collective-permute-start(bf16[768,768]{1,0:T(8,128)(2,1)S(1)} %get-tuple-element.46.key_ref), channel_id=1, source_target_pairs={{0,4},{1,5},{2,6},{3,7},{4,8},{5,9},{6,10},{7,11},{8,12},{9,13},{1... | collective-permute-start | bytes 3538952 | tf_op jit(solution)/shard_map/ppermute | solution.py:491
  88.8 18.2 %queries_own_frame.2 = (bf16[768,768]{1,0:T(8,128)(2,1)S(1)}, f32[768,768]{1,0:T(8,128)S(1)}, f32[768,768]{1,0:T(8,128)S(1)}, f32[768,768]{1,0:T(8,128)S(1)}) custom-call(f32[2,128]{1,0:T(2,128)S(1)} %pad_maximum_fusion.2.refs_3_.gain_ref, bf16[768,3072]{1,0:T(8,128)(2,1)S(1)} %get-tuple-element.45.normed_ref, ...), custom_call_target="tpu_custom_call" | custom-call | flops 7247757 | bytes 20054 | tf_op jit(solution)/shard_map/queries_own_frame/pallas_call | solution.py:286
  108.6 4.9 %collective-permute-done.5.refs_5_ = bf16[768,768]{1,0:T(8,128)(2,1)S(1)} collective-permute-done((bf16[768,768]{1,0:T(8,128)(2,1)S(1)}, bf16[768,768]{1,0:T(8,128)(2,1)S(1)}, u32[]{:S(2)}, u32[]{:S(2)}) %collective-permute-start.5) | collective-permute-done | bytes 1179680 | tf_op jit(solution)/shard_map/ppermute | solution.py:491
  113.4 6.9 %earlier_frame.2 = bf16[768,768]{1,0:T(8,128)(2,1)S(1)} custom-call(s32[3]{0:T(128)S(1)} %copy-done.7, bf16[768,768]{1,0:T(8,128)(2,1)S(1)} %get-tuple-element.49.refs_1_, f32[768,768]{1,0:T(8,128)S(1)} %get-tuple-element.50.refs_2_, f32[768,768]{1,0:T(8,128)S(1)} %get-tuple-element.51.refs_3_, f32[768,768]{1,0:T(8,128)S(1)} %get-tuple-element.52.refs_4_, ...), custom_call_target="tpu_custom_call" | custom-call | flops 3623878 | bytes 12976 | tf_op jit(solution)/shard_map/earlier_frame/pallas_call | solution.py:347
  121.2 2.3 collective-permute-start.9
  123.5 23.9 %collective-permute-done.9.refs_1_ = bf16[768,768]{1,0:T(8,128)(2,1)S(1)} collective-permute-done((bf16[768,768]{1,0:T(8,128)(2,1)S(1)}, bf16[768,768]{1,0:T(8,128)(2,1)S(1)}, u32[]{:S(2)}, u32[]{:S(2)}) %collective-permute-start.9) | collective-permute-done | bytes 1179680 | tf_op jit(solution)/shard_map/ppermute | solution.py:491
  147.5 2.9 collective-permute-start.13
  150.3 2.4 collective-permute-start.14
  153.9 1.9 collective-permute-start.15
  155.8 11.9 %collective-permute-done.13.refs_2_ = bf16[768,768]{1,0:T(8,128)(2,1)S(1)} collective-permute-done((bf16[768,768]{1,0:T(8,128)(2,1)S(1)}, bf16[768,768]{1,0:T(8,128)(2,1)S(1)}, u32[]{:S(2)}, u32[]{:S(2)}) %collective-permute-start.13) | collective-permute-done | bytes 1179680 | tf_op jit(solution)/shard_map/ppermute | solution.py:491
  167.7 3.1 collective-permute-done.14.refs_3_
  173.3 2.1 collective-permute-start.20
  176.3 2.4 collective-permute-start.17
  179.5 3.0 collective-permute-start.18
  186.6 16.0 %projection_start.2.refs_1_ = bf16[768,3072]{1,0:T(8,128)(2,1)S(1)} custom-call(s32[1]{0:T(128)} %bitcast.refs_0_, bf16[768,768]{1,0:T(8,128)(2,1)S(1)} %copy-done.3, bf16[768,768]{1,0:T(8,128)(2,1)S(1)} %collective-permute-done.13.refs_2_, bf16[768,768]{1,0:T(8,128)(2,1)S(1)} %copy-done.1, bf16[768,3072]{1,0:T(8,128)(2,1)} %refs_7_.1, ...), custom_call_target="tpu_custom_call" | custom-call | flops 10871635 | bytes 18874 | tf_op jit(solution)/shard_map/projection_start/pallas_call | solution.py:454
  202.7 6.9 %collective-permute-done.15.refs_2_ = bf16[768,3072]{1,0:T(8,128)(2,1)} collective-permute-done((bf16[768,3072]{1,0:T(8,128)(2,1)}, bf16[768,3072]{1,0:T(8,128)(2,1)}, u32[]{:S(2)}, u32[]{:S(2)}) %collective-permute-start.15) | collective-permute-done | bytes 4718624 | tf_op jit(solution)/shard_map/ppermute | solution.py:491
  209.6 9.9 %projection_end.2.refs_5_ = bf16[768,3072]{1,0:T(8,128)(2,1)} custom-call(s32[1]{0:T(128)} %bitcast.refs_0_, bf16[768,3072]{1,0:T(8,128)(2,1)S(1)} %projection_start.2.refs_1_, bf16[768,3072]{1,0:T(8,128)(2,1)} %collective-permute-done.15.refs_2_, f32[1,3072]{1,0:T(1,128)S(1)} %fusion.refs_3_, bf16[384,768]{1,0:T(8,128)(2,1)} %collective-permute-done.17.refs_4_, ...), custom_call_target="tpu_custom_call" | custom-call | flops 3623878 | bytes 18874 | tf_op jit(solution)/shard_map/projection_end/pallas_call | solution.py:454
  219.5 16.5 %norm_keys_values.3 = (bf16[768,768]{1,0:T(8,128)(2,1)S(1)}, bf16[768,768]{1,0:T(8,128)(2,1)S(1)}, bf16[768,3072]{1,0:T(8,128)(2,1)S(1)}, bf16[768,3072]{1,0:T(8,128)(2,1)}) custom-call(s32[3]{0:T(128)S(1)} %copy-done.8, f32[1,3072]{1,0:T(1,128)S(1)} %copy-done.5, f32[1,3072]{1,0:T(1,128)S(1)} %get-tuple-element.86.refs_2_, ...), custom_call_target="tpu_custom_call" | custom-call | flops 7247757 | bytes 25952 | tf_op jit(solution)/shard_map/norm_keys_values/pallas_call | solution.py:176
  236.1 1.9 collective-permute-start.21
  238.0 1.9 collective-permute-start.22
  239.9 18.2 %queries_own_frame.3 = (bf16[768,768]{1,0:T(8,128)(2,1)S(1)}, f32[768,768]{1,0:T(8,128)S(1)}, f32[768,768]{1,0:T(8,128)S(1)}, f32[768,768]{1,0:T(8,128)S(1)}) custom-call(f32[2,128]{1,0:T(2,128)S(1)} %pad_maximum_fusion.2.refs_3_.gain_ref, bf16[768,3072]{1,0:T(8,128)(2,1)S(1)} %get-tuple-element.73.normed_ref, ...), custom_call_target="tpu_custom_call" | custom-call | flops 7247757 | bytes 20054 | tf_op jit(solution)/shard_map/queries_own_frame/pallas_call | solution.py:286
  258.1 8.1 %collective-permute-done.22.refs_6_ = bf16[768,768]{1,0:T(8,128)(2,1)S(1)} collective-permute-done((bf16[768,768]{1,0:T(8,128)(2,1)S(1)}, bf16[768,768]{1,0:T(8,128)(2,1)S(1)}, u32[]{:S(2)}, u32[]{:S(2)}) %collective-permute-start.22) | collective-permute-done | bytes 1179680 | tf_op jit(solution)/shard_map/ppermute | solution.py:491
  266.2 6.9 %earlier_frame.3 = (bf16[384,768]{1,0:T(8,128)(2,1)S(1)}, bf16[384,768]{1,0:T(8,128)(2,1)S(1)}) custom-call(s32[3]{0:T(128)S(1)} %copy-done.8, bf16[768,768]{1,0:T(8,128)(2,1)S(1)} %get-tuple-element.76.refs_1_, f32[768,768]{1,0:T(8,128)S(1)} %get-tuple-element.77.refs_2_, f32[768,768]{1,0:T(8,128)S(1)} %get-tuple-element.78.refs_3_, ...), custom_call_target="tpu_custom_call" | custom-call | flops 3623878 | bytes 12976 | tf_op jit(solution)/shard_map/earlier_frame/pallas_call | solution.py:347
  277.3 12.2 %collective-permute-done.23.refs_3_ = bf16[384,768]{1,0:T(8,128)(2,1)S(1)} collective-permute-done((bf16[384,768]{1,0:T(8,128)(2,1)S(1)}, bf16[384,768]{1,0:T(8,128)(2,1)S(1)}, u32[]{:S(2)}, u32[]{:S(2)}) %collective-permute-start.23) | collective-permute-done | bytes 589856 | tf_op jit(solution)/shard_map/ppermute | solution.py:491
  292.3 7.0 %collective-permute-done.24.refs_4_ = bf16[384,768]{1,0:T(8,128)(2,1)S(1)} collective-permute-done((bf16[384,768]{1,0:T(8,128)(2,1)S(1)}, bf16[384,768]{1,0:T(8,128)(2,1)S(1)}, u32[]{:S(2)}, u32[]{:S(2)}) %collective-permute-start.24) | collective-permute-done | bytes 589856 | tf_op jit(solution)/shard_map/ppermute | solution.py:491
  301.5 16.0 %projection_start.3.refs_1_ = bf16[768,3072]{1,0:T(8,128)(2,1)S(1)} custom-call(s32[1]{0:T(128)} %bitcast.refs_0_, bf16[384,768]{1,0:T(8,128)(2,1)S(1)} %get-tuple-element.80.refs_1_, bf16[384,768]{1,0:T(8,128)(2,1)S(1)} %get-tuple-element.81.refs_2_, bf16[384,768]{1,0:T(8,128)(2,1)S(1)} %collective-permute-done.23.refs_3_, ...), custom_call_target="tpu_custom_call" | custom-call | flops 10871635 | bytes 18874 | tf_op jit(solution)/shard_map/projection_start/pallas_call | solution.py:454
  317.6 8.6 %projection_end.3 = bf16[768,3072]{1,0:T(8,128)(2,1)} custom-call(s32[1]{0:T(128)} %bitcast.refs_0_, bf16[768,3072]{1,0:T(8,128)(2,1)S(1)} %projection_start.3.refs_1_, bf16[768,3072]{1,0:T(8,128)(2,1)S(1)} %bitcast.21, f32[1,3072]{1,0:T(1,128)S(1)} %copy-done.6, bf16[192,768]{1,0:T(8,128)(2,1)S(1)} %collective-permute-done.27.refs_4_, ...), custom_call_target="tpu_custom_call" | custom-call | flops 3623878 | bytes 18874 | tf_op jit(solution)/shard_map/projection_end/pallas_call | solution.py:454
  (100 shorter events, 42.8 us)
Async XLA Ops:
  0.0 60.2 %collective-permute-start = (bf16[768,3072]{1,0:T(8,128)(2,1)}, bf16[768,3072]{1,0:T(8,128)(2,1)}, u32[]{:S(2)}, u32[]{:S(2)}) collective-permute-start(bf16[768,3072]{1,0:T(8,128)(2,1)} %bitcast.23), channel_id=1, source_target_pairs={{0,4},{1,5},{2,6},{3,7},{4,8},{5,9},{6,10},{7,11},{8,12},{9,13},{1... | collective-permute-start | bytes 14155784 | tf_op jit(solution)/shard_map/ppermute | solution.py:491
  3.7 0.8 collective-permute-start.1
  6.1 51.5 %copy-start.14 = (f32[50]{0:T(128)S(1)}, f32[50]{0:T(128)}, u32[]{:S(2)}) copy-start(f32[50]{0:T(128)} %param.12) | copy-start | bytes 604
  6.1 54.1 %collective-permute-start.2 = (bf16[384,3072]{1,0:T(8,128)(2,1)}, bf16[384,3072]{1,0:T(8,128)(2,1)}, u32[]{:S(2)}, u32[]{:S(2)}) collective-permute-start(bf16[384,3072]{1,0:T(8,128)(2,1)} %pad_maximum_fusion), channel_id=1, source_target_pairs={{0,2},{1,3},{2,0},{3,1}} | collective-permute-start | bytes 7077896 | tf_op jit(solution)/shard_map/ppermute | solution.py:491
  9.8 67.6 %collective-permute-start.3 = (bf16[768,1536]{1,0:T(8,128)(2,1)}, bf16[768,1536]{1,0:T(8,128)(2,1)}, u32[]{:S(2)}, u32[]{:S(2)}) collective-permute-start(bf16[768,1536]{1,0:T(8,128)(2,1)} %constant_dynamic-slice_fusion), channel_id=1, source_target_pairs={{0,1},{1,0},{2,3},{3,2},{4,5},{5,4},{6,7},{7,6},{8,9},{9,8},{10,11... | collective-permute-start | bytes 7077896 | tf_op jit(solution)/shard_map/ppermute | solution.py:491
  11.3 66.1 %collective-permute-start.4 = (bf16[768,1536]{1,0:T(8,128)(2,1)}, bf16[768,1536]{1,0:T(8,128)(2,1)}, u32[]{:S(2)}, u32[]{:S(2)}) collective-permute-start(bf16[768,1536]{1,0:T(8,128)(2,1)} %constant_dynamic-slice_fusion), channel_id=1, source_target_pairs={{0,2},{1,3},{2,0},{3,1},{4,6},{5,7},{6,4},{7,5},{8,10},{9,11},{10,... | collective-permute-start | bytes 7077896 | tf_op jit(solution)/shard_map/ppermute | solution.py:491
  12.8 42.9 %collective-permute-start.16 = (s32[1]{0:T(128)}, s32[1]{0:T(128)}, u32[]{:S(2)}, u32[]{:S(2)}) collective-permute-start(s32[1]{0:T(128)} %param.10), channel_id=1, source_target_pairs={{0,4},{1,5},{2,6},{3,7},{4,8},{5,9},{6,10},{7,11},{8,12},{9,13},{1... | collective-permute-start | bytes 20 | tf_op jit(solution)/shard_map/ppermute | solution.py:491
  78.8 28.2 %collective-permute-start.7 = (bf16[384,1536]{1,0:T(8,128)(2,1)S(1)}, bf16[384,1536]{1,0:T(8,128)(2,1)S(1)}, u32[]{:S(2)}, u32[]{:S(2)}) collective-permute-start(bf16[384,1536]{1,0:T(8,128)(2,1)S(1)} %slice.48), channel_id=1, source_target_pairs={{0,2},{1,3},{2,0},{3,1},{4,6},{5,7},{6,4},{7,5},{8,10},{9,11},{10,... | collective-permute-start | bytes 3538952 | tf_op jit(solution)/shard_map/ppermute | solution.py:491
  81.7 26.9 %collective-permute-start.8 = (bf16[384,1536]{1,0:T(8,128)(2,1)S(1)}, bf16[384,1536]{1,0:T(8,128)(2,1)S(1)}, u32[]{:S(2)}, u32[]{:S(2)}) collective-permute-start(bf16[384,1536]{1,0:T(8,128)(2,1)S(1)} %slice.49), channel_id=1, source_target_pairs={{0,1},{1,0},{2,3},{3,2},{4,5},{5,4},{6,7},{7,6},{8,9},{9,8},{10,11... | collective-permute-start | bytes 3538952 | tf_op jit(solution)/shard_map/ppermute | solution.py:491
  83.3 25.3 %collective-permute-start.6 = (bf16[768,768]{1,0:T(8,128)(2,1)S(1)}, bf16[768,768]{1,0:T(8,128)(2,1)S(1)}, u32[]{:S(2)}, u32[]{:S(2)}) collective-permute-start(bf16[768,768]{1,0:T(8,128)(2,1)S(1)} %get-tuple-element.48.value_ref), channel_id=1, source_target_pairs={{0,4},{1,5},{2,6},{3,7},{4,8},{5,9},{6,10},{7,11},{8,12},{9,13},{1... | collective-permute-start | bytes 3538952 | tf_op jit(solution)/shard_map/ppermute | solution.py:491
  85.2 28.2 %collective-permute-start.5 = (bf16[768,768]{1,0:T(8,128)(2,1)S(1)}, bf16[768,768]{1,0:T(8,128)(2,1)S(1)}, u32[]{:S(2)}, u32[]{:S(2)}) collective-permute-start(bf16[768,768]{1,0:T(8,128)(2,1)S(1)} %get-tuple-element.46.key_ref), channel_id=1, source_target_pairs={{0,4},{1,5},{2,6},{3,7},{4,8},{5,9},{6,10},{7,11},{8,12},{9,13},{1... | collective-permute-start | bytes 3538952 | tf_op jit(solution)/shard_map/ppermute | solution.py:491
  120.5 26.9 %collective-permute-start.12 = (bf16[768,1536]{1,0:T(8,128)(2,1)S(1)}, bf16[768,1536]{1,0:T(8,128)(2,1)S(1)}, u32[]{:S(2)}, u32[]{:S(2)}) collective-permute-start(bf16[768,1536]{1,0:T(8,128)(2,1)S(1)} %constant_dynamic-update-slice_fusion.refs_6_.refs_8_), channel_id=1, source_target_pairs={{0,4},{1,5},{2,6},{3,7},{4,0},{5,1},{6,2},{7,3},{8,12},{9,13},{10,... | collective-permute-start | bytes 7077896 | tf_op jit(solution)/shard_map/ppermute | solution.py:491
  120.6 26.8 %collective-permute-start.10 = (bf16[768,1536]{1,0:T(8,128)(2,1)}, bf16[768,1536]{1,0:T(8,128)(2,1)S(1)}, u32[]{:S(2)}, u32[]{:S(2)}) collective-permute-start(bf16[768,1536]{1,0:T(8,128)(2,1)} %collective-permute-done.3.refs_5_.refs_8_), channel_id=1, source_target_pairs={{0,4},{1,5},{2,6},{3,7},{4,0},{5,1},{6,2},{7,3},{8,12},{9,13},{10,... | collective-permute-start | bytes 7077896 | tf_op jit(solution)/shard_map/ppermute | solution.py:491
  121.1 26.3 %collective-permute-start.11 = (bf16[768,1536]{1,0:T(8,128)(2,1)}, bf16[768,1536]{1,0:T(8,128)(2,1)S(1)}, u32[]{:S(2)}, u32[]{:S(2)}) collective-permute-start(bf16[768,1536]{1,0:T(8,128)(2,1)} %collective-permute-done.4.refs_6_.refs_9_), channel_id=1, source_target_pairs={{0,4},{1,5},{2,6},{3,7},{4,0},{5,1},{6,2},{7,3},{8,12},{9,13},{10,... | collective-permute-start | bytes 7077896 | tf_op jit(solution)/shard_map/ppermute | solution.py:491
  121.2 26.2 %collective-permute-start.9 = (bf16[768,768]{1,0:T(8,128)(2,1)S(1)}, bf16[768,768]{1,0:T(8,128)(2,1)S(1)}, u32[]{:S(2)}, u32[]{:S(2)}) collective-permute-start(bf16[768,768]{1,0:T(8,128)(2,1)S(1)} %earlier_frame.2), channel_id=1, source_target_pairs={{0,4},{1,5},{2,6},{3,7},{4,8},{5,9},{6,10},{7,11},{8,12},{9,13},{1... | collective-permute-start | bytes 3538952 | tf_op jit(solution)/shard_map/ppermute | solution.py:491
  147.5 20.3 %collective-permute-start.13 = (bf16[768,768]{1,0:T(8,128)(2,1)S(1)}, bf16[768,768]{1,0:T(8,128)(2,1)S(1)}, u32[]{:S(2)}, u32[]{:S(2)}) collective-permute-start(bf16[768,768]{1,0:T(8,128)(2,1)S(1)} %collective-permute-done.9.refs_1_), channel_id=1, source_target_pairs={{4,5},{5,4},{6,7},{7,6},{8,9},{9,8},{10,11},{11,10},{12,13},{13,12... | collective-permute-start | bytes 3538952 | tf_op jit(solution)/shard_map/ppermute | solution.py:491
  150.3 20.5 %collective-permute-start.14 = (bf16[768,768]{1,0:T(8,128)(2,1)S(1)}, bf16[768,768]{1,0:T(8,128)(2,1)S(1)}, u32[]{:S(2)}, u32[]{:S(2)}) collective-permute-start(bf16[768,768]{1,0:T(8,128)(2,1)S(1)} %collective-permute-done.9.refs_1_), channel_id=1, source_target_pairs={{4,6},{5,7},{6,4},{7,5},{8,10},{9,11},{10,8},{11,9},{12,14},{13,15... | collective-permute-start | bytes 3538952 | tf_op jit(solution)/shard_map/ppermute | solution.py:491
  153.9 55.7 %collective-permute-start.15 = (bf16[768,3072]{1,0:T(8,128)(2,1)}, bf16[768,3072]{1,0:T(8,128)(2,1)}, u32[]{:S(2)}, u32[]{:S(2)}) collective-permute-start(bf16[768,3072]{1,0:T(8,128)(2,1)} %get-tuple-element.70), channel_id=1, source_target_pairs={{0,4},{1,5},{2,6},{3,7},{4,8},{5,9},{6,10},{7,11},{8,12},{9,13},{1... | collective-permute-start | bytes 14155784 | tf_op jit(solution)/shard_map/ppermute | solution.py:491
  170.8 0.9 collective-permute-start.19
  173.3 46.2 %collective-permute-start.20 = (bf16[384,3072]{1,0:T(8,128)(2,1)}, bf16[384,3072]{1,0:T(8,128)(2,1)}, u32[]{:S(2)}, u32[]{:S(2)}) collective-permute-start(bf16[384,3072]{1,0:T(8,128)(2,1)} %pad_maximum_fusion.1), channel_id=1, source_target_pairs={{0,2},{1,3},{2,0},{3,1}} | collective-permute-start | bytes 7077896 | tf_op jit(solution)/shard_map/ppermute | solution.py:491
  176.3 26.4 %collective-permute-start.17 = (bf16[384,768]{1,0:T(8,128)(2,1)}, bf16[384,768]{1,0:T(8,128)(2,1)}, u32[]{:S(2)}, u32[]{:S(2)}) collective-permute-start(bf16[384,768]{1,0:T(8,128)(2,1)} %slice.53), channel_id=1, source_target_pairs={{4,6},{5,7},{6,4},{7,5},{8,10},{9,11},{10,8},{11,9},{12,14},{13,15... | collective-permute-start | bytes 1769480 | tf_op jit(solution)/shard_map/ppermute | solution.py:491
  179.5 23.1 %collective-permute-start.18 = (bf16[384,768]{1,0:T(8,128)(2,1)}, bf16[384,768]{1,0:T(8,128)(2,1)}, u32[]{:S(2)}, u32[]{:S(2)}) collective-permute-start(bf16[384,768]{1,0:T(8,128)(2,1)} %slice.54), channel_id=1, source_target_pairs={{4,5},{5,4},{6,7},{7,6},{8,9},{9,8},{10,11},{11,10},{12,13},{13,12... | collective-permute-start | bytes 1769480 | tf_op jit(solution)/shard_map/ppermute | solution.py:491
  236.1 22.1 %collective-permute-start.21 = (bf16[768,768]{1,0:T(8,128)(2,1)S(1)}, bf16[768,768]{1,0:T(8,128)(2,1)S(1)}, u32[]{:S(2)}, u32[]{:S(2)}) collective-permute-start(bf16[768,768]{1,0:T(8,128)(2,1)S(1)} %get-tuple-element.74.key_ref), channel_id=1, source_target_pairs={{0,4},{1,5},{2,6},{3,7},{4,8},{5,9},{6,10},{7,11},{8,12},{9,13},{1... | collective-permute-start | bytes 3538952 | tf_op jit(solution)/shard_map/ppermute | solution.py:491
  238.0 28.2 %collective-permute-start.22 = (bf16[768,768]{1,0:T(8,128)(2,1)S(1)}, bf16[768,768]{1,0:T(8,128)(2,1)S(1)}, u32[]{:S(2)}, u32[]{:S(2)}) collective-permute-start(bf16[768,768]{1,0:T(8,128)(2,1)S(1)} %get-tuple-element.75.value_ref), channel_id=1, source_target_pairs={{0,4},{1,5},{2,6},{3,7},{4,8},{5,9},{6,10},{7,11},{8,12},{9,13},{1... | collective-permute-start | bytes 3538952 | tf_op jit(solution)/shard_map/ppermute | solution.py:491
  273.2 16.3 %collective-permute-start.23 = (bf16[384,768]{1,0:T(8,128)(2,1)S(1)}, bf16[384,768]{1,0:T(8,128)(2,1)S(1)}, u32[]{:S(2)}, u32[]{:S(2)}) collective-permute-start(bf16[384,768]{1,0:T(8,128)(2,1)S(1)} %get-tuple-element.80.refs_1_), channel_id=1, source_target_pairs={{0,1},{1,0},{2,3},{3,2},{4,5},{5,4},{6,7},{7,6},{8,9},{9,8},{10,11... | collective-permute-start | bytes 1769480 | tf_op jit(solution)/shard_map/ppermute | solution.py:491
  274.3 16.8 %collective-permute-start.25 = (bf16[384,768]{1,0:T(8,128)(2,1)S(1)}, bf16[384,768]{1,0:T(8,128)(2,1)S(1)}, u32[]{:S(2)}, u32[]{:S(2)}) collective-permute-start(bf16[384,768]{1,0:T(8,128)(2,1)S(1)} %get-tuple-element.80.refs_1_), channel_id=1, source_target_pairs={{0,2},{1,3},{2,0},{3,1},{4,6},{5,7},{6,4},{7,5},{8,10},{9,11},{10,... | collective-permute-start | bytes 1769480 | tf_op jit(solution)/shard_map/ppermute | solution.py:491
  275.8 23.4 %collective-permute-start.24 = (bf16[384,768]{1,0:T(8,128)(2,1)S(1)}, bf16[384,768]{1,0:T(8,128)(2,1)S(1)}, u32[]{:S(2)}, u32[]{:S(2)}) collective-permute-start(bf16[384,768]{1,0:T(8,128)(2,1)S(1)} %get-tuple-element.81.refs_2_), channel_id=1, source_target_pairs={{0,1},{1,0},{2,3},{3,2},{4,5},{5,4},{6,7},{7,6},{8,9},{9,8},{10,11... | collective-permute-start | bytes 1769480 | tf_op jit(solution)/shard_map/ppermute | solution.py:491
  276.8 24.1 %collective-permute-start.26 = (bf16[384,768]{1,0:T(8,128)(2,1)S(1)}, bf16[384,768]{1,0:T(8,128)(2,1)S(1)}, u32[]{:S(2)}, u32[]{:S(2)}) collective-permute-start(bf16[384,768]{1,0:T(8,128)(2,1)S(1)} %get-tuple-element.81.refs_2_), channel_id=1, source_target_pairs={{0,2},{1,3},{2,0},{3,1},{4,6},{5,7},{6,4},{7,5},{8,10},{9,11},{10,... | collective-permute-start | bytes 1769480 | tf_op jit(solution)/shard_map/ppermute | solution.py:491
  289.5 28.0 %collective-permute-start.27 = (bf16[192,768]{1,0:T(8,128)(2,1)S(1)}, bf16[192,768]{1,0:T(8,128)(2,1)S(1)}, u32[]{:S(2)}, u32[]{:S(2)}) collective-permute-start(bf16[192,768]{1,0:T(8,128)(2,1)S(1)} %slice.63), channel_id=1, source_target_pairs={{0,2},{1,3},{2,0},{3,1},{4,6},{5,7},{6,4},{7,5},{8,10},{9,11},{10,... | collective-permute-start | bytes 884744 | tf_op jit(solution)/shard_map/ppermute | solution.py:491
  291.1 26.4 %collective-permute-start.28 = (bf16[192,768]{1,0:T(8,128)(2,1)S(1)}, bf16[192,768]{1,0:T(8,128)(2,1)S(1)}, u32[]{:S(2)}, u32[]{:S(2)}) collective-permute-start(bf16[192,768]{1,0:T(8,128)(2,1)S(1)} %slice.64), channel_id=1, source_target_pairs={{0,1},{1,0},{2,3},{3,2},{4,5},{5,4},{6,7},{7,6},{8,9},{9,8},{10,11... | collective-permute-start | bytes 884744 | tf_op jit(solution)/shard_map/ppermute | solution.py:491
  299.3 18.3 %collective-permute-start.29 = (bf16[192,768]{1,0:T(8,128)(2,1)S(1)}, bf16[192,768]{1,0:T(8,128)(2,1)S(1)}, u32[]{:S(2)}, u32[]{:S(2)}) collective-permute-start(bf16[192,768]{1,0:T(8,128)(2,1)S(1)} %slice.65), channel_id=1, source_target_pairs={{0,2},{1,3},{2,0},{3,1},{4,6},{5,7},{6,4},{7,5},{8,10},{9,11},{10,... | collective-permute-start | bytes 884744 | tf_op jit(solution)/shard_map/ppermute | solution.py:491
  300.9 16.7 %collective-permute-start.30 = (bf16[192,768]{1,0:T(8,128)(2,1)S(1)}, bf16[192,768]{1,0:T(8,128)(2,1)S(1)}, u32[]{:S(2)}, u32[]{:S(2)}) collective-permute-start(bf16[192,768]{1,0:T(8,128)(2,1)S(1)} %slice.66), channel_id=1, source_target_pairs={{0,1},{1,0},{2,3},{3,2},{4,5},{5,4},{6,7},{7,6},{8,9},{9,8},{10,11... | collective-permute-start | bytes 884744 | tf_op jit(solution)/shard_map/ppermute | solution.py:491
  (18 other events, 262.6 us)

commit v12 on v11

--- a/solution.py
+++ b/solution.py
@@ -10,7 +10,6 @@
 
 HD = 128
 STEPS = 2
-CHUNKS = 2
 EPS = 1e-6
 AXES = ("queue", "tensor")
 F32 = jnp.float32
@@ -64,7 +63,7 @@
 def key_value_kernel(*refs, half):
     info_ref, scale_ref, shift_ref, gain_ref, w_any, z_any, noise_any, near_any = refs[:8]
     pair_refs = refs[8 : 7 + half]
-    key_ref, value_ref, normed_any, state_any = refs[7 + half : 11 + half]
+    first_ref, second_ref, normed_any, state_any = refs[7 + half : 11 + half]
     state_ref, normed_ref, inverse_ref, w_ref, sem, out_sems, w_sems = refs[11 + half :]
     step = pl.program_id(0)
     rows, width = state_ref.shape
@@ -83,7 +82,7 @@
             return pair_refs[j - 1], f * piece_rows
         return (noise_any, near_any)[f], 0
 
-    cols = key_ref.shape[1]
+    cols = first_ref.shape[2]
     blocks = pl.num_programs(0) // 2
     state_copy = pltpu.make_async_copy(state_ref, state_any, out_sems.at[0])
     normed_copy = pltpu.make_async_copy(normed_ref, normed_any, out_sems.at[1])
@@ -144,22 +143,37 @@
 
     for part in range(2):
 
-        @pl.when(step == part * blocks)
+        @pl.when(step == part)
         def _():
             for copy in weights_of(part):
                 copy.wait()
 
-    at = pl.ds(pl.multiple_of(lax.rem(step, blocks) * cols, HD), cols)
-
-    @pl.when(step < blocks)
-    def _():
+    block = jnp.where(step < 2, 0, lax.rem(step - 2 + blocks - 1, blocks - 1) + 1)
+    at = pl.ds(pl.multiple_of(block * cols, HD), cols)
+
+    def keys():
         product = jnp.dot(normed_ref[...], w_ref[0, :, at], preferred_element_type=F32)
-        key_ref[...] = head_normalized(product, gain_ref[1:2])
-
-    @pl.when(step >= blocks)
-    def _():
+        return head_normalized(product, gain_ref[1:2])
+
+    def values():
         product = jnp.dot(normed_ref[...], w_ref[1, :, at], preferred_element_type=F32)
-        value_ref[...] = product.astype(BF16)
+        return product.astype(BF16)
+
+    @pl.when(step == 0)
+    def _():
+        first_ref[0] = keys()
+
+    @pl.when(step == 1)
+    def _():
+        first_ref[0] = values()
+
+    @pl.when(jnp.logical_and(step > 1, step < 1 + blocks))
+    def _():
+        second_ref[0] = keys()
+
+    @pl.when(step >= 1 + blocks)
+    def _():
+        second_ref[0] = values()
 
     @pl.when(step == pl.num_programs(0) - 1)
     def _():
@@ -173,6 +187,11 @@
     cols = tile_cols(head_cols)
     half = len(noise_pieces)
     blocks = head_cols // cols
+
+    def second_block(j, i):
+        j = jnp.maximum(j - 2, 0)
+        return j // (blocks - 1), 0, j % (blocks - 1)
+
     return pl.pallas_call(
         functools.partial(key_value_kernel, half=half),
         grid_spec=pltpu.PrefetchScalarGridSpec(
@@ -185,8 +204,8 @@
             ]
             + [ANY] * (3 + half),
             out_specs=[
-                pl.BlockSpec((rows, cols), lambda j, i: (0, jnp.minimum(j, blocks - 1))),
-                pl.BlockSpec((rows, cols), lambda j, i: (0, jnp.maximum(j - blocks, 0))),
+                pl.BlockSpec((1, rows, cols), lambda j, i: (jnp.minimum(j, 1), 0, 0)),
+                pl.BlockSpec((1, rows, cols), second_block),
                 ANY,
                 ANY,
             ],
@@ -201,8 +220,8 @@
             ],
         ),
         out_shape=[
-            jax.ShapeDtypeStruct((rows, head_cols), BF16),
-            jax.ShapeDtypeStruct((rows, head_cols), BF16),
+            jax.ShapeDtypeStruct((2, rows, cols), BF16),
+            jax.ShapeDtypeStruct((2, rows, head_cols - cols), BF16),
             jax.ShapeDtypeStruct((rows, width), BF16),
             pltpu.HBM((rows, width), BF16),
         ],
@@ -250,7 +269,7 @@
 
 
 def own_kernel(
-    gain_ref, normed_ref, key_ref, value_ref, w_any,
+    gain_ref, normed_ref, first_ref, second_ref, w_any,
     query_ref, acc_ref, top_ref, total_ref, w_ref, w_sems,
 ):
     step = pl.program_id(0)
@@ -267,18 +286,20 @@
     product = jnp.dot(normed_ref[...], w_ref[:, inside], preferred_element_type=F32)
     query = head_normalized(product, gain_ref[0:1])
     query_ref[...] = query
+    keys = jnp.where(step == 0, first_ref[0], second_ref[0])
+    values = jnp.where(step == 0, first_ref[1], second_ref[1])
 
     def finish(scores, row, at):
         top = over_lanes(scores, jnp.maximum, jnp.max)
-        acc, total = weigh(scores, top, value_ref[:, at])
+        acc, total = weigh(scores, top, values[:, at])
         acc_ref[row, at] = acc
         total_ref[row, at] = total
         top_ref[row, at] = jnp.broadcast_to(top, acc.shape)
 
-    attention_tiles(query, key_ref, finish)
-
-
-def own_attention(gains, normed, qkv_weight, key, value):
+    attention_tiles(query, keys, finish)
+
+
+def own_attention(gains, normed, qkv_weight, first, second):
     rows, width = normed.shape
     head_cols = qkv_weight.shape[2]
     cols = tile_cols(head_cols)
@@ -289,8 +310,8 @@
         in_specs=[
             pl.BlockSpec((2, HD), lambda j: (0, 0)),
             pl.BlockSpec((rows, width), lambda j: (0, 0)),
-            by_heads,
-            by_heads,
+            pl.BlockSpec((2, rows, cols), lambda j: (0, 0, 0)),
+            pl.BlockSpec((2, rows, cols), lambda j: (0, 0, jnp.maximum(j - 1, 0))),
             ANY,
         ],
         out_specs=[by_heads] * 4,
@@ -307,63 +328,49 @@
             rows * rows * head_cols // HD,
         ),
         name="queries_own_frame",
-    )(gains, normed, key, value, in_hbm(qkv_weight))
-
-
-def earlier_kernel(*refs, chunks):
-    info_ref, query_ref, acc_ref, top_ref, total_ref, key_ref, value_ref = refs[:7]
-    out_refs = refs[7:]
-    rows = query_ref.shape[0] // chunks
-
-    def store(row, at, result):
-        for c, out_ref in enumerate(out_refs):
-            first, end = max(row.start, c * rows), min(row.stop, (c + 1) * rows)
-            if first < end:
-                inside = slice(first - c * rows, end - c * rows)
-                out_ref[inside, at] = result[first - row.start : end - row.start]
-
+    )(gains, normed, first, second, in_hbm(qkv_weight))
+
+
+def earlier_kernel(info_ref, query_ref, acc_ref, top_ref, total_ref, kv_ref, out_ref):
     @pl.when(info_ref[0] != 0)
     def _():
-        every = slice(0, query_ref.shape[0])
-        store(every, slice(None), (acc_ref[...] / total_ref[...]).astype(BF16))
+        out_ref[...] = (acc_ref[...] / total_ref[...]).astype(BF16)
 
     @pl.when(info_ref[0] == 0)
     def _():
         def finish(scores, row, at):
             old_top = top_ref[row, at][:, :1]
             top = jnp.maximum(over_lanes(scores, jnp.maximum, jnp.max), old_top)
-            acc, total = weigh(scores, top, value_ref[:, at])
+            acc, total = weigh(scores, top, kv_ref[1, :, at])
             kept = jnp.exp2(old_top - top)
             acc = acc + acc_ref[row, at] * kept
             total = total + total_ref[row, at] * kept
-            store(row, at, (acc / total).astype(BF16))
-
-        attention_tiles(query_ref[...], key_ref, finish)
-
-
-def earlier_attention(info, query, acc, top, total, key, value, chunks):
-    rows, head_cols = query.shape
-    cols = tile_cols(head_cols)
+            out_ref[row, at] = (acc / total).astype(BF16)
+
+        attention_tiles(query_ref[...], kv_ref[0], finish)
+
+
+def earlier_attention(info, query, acc, top, total, kv, first_block):
+    rows = query.shape[0]
+    group = kv.shape[2]
+    cols = tile_cols(query.shape[1])
+    by_heads = pl.BlockSpec((rows, cols), lambda j, i: (0, first_block + j))
     return pl.pallas_call(
-        functools.partial(earlier_kernel, chunks=chunks),
+        earlier_kernel,
         grid_spec=pltpu.PrefetchScalarGridSpec(
             num_scalar_prefetch=1,
-            grid=(head_cols // cols,),
-            in_specs=[pl.BlockSpec((rows, cols), lambda j, i: (0, j))] * 6,
-            out_specs=[pl.BlockSpec((rows // chunks, cols), lambda j, i: (0, j))] * chunks,
-        ),
-        out_shape=[jax.ShapeDtypeStruct((rows // chunks, head_cols), BF16)] * chunks,
+            grid=(group // cols,),
+            in_specs=[by_heads] * 4 + [pl.BlockSpec((2, rows, cols), lambda j, i: (0, 0, j))],
+            out_specs=pl.BlockSpec((rows, cols), lambda j, i: (0, j)),
+        ),
+        out_shape=jax.ShapeDtypeStruct((rows, group), BF16),
         compiler_params=compiler_params(24),
-        cost_estimate=cost(
-            8 * rows * rows * head_cols,
-            22 * rows * head_cols,
-            rows * rows * head_cols // HD,
-        ),
+        cost_estimate=cost(8 * rows * rows * group, 20 * rows * group, rows * rows * group // HD),
         name="earlier_frame",
-    )(info, query, acc, top, total, key, value)
-
-
-def output_kernel(*refs, part_counts, whole_weights, half_blocks, last):
+    )(info, query, acc, top, total, kv)
+
+
+def output_kernel(*refs, part_places, whole_weights, half_blocks, last):
     parity_ref = refs[0]
     at = 1
     acc_in = resid_ref = gate_ref = None
@@ -371,10 +378,10 @@
         acc_in, resid_ref, gate_ref = refs[1:4]
         at = 4
     pieces = []
-    for count in part_counts:
-        pieces.append(refs[at : at + count])
-        at += count
-    size = len(part_counts)
+    for places in part_places:
+        pieces.append(refs[at : at + len(places)])
+        at += len(places)
+    size = len(part_places)
     wholes = refs[at : at + whole_weights]
     at += whole_weights
     halves = refs[at : at + 2 * (size - whole_weights)]
@@ -393,13 +400,11 @@
         return pltpu.make_async_copy(source, w_ref.at[half, k], w_sems.at[half, k])
 
     def held_copies(k):
-        row = 0
-        for number, part in enumerate(pieces[k]):
-            count = part.shape[0]
+        for number, (part, place) in enumerate(zip(pieces[k], part_places[k])):
+            rows, cols = (pl.ds(first, count) for first, count in zip(place, part.shape))
             yield pltpu.make_async_copy(
-                part, held_ref.at[k, pl.ds(row, count)], held_sems.at[k, number]
+                part, held_ref.at[k, rows, cols], held_sems.at[k, number]
             )
-            row += count
 
     @pl.when(step == 0)
     def _():
@@ -437,13 +442,13 @@
 
 def output_projection(parity, pieces, wholes, mine, theirs, finish=None):
     head_cols, half_width = mine[0].shape
-    rows = sum(part.shape[0] for part in pieces[0])
     width = 2 * half_width
+    rows = max(row + part.shape[0] for part, row, _ in pieces[0])
     size = len(pieces)
     cols = half_width // 2 if half_width % 512 == 0 else half_width
     half_blocks = half_width // cols
     parts = max(len(p) for p in pieces)
-    flat = [part for group in pieces for part in group]
+    flat = [part for group in pieces for part, _, _ in group]
     weights = [in_hbm(array) for array in [*wholes, *mine, *theirs]]
     last = finish is not None
 
@@ -454,7 +459,7 @@
     return pl.pallas_call(
         functools.partial(
             output_kernel,
-            part_counts=tuple(len(p) for p in pieces),
+            part_places=tuple(tuple((row, col) for _, row, col in p) for p in pieces),
             whole_weights=len(wholes),
             half_blocks=half_blocks,
             last=last,
@@ -554,38 +559,41 @@
         return row[:, :width], 1.0 + row[:, width : 2 * width], rate * row[:, 2 * width :]
 
     shift, scale1, own_gate = modulation(levels[0])
-    arriving_gate = modulation(ring(levels, to_next)[0])[2]
     info = jnp.stack([queue_index == 0, tensor_index // 2, tensor_index % 2])
     info = info.astype(jnp.int32)
     gains = jnp.stack([q_gain * SCORE_SCALE, k_gain])
 
     for step_index in range(STEPS):
         final = step_index == STEPS - 1
-        key, value, normed, state = project_keys_values(
+        *made, normed, state = project_keys_values(
             info, scale1, shift, gains, qkv_weight, frame, noise, noise_pieces
         )
         if not final:
-            value, mine = lax.optimization_barrier((value, mine))
-        earlier = [ring(block, to_next) for block in (key, value)]
-        query, *own = own_attention(gains, normed, qkv_weight, key, value)
+            made[1], mine, sent_levels = lax.optimization_barrier((made[1], mine, levels))
+            arriving_level = ring(sent_levels, to_next)
+        earlier = [ring(group, to_next) for group in made]
+        query, *own = own_attention(gains, normed, qkv_weight, *made)
         if not final:
             mine_corners = two_hops(mine, *mesh_sizes)
             earlier, mine_corners = lax.optimization_barrier((earlier, mine_corners))
-        attended = earlier_attention(
-            info, query, *own, *earlier, CHUNKS if final else 1
-        )
+        attended, columns, block = [], [], 0
+        for group in earlier:
+            attended.append(earlier_attention(info, query, *own, group, block))
+            columns.append(block * made[0].shape[2])
+            block += group.shape[2] // made[0].shape[2]
         targets = range(queue_size) if final else range(1, queue_size)
         resid, gate = state, own_gate
         if not final:
-            attended, mine, mine_corners = lax.optimization_barrier(
-                (attended, mine, mine_corners)
+            attended, mine, mine_corners, arriving_level = lax.optimization_barrier(
+                (attended, mine, mine_corners, arriving_level)
             )
             mine_corners = [jnp.concatenate(parts, axis=0) for parts in mine_corners]
             theirs = [sibling(block) for block in mine]
             theirs_corners = [sibling(block) for block in mine_corners]
             attended = [ring(block, to_next) for block in attended]
             sent_state, attended = lax.optimization_barrier((state, attended))
-            resid, gate = ring(sent_state, to_next), arriving_gate
+            resid = ring(sent_state, to_next)
+            gate = modulation(arriving_level[0])[2]
             attended, theirs, theirs_corners = lax.optimization_barrier(
                 (attended, theirs, theirs_corners)
             )
@@ -594,8 +602,13 @@
             near, noise = lax.optimization_barrier((near, fresh_noise[step_index + 1]))
             noise_pieces = gather_noise(noise)
         beyond = [two_hops(blocks, *mesh_sizes, targets) for blocks in near]
-        direct = [attended] + [list(parts) for parts in zip(*near)]
-        corners = [[half for parts in p for half in parts] for p in zip(*beyond)]
+        direct = [[(block, 0, col) for block, col in zip(attended, columns)]]
+        direct += [[(block, 0, col) for block, col in zip(p, columns)] for p in zip(*near)]
+        corners = [
+            [(half, h * (rows // 2), col) for parts, col in zip(p, columns)
+             for h, half in enumerate(parts)]
+            for p in zip(*beyond)
+        ]
         begun = output_projection(parity, direct, [out_weight], mine, theirs)
         frame = output_projection(
             parity, corners, [], mine_corners, theirs_corners, (begun, resid, gate)

time: 327 us -> 339 us (1.037)
  the two profiles are of different devices: /device:TPU:8 before, /device:TPU:1 now
where the time goes in v12:
time: 339 us; the launch traced here: 333 us
  Pallas kernels  134 us (40%)
  starting transfers between devices  87.6 us (26%)
  waiting for transfers between devices  83.3 us (25%)
  local copies, waits for them, and re-layouts  18.1 us (5%)
  other arithmetic  6.84 us (2%)
    ppermute x36, starting transfers between devices, send(): return lax.ppermute(block, AXES, pairs)  87.6 us
    ppermute x36, waiting for transfers between devices, send(): return lax.ppermute(block, AXES, pairs)  83.3 us
    pallas_call x4, Pallas kernels, output_projection(): pl.pallas_call(functools.partial(output_kernel, part_places=tuple((tuple(...  49.6 us
    pallas_call x2, Pallas kernels, own_attention(): pl.pallas_call(own_kernel, grid=(head_cols // cols,), in_specs=[pl.BlockS...  36.5 us
    pallas_call x2, Pallas kernels, project_keys_values(): pl.pallas_call(functools.partial(key_value_kernel, half=half), grid_spec=...  33 us
    pallas_call x4, Pallas kernels, earlier_attention(): pl.pallas_call(earlier_kernel, grid_spec=pltpu.PrefetchScalarGridSpec(num...  15.1 us
    unnamed x47, local copies, waits for them, and re-layouts  6.83 us
  transfers between devices with their start and end apart: 36, of which 9 were waited for; matrix products, arithmetic and copies ran while one was open for 5% of the time, Pallas kernels for 33%

profile of v12, /device:TPU:1, one launch (start us, length us, event | category | flops | bytes accessed | tf_op | source)
XLA Modules:
  0.0 333.4 jit_solution(11767426892087587425)
XLA Ops:
  0.0 4.6 %collective-permute-start = (bf16[768,3072]{1,0:T(8,128)(2,1)}, bf16[768,3072]{1,0:T(8,128)(2,1)}, u32[]{:S(2)}, u32[]{:S(2)}) collective-permute-start(bf16[768,3072]{1,0:T(8,128)(2,1)} %bitcast.23), channel_id=1, source_target_pairs={{0,4},{1,5},{2,6},{3,7},{4,8},{5,9},{6,10},{7,11},{8,12},{9,13},{1... | collective-permute-start | bytes 14155784 | tf_op jit(solution)/shard_map/ppermute | solution.py:496
  8.7 2.2 collective-permute-start.2
  18.5 37.4 %collective-permute-done.refs_5_ = bf16[768,3072]{1,0:T(8,128)(2,1)} collective-permute-done((bf16[768,3072]{1,0:T(8,128)(2,1)}, bf16[768,3072]{1,0:T(8,128)(2,1)}, u32[]{:S(2)}, u32[]{:S(2)}) %collective-permute-start) | collective-permute-done | bytes 4718624 | tf_op jit(solution)/shard_map/ppermute | solution.py:496
  56.0 16.5 %norm_keys_values.2 = (bf16[2,768,256]{2,1,0:T(8,128)(2,1)S(1)}, bf16[2,768,512]{2,1,0:T(8,128)(2,1)S(1)}, bf16[768,3072]{1,0:T(8,128)(2,1)S(1)}, bf16[768,3072]{1,0:T(8,128)(2,1)}) custom-call(s32[3]{0:T(128)S(1)} %pad_add_fusion.refs_0_.info_ref, f32[1,3072]{1,0:T(1,128)S(1)} %get-tuple-element.97.refs_1_, f32[1,3072]{1,0:T(1,128)S(1)} %get-tuple-element.96.refs_2_, ...), custom_call_target="tpu_custom_call" | custom-call | flops 7247757 | bytes 25952 | tf_op jit(solution)/shard_map/norm_keys_values/pallas_call | solution.py:195
  72.5 4.4 %collective-permute-start.6 = (bf16[2,768,512]{2,1,0:T(8,128)(2,1)S(1)}, bf16[2,768,512]{2,1,0:T(8,128)(2,1)S(1)}, u32[]{:S(2)}, u32[]{:S(2)}) collective-permute-start(bf16[2,768,512]{2,1,0:T(8,128)(2,1)S(1)} %get-tuple-element.53.second_ref), channel_id=1, source_target_pairs={{0,4},{1,5},{2,6},{3,7},{4,8},{5,9},{6,10},{7,11},{8,12},{9,13},{1... | collective-permute-start | bytes 4718600 | tf_op jit(solution)/shard_map/ppermute | solution.py:496
  82.2 2.5 collective-permute-start.5
  84.6 3.6 %collective-permute-start.9 = (s32[1]{0:T(128)}, s32[1]{0:T(128)}, u32[]{:S(2)}, u32[]{:S(2)}) collective-permute-start(s32[1]{0:T(128)} %param.10), channel_id=1, source_target_pairs={{0,4},{1,5},{2,6},{3,7},{4,8},{5,9},{6,10},{7,11},{8,12},{9,13},{1... | collective-permute-start | bytes 20 | tf_op jit(solution)/shard_map/ppermute | solution.py:496
  88.2 18.3 %queries_own_frame.2 = (bf16[768,768]{1,0:T(8,128)(2,1)S(1)}, f32[768,768]{1,0:T(8,128)S(1)}, f32[768,768]{1,0:T(8,128)S(1)}, f32[768,768]{1,0:T(8,128)S(1)}) custom-call(f32[2,128]{1,0:T(2,128)S(1)} %pad_maximum_fusion.2.refs_3_.gain_ref, bf16[768,3072]{1,0:T(8,128)(2,1)S(1)} %get-tuple-element.50.normed_ref, ...), custom_call_target="tpu_custom_call" | custom-call | flops 7247757 | bytes 20054 | tf_op jit(solution)/shard_map/queries_own_frame/pallas_call | solution.py:307
  106.5 7.7 %collective-permute-done.5.kv_ref = bf16[2,768,256]{2,1,0:T(8,128)(2,1)S(1)} collective-permute-done((bf16[2,768,256]{2,1,0:T(8,128)(2,1)S(1)}, bf16[2,768,256]{2,1,0:T(8,128)(2,1)S(1)}, u32[]{:S(2)}, u32[]{:S(2)}) %collective-permute-start.5) | collective-permute-done | bytes 786464 | tf_op jit(solution)/shard_map/ppermute | solution.py:496
  114.2 4.8 %earlier_frame.5 = bf16[768,512]{1,0:T(8,128)(2,1)S(1)} custom-call(s32[3]{0:T(128)S(1)} %pad_add_fusion.refs_0_.info_ref, bf16[768,768]{1,0:T(8,128)(2,1)S(1)} %get-tuple-element.54.query_ref, f32[768,768]{1,0:T(8,128)S(1)} %get-tuple-element.55.acc_ref, f32[768,768]{1,0:T(8,128)S(1)} %get-tuple-element.56.top_ref, ...), custom_call_target="tpu_custom_call" | custom-call | flops 2415919 | bytes 7864 | tf_op jit(solution)/shard_map/earlier_frame/pallas_call | solution.py:358
  119.1 2.6 earlier_frame.4
  121.9 13.7 %collective-permute-start.14 = (bf16[768,1536]{1,0:T(8,128)(2,1)S(1)}, bf16[768,1536]{1,0:T(8,128)(2,1)S(1)}, u32[]{:S(2)}, u32[]{:S(2)}) collective-permute-start(bf16[768,1536]{1,0:T(8,128)(2,1)S(1)} %constant_dynamic-update-slice_fusion.refs_8_), channel_id=1, source_target_pairs={{0,4},{1,5},{2,6},{3,7},{4,0},{5,1},{6,2},{7,3},{8,12},{9,13},{10,... | collective-permute-start | bytes 7077896 | tf_op jit(solution)/shard_map/ppermute | solution.py:496
  140.0 11.2 %collective-permute-done.10.refs_1_ = bf16[768,256]{1,0:T(8,128)(2,1)S(1)} collective-permute-done((bf16[768,256]{1,0:T(8,128)(2,1)S(1)}, bf16[768,256]{1,0:T(8,128)(2,1)S(1)}, u32[]{:S(2)}, u32[]{:S(2)}) %collective-permute-start.10) | collective-permute-done | bytes 393248 | tf_op jit(solution)/shard_map/ppermute | solution.py:496
  151.3 2.5 collective-permute-start.17
  156.9 4.9 %collective-permute-start.19 = (bf16[768,3072]{1,0:T(8,128)(2,1)}, bf16[768,3072]{1,0:T(8,128)(2,1)}, u32[]{:S(2)}, u32[]{:S(2)}) collective-permute-start(bf16[768,3072]{1,0:T(8,128)(2,1)} %get-tuple-element.81), channel_id=1, source_target_pairs={{0,4},{1,5},{2,6},{3,7},{4,8},{5,9},{6,10},{7,11},{8,12},{9,13},{1... | collective-permute-start | bytes 14155784 | tf_op jit(solution)/shard_map/ppermute | solution.py:496
  161.9 2.7 collective-permute-start.15
  164.6 3.2 collective-permute-start.16
  168.5 3.3 collective-permute-done.15.refs_3_
  179.3 3.1 collective-permute-start.20
  186.2 2.5 collective-permute-start.23
  192.6 2.9 collective-permute-start.21
  201.2 15.4 %projection_start.2.refs_1_ = bf16[768,3072]{1,0:T(8,128)(2,1)S(1)} custom-call(s32[1]{0:T(128)} %bitcast.refs_0_, bf16[768,256]{1,0:T(8,128)(2,1)S(1)} %copy-done.7, bf16[768,512]{1,0:T(8,128)(2,1)S(1)} %copy-done.5, bf16[768,256]{1,0:T(8,128)(2,1)S(1)} %collective-permute-done.15.refs_3_, bf16[768,512]{1,0:T(8,128)(2,1)S(1)} %collective-permute-done.17.refs_4_, ...), custom_call_target="tpu_custom_call" | custom-call | flops 10871635 | bytes 18874 | tf_op jit(solution)/shard_map/projection_start/pallas_call | solution.py:459
  216.7 9.9 %projection_end.2.refs_5_ = bf16[768,3072]{1,0:T(8,128)(2,1)} custom-call(s32[1]{0:T(128)} %bitcast.refs_0_, bf16[768,3072]{1,0:T(8,128)(2,1)S(1)} %projection_start.2.refs_1_, bf16[768,3072]{1,0:T(8,128)(2,1)} %collective-permute-done.19.refs_2_, f32[1,3072]{1,0:T(1,128)S(1)} %fusion.refs_3_, bf16[384,256]{1,0:T(8,128)(2,1)} %collective-permute-done.20.refs_4_, ...), custom_call_target="tpu_custom_call" | custom-call | flops 3623878 | bytes 18874 | tf_op jit(solution)/shard_map/projection_end/pallas_call | solution.py:459
  226.6 16.5 %norm_keys_values.3 = (bf16[2,768,256]{2,1,0:T(8,128)(2,1)S(1)}, bf16[2,768,512]{2,1,0:T(8,128)(2,1)S(1)}, bf16[768,3072]{1,0:T(8,128)(2,1)S(1)}, bf16[768,3072]{1,0:T(8,128)(2,1)}) custom-call(s32[3]{0:T(128)S(1)} %copy-done.12, f32[1,3072]{1,0:T(1,128)S(1)} %copy-done.9, f32[1,3072]{1,0:T(1,128)S(1)} %get-tuple-element.96.refs_2_, ...), custom_call_target="tpu_custom_call" | custom-call | flops 7247757 | bytes 25952 | tf_op jit(solution)/shard_map/norm_keys_values/pallas_call | solution.py:195
  243.2 10.6 %collective-permute-start.27 = (bf16[2,768,512]{2,1,0:T(8,128)(2,1)S(1)}, bf16[2,768,512]{2,1,0:T(8,128)(2,1)S(1)}, u32[]{:S(2)}, u32[]{:S(2)}) collective-permute-start(bf16[2,768,512]{2,1,0:T(8,128)(2,1)S(1)} %get-tuple-element.87.second_ref), channel_id=1, source_target_pairs={{0,4},{1,5},{2,6},{3,7},{4,8},{5,9},{6,10},{7,11},{8,12},{9,13},{1... | collective-permute-start | bytes 4718600 | tf_op jit(solution)/shard_map/ppermute | solution.py:496
  255.9 18.2 %queries_own_frame.3 = (bf16[768,768]{1,0:T(8,128)(2,1)S(1)}, f32[768,768]{1,0:T(8,128)S(1)}, f32[768,768]{1,0:T(8,128)S(1)}, f32[768,768]{1,0:T(8,128)S(1)}) custom-call(f32[2,128]{1,0:T(2,128)S(1)} %pad_maximum_fusion.2.refs_3_.gain_ref, bf16[768,3072]{1,0:T(8,128)(2,1)S(1)} %get-tuple-element.85.normed_ref, ...), custom_call_target="tpu_custom_call" | custom-call | flops 7247757 | bytes 20054 | tf_op jit(solution)/shard_map/queries_own_frame/pallas_call | solution.py:307
  274.2 4.9 %earlier_frame.7.refs_2_ = bf16[768,512]{1,0:T(8,128)(2,1)S(1)} custom-call(s32[3]{0:T(128)S(1)} %copy-done.12, bf16[768,768]{1,0:T(8,128)(2,1)S(1)} %get-tuple-element.88.query_ref, f32[768,768]{1,0:T(8,128)S(1)} %get-tuple-element.89.acc_ref, f32[768,768]{1,0:T(8,128)S(1)} %get-tuple-element.90.top_ref, f32[768,768]{1,0:T(8,128)S(1)} %get-tuple-element.91.total_ref, ...), custom_call_target="tpu_custom_call" | custom-call | flops 2415919 | bytes 7864 | tf_op jit(solution)/shard_map/earlier_frame/pallas_call | solution.py:358
  279.9 2.8 earlier_frame.6.refs_1_
  284.9 13.8 %collective-permute-done.29.refs_4_ = bf16[768,512]{1,0:T(8,128)(2,1)S(1)} collective-permute-done((bf16[768,512]{1,0:T(8,128)(2,1)S(1)}, bf16[768,512]{1,0:T(8,128)(2,1)S(1)}, u32[]{:S(2)}, u32[]{:S(2)}) %collective-permute-start.29) | collective-permute-done | bytes 786464 | tf_op jit(solution)/shard_map/ppermute | solution.py:496
  300.3 6.9 %collective-permute-done.28.refs_3_ = bf16[768,256]{1,0:T(8,128)(2,1)S(1)} collective-permute-done((bf16[768,256]{1,0:T(8,128)(2,1)S(1)}, bf16[768,256]{1,0:T(8,128)(2,1)S(1)}, u32[]{:S(2)}, u32[]{:S(2)}) %collective-permute-start.28) | collective-permute-done | bytes 393248 | tf_op jit(solution)/shard_map/ppermute | solution.py:496
  308.7 15.9 %projection_start.3.refs_1_ = bf16[768,3072]{1,0:T(8,128)(2,1)S(1)} custom-call(s32[1]{0:T(128)} %bitcast.refs_0_, bf16[768,256]{1,0:T(8,128)(2,1)S(1)} %earlier_frame.6.refs_1_, bf16[768,512]{1,0:T(8,128)(2,1)S(1)} %earlier_frame.7.refs_2_, bf16[768,256]{1,0:T(8,128)(2,1)S(1)} %collective-permute-done.28.refs_3_, ...), custom_call_target="tpu_custom_call" | custom-call | flops 10871635 | bytes 18874 | tf_op jit(solution)/shard_map/projection_start/pallas_call | solution.py:459
  324.7 8.4 %projection_end.3 = bf16[768,3072]{1,0:T(8,128)(2,1)} custom-call(s32[1]{0:T(128)} %bitcast.refs_0_, bf16[768,3072]{1,0:T(8,128)(2,1)S(1)} %projection_start.3.refs_1_, bf16[768,3072]{1,0:T(8,128)(2,1)S(1)} %bitcast.21, f32[1,3072]{1,0:T(1,128)S(1)} %copy-done.10, bf16[384,256]{1,0:T(8,128)(2,1)S(1)} %collective-permute-done.32.refs_4_, ...), custom_call_target="tpu_custom_call" | custom-call | flops 3623878 | bytes 18874 | tf_op jit(solution)/shard_map/projection_end/pallas_call | solution.py:459
  (123 shorter events, 52.0 us)
Async XLA Ops:
  0.0 56.0 %collective-permute-start = (bf16[768,3072]{1,0:T(8,128)(2,1)}, bf16[768,3072]{1,0:T(8,128)(2,1)}, u32[]{:S(2)}, u32[]{:S(2)}) collective-permute-start(bf16[768,3072]{1,0:T(8,128)(2,1)} %bitcast.23), channel_id=1, source_target_pairs={{0,4},{1,5},{2,6},{3,7},{4,8},{5,9},{6,10},{7,11},{8,12},{9,13},{1... | collective-permute-start | bytes 14155784 | tf_op jit(solution)/shard_map/ppermute | solution.py:496
  12.5 60.0 %collective-permute-start.3 = (bf16[768,1536]{1,0:T(8,128)(2,1)}, bf16[768,1536]{1,0:T(8,128)(2,1)}, u32[]{:S(2)}, u32[]{:S(2)}) collective-permute-start(bf16[768,1536]{1,0:T(8,128)(2,1)} %constant_dynamic-slice_fusion), channel_id=1, source_target_pairs={{0,1},{1,0},{2,3},{3,2},{4,5},{5,4},{6,7},{7,6},{8,9},{9,8},{10,11... | collective-permute-start | bytes 7077896 | tf_op jit(solution)/shard_map/ppermute | solution.py:496
  13.7 58.8 %collective-permute-start.4 = (bf16[768,1536]{1,0:T(8,128)(2,1)}, bf16[768,1536]{1,0:T(8,128)(2,1)}, u32[]{:S(2)}, u32[]{:S(2)}) collective-permute-start(bf16[768,1536]{1,0:T(8,128)(2,1)} %constant_dynamic-slice_fusion), channel_id=1, source_target_pairs={{0,2},{1,3},{2,0},{3,1},{4,6},{5,7},{6,4},{7,5},{8,10},{9,11},{10,... | collective-permute-start | bytes 7077896 | tf_op jit(solution)/shard_map/ppermute | solution.py:496
  72.5 41.7 %collective-permute-start.6 = (bf16[2,768,512]{2,1,0:T(8,128)(2,1)S(1)}, bf16[2,768,512]{2,1,0:T(8,128)(2,1)S(1)}, u32[]{:S(2)}, u32[]{:S(2)}) collective-permute-start(bf16[2,768,512]{2,1,0:T(8,128)(2,1)S(1)} %get-tuple-element.53.second_ref), channel_id=1, source_target_pairs={{0,4},{1,5},{2,6},{3,7},{4,8},{5,9},{6,10},{7,11},{8,12},{9,13},{1... | collective-permute-start | bytes 4718600 | tf_op jit(solution)/shard_map/ppermute | solution.py:496
  78.2 36.0 %collective-permute-start.7 = (bf16[384,1536]{1,0:T(8,128)(2,1)S(1)}, bf16[384,1536]{1,0:T(8,128)(2,1)S(1)}, u32[]{:S(2)}, u32[]{:S(2)}) collective-permute-start(bf16[384,1536]{1,0:T(8,128)(2,1)S(1)} %slice.54), channel_id=1, source_target_pairs={{0,2},{1,3},{2,0},{3,1},{4,6},{5,7},{6,4},{7,5},{8,10},{9,11},{10,... | collective-permute-start | bytes 3538952 | tf_op jit(solution)/shard_map/ppermute | solution.py:496
  80.9 33.3 %collective-permute-start.8 = (bf16[384,1536]{1,0:T(8,128)(2,1)S(1)}, bf16[384,1536]{1,0:T(8,128)(2,1)S(1)}, u32[]{:S(2)}, u32[]{:S(2)}) collective-permute-start(bf16[384,1536]{1,0:T(8,128)(2,1)S(1)} %slice.55), channel_id=1, source_target_pairs={{0,1},{1,0},{2,3},{3,2},{4,5},{5,4},{6,7},{7,6},{8,9},{9,8},{10,11... | collective-permute-start | bytes 3538952 | tf_op jit(solution)/shard_map/ppermute | solution.py:496
  82.2 32.1 %collective-permute-start.5 = (bf16[2,768,256]{2,1,0:T(8,128)(2,1)S(1)}, bf16[2,768,256]{2,1,0:T(8,128)(2,1)S(1)}, u32[]{:S(2)}, u32[]{:S(2)}) collective-permute-start(bf16[2,768,256]{2,1,0:T(8,128)(2,1)S(1)} %get-tuple-element.51.first_ref), channel_id=1, source_target_pairs={{0,4},{1,5},{2,6},{3,7},{4,8},{5,9},{6,10},{7,11},{8,12},{9,13},{1... | collective-permute-start | bytes 2359304 | tf_op jit(solution)/shard_map/ppermute | solution.py:496
  84.6 37.1 %collective-permute-start.9 = (s32[1]{0:T(128)}, s32[1]{0:T(128)}, u32[]{:S(2)}, u32[]{:S(2)}) collective-permute-start(s32[1]{0:T(128)} %param.10), channel_id=1, source_target_pairs={{0,4},{1,5},{2,6},{3,7},{4,8},{5,9},{6,10},{7,11},{8,12},{9,13},{1... | collective-permute-start | bytes 20 | tf_op jit(solution)/shard_map/ppermute | solution.py:496
  121.9 29.3 %collective-permute-start.14 = (bf16[768,1536]{1,0:T(8,128)(2,1)S(1)}, bf16[768,1536]{1,0:T(8,128)(2,1)S(1)}, u32[]{:S(2)}, u32[]{:S(2)}) collective-permute-start(bf16[768,1536]{1,0:T(8,128)(2,1)S(1)} %constant_dynamic-update-slice_fusion.refs_8_), channel_id=1, source_target_pairs={{0,4},{1,5},{2,6},{3,7},{4,0},{5,1},{6,2},{7,3},{8,12},{9,13},{10,... | collective-permute-start | bytes 7077896 | tf_op jit(solution)/shard_map/ppermute | solution.py:496
  135.7 15.6 %collective-permute-start.12 = (bf16[768,1536]{1,0:T(8,128)(2,1)}, bf16[768,1536]{1,0:T(8,128)(2,1)S(1)}, u32[]{:S(2)}, u32[]{:S(2)}) collective-permute-start(bf16[768,1536]{1,0:T(8,128)(2,1)} %collective-permute-done.3.refs_8_), channel_id=1, source_target_pairs={{0,4},{1,5},{2,6},{3,7},{4,0},{5,1},{6,2},{7,3},{8,12},{9,13},{10,... | collective-permute-start | bytes 7077896 | tf_op jit(solution)/shard_map/ppermute | solution.py:496
  135.7 15.5 %collective-permute-start.13 = (bf16[768,1536]{1,0:T(8,128)(2,1)}, bf16[768,1536]{1,0:T(8,128)(2,1)S(1)}, u32[]{:S(2)}, u32[]{:S(2)}) collective-permute-start(bf16[768,1536]{1,0:T(8,128)(2,1)} %collective-permute-done.4.refs_9_), channel_id=1, source_target_pairs={{0,4},{1,5},{2,6},{3,7},{4,0},{5,1},{6,2},{7,3},{8,12},{9,13},{10,... | collective-permute-start | bytes 7077896 | tf_op jit(solution)/shard_map/ppermute | solution.py:496
  136.2 15.0 %collective-permute-start.11 = (bf16[768,512]{1,0:T(8,128)(2,1)S(1)}, bf16[768,512]{1,0:T(8,128)(2,1)S(1)}, u32[]{:S(2)}, u32[]{:S(2)}) collective-permute-start(bf16[768,512]{1,0:T(8,128)(2,1)S(1)} %earlier_frame.5), channel_id=1, source_target_pairs={{0,4},{1,5},{2,6},{3,7},{4,8},{5,9},{6,10},{7,11},{8,12},{9,13},{1... | collective-permute-start | bytes 2359304 | tf_op jit(solution)/shard_map/ppermute | solution.py:496
  138.1 13.1 %collective-permute-start.10 = (bf16[768,256]{1,0:T(8,128)(2,1)S(1)}, bf16[768,256]{1,0:T(8,128)(2,1)S(1)}, u32[]{:S(2)}, u32[]{:S(2)}) collective-permute-start(bf16[768,256]{1,0:T(8,128)(2,1)S(1)} %earlier_frame.4), channel_id=1, source_target_pairs={{0,4},{1,5},{2,6},{3,7},{4,8},{5,9},{6,10},{7,11},{8,12},{9,13},{1... | collective-permute-start | bytes 1179656 | tf_op jit(solution)/shard_map/ppermute | solution.py:496
  151.3 22.2 %collective-permute-start.17 = (bf16[768,512]{1,0:T(8,128)(2,1)S(1)}, bf16[768,512]{1,0:T(8,128)(2,1)S(1)}, u32[]{:S(2)}, u32[]{:S(2)}) collective-permute-start(bf16[768,512]{1,0:T(8,128)(2,1)S(1)} %collective-permute-done.11.refs_2_), channel_id=1, source_target_pairs={{4,5},{5,4},{6,7},{7,6},{8,9},{9,8},{10,11},{11,10},{12,13},{13,12... | collective-permute-start | bytes 2359304 | tf_op jit(solution)/shard_map/ppermute | solution.py:496
  153.8 19.6 %collective-permute-start.18 = (bf16[768,512]{1,0:T(8,128)(2,1)S(1)}, bf16[768,512]{1,0:T(8,128)(2,1)S(1)}, u32[]{:S(2)}, u32[]{:S(2)}) collective-permute-start(bf16[768,512]{1,0:T(8,128)(2,1)S(1)} %collective-permute-done.11.refs_2_), channel_id=1, source_target_pairs={{4,6},{5,7},{6,4},{7,5},{8,10},{9,11},{10,8},{11,9},{12,14},{13,15... | collective-permute-start | bytes 2359304 | tf_op jit(solution)/shard_map/ppermute | solution.py:496
  156.9 59.8 %collective-permute-start.19 = (bf16[768,3072]{1,0:T(8,128)(2,1)}, bf16[768,3072]{1,0:T(8,128)(2,1)}, u32[]{:S(2)}, u32[]{:S(2)}) collective-permute-start(bf16[768,3072]{1,0:T(8,128)(2,1)} %get-tuple-element.81), channel_id=1, source_target_pairs={{0,4},{1,5},{2,6},{3,7},{4,8},{5,9},{6,10},{7,11},{8,12},{9,13},{1... | collective-permute-start | bytes 14155784 | tf_op jit(solution)/shard_map/ppermute | solution.py:496
  161.9 10.0 %collective-permute-start.15 = (bf16[768,256]{1,0:T(8,128)(2,1)S(1)}, bf16[768,256]{1,0:T(8,128)(2,1)S(1)}, u32[]{:S(2)}, u32[]{:S(2)}) collective-permute-start(bf16[768,256]{1,0:T(8,128)(2,1)S(1)} %collective-permute-done.10.refs_1_), channel_id=1, source_target_pairs={{4,5},{5,4},{6,7},{7,6},{8,9},{9,8},{10,11},{11,10},{12,13},{13,12... | collective-permute-start | bytes 1179656 | tf_op jit(solution)/shard_map/ppermute | solution.py:496
  176.5 50.1 %collective-permute-start.25 = (bf16[384,3072]{1,0:T(8,128)(2,1)}, bf16[384,3072]{1,0:T(8,128)(2,1)}, u32[]{:S(2)}, u32[]{:S(2)}) collective-permute-start(bf16[384,3072]{1,0:T(8,128)(2,1)} %pad_maximum_fusion.1), channel_id=1, source_target_pairs={{0,2},{1,3},{2,0},{3,1}} | collective-permute-start | bytes 7077896 | tf_op jit(solution)/shard_map/ppermute | solution.py:496
  179.3 13.3 %collective-permute-start.20 = (bf16[384,256]{1,0:T(8,128)(2,1)}, bf16[384,256]{1,0:T(8,128)(2,1)}, u32[]{:S(2)}, u32[]{:S(2)}) collective-permute-start(bf16[384,256]{1,0:T(8,128)(2,1)} %slice.59), channel_id=1, source_target_pairs={{4,6},{5,7},{6,4},{7,5},{8,10},{9,11},{10,8},{11,9},{12,14},{13,15... | collective-permute-start | bytes 589832 | tf_op jit(solution)/shard_map/ppermute | solution.py:496
  183.3 33.4 %collective-permute-start.22 = (bf16[384,512]{1,0:T(8,128)(2,1)}, bf16[384,512]{1,0:T(8,128)(2,1)}, u32[]{:S(2)}, u32[]{:S(2)}) collective-permute-start(bf16[384,512]{1,0:T(8,128)(2,1)} %slice.61), channel_id=1, source_target_pairs={{4,6},{5,7},{6,4},{7,5},{8,10},{9,11},{10,8},{11,9},{12,14},{13,15... | collective-permute-start | bytes 1179656 | tf_op jit(solution)/shard_map/ppermute | solution.py:496
  186.2 30.5 %collective-permute-start.23 = (bf16[384,512]{1,0:T(8,128)(2,1)}, bf16[384,512]{1,0:T(8,128)(2,1)}, u32[]{:S(2)}, u32[]{:S(2)}) collective-permute-start(bf16[384,512]{1,0:T(8,128)(2,1)} %slice.62), channel_id=1, source_target_pairs={{4,5},{5,4},{6,7},{7,6},{8,9},{9,8},{10,11},{11,10},{12,13},{13,12... | collective-permute-start | bytes 1179656 | tf_op jit(solution)/shard_map/ppermute | solution.py:496
  192.6 24.1 %collective-permute-start.21 = (bf16[384,256]{1,0:T(8,128)(2,1)S(1)}, bf16[384,256]{1,0:T(8,128)(2,1)S(1)}, u32[]{:S(2)}, u32[]{:S(2)}) collective-permute-start(bf16[384,256]{1,0:T(8,128)(2,1)S(1)} %slice.60), channel_id=1, source_target_pairs={{4,5},{5,4},{6,7},{7,6},{8,9},{9,8},{10,11},{11,10},{12,13},{13,12... | collective-permute-start | bytes 589832 | tf_op jit(solution)/shard_map/ppermute | solution.py:496
  243.2 31.0 %collective-permute-start.27 = (bf16[2,768,512]{2,1,0:T(8,128)(2,1)S(1)}, bf16[2,768,512]{2,1,0:T(8,128)(2,1)S(1)}, u32[]{:S(2)}, u32[]{:S(2)}) collective-permute-start(bf16[2,768,512]{2,1,0:T(8,128)(2,1)S(1)} %get-tuple-element.87.second_ref), channel_id=1, source_target_pairs={{0,4},{1,5},{2,6},{3,7},{4,8},{5,9},{6,10},{7,11},{8,12},{9,13},{1... | collective-permute-start | bytes 4718600 | tf_op jit(solution)/shard_map/ppermute | solution.py:496
  253.8 26.1 %collective-permute-start.26 = (bf16[2,768,256]{2,1,0:T(8,128)(2,1)S(1)}, bf16[2,768,256]{2,1,0:T(8,128)(2,1)S(1)}, u32[]{:S(2)}, u32[]{:S(2)}) collective-permute-start(bf16[2,768,256]{2,1,0:T(8,128)(2,1)S(1)} %get-tuple-element.86.first_ref), channel_id=1, source_target_pairs={{0,4},{1,5},{2,6},{3,7},{4,8},{5,9},{6,10},{7,11},{8,12},{9,13},{1... | collective-permute-start | bytes 2359304 | tf_op jit(solution)/shard_map/ppermute | solution.py:496
  279.0 19.7 %collective-permute-start.29 = (bf16[768,512]{1,0:T(8,128)(2,1)S(1)}, bf16[768,512]{1,0:T(8,128)(2,1)S(1)}, u32[]{:S(2)}, u32[]{:S(2)}) collective-permute-start(bf16[768,512]{1,0:T(8,128)(2,1)S(1)} %earlier_frame.7.refs_2_), channel_id=1, source_target_pairs={{0,1},{1,0},{2,3},{3,2},{4,5},{5,4},{6,7},{7,6},{8,9},{9,8},{10,11... | collective-permute-start | bytes 2359304 | tf_op jit(solution)/shard_map/ppermute | solution.py:496
  279.9 19.6 %collective-permute-start.31 = (bf16[768,512]{1,0:T(8,128)(2,1)S(1)}, bf16[768,512]{1,0:T(8,128)(2,1)S(1)}, u32[]{:S(2)}, u32[]{:S(2)}) collective-permute-start(bf16[768,512]{1,0:T(8,128)(2,1)S(1)} %earlier_frame.7.refs_2_), channel_id=1, source_target_pairs={{0,2},{1,3},{2,0},{3,1},{4,6},{5,7},{6,4},{7,5},{8,10},{9,11},{10,... | collective-permute-start | bytes 2359304 | tf_op jit(solution)/shard_map/ppermute | solution.py:496
  282.7 24.4 %collective-permute-start.28 = (bf16[768,256]{1,0:T(8,128)(2,1)S(1)}, bf16[768,256]{1,0:T(8,128)(2,1)S(1)}, u32[]{:S(2)}, u32[]{:S(2)}) collective-permute-start(bf16[768,256]{1,0:T(8,128)(2,1)S(1)} %earlier_frame.6.refs_1_), channel_id=1, source_target_pairs={{0,1},{1,0},{2,3},{3,2},{4,5},{5,4},{6,7},{7,6},{8,9},{9,8},{10,11... | collective-permute-start | bytes 1179656 | tf_op jit(solution)/shard_map/ppermute | solution.py:496
  283.5 24.4 %collective-permute-start.30 = (bf16[768,256]{1,0:T(8,128)(2,1)S(1)}, bf16[768,256]{1,0:T(8,128)(2,1)S(1)}, u32[]{:S(2)}, u32[]{:S(2)}) collective-permute-start(bf16[768,256]{1,0:T(8,128)(2,1)S(1)} %earlier_frame.6.refs_1_), channel_id=1, source_target_pairs={{0,2},{1,3},{2,0},{3,1},{4,6},{5,7},{6,4},{7,5},{8,10},{9,11},{10,... | collective-permute-start | bytes 1179656 | tf_op jit(solution)/shard_map/ppermute | solution.py:496
  298.8 25.9 %collective-permute-start.34 = (bf16[384,512]{1,0:T(8,128)(2,1)S(1)}, bf16[384,512]{1,0:T(8,128)(2,1)S(1)}, u32[]{:S(2)}, u32[]{:S(2)}) collective-permute-start(bf16[384,512]{1,0:T(8,128)(2,1)S(1)} %slice.73), channel_id=1, source_target_pairs={{0,2},{1,3},{2,0},{3,1},{4,6},{5,7},{6,4},{7,5},{8,10},{9,11},{10,... | collective-permute-start | bytes 1179656 | tf_op jit(solution)/shard_map/ppermute | solution.py:496
  299.6 25.1 %collective-permute-start.35 = (bf16[384,512]{1,0:T(8,128)(2,1)S(1)}, bf16[384,512]{1,0:T(8,128)(2,1)S(1)}, u32[]{:S(2)}, u32[]{:S(2)}) collective-permute-start(bf16[384,512]{1,0:T(8,128)(2,1)S(1)} %slice.74), channel_id=1, source_target_pairs={{0,1},{1,0},{2,3},{3,2},{4,5},{5,4},{6,7},{7,6},{8,9},{9,8},{10,11... | collective-permute-start | bytes 1179656 | tf_op jit(solution)/shard_map/ppermute | solution.py:496
  307.2 17.4 %collective-permute-start.32 = (bf16[384,256]{1,0:T(8,128)(2,1)S(1)}, bf16[384,256]{1,0:T(8,128)(2,1)S(1)}, u32[]{:S(2)}, u32[]{:S(2)}) collective-permute-start(bf16[384,256]{1,0:T(8,128)(2,1)S(1)} %slice.71), channel_id=1, source_target_pairs={{0,2},{1,3},{2,0},{3,1},{4,6},{5,7},{6,4},{7,5},{8,10},{9,11},{10,... | collective-permute-start | bytes 589832 | tf_op jit(solution)/shard_map/ppermute | solution.py:496
  308.0 16.6 %collective-permute-start.33 = (bf16[384,256]{1,0:T(8,128)(2,1)S(1)}, bf16[384,256]{1,0:T(8,128)(2,1)S(1)}, u32[]{:S(2)}, u32[]{:S(2)}) collective-permute-start(bf16[384,256]{1,0:T(8,128)(2,1)S(1)} %slice.72), channel_id=1, source_target_pairs={{0,1},{1,0},{2,3},{3,2},{4,5},{5,4},{6,7},{7,6},{8,9},{9,8},{10,11... | collective-permute-start | bytes 589832 | tf_op jit(solution)/shard_map/ppermute | solution.py:496
  (27 other events, 413.9 us)

commit v13 on v12

--- a/solution.py
+++ b/solution.py
@@ -537,17 +537,25 @@
     def sibling(block):
         return send(block, lambda q, t: (q ^ 1, t), *mesh_sizes)
 
-    def gather_noise(noise):
+    def gather_noise(noise, at_once):
         args = (*mesh_sizes, [0])
         half = tensor_size // 2
         near = send(noise, lambda q, t: (q, t ^ 1), *args)
-        pair = jnp.concatenate([noise, near], axis=0)
-        return [near, *[send(pair, away(j, half), *args) for j in range(1, half)]]
+        pairs = []
+        for j in range(1, half):
+            if at_once:
+                straight = send(noise, away(j, half), *args)
+                across = send(noise, lambda q, t: away(j, half)(q, t ^ 1), *args)
+                pairs.append(jnp.concatenate([straight, across], axis=0))
+            else:
+                pair = jnp.concatenate([noise, near], axis=0)
+                pairs.append(send(pair, away(j, half), *args))
+        return [near, *pairs]
 
     to_next = range(queue_size - 1)
     frame = ring(latents[0], to_next)
     noise = fresh_noise[0]
-    noise_pieces = gather_noise(noise)
+    noise_pieces = gather_noise(noise, True)
     half_weight = lax.dynamic_slice(
         out_weight, (0, parity[0] * (width // 2)), (out_weight.shape[0], width // 2)
     )
@@ -569,7 +577,7 @@
             info, scale1, shift, gains, qkv_weight, frame, noise, noise_pieces
         )
         if not final:
-            made[1], mine, sent_levels = lax.optimization_barrier((made[1], mine, levels))
+            state, mine, sent_levels = lax.optimization_barrier((state, mine, levels))
             arriving_level = ring(sent_levels, to_next)
         earlier = [ring(group, to_next) for group in made]
         query, *own = own_attention(gains, normed, qkv_weight, *made)
@@ -600,7 +608,7 @@
         near = [one_hop(block, *mesh_sizes, targets) for block in attended]
         if not final:
             near, noise = lax.optimization_barrier((near, fresh_noise[step_index + 1]))
-            noise_pieces = gather_noise(noise)
+            noise_pieces = gather_noise(noise, False)
         beyond = [two_hops(blocks, *mesh_sizes, targets) for blocks in near]
         direct = [[(block, 0, col) for block, col in zip(attended, columns)]]
         direct += [[(block, 0, col) for block, col in zip(p, columns)] for p in zip(*near)]

time: 339 us -> 346 us (1.021)
  waiting for transfers between devices: 83.3 us -> 91.2 us
  starting transfers between devices: 87.6 us -> 83.6 us
    ppermute x36 -> x37, waiting for transfers between devices: 83.3 us -> 91.2 us  [send(): return lax.ppermute(block, AXES, pairs)]
    ppermute x36 -> x37, starting transfers between devices: 87.6 us -> 83.6 us  [send(): return lax.ppermute(block, AXES, pairs)]
  transfers between devices with their start and end apart: 36 -> 37, of which waited for: 9 -> 10; matrix products, arithmetic and copies ran while one was open for 5% -> 6% of each run, Pallas kernels for 33% -> 32%
where the time goes in v13:
time: 346 us; the launch traced here: 340 us
  Pallas kernels  134 us (39%)
  waiting for transfers between devices  91.2 us (26%)
  starting transfers between devices  83.6 us (24%)
  local copies, waits for them, and re-layouts  19.8 us (6%)
  other arithmetic  8.07 us (2%)
    ppermute x37, waiting for transfers between devices, send(): return lax.ppermute(block, AXES, pairs)  91.2 us
    ppermute x37, starting transfers between devices, send(): return lax.ppermute(block, AXES, pairs)  83.6 us
    pallas_call x4, Pallas kernels, output_projection(): pl.pallas_call(functools.partial(output_kernel, part_places=tuple((tuple(...  49.6 us
    pallas_call x2, Pallas kernels, own_attention(): pl.pallas_call(own_kernel, grid=(head_cols // cols,), in_specs=[pl.BlockS...  36.5 us
    pallas_call x2, Pallas kernels, project_keys_values(): pl.pallas_call(functools.partial(key_value_kernel, half=half), grid_spec=...  33 us
    pallas_call x4, Pallas kernels, earlier_attention(): pl.pallas_call(earlier_kernel, grid_spec=pltpu.PrefetchScalarGridSpec(num...  15.1 us
  transfers between devices with their start and end apart: 37, of which 10 were waited for; matrix products, arithmetic and copies ran while one was open for 6% of the time, Pallas kernels for 32%

profile of v13, /device:TPU:1, one launch (start us, length us, event | category | flops | bytes accessed | tf_op | source)
XLA Modules:
  0.0 340.1 jit_solution(3473036388366984542)
XLA Ops:
  0.0 4.6 %collective-permute-start = (bf16[768,3072]{1,0:T(8,128)(2,1)}, bf16[768,3072]{1,0:T(8,128)(2,1)}, u32[]{:S(2)}, u32[]{:S(2)}) collective-permute-start(bf16[768,3072]{1,0:T(8,128)(2,1)} %bitcast.23), channel_id=1, source_target_pairs={{0,4},{1,5},{2,6},{3,7},{4,8},{5,9},{6,10},{7,11},{8,12},{9,13},{1... | collective-permute-start | bytes 14155784 | tf_op jit(solution)/shard_map/ppermute | solution.py:496
  8.9 3.3 constant_dynamic-slice_fusion
  21.7 34.3 %collective-permute-done.refs_5_ = bf16[768,3072]{1,0:T(8,128)(2,1)} collective-permute-done((bf16[768,3072]{1,0:T(8,128)(2,1)}, bf16[768,3072]{1,0:T(8,128)(2,1)}, u32[]{:S(2)}, u32[]{:S(2)}) %collective-permute-start) | collective-permute-done | bytes 4718624 | tf_op jit(solution)/shard_map/ppermute | solution.py:496
  56.0 16.5 %norm_keys_values.2 = (bf16[2,768,256]{2,1,0:T(8,128)(2,1)S(1)}, bf16[2,768,512]{2,1,0:T(8,128)(2,1)S(1)}, bf16[768,3072]{1,0:T(8,128)(2,1)S(1)}, bf16[768,3072]{1,0:T(8,128)(2,1)}) custom-call(s32[3]{0:T(128)S(1)} %pad_add_fusion.refs_0_.info_ref, f32[1,3072]{1,0:T(1,128)S(1)} %get-tuple-element.97.refs_1_, f32[1,3072]{1,0:T(1,128)S(1)} %get-tuple-element.96.refs_2_, ...), custom_call_target="tpu_custom_call" | custom-call | flops 7247757 | bytes 25952 | tf_op jit(solution)/shard_map/norm_keys_values/pallas_call | solution.py:195
  72.5 4.4 %collective-permute-start.7 = (bf16[2,768,512]{2,1,0:T(8,128)(2,1)S(1)}, bf16[2,768,512]{2,1,0:T(8,128)(2,1)S(1)}, u32[]{:S(2)}, u32[]{:S(2)}) collective-permute-start(bf16[2,768,512]{2,1,0:T(8,128)(2,1)S(1)} %get-tuple-element.53.second_ref), channel_id=1, source_target_pairs={{0,4},{1,5},{2,6},{3,7},{4,8},{5,9},{6,10},{7,11},{8,12},{9,13},{1... | collective-permute-start | bytes 4718600 | tf_op jit(solution)/shard_map/ppermute | solution.py:496
  76.9 2.8 collective-permute-done.5.refs_9_
  85.9 2.4 collective-permute-start.10
  88.3 18.2 %queries_own_frame.2 = (bf16[768,768]{1,0:T(8,128)(2,1)S(1)}, f32[768,768]{1,0:T(8,128)S(1)}, f32[768,768]{1,0:T(8,128)S(1)}, f32[768,768]{1,0:T(8,128)S(1)}) custom-call(f32[2,128]{1,0:T(2,128)S(1)} %pad_maximum_fusion.2.refs_3_.gain_ref, bf16[768,3072]{1,0:T(8,128)(2,1)S(1)} %get-tuple-element.51.normed_ref, ...), custom_call_target="tpu_custom_call" | custom-call | flops 7247757 | bytes 20054 | tf_op jit(solution)/shard_map/queries_own_frame/pallas_call | solution.py:307
  106.6 16.7 %collective-permute-done.6.kv_ref = bf16[2,768,256]{2,1,0:T(8,128)(2,1)S(1)} collective-permute-done((bf16[2,768,256]{2,1,0:T(8,128)(2,1)S(1)}, bf16[2,768,256]{2,1,0:T(8,128)(2,1)S(1)}, u32[]{:S(2)}, u32[]{:S(2)}) %collective-permute-start.6) | collective-permute-done | bytes 786464 | tf_op jit(solution)/shard_map/ppermute | solution.py:496
  123.3 4.8 %earlier_frame.5 = bf16[768,512]{1,0:T(8,128)(2,1)S(1)} custom-call(s32[3]{0:T(128)S(1)} %pad_add_fusion.refs_0_.info_ref, bf16[768,768]{1,0:T(8,128)(2,1)S(1)} %get-tuple-element.54.query_ref, f32[768,768]{1,0:T(8,128)S(1)} %get-tuple-element.55.acc_ref, f32[768,768]{1,0:T(8,128)S(1)} %get-tuple-element.56.top_ref, ...), custom_call_target="tpu_custom_call" | custom-call | flops 2415919 | bytes 7864 | tf_op jit(solution)/shard_map/earlier_frame/pallas_call | solution.py:358
  128.1 2.6 earlier_frame.4
  131.0 13.7 %collective-permute-start.15 = (bf16[768,1536]{1,0:T(8,128)(2,1)S(1)}, bf16[768,1536]{1,0:T(8,128)(2,1)S(1)}, u32[]{:S(2)}, u32[]{:S(2)}) collective-permute-start(bf16[768,1536]{1,0:T(8,128)(2,1)S(1)} %constant_dynamic-update-slice_fusion.refs_8_), channel_id=1, source_target_pairs={{0,4},{1,5},{2,6},{3,7},{4,0},{5,1},{6,2},{7,3},{8,12},{9,13},{10,... | collective-permute-start | bytes 7077896 | tf_op jit(solution)/shard_map/ppermute | solution.py:496
  149.0 11.2 %collective-permute-done.11.refs_1_ = bf16[768,256]{1,0:T(8,128)(2,1)S(1)} collective-permute-done((bf16[768,256]{1,0:T(8,128)(2,1)S(1)}, bf16[768,256]{1,0:T(8,128)(2,1)S(1)}, u32[]{:S(2)}, u32[]{:S(2)}) %collective-permute-start.11) | collective-permute-done | bytes 393248 | tf_op jit(solution)/shard_map/ppermute | solution.py:496
  165.1 4.4 %collective-permute-start.20 = (bf16[768,3072]{1,0:T(8,128)(2,1)}, bf16[768,3072]{1,0:T(8,128)(2,1)}, u32[]{:S(2)}, u32[]{:S(2)}) collective-permute-start(bf16[768,3072]{1,0:T(8,128)(2,1)} %get-tuple-element.81), channel_id=1, source_target_pairs={{0,4},{1,5},{2,6},{3,7},{4,8},{5,9},{6,10},{7,11},{8,12},{9,13},{1... | collective-permute-start | bytes 14155784 | tf_op jit(solution)/shard_map/ppermute | solution.py:496
  169.5 3.6 %collective-permute-start.16 = (bf16[768,256]{1,0:T(8,128)(2,1)S(1)}, bf16[768,256]{1,0:T(8,128)(2,1)S(1)}, u32[]{:S(2)}, u32[]{:S(2)}) collective-permute-start(bf16[768,256]{1,0:T(8,128)(2,1)S(1)} %collective-permute-done.11.refs_1_), channel_id=1, source_target_pairs={{4,5},{5,4},{6,7},{7,6},{8,9},{9,8},{10,11},{11,10},{12,13},{13,12... | collective-permute-start | bytes 1179656 | tf_op jit(solution)/shard_map/ppermute | solution.py:496
  173.1 3.6 %collective-permute-start.17 = (bf16[768,256]{1,0:T(8,128)(2,1)S(1)}, bf16[768,256]{1,0:T(8,128)(2,1)S(1)}, u32[]{:S(2)}, u32[]{:S(2)}) collective-permute-start(bf16[768,256]{1,0:T(8,128)(2,1)S(1)} %collective-permute-done.11.refs_1_), channel_id=1, source_target_pairs={{4,6},{5,7},{6,4},{7,5},{8,10},{9,11},{10,8},{11,9},{12,14},{13,15... | collective-permute-start | bytes 1179656 | tf_op jit(solution)/shard_map/ppermute | solution.py:496
  179.4 2.8 collective-permute-done.17.refs_5_
  185.3 2.1 collective-permute-start.26
  188.1 3.4 collective-permute-start.21
  200.7 3.5 %collective-permute-start.22 = (bf16[384,256]{1,0:T(8,128)(2,1)S(1)}, bf16[384,256]{1,0:T(8,128)(2,1)S(1)}, u32[]{:S(2)}, u32[]{:S(2)}) collective-permute-start(bf16[384,256]{1,0:T(8,128)(2,1)S(1)} %slice.60), channel_id=1, source_target_pairs={{4,5},{5,4},{6,7},{7,6},{8,9},{9,8},{10,11},{11,10},{12,13},{13,12... | collective-permute-start | bytes 589832 | tf_op jit(solution)/shard_map/ppermute | solution.py:496
  210.0 15.4 %projection_start.2.refs_1_ = bf16[768,3072]{1,0:T(8,128)(2,1)S(1)} custom-call(s32[1]{0:T(128)} %bitcast.refs_0_, bf16[768,256]{1,0:T(8,128)(2,1)S(1)} %copy-done.7, bf16[768,512]{1,0:T(8,128)(2,1)S(1)} %copy-done.5, bf16[768,256]{1,0:T(8,128)(2,1)S(1)} %collective-permute-done.16.refs_3_, bf16[768,512]{1,0:T(8,128)(2,1)S(1)} %collective-permute-done.18.refs_4_, ...), custom_call_target="tpu_custom_call" | custom-call | flops 10871635 | bytes 18874 | tf_op jit(solution)/shard_map/projection_start/pallas_call | solution.py:459
  225.5 9.9 %projection_end.2.refs_5_ = bf16[768,3072]{1,0:T(8,128)(2,1)} custom-call(s32[1]{0:T(128)} %bitcast.refs_0_, bf16[768,3072]{1,0:T(8,128)(2,1)S(1)} %projection_start.2.refs_1_, bf16[768,3072]{1,0:T(8,128)(2,1)} %collective-permute-done.20.refs_2_, f32[1,3072]{1,0:T(1,128)S(1)} %fusion.refs_3_, bf16[384,256]{1,0:T(8,128)(2,1)} %collective-permute-done.21.refs_4_, ...), custom_call_target="tpu_custom_call" | custom-call | flops 3623878 | bytes 18874 | tf_op jit(solution)/shard_map/projection_end/pallas_call | solution.py:459
  235.4 16.5 %norm_keys_values.3 = (bf16[2,768,256]{2,1,0:T(8,128)(2,1)S(1)}, bf16[2,768,512]{2,1,0:T(8,128)(2,1)S(1)}, bf16[768,3072]{1,0:T(8,128)(2,1)S(1)}, bf16[768,3072]{1,0:T(8,128)(2,1)}) custom-call(s32[3]{0:T(128)S(1)} %copy-done.12, f32[1,3072]{1,0:T(1,128)S(1)} %copy-done.9, f32[1,3072]{1,0:T(1,128)S(1)} %get-tuple-element.96.refs_2_, ...), custom_call_target="tpu_custom_call" | custom-call | flops 7247757 | bytes 25952 | tf_op jit(solution)/shard_map/norm_keys_values/pallas_call | solution.py:195
  251.9 7.9 %collective-permute-start.28 = (bf16[2,768,512]{2,1,0:T(8,128)(2,1)S(1)}, bf16[2,768,512]{2,1,0:T(8,128)(2,1)S(1)}, u32[]{:S(2)}, u32[]{:S(2)}) collective-permute-start(bf16[2,768,512]{2,1,0:T(8,128)(2,1)S(1)} %get-tuple-element.87.second_ref), channel_id=1, source_target_pairs={{0,4},{1,5},{2,6},{3,7},{4,8},{5,9},{6,10},{7,11},{8,12},{9,13},{1... | collective-permute-start | bytes 4718600 | tf_op jit(solution)/shard_map/ppermute | solution.py:496
  259.8 2.1 collective-permute-start.27
  261.9 18.2 %queries_own_frame.3 = (bf16[768,768]{1,0:T(8,128)(2,1)S(1)}, f32[768,768]{1,0:T(8,128)S(1)}, f32[768,768]{1,0:T(8,128)S(1)}, f32[768,768]{1,0:T(8,128)S(1)}) custom-call(f32[2,128]{1,0:T(2,128)S(1)} %pad_maximum_fusion.2.refs_3_.gain_ref, bf16[768,3072]{1,0:T(8,128)(2,1)S(1)} %get-tuple-element.85.normed_ref, ...), custom_call_target="tpu_custom_call" | custom-call | flops 7247757 | bytes 20054 | tf_op jit(solution)/shard_map/queries_own_frame/pallas_call | solution.py:307
  280.2 4.9 %earlier_frame.7.refs_2_ = bf16[768,512]{1,0:T(8,128)(2,1)S(1)} custom-call(s32[3]{0:T(128)S(1)} %copy-done.12, bf16[768,768]{1,0:T(8,128)(2,1)S(1)} %get-tuple-element.88.query_ref, f32[768,768]{1,0:T(8,128)S(1)} %get-tuple-element.89.acc_ref, f32[768,768]{1,0:T(8,128)S(1)} %get-tuple-element.90.top_ref, f32[768,768]{1,0:T(8,128)S(1)} %get-tuple-element.91.total_ref, ...), custom_call_target="tpu_custom_call" | custom-call | flops 2415919 | bytes 7864 | tf_op jit(solution)/shard_map/earlier_frame/pallas_call | solution.py:358
  287.2 2.8 earlier_frame.6.refs_1_
  291.2 13.7 %collective-permute-done.30.refs_4_ = bf16[768,512]{1,0:T(8,128)(2,1)S(1)} collective-permute-done((bf16[768,512]{1,0:T(8,128)(2,1)S(1)}, bf16[768,512]{1,0:T(8,128)(2,1)S(1)}, u32[]{:S(2)}, u32[]{:S(2)}) %collective-permute-start.30) | collective-permute-done | bytes 786464 | tf_op jit(solution)/shard_map/ppermute | solution.py:496
  307.0 6.4 %collective-permute-done.29.refs_3_ = bf16[768,256]{1,0:T(8,128)(2,1)S(1)} collective-permute-done((bf16[768,256]{1,0:T(8,128)(2,1)S(1)}, bf16[768,256]{1,0:T(8,128)(2,1)S(1)}, u32[]{:S(2)}, u32[]{:S(2)}) %collective-permute-start.29) | collective-permute-done | bytes 393248 | tf_op jit(solution)/shard_map/ppermute | solution.py:496
  315.4 15.9 %projection_start.3.refs_1_ = bf16[768,3072]{1,0:T(8,128)(2,1)S(1)} custom-call(s32[1]{0:T(128)} %bitcast.refs_0_, bf16[768,256]{1,0:T(8,128)(2,1)S(1)} %earlier_frame.6.refs_1_, bf16[768,512]{1,0:T(8,128)(2,1)S(1)} %earlier_frame.7.refs_2_, bf16[768,256]{1,0:T(8,128)(2,1)S(1)} %collective-permute-done.29.refs_3_, ...), custom_call_target="tpu_custom_call" | custom-call | flops 10871635 | bytes 18874 | tf_op jit(solution)/shard_map/projection_start/pallas_call | solution.py:459
  331.4 8.4 %projection_end.3 = bf16[768,3072]{1,0:T(8,128)(2,1)} custom-call(s32[1]{0:T(128)} %bitcast.refs_0_, bf16[768,3072]{1,0:T(8,128)(2,1)S(1)} %projection_start.3.refs_1_, bf16[768,3072]{1,0:T(8,128)(2,1)S(1)} %bitcast.21, f32[1,3072]{1,0:T(1,128)S(1)} %copy-done.10, bf16[384,256]{1,0:T(8,128)(2,1)S(1)} %collective-permute-done.33.refs_4_, ...), custom_call_target="tpu_custom_call" | custom-call | flops 3623878 | bytes 18874 | tf_op jit(solution)/shard_map/projection_end/pallas_call | solution.py:459
  (123 shorter events, 55.9 us)
Async XLA Ops:
  0.0 56.0 %collective-permute-start = (bf16[768,3072]{1,0:T(8,128)(2,1)}, bf16[768,3072]{1,0:T(8,128)(2,1)}, u32[]{:S(2)}, u32[]{:S(2)}) collective-permute-start(bf16[768,3072]{1,0:T(8,128)(2,1)} %bitcast.23), channel_id=1, source_target_pairs={{0,4},{1,5},{2,6},{3,7},{4,8},{5,9},{6,10},{7,11},{8,12},{9,13},{1... | collective-permute-start | bytes 14155784 | tf_op jit(solution)/shard_map/ppermute | solution.py:496
  7.1 13.1 %collective-permute-start.3 = (bf16[192,3072]{1,0:T(8,128)(2,1)S(1)}, bf16[192,3072]{1,0:T(8,128)(2,1)}, u32[]{:S(2)}, u32[]{:S(2)}) collective-permute-start(bf16[192,3072]{1,0:T(8,128)(2,1)S(1)} %get-tuple-element.94.refs_6_), channel_id=1, source_target_pairs={{0,3},{1,2},{2,1},{3,0}} | collective-permute-start | bytes 3538952 | tf_op jit(solution)/shard_map/ppermute | solution.py:496
  12.1 64.7 %collective-permute-start.4 = (bf16[768,1536]{1,0:T(8,128)(2,1)}, bf16[768,1536]{1,0:T(8,128)(2,1)}, u32[]{:S(2)}, u32[]{:S(2)}) collective-permute-start(bf16[768,1536]{1,0:T(8,128)(2,1)} %constant_dynamic-slice_fusion), channel_id=1, source_target_pairs={{0,1},{1,0},{2,3},{3,2},{4,5},{5,4},{6,7},{7,6},{8,9},{9,8},{10,11... | collective-permute-start | bytes 7077896 | tf_op jit(solution)/shard_map/ppermute | solution.py:496
  13.4 66.3 %collective-permute-start.5 = (bf16[768,1536]{1,0:T(8,128)(2,1)}, bf16[768,1536]{1,0:T(8,128)(2,1)}, u32[]{:S(2)}, u32[]{:S(2)}) collective-permute-start(bf16[768,1536]{1,0:T(8,128)(2,1)} %constant_dynamic-slice_fusion), channel_id=1, source_target_pairs={{0,2},{1,3},{2,0},{3,1},{4,6},{5,7},{6,4},{7,5},{8,10},{9,11},{10,... | collective-permute-start | bytes 7077896 | tf_op jit(solution)/shard_map/ppermute | solution.py:496
  72.5 50.8 %collective-permute-start.7 = (bf16[2,768,512]{2,1,0:T(8,128)(2,1)S(1)}, bf16[2,768,512]{2,1,0:T(8,128)(2,1)S(1)}, u32[]{:S(2)}, u32[]{:S(2)}) collective-permute-start(bf16[2,768,512]{2,1,0:T(8,128)(2,1)S(1)} %get-tuple-element.53.second_ref), channel_id=1, source_target_pairs={{0,4},{1,5},{2,6},{3,7},{4,8},{5,9},{6,10},{7,11},{8,12},{9,13},{1... | collective-permute-start | bytes 4718600 | tf_op jit(solution)/shard_map/ppermute | solution.py:496
  81.0 42.3 %collective-permute-start.8 = (bf16[384,1536]{1,0:T(8,128)(2,1)S(1)}, bf16[384,1536]{1,0:T(8,128)(2,1)S(1)}, u32[]{:S(2)}, u32[]{:S(2)}) collective-permute-start(bf16[384,1536]{1,0:T(8,128)(2,1)S(1)} %slice.54), channel_id=1, source_target_pairs={{0,2},{1,3},{2,0},{3,1},{4,6},{5,7},{6,4},{7,5},{8,10},{9,11},{10,... | collective-permute-start | bytes 3538952 | tf_op jit(solution)/shard_map/ppermute | solution.py:496
  83.1 40.2 %collective-permute-start.9 = (bf16[384,1536]{1,0:T(8,128)(2,1)S(1)}, bf16[384,1536]{1,0:T(8,128)(2,1)S(1)}, u32[]{:S(2)}, u32[]{:S(2)}) collective-permute-start(bf16[384,1536]{1,0:T(8,128)(2,1)S(1)} %slice.55), channel_id=1, source_target_pairs={{0,1},{1,0},{2,3},{3,2},{4,5},{5,4},{6,7},{7,6},{8,9},{9,8},{10,11... | collective-permute-start | bytes 3538952 | tf_op jit(solution)/shard_map/ppermute | solution.py:496
  84.0 39.3 %collective-permute-start.6 = (bf16[2,768,256]{2,1,0:T(8,128)(2,1)S(1)}, bf16[2,768,256]{2,1,0:T(8,128)(2,1)S(1)}, u32[]{:S(2)}, u32[]{:S(2)}) collective-permute-start(bf16[2,768,256]{2,1,0:T(8,128)(2,1)S(1)} %get-tuple-element.52.first_ref), channel_id=1, source_target_pairs={{0,4},{1,5},{2,6},{3,7},{4,8},{5,9},{6,10},{7,11},{8,12},{9,13},{1... | collective-permute-start | bytes 2359304 | tf_op jit(solution)/shard_map/ppermute | solution.py:496
  85.9 44.9 %collective-permute-start.10 = (s32[1]{0:T(128)}, s32[1]{0:T(128)}, u32[]{:S(2)}, u32[]{:S(2)}) collective-permute-start(s32[1]{0:T(128)} %param.10), channel_id=1, source_target_pairs={{0,4},{1,5},{2,6},{3,7},{4,8},{5,9},{6,10},{7,11},{8,12},{9,13},{1... | collective-permute-start | bytes 20 | tf_op jit(solution)/shard_map/ppermute | solution.py:496
  131.0 29.2 %collective-permute-start.15 = (bf16[768,1536]{1,0:T(8,128)(2,1)S(1)}, bf16[768,1536]{1,0:T(8,128)(2,1)S(1)}, u32[]{:S(2)}, u32[]{:S(2)}) collective-permute-start(bf16[768,1536]{1,0:T(8,128)(2,1)S(1)} %constant_dynamic-update-slice_fusion.refs_8_), channel_id=1, source_target_pairs={{0,4},{1,5},{2,6},{3,7},{4,0},{5,1},{6,2},{7,3},{8,12},{9,13},{10,... | collective-permute-start | bytes 7077896 | tf_op jit(solution)/shard_map/ppermute | solution.py:496
  144.6 15.6 %collective-permute-start.13 = (bf16[768,1536]{1,0:T(8,128)(2,1)}, bf16[768,1536]{1,0:T(8,128)(2,1)S(1)}, u32[]{:S(2)}, u32[]{:S(2)}) collective-permute-start(bf16[768,1536]{1,0:T(8,128)(2,1)} %collective-permute-done.4.refs_8_), channel_id=1, source_target_pairs={{0,4},{1,5},{2,6},{3,7},{4,0},{5,1},{6,2},{7,3},{8,12},{9,13},{10,... | collective-permute-start | bytes 7077896 | tf_op jit(solution)/shard_map/ppermute | solution.py:496
  144.7 15.5 %collective-permute-start.14 = (bf16[768,1536]{1,0:T(8,128)(2,1)}, bf16[768,1536]{1,0:T(8,128)(2,1)S(1)}, u32[]{:S(2)}, u32[]{:S(2)}) collective-permute-start(bf16[768,1536]{1,0:T(8,128)(2,1)} %collective-permute-done.5.refs_9_), channel_id=1, source_target_pairs={{0,4},{1,5},{2,6},{3,7},{4,0},{5,1},{6,2},{7,3},{8,12},{9,13},{10,... | collective-permute-start | bytes 7077896 | tf_op jit(solution)/shard_map/ppermute | solution.py:496
  145.2 15.0 %collective-permute-start.12 = (bf16[768,512]{1,0:T(8,128)(2,1)S(1)}, bf16[768,512]{1,0:T(8,128)(2,1)S(1)}, u32[]{:S(2)}, u32[]{:S(2)}) collective-permute-start(bf16[768,512]{1,0:T(8,128)(2,1)S(1)} %earlier_frame.5), channel_id=1, source_target_pairs={{0,4},{1,5},{2,6},{3,7},{4,8},{5,9},{6,10},{7,11},{8,12},{9,13},{1... | collective-permute-start | bytes 2359304 | tf_op jit(solution)/shard_map/ppermute | solution.py:496
  147.1 13.1 %collective-permute-start.11 = (bf16[768,256]{1,0:T(8,128)(2,1)S(1)}, bf16[768,256]{1,0:T(8,128)(2,1)S(1)}, u32[]{:S(2)}, u32[]{:S(2)}) collective-permute-start(bf16[768,256]{1,0:T(8,128)(2,1)S(1)} %earlier_frame.4), channel_id=1, source_target_pairs={{0,4},{1,5},{2,6},{3,7},{4,8},{5,9},{6,10},{7,11},{8,12},{9,13},{1... | collective-permute-start | bytes 1179656 | tf_op jit(solution)/shard_map/ppermute | solution.py:496
  160.2 22.0 %collective-permute-start.18 = (bf16[768,512]{1,0:T(8,128)(2,1)S(1)}, bf16[768,512]{1,0:T(8,128)(2,1)S(1)}, u32[]{:S(2)}, u32[]{:S(2)}) collective-permute-start(bf16[768,512]{1,0:T(8,128)(2,1)S(1)} %collective-permute-done.12.refs_2_), channel_id=1, source_target_pairs={{4,5},{5,4},{6,7},{7,6},{8,9},{9,8},{10,11},{11,10},{12,13},{13,12... | collective-permute-start | bytes 2359304 | tf_op jit(solution)/shard_map/ppermute | solution.py:496
  162.2 20.0 %collective-permute-start.19 = (bf16[768,512]{1,0:T(8,128)(2,1)S(1)}, bf16[768,512]{1,0:T(8,128)(2,1)S(1)}, u32[]{:S(2)}, u32[]{:S(2)}) collective-permute-start(bf16[768,512]{1,0:T(8,128)(2,1)S(1)} %collective-permute-done.12.refs_2_), channel_id=1, source_target_pairs={{4,6},{5,7},{6,4},{7,5},{8,10},{9,11},{10,8},{11,9},{12,14},{13,15... | collective-permute-start | bytes 2359304 | tf_op jit(solution)/shard_map/ppermute | solution.py:496
  165.1 60.5 %collective-permute-start.20 = (bf16[768,3072]{1,0:T(8,128)(2,1)}, bf16[768,3072]{1,0:T(8,128)(2,1)}, u32[]{:S(2)}, u32[]{:S(2)}) collective-permute-start(bf16[768,3072]{1,0:T(8,128)(2,1)} %get-tuple-element.81), channel_id=1, source_target_pairs={{0,4},{1,5},{2,6},{3,7},{4,8},{5,9},{6,10},{7,11},{8,12},{9,13},{1... | collective-permute-start | bytes 14155784 | tf_op jit(solution)/shard_map/ppermute | solution.py:496
  185.3 50.1 %collective-permute-start.26 = (bf16[384,3072]{1,0:T(8,128)(2,1)}, bf16[384,3072]{1,0:T(8,128)(2,1)}, u32[]{:S(2)}, u32[]{:S(2)}) collective-permute-start(bf16[384,3072]{1,0:T(8,128)(2,1)} %pad_maximum_fusion.1), channel_id=1, source_target_pairs={{0,2},{1,3},{2,0},{3,1}} | collective-permute-start | bytes 7077896 | tf_op jit(solution)/shard_map/ppermute | solution.py:496
  188.1 12.6 %collective-permute-start.21 = (bf16[384,256]{1,0:T(8,128)(2,1)}, bf16[384,256]{1,0:T(8,128)(2,1)}, u32[]{:S(2)}, u32[]{:S(2)}) collective-permute-start(bf16[384,256]{1,0:T(8,128)(2,1)} %slice.59), channel_id=1, source_target_pairs={{4,6},{5,7},{6,4},{7,5},{8,10},{9,11},{10,8},{11,9},{12,14},{13,15... | collective-permute-start | bytes 589832 | tf_op jit(solution)/shard_map/ppermute | solution.py:496
  192.3 33.2 %collective-permute-start.23 = (bf16[384,512]{1,0:T(8,128)(2,1)}, bf16[384,512]{1,0:T(8,128)(2,1)}, u32[]{:S(2)}, u32[]{:S(2)}) collective-permute-start(bf16[384,512]{1,0:T(8,128)(2,1)} %slice.61), channel_id=1, source_target_pairs={{4,6},{5,7},{6,4},{7,5},{8,10},{9,11},{10,8},{11,9},{12,14},{13,15... | collective-permute-start | bytes 1179656 | tf_op jit(solution)/shard_map/ppermute | solution.py:496
  195.0 30.5 %collective-permute-start.24 = (bf16[384,512]{1,0:T(8,128)(2,1)}, bf16[384,512]{1,0:T(8,128)(2,1)}, u32[]{:S(2)}, u32[]{:S(2)}) collective-permute-start(bf16[384,512]{1,0:T(8,128)(2,1)} %slice.62), channel_id=1, source_target_pairs={{4,5},{5,4},{6,7},{7,6},{8,9},{9,8},{10,11},{11,10},{12,13},{13,12... | collective-permute-start | bytes 1179656 | tf_op jit(solution)/shard_map/ppermute | solution.py:496
  200.7 24.7 %collective-permute-start.22 = (bf16[384,256]{1,0:T(8,128)(2,1)S(1)}, bf16[384,256]{1,0:T(8,128)(2,1)S(1)}, u32[]{:S(2)}, u32[]{:S(2)}) collective-permute-start(bf16[384,256]{1,0:T(8,128)(2,1)S(1)} %slice.60), channel_id=1, source_target_pairs={{4,5},{5,4},{6,7},{7,6},{8,9},{9,8},{10,11},{11,10},{12,13},{13,12... | collective-permute-start | bytes 589832 | tf_op jit(solution)/shard_map/ppermute | solution.py:496
  251.9 28.2 %collective-permute-start.28 = (bf16[2,768,512]{2,1,0:T(8,128)(2,1)S(1)}, bf16[2,768,512]{2,1,0:T(8,128)(2,1)S(1)}, u32[]{:S(2)}, u32[]{:S(2)}) collective-permute-start(bf16[2,768,512]{2,1,0:T(8,128)(2,1)S(1)} %get-tuple-element.87.second_ref), channel_id=1, source_target_pairs={{0,4},{1,5},{2,6},{3,7},{4,8},{5,9},{6,10},{7,11},{8,12},{9,13},{1... | collective-permute-start | bytes 4718600 | tf_op jit(solution)/shard_map/ppermute | solution.py:496
  259.8 27.4 %collective-permute-start.27 = (bf16[2,768,256]{2,1,0:T(8,128)(2,1)S(1)}, bf16[2,768,256]{2,1,0:T(8,128)(2,1)S(1)}, u32[]{:S(2)}, u32[]{:S(2)}) collective-permute-start(bf16[2,768,256]{2,1,0:T(8,128)(2,1)S(1)} %get-tuple-element.86.first_ref), channel_id=1, source_target_pairs={{0,4},{1,5},{2,6},{3,7},{4,8},{5,9},{6,10},{7,11},{8,12},{9,13},{1... | collective-permute-start | bytes 2359304 | tf_op jit(solution)/shard_map/ppermute | solution.py:496
  285.0 19.9 %collective-permute-start.30 = (bf16[768,512]{1,0:T(8,128)(2,1)S(1)}, bf16[768,512]{1,0:T(8,128)(2,1)S(1)}, u32[]{:S(2)}, u32[]{:S(2)}) collective-permute-start(bf16[768,512]{1,0:T(8,128)(2,1)S(1)} %earlier_frame.7.refs_2_), channel_id=1, source_target_pairs={{0,1},{1,0},{2,3},{3,2},{4,5},{5,4},{6,7},{7,6},{8,9},{9,8},{10,11... | collective-permute-start | bytes 2359304 | tf_op jit(solution)/shard_map/ppermute | solution.py:496
  286.8 19.6 %collective-permute-start.32 = (bf16[768,512]{1,0:T(8,128)(2,1)S(1)}, bf16[768,512]{1,0:T(8,128)(2,1)S(1)}, u32[]{:S(2)}, u32[]{:S(2)}) collective-permute-start(bf16[768,512]{1,0:T(8,128)(2,1)S(1)} %earlier_frame.7.refs_2_), channel_id=1, source_target_pairs={{0,2},{1,3},{2,0},{3,1},{4,6},{5,7},{6,4},{7,5},{8,10},{9,11},{10,... | collective-permute-start | bytes 2359304 | tf_op jit(solution)/shard_map/ppermute | solution.py:496
  290.0 23.4 %collective-permute-start.29 = (bf16[768,256]{1,0:T(8,128)(2,1)S(1)}, bf16[768,256]{1,0:T(8,128)(2,1)S(1)}, u32[]{:S(2)}, u32[]{:S(2)}) collective-permute-start(bf16[768,256]{1,0:T(8,128)(2,1)S(1)} %earlier_frame.6.refs_1_), channel_id=1, source_target_pairs={{0,1},{1,0},{2,3},{3,2},{4,5},{5,4},{6,7},{7,6},{8,9},{9,8},{10,11... | collective-permute-start | bytes 1179656 | tf_op jit(solution)/shard_map/ppermute | solution.py:496
  290.3 24.5 %collective-permute-start.31 = (bf16[768,256]{1,0:T(8,128)(2,1)S(1)}, bf16[768,256]{1,0:T(8,128)(2,1)S(1)}, u32[]{:S(2)}, u32[]{:S(2)}) collective-permute-start(bf16[768,256]{1,0:T(8,128)(2,1)S(1)} %earlier_frame.6.refs_1_), channel_id=1, source_target_pairs={{0,2},{1,3},{2,0},{3,1},{4,6},{5,7},{6,4},{7,5},{8,10},{9,11},{10,... | collective-permute-start | bytes 1179656 | tf_op jit(solution)/shard_map/ppermute | solution.py:496
  305.0 26.4 %collective-permute-start.35 = (bf16[384,512]{1,0:T(8,128)(2,1)S(1)}, bf16[384,512]{1,0:T(8,128)(2,1)S(1)}, u32[]{:S(2)}, u32[]{:S(2)}) collective-permute-start(bf16[384,512]{1,0:T(8,128)(2,1)S(1)} %slice.73), channel_id=1, source_target_pairs={{0,2},{1,3},{2,0},{3,1},{4,6},{5,7},{6,4},{7,5},{8,10},{9,11},{10,... | collective-permute-start | bytes 1179656 | tf_op jit(solution)/shard_map/ppermute | solution.py:496
  306.4 24.9 %collective-permute-start.36 = (bf16[384,512]{1,0:T(8,128)(2,1)S(1)}, bf16[384,512]{1,0:T(8,128)(2,1)S(1)}, u32[]{:S(2)}, u32[]{:S(2)}) collective-permute-start(bf16[384,512]{1,0:T(8,128)(2,1)S(1)} %slice.74), channel_id=1, source_target_pairs={{0,1},{1,0},{2,3},{3,2},{4,5},{5,4},{6,7},{7,6},{8,9},{9,8},{10,11... | collective-permute-start | bytes 1179656 | tf_op jit(solution)/shard_map/ppermute | solution.py:496
  313.4 17.9 %collective-permute-start.33 = (bf16[384,256]{1,0:T(8,128)(2,1)S(1)}, bf16[384,256]{1,0:T(8,128)(2,1)S(1)}, u32[]{:S(2)}, u32[]{:S(2)}) collective-permute-start(bf16[384,256]{1,0:T(8,128)(2,1)S(1)} %slice.71), channel_id=1, source_target_pairs={{0,2},{1,3},{2,0},{3,1},{4,6},{5,7},{6,4},{7,5},{8,10},{9,11},{10,... | collective-permute-start | bytes 589832 | tf_op jit(solution)/shard_map/ppermute | solution.py:496
  314.9 16.4 %collective-permute-start.34 = (bf16[384,256]{1,0:T(8,128)(2,1)S(1)}, bf16[384,256]{1,0:T(8,128)(2,1)S(1)}, u32[]{:S(2)}, u32[]{:S(2)}) collective-permute-start(bf16[384,256]{1,0:T(8,128)(2,1)S(1)} %slice.72), channel_id=1, source_target_pairs={{0,1},{1,0},{2,3},{3,2},{4,5},{5,4},{6,7},{7,6},{8,9},{9,8},{10,11... | collective-permute-start | bytes 589832 | tf_op jit(solution)/shard_map/ppermute | solution.py:496
  (27 other events, 402.8 us)

commit v14 on v11

--- a/solution.py
+++ b/solution.py
@@ -554,7 +554,6 @@
         return row[:, :width], 1.0 + row[:, width : 2 * width], rate * row[:, 2 * width :]
 
     shift, scale1, own_gate = modulation(levels[0])
-    arriving_gate = modulation(ring(levels, to_next)[0])[2]
     info = jnp.stack([queue_index == 0, tensor_index // 2, tensor_index % 2])
     info = info.astype(jnp.int32)
     gains = jnp.stack([q_gain * SCORE_SCALE, k_gain])
@@ -565,7 +564,8 @@
             info, scale1, shift, gains, qkv_weight, frame, noise, noise_pieces
         )
         if not final:
-            value, mine = lax.optimization_barrier((value, mine))
+            value, mine, sent_levels = lax.optimization_barrier((value, mine, levels))
+            arriving_level = ring(sent_levels, to_next)
         earlier = [ring(block, to_next) for block in (key, value)]
         query, *own = own_attention(gains, normed, qkv_weight, key, value)
         if not final:
@@ -577,15 +577,15 @@
         targets = range(queue_size) if final else range(1, queue_size)
         resid, gate = state, own_gate
         if not final:
-            attended, mine, mine_corners = lax.optimization_barrier(
-                (attended, mine, mine_corners)
+            attended, mine, mine_corners, arriving_level = lax.optimization_barrier(
+                (attended, mine, mine_corners, arriving_level)
             )
             mine_corners = [jnp.concatenate(parts, axis=0) for parts in mine_corners]
             theirs = [sibling(block) for block in mine]
             theirs_corners = [sibling(block) for block in mine_corners]
             attended = [ring(block, to_next) for block in attended]
             sent_state, attended = lax.optimization_barrier((state, attended))
-            resid, gate = ring(sent_state, to_next), arriving_gate
+            resid, gate = ring(sent_state, to_next), modulation(arriving_level[0])[2]
             attended, theirs, theirs_corners = lax.optimization_barrier(
                 (attended, theirs, theirs_corners)
             )

time: 327 us -> 330 us (level)
  the two profiles are of different devices: /device:TPU:8 before, /device:TPU:1 now
where the time goes in v14:
time: 330 us; the launch traced here: 329 us
  Pallas kernels  134 us (41%)
  waiting for transfers between devices  102 us (31%)
  starting transfers between devices  69 us (21%)
  local copies, waits for them, and re-layouts  13.6 us (4%)
  other arithmetic  7 us (2%)
  between operations  3.48 us (1%)
    ppermute x31, waiting for transfers between devices, send(): return lax.ppermute(block, AXES, pairs)  102 us
    ppermute x31, starting transfers between devices, send(): return lax.ppermute(block, AXES, pairs)  69 us
    pallas_call x4, Pallas kernels, output_projection(): pl.pallas_call(functools.partial(output_kernel, part_counts=tuple((len(p)...  50.5 us
    pallas_call x2, Pallas kernels, own_attention(): pl.pallas_call(own_kernel, grid=(head_cols // cols,), in_specs=[pl.BlockS...  36.4 us
    pallas_call x2, Pallas kernels, project_keys_values(): pl.pallas_call(functools.partial(key_value_kernel, half=half), grid_spec=...  33 us
    pallas_call x2, Pallas kernels, earlier_attention(): pl.pallas_call(functools.partial(earlier_kernel, chunks=chunks), grid_spe...  13.9 us
  transfers between devices with their start and end apart: 31, of which 10 were waited for; matrix products, arithmetic and copies ran while one was open for 5% of the time, Pallas kernels for 31%

profile of v14, /device:TPU:1, one launch (start us, length us, event | category | flops | bytes accessed | tf_op | source)
XLA Modules:
  0.0 329.1 jit_solution(10140882818340464792)
XLA Ops:
  0.0 4.6 %collective-permute-start = (bf16[768,3072]{1,0:T(8,128)(2,1)}, bf16[768,3072]{1,0:T(8,128)(2,1)}, u32[]{:S(2)}, u32[]{:S(2)}) collective-permute-start(bf16[768,3072]{1,0:T(8,128)(2,1)} %bitcast.23), channel_id=1, source_target_pairs={{0,4},{1,5},{2,6},{3,7},{4,8},{5,9},{6,10},{7,11},{8,12},{9,13},{1... | collective-permute-start | bytes 14155784 | tf_op jit(solution)/shard_map/ppermute | solution.py:491
  8.7 2.2 collective-permute-start.2
  18.6 37.4 %collective-permute-done.refs_5_ = bf16[768,3072]{1,0:T(8,128)(2,1)} collective-permute-done((bf16[768,3072]{1,0:T(8,128)(2,1)}, bf16[768,3072]{1,0:T(8,128)(2,1)}, u32[]{:S(2)}, u32[]{:S(2)}) %collective-permute-start) | collective-permute-done | bytes 4718624 | tf_op jit(solution)/shard_map/ppermute | solution.py:491
  56.0 16.5 %norm_keys_values.2 = (bf16[768,768]{1,0:T(8,128)(2,1)S(1)}, bf16[768,768]{1,0:T(8,128)(2,1)S(1)}, bf16[768,3072]{1,0:T(8,128)(2,1)S(1)}, bf16[768,3072]{1,0:T(8,128)(2,1)}) custom-call(s32[3]{0:T(128)S(1)} %pad_add_fusion.refs_0_, f32[1,3072]{1,0:T(1,128)S(1)} %get-tuple-element.91.refs_1_, f32[1,3072]{1,0:T(1,128)S(1)} %get-tuple-element.90.refs_2_, ...), custom_call_target="tpu_custom_call" | custom-call | flops 7247757 | bytes 25952 | tf_op jit(solution)/shard_map/norm_keys_values/pallas_call | solution.py:176
  77.8 4.9 %collective-permute-start.6 = (bf16[768,768]{1,0:T(8,128)(2,1)S(1)}, bf16[768,768]{1,0:T(8,128)(2,1)S(1)}, u32[]{:S(2)}, u32[]{:S(2)}) collective-permute-start(bf16[768,768]{1,0:T(8,128)(2,1)S(1)} %get-tuple-element.50.value_ref), channel_id=1, source_target_pairs={{0,4},{1,5},{2,6},{3,7},{4,8},{5,9},{6,10},{7,11},{8,12},{9,13},{1... | collective-permute-start | bytes 3538952 | tf_op jit(solution)/shard_map/ppermute | solution.py:491
  82.7 1.9 collective-permute-start.5
  84.7 3.6 %collective-permute-start.9 = (s32[1]{0:T(128)}, s32[1]{0:T(128)}, u32[]{:S(2)}, u32[]{:S(2)}) collective-permute-start(s32[1]{0:T(128)} %param.10), channel_id=1, source_target_pairs={{0,4},{1,5},{2,6},{3,7},{4,8},{5,9},{6,10},{7,11},{8,12},{9,13},{1... | collective-permute-start | bytes 20 | tf_op jit(solution)/shard_map/ppermute | solution.py:491
  88.3 18.2 %queries_own_frame.2 = (bf16[768,768]{1,0:T(8,128)(2,1)S(1)}, f32[768,768]{1,0:T(8,128)S(1)}, f32[768,768]{1,0:T(8,128)S(1)}, f32[768,768]{1,0:T(8,128)S(1)}) custom-call(f32[2,128]{1,0:T(2,128)S(1)} %pad_maximum_fusion.2.refs_3_.gain_ref, bf16[768,3072]{1,0:T(8,128)(2,1)S(1)} %get-tuple-element.47.normed_ref, ...), custom_call_target="tpu_custom_call" | custom-call | flops 7247757 | bytes 20054 | tf_op jit(solution)/shard_map/queries_own_frame/pallas_call | solution.py:286
  106.5 8.3 %collective-permute-done.6.refs_6_ = bf16[768,768]{1,0:T(8,128)(2,1)S(1)} collective-permute-done((bf16[768,768]{1,0:T(8,128)(2,1)S(1)}, bf16[768,768]{1,0:T(8,128)(2,1)S(1)}, u32[]{:S(2)}, u32[]{:S(2)}) %collective-permute-start.6) | collective-permute-done | bytes 1179680 | tf_op jit(solution)/shard_map/ppermute | solution.py:491
  116.5 6.9 %earlier_frame.2 = bf16[768,768]{1,0:T(8,128)(2,1)S(1)} custom-call(s32[3]{0:T(128)S(1)} %pad_add_fusion.refs_0_, bf16[768,768]{1,0:T(8,128)(2,1)S(1)} %get-tuple-element.51.refs_1_, f32[768,768]{1,0:T(8,128)S(1)} %get-tuple-element.52.refs_2_, f32[768,768]{1,0:T(8,128)S(1)} %get-tuple-element.53.refs_3_, f32[768,768]{1,0:T(8,128)S(1)} %get-tuple-element.54.refs_4_, ...), custom_call_target="tpu_custom_call" | custom-call | flops 3623878 | bytes 12976 | tf_op jit(solution)/shard_map/earlier_frame/pallas_call | solution.py:347
  123.7 12.5 %collective-permute-start.13 = (bf16[768,1536]{1,0:T(8,128)(2,1)S(1)}, bf16[768,1536]{1,0:T(8,128)(2,1)S(1)}, u32[]{:S(2)}, u32[]{:S(2)}) collective-permute-start(bf16[768,1536]{1,0:T(8,128)(2,1)S(1)} %constant_dynamic-update-slice_fusion.refs_6_.refs_8_), channel_id=1, source_target_pairs={{0,4},{1,5},{2,6},{3,7},{4,0},{5,1},{6,2},{7,3},{8,12},{9,13},{10,... | collective-permute-start | bytes 7077896 | tf_op jit(solution)/shard_map/ppermute | solution.py:491
  138.6 13.1 %collective-permute-done.10.refs_1_ = bf16[768,768]{1,0:T(8,128)(2,1)S(1)} collective-permute-done((bf16[768,768]{1,0:T(8,128)(2,1)S(1)}, bf16[768,768]{1,0:T(8,128)(2,1)S(1)}, u32[]{:S(2)}, u32[]{:S(2)}) %collective-permute-start.10) | collective-permute-done | bytes 1179680 | tf_op jit(solution)/shard_map/ppermute | solution.py:491
  151.7 2.4 collective-permute-start.14
  154.1 2.1 collective-permute-start.15
  157.4 4.9 %collective-permute-start.16 = (bf16[768,3072]{1,0:T(8,128)(2,1)}, bf16[768,3072]{1,0:T(8,128)(2,1)}, u32[]{:S(2)}, u32[]{:S(2)}) collective-permute-start(bf16[768,3072]{1,0:T(8,128)(2,1)} %get-tuple-element.73), channel_id=1, source_target_pairs={{0,4},{1,5},{2,6},{3,7},{4,8},{5,9},{6,10},{7,11},{8,12},{9,13},{1... | collective-permute-start | bytes 14155784 | tf_op jit(solution)/shard_map/ppermute | solution.py:491
  162.3 8.5 %collective-permute-done.14.refs_2_ = bf16[768,768]{1,0:T(8,128)(2,1)S(1)} collective-permute-done((bf16[768,768]{1,0:T(8,128)(2,1)S(1)}, bf16[768,768]{1,0:T(8,128)(2,1)S(1)}, u32[]{:S(2)}, u32[]{:S(2)}) %collective-permute-start.14) | collective-permute-done | bytes 1179680 | tf_op jit(solution)/shard_map/ppermute | solution.py:491
  173.9 2.1 collective-permute-start.20
  176.9 2.1 collective-permute-start.17
  179.9 2.9 collective-permute-start.18
  190.3 16.0 %projection_start.2.refs_1_ = bf16[768,3072]{1,0:T(8,128)(2,1)S(1)} custom-call(s32[1]{0:T(128)} %bitcast.refs_0_, bf16[768,768]{1,0:T(8,128)(2,1)S(1)} %copy-done.3, bf16[768,768]{1,0:T(8,128)(2,1)S(1)} %collective-permute-done.14.refs_2_, bf16[768,768]{1,0:T(8,128)(2,1)S(1)} %copy-done.1, bf16[768,3072]{1,0:T(8,128)(2,1)} %refs_7_.1, ...), custom_call_target="tpu_custom_call" | custom-call | flops 10871635 | bytes 18874 | tf_op jit(solution)/shard_map/projection_start/pallas_call | solution.py:454
  206.3 7.4 %collective-permute-done.16.refs_2_ = bf16[768,3072]{1,0:T(8,128)(2,1)} collective-permute-done((bf16[768,3072]{1,0:T(8,128)(2,1)}, bf16[768,3072]{1,0:T(8,128)(2,1)}, u32[]{:S(2)}, u32[]{:S(2)}) %collective-permute-start.16) | collective-permute-done | bytes 4718624 | tf_op jit(solution)/shard_map/ppermute | solution.py:491
  213.7 9.9 %projection_end.2.refs_5_ = bf16[768,3072]{1,0:T(8,128)(2,1)} custom-call(s32[1]{0:T(128)} %bitcast.refs_0_, bf16[768,3072]{1,0:T(8,128)(2,1)S(1)} %projection_start.2.refs_1_, bf16[768,3072]{1,0:T(8,128)(2,1)} %collective-permute-done.16.refs_2_, f32[1,3072]{1,0:T(1,128)S(1)} %fusion.refs_3_, bf16[384,768]{1,0:T(8,128)(2,1)} %collective-permute-done.17.refs_4_, ...), custom_call_target="tpu_custom_call" | custom-call | flops 3623878 | bytes 18874 | tf_op jit(solution)/shard_map/projection_end/pallas_call | solution.py:454
  223.6 16.5 %norm_keys_values.3 = (bf16[768,768]{1,0:T(8,128)(2,1)S(1)}, bf16[768,768]{1,0:T(8,128)(2,1)S(1)}, bf16[768,3072]{1,0:T(8,128)(2,1)S(1)}, bf16[768,3072]{1,0:T(8,128)(2,1)}) custom-call(s32[3]{0:T(128)S(1)} %copy-done.8, f32[1,3072]{1,0:T(1,128)S(1)} %copy-done.5, f32[1,3072]{1,0:T(1,128)S(1)} %get-tuple-element.90.refs_2_, ...), custom_call_target="tpu_custom_call" | custom-call | flops 7247757 | bytes 25952 | tf_op jit(solution)/shard_map/norm_keys_values/pallas_call | solution.py:176
  240.2 5.1 %collective-permute-start.21 = (bf16[768,768]{1,0:T(8,128)(2,1)S(1)}, bf16[768,768]{1,0:T(8,128)(2,1)S(1)}, u32[]{:S(2)}, u32[]{:S(2)}) collective-permute-start(bf16[768,768]{1,0:T(8,128)(2,1)S(1)} %get-tuple-element.78.key_ref), channel_id=1, source_target_pairs={{0,4},{1,5},{2,6},{3,7},{4,8},{5,9},{6,10},{7,11},{8,12},{9,13},{1... | collective-permute-start | bytes 3538952 | tf_op jit(solution)/shard_map/ppermute | solution.py:491
  245.2 1.9 collective-permute-start.22
  247.2 18.2 %queries_own_frame.3 = (bf16[768,768]{1,0:T(8,128)(2,1)S(1)}, f32[768,768]{1,0:T(8,128)S(1)}, f32[768,768]{1,0:T(8,128)S(1)}, f32[768,768]{1,0:T(8,128)S(1)}) custom-call(f32[2,128]{1,0:T(2,128)S(1)} %pad_maximum_fusion.2.refs_3_.gain_ref, bf16[768,3072]{1,0:T(8,128)(2,1)S(1)} %get-tuple-element.77.normed_ref, ...), custom_call_target="tpu_custom_call" | custom-call | flops 7247757 | bytes 20054 | tf_op jit(solution)/shard_map/queries_own_frame/pallas_call | solution.py:286
  265.4 5.6 %collective-permute-done.22.refs_6_ = bf16[768,768]{1,0:T(8,128)(2,1)S(1)} collective-permute-done((bf16[768,768]{1,0:T(8,128)(2,1)S(1)}, bf16[768,768]{1,0:T(8,128)(2,1)S(1)}, u32[]{:S(2)}, u32[]{:S(2)}) %collective-permute-start.22) | collective-permute-done | bytes 1179680 | tf_op jit(solution)/shard_map/ppermute | solution.py:491
  271.0 6.9 %earlier_frame.3 = (bf16[384,768]{1,0:T(8,128)(2,1)S(1)}, bf16[384,768]{1,0:T(8,128)(2,1)S(1)}) custom-call(s32[3]{0:T(128)S(1)} %copy-done.8, bf16[768,768]{1,0:T(8,128)(2,1)S(1)} %get-tuple-element.80.refs_1_, f32[768,768]{1,0:T(8,128)S(1)} %get-tuple-element.81.refs_2_, f32[768,768]{1,0:T(8,128)S(1)} %get-tuple-element.82.refs_3_, ...), custom_call_target="tpu_custom_call" | custom-call | flops 3623878 | bytes 12976 | tf_op jit(solution)/shard_map/earlier_frame/pallas_call | solution.py:347
  280.9 12.5 %collective-permute-done.23.refs_3_ = bf16[384,768]{1,0:T(8,128)(2,1)S(1)} collective-permute-done((bf16[384,768]{1,0:T(8,128)(2,1)S(1)}, bf16[384,768]{1,0:T(8,128)(2,1)S(1)}, u32[]{:S(2)}, u32[]{:S(2)}) %collective-permute-start.23) | collective-permute-done | bytes 589856 | tf_op jit(solution)/shard_map/ppermute | solution.py:491
  295.3 7.0 %collective-permute-done.24.refs_4_ = bf16[384,768]{1,0:T(8,128)(2,1)S(1)} collective-permute-done((bf16[384,768]{1,0:T(8,128)(2,1)S(1)}, bf16[384,768]{1,0:T(8,128)(2,1)S(1)}, u32[]{:S(2)}, u32[]{:S(2)}) %collective-permute-start.24) | collective-permute-done | bytes 589856 | tf_op jit(solution)/shard_map/ppermute | solution.py:491
  304.2 16.1 %projection_start.3.refs_1_ = bf16[768,3072]{1,0:T(8,128)(2,1)S(1)} custom-call(s32[1]{0:T(128)} %bitcast.refs_0_, bf16[384,768]{1,0:T(8,128)(2,1)S(1)} %get-tuple-element.84.refs_1_, bf16[384,768]{1,0:T(8,128)(2,1)S(1)} %get-tuple-element.85.refs_2_, bf16[384,768]{1,0:T(8,128)(2,1)S(1)} %collective-permute-done.23.refs_3_, ...), custom_call_target="tpu_custom_call" | custom-call | flops 10871635 | bytes 18874 | tf_op jit(solution)/shard_map/projection_start/pallas_call | solution.py:454
  320.4 8.6 %projection_end.3 = bf16[768,3072]{1,0:T(8,128)(2,1)} custom-call(s32[1]{0:T(128)} %bitcast.refs_0_, bf16[768,3072]{1,0:T(8,128)(2,1)S(1)} %projection_start.3.refs_1_, bf16[768,3072]{1,0:T(8,128)(2,1)S(1)} %bitcast.21, f32[1,3072]{1,0:T(1,128)S(1)} %copy-done.6, bf16[192,768]{1,0:T(8,128)(2,1)S(1)} %collective-permute-done.27.refs_4_, ...), custom_call_target="tpu_custom_call" | custom-call | flops 3623878 | bytes 18874 | tf_op jit(solution)/shard_map/projection_end/pallas_call | solution.py:454
  (101 shorter events, 38.7 us)
Async XLA Ops:
  0.0 56.0 %collective-permute-start = (bf16[768,3072]{1,0:T(8,128)(2,1)}, bf16[768,3072]{1,0:T(8,128)(2,1)}, u32[]{:S(2)}, u32[]{:S(2)}) collective-permute-start(bf16[768,3072]{1,0:T(8,128)(2,1)} %bitcast.23), channel_id=1, source_target_pairs={{0,4},{1,5},{2,6},{3,7},{4,8},{5,9},{6,10},{7,11},{8,12},{9,13},{1... | collective-permute-start | bytes 14155784 | tf_op jit(solution)/shard_map/ppermute | solution.py:491
  6.4 0.8 collective-permute-start.1
  8.7 9.8 %collective-permute-start.2 = (bf16[384,3072]{1,0:T(8,128)(2,1)}, bf16[384,3072]{1,0:T(8,128)(2,1)}, u32[]{:S(2)}, u32[]{:S(2)}) collective-permute-start(bf16[384,3072]{1,0:T(8,128)(2,1)} %pad_maximum_fusion), channel_id=1, source_target_pairs={{0,2},{1,3},{2,0},{3,1}} | collective-permute-start | bytes 7077896 | tf_op jit(solution)/shard_map/ppermute | solution.py:491
  12.5 60.0 %collective-permute-start.3 = (bf16[768,1536]{1,0:T(8,128)(2,1)}, bf16[768,1536]{1,0:T(8,128)(2,1)}, u32[]{:S(2)}, u32[]{:S(2)}) collective-permute-start(bf16[768,1536]{1,0:T(8,128)(2,1)} %constant_dynamic-slice_fusion), channel_id=1, source_target_pairs={{0,1},{1,0},{2,3},{3,2},{4,5},{5,4},{6,7},{7,6},{8,9},{9,8},{10,11... | collective-permute-start | bytes 7077896 | tf_op jit(solution)/shard_map/ppermute | solution.py:491
  13.7 58.8 %collective-permute-start.4 = (bf16[768,1536]{1,0:T(8,128)(2,1)}, bf16[768,1536]{1,0:T(8,128)(2,1)}, u32[]{:S(2)}, u32[]{:S(2)}) collective-permute-start(bf16[768,1536]{1,0:T(8,128)(2,1)} %constant_dynamic-slice_fusion), channel_id=1, source_target_pairs={{0,2},{1,3},{2,0},{3,1},{4,6},{5,7},{6,4},{7,5},{8,10},{9,11},{10,... | collective-permute-start | bytes 7077896 | tf_op jit(solution)/shard_map/ppermute | solution.py:491
  16.3 100.2 %copy-start.7 = (s32[3]{0:T(128)}, s32[3]{0:T(128)S(1)}, u32[]{:S(2)}) copy-start(s32[3]{0:T(128)S(1)} %pad_add_fusion.refs_0_) | copy-start | bytes 40
  73.9 32.6 %collective-permute-start.7 = (bf16[384,1536]{1,0:T(8,128)(2,1)S(1)}, bf16[384,1536]{1,0:T(8,128)(2,1)S(1)}, u32[]{:S(2)}, u32[]{:S(2)}) collective-permute-start(bf16[384,1536]{1,0:T(8,128)(2,1)S(1)} %slice.48), channel_id=1, source_target_pairs={{0,2},{1,3},{2,0},{3,1},{4,6},{5,7},{6,4},{7,5},{8,10},{9,11},{10,... | collective-permute-start | bytes 3538952 | tf_op jit(solution)/shard_map/ppermute | solution.py:491
  76.5 30.0 %collective-permute-start.8 = (bf16[384,1536]{1,0:T(8,128)(2,1)S(1)}, bf16[384,1536]{1,0:T(8,128)(2,1)S(1)}, u32[]{:S(2)}, u32[]{:S(2)}) collective-permute-start(bf16[384,1536]{1,0:T(8,128)(2,1)S(1)} %slice.49), channel_id=1, source_target_pairs={{0,1},{1,0},{2,3},{3,2},{4,5},{5,4},{6,7},{7,6},{8,9},{9,8},{10,11... | collective-permute-start | bytes 3538952 | tf_op jit(solution)/shard_map/ppermute | solution.py:491
  77.8 37.0 %collective-permute-start.6 = (bf16[768,768]{1,0:T(8,128)(2,1)S(1)}, bf16[768,768]{1,0:T(8,128)(2,1)S(1)}, u32[]{:S(2)}, u32[]{:S(2)}) collective-permute-start(bf16[768,768]{1,0:T(8,128)(2,1)S(1)} %get-tuple-element.50.value_ref), channel_id=1, source_target_pairs={{0,4},{1,5},{2,6},{3,7},{4,8},{5,9},{6,10},{7,11},{8,12},{9,13},{1... | collective-permute-start | bytes 3538952 | tf_op jit(solution)/shard_map/ppermute | solution.py:491
  82.7 33.8 %collective-permute-start.5 = (bf16[768,768]{1,0:T(8,128)(2,1)S(1)}, bf16[768,768]{1,0:T(8,128)(2,1)S(1)}, u32[]{:S(2)}, u32[]{:S(2)}) collective-permute-start(bf16[768,768]{1,0:T(8,128)(2,1)S(1)} %get-tuple-element.48.key_ref), channel_id=1, source_target_pairs={{0,4},{1,5},{2,6},{3,7},{4,8},{5,9},{6,10},{7,11},{8,12},{9,13},{1... | collective-permute-start | bytes 3538952 | tf_op jit(solution)/shard_map/ppermute | solution.py:491
  84.7 38.8 %collective-permute-start.9 = (s32[1]{0:T(128)}, s32[1]{0:T(128)}, u32[]{:S(2)}, u32[]{:S(2)}) collective-permute-start(s32[1]{0:T(128)} %param.10), channel_id=1, source_target_pairs={{0,4},{1,5},{2,6},{3,7},{4,8},{5,9},{6,10},{7,11},{8,12},{9,13},{1... | collective-permute-start | bytes 20 | tf_op jit(solution)/shard_map/ppermute | solution.py:491
  123.7 28.1 %collective-permute-start.13 = (bf16[768,1536]{1,0:T(8,128)(2,1)S(1)}, bf16[768,1536]{1,0:T(8,128)(2,1)S(1)}, u32[]{:S(2)}, u32[]{:S(2)}) collective-permute-start(bf16[768,1536]{1,0:T(8,128)(2,1)S(1)} %constant_dynamic-update-slice_fusion.refs_6_.refs_8_), channel_id=1, source_target_pairs={{0,4},{1,5},{2,6},{3,7},{4,0},{5,1},{6,2},{7,3},{8,12},{9,13},{10,... | collective-permute-start | bytes 7077896 | tf_op jit(solution)/shard_map/ppermute | solution.py:491
  136.2 15.6 %collective-permute-start.11 = (bf16[768,1536]{1,0:T(8,128)(2,1)}, bf16[768,1536]{1,0:T(8,128)(2,1)S(1)}, u32[]{:S(2)}, u32[]{:S(2)}) collective-permute-start(bf16[768,1536]{1,0:T(8,128)(2,1)} %collective-permute-done.3.refs_5_.refs_8_), channel_id=1, source_target_pairs={{0,4},{1,5},{2,6},{3,7},{4,0},{5,1},{6,2},{7,3},{8,12},{9,13},{10,... | collective-permute-start | bytes 7077896 | tf_op jit(solution)/shard_map/ppermute | solution.py:491
  136.2 15.5 %collective-permute-start.12 = (bf16[768,1536]{1,0:T(8,128)(2,1)}, bf16[768,1536]{1,0:T(8,128)(2,1)S(1)}, u32[]{:S(2)}, u32[]{:S(2)}) collective-permute-start(bf16[768,1536]{1,0:T(8,128)(2,1)} %collective-permute-done.4.refs_6_.refs_9_), channel_id=1, source_target_pairs={{0,4},{1,5},{2,6},{3,7},{4,0},{5,1},{6,2},{7,3},{8,12},{9,13},{10,... | collective-permute-start | bytes 7077896 | tf_op jit(solution)/shard_map/ppermute | solution.py:491
  136.7 15.0 %collective-permute-start.10 = (bf16[768,768]{1,0:T(8,128)(2,1)S(1)}, bf16[768,768]{1,0:T(8,128)(2,1)S(1)}, u32[]{:S(2)}, u32[]{:S(2)}) collective-permute-start(bf16[768,768]{1,0:T(8,128)(2,1)S(1)} %earlier_frame.2), channel_id=1, source_target_pairs={{0,4},{1,5},{2,6},{3,7},{4,8},{5,9},{6,10},{7,11},{8,12},{9,13},{1... | collective-permute-start | bytes 3538952 | tf_op jit(solution)/shard_map/ppermute | solution.py:491
  151.7 19.1 %collective-permute-start.14 = (bf16[768,768]{1,0:T(8,128)(2,1)S(1)}, bf16[768,768]{1,0:T(8,128)(2,1)S(1)}, u32[]{:S(2)}, u32[]{:S(2)}) collective-permute-start(bf16[768,768]{1,0:T(8,128)(2,1)S(1)} %collective-permute-done.10.refs_1_), channel_id=1, source_target_pairs={{4,5},{5,4},{6,7},{7,6},{8,9},{9,8},{10,11},{11,10},{12,13},{13,12... | collective-permute-start | bytes 3538952 | tf_op jit(solution)/shard_map/ppermute | solution.py:491
  154.1 17.2 %collective-permute-start.15 = (bf16[768,768]{1,0:T(8,128)(2,1)S(1)}, bf16[768,768]{1,0:T(8,128)(2,1)S(1)}, u32[]{:S(2)}, u32[]{:S(2)}) collective-permute-start(bf16[768,768]{1,0:T(8,128)(2,1)S(1)} %collective-permute-done.10.refs_1_), channel_id=1, source_target_pairs={{4,6},{5,7},{6,4},{7,5},{8,10},{9,11},{10,8},{11,9},{12,14},{13,15... | collective-permute-start | bytes 3538952 | tf_op jit(solution)/shard_map/ppermute | solution.py:491
  157.4 56.3 %collective-permute-start.16 = (bf16[768,3072]{1,0:T(8,128)(2,1)}, bf16[768,3072]{1,0:T(8,128)(2,1)}, u32[]{:S(2)}, u32[]{:S(2)}) collective-permute-start(bf16[768,3072]{1,0:T(8,128)(2,1)} %get-tuple-element.73), channel_id=1, source_target_pairs={{0,4},{1,5},{2,6},{3,7},{4,8},{5,9},{6,10},{7,11},{8,12},{9,13},{1... | collective-permute-start | bytes 14155784 | tf_op jit(solution)/shard_map/ppermute | solution.py:491
  171.4 0.9 collective-permute-start.19
  173.9 49.7 %collective-permute-start.20 = (bf16[384,3072]{1,0:T(8,128)(2,1)}, bf16[384,3072]{1,0:T(8,128)(2,1)}, u32[]{:S(2)}, u32[]{:S(2)}) collective-permute-start(bf16[384,3072]{1,0:T(8,128)(2,1)} %pad_maximum_fusion.1), channel_id=1, source_target_pairs={{0,2},{1,3},{2,0},{3,1}} | collective-permute-start | bytes 7077896 | tf_op jit(solution)/shard_map/ppermute | solution.py:491
  176.9 29.4 %collective-permute-start.17 = (bf16[384,768]{1,0:T(8,128)(2,1)}, bf16[384,768]{1,0:T(8,128)(2,1)}, u32[]{:S(2)}, u32[]{:S(2)}) collective-permute-start(bf16[384,768]{1,0:T(8,128)(2,1)} %slice.53), channel_id=1, source_target_pairs={{4,6},{5,7},{6,4},{7,5},{8,10},{9,11},{10,8},{11,9},{12,14},{13,15... | collective-permute-start | bytes 1769480 | tf_op jit(solution)/shard_map/ppermute | solution.py:491
  179.9 26.5 %collective-permute-start.18 = (bf16[384,768]{1,0:T(8,128)(2,1)}, bf16[384,768]{1,0:T(8,128)(2,1)}, u32[]{:S(2)}, u32[]{:S(2)}) collective-permute-start(bf16[384,768]{1,0:T(8,128)(2,1)} %slice.54), channel_id=1, source_target_pairs={{4,5},{5,4},{6,7},{7,6},{8,9},{9,8},{10,11},{11,10},{12,13},{13,12... | collective-permute-start | bytes 1769480 | tf_op jit(solution)/shard_map/ppermute | solution.py:491
  240.2 25.2 %collective-permute-start.21 = (bf16[768,768]{1,0:T(8,128)(2,1)S(1)}, bf16[768,768]{1,0:T(8,128)(2,1)S(1)}, u32[]{:S(2)}, u32[]{:S(2)}) collective-permute-start(bf16[768,768]{1,0:T(8,128)(2,1)S(1)} %get-tuple-element.78.key_ref), channel_id=1, source_target_pairs={{0,4},{1,5},{2,6},{3,7},{4,8},{5,9},{6,10},{7,11},{8,12},{9,13},{1... | collective-permute-start | bytes 3538952 | tf_op jit(solution)/shard_map/ppermute | solution.py:491
  245.2 25.8 %collective-permute-start.22 = (bf16[768,768]{1,0:T(8,128)(2,1)S(1)}, bf16[768,768]{1,0:T(8,128)(2,1)S(1)}, u32[]{:S(2)}, u32[]{:S(2)}) collective-permute-start(bf16[768,768]{1,0:T(8,128)(2,1)S(1)} %get-tuple-element.79.value_ref), channel_id=1, source_target_pairs={{0,4},{1,5},{2,6},{3,7},{4,8},{5,9},{6,10},{7,11},{8,12},{9,13},{1... | collective-permute-start | bytes 3538952 | tf_op jit(solution)/shard_map/ppermute | solution.py:491
  277.9 15.5 %collective-permute-start.23 = (bf16[384,768]{1,0:T(8,128)(2,1)S(1)}, bf16[384,768]{1,0:T(8,128)(2,1)S(1)}, u32[]{:S(2)}, u32[]{:S(2)}) collective-permute-start(bf16[384,768]{1,0:T(8,128)(2,1)S(1)} %get-tuple-element.84.refs_1_), channel_id=1, source_target_pairs={{0,1},{1,0},{2,3},{3,2},{4,5},{5,4},{6,7},{7,6},{8,9},{9,8},{10,11... | collective-permute-start | bytes 1769480 | tf_op jit(solution)/shard_map/ppermute | solution.py:491
  278.5 16.3 %collective-permute-start.25 = (bf16[384,768]{1,0:T(8,128)(2,1)S(1)}, bf16[384,768]{1,0:T(8,128)(2,1)S(1)}, u32[]{:S(2)}, u32[]{:S(2)}) collective-permute-start(bf16[384,768]{1,0:T(8,128)(2,1)S(1)} %get-tuple-element.84.refs_1_), channel_id=1, source_target_pairs={{0,2},{1,3},{2,0},{3,1},{4,6},{5,7},{6,4},{7,5},{8,10},{9,11},{10,... | collective-permute-start | bytes 1769480 | tf_op jit(solution)/shard_map/ppermute | solution.py:491
  279.7 22.6 %collective-permute-start.24 = (bf16[384,768]{1,0:T(8,128)(2,1)S(1)}, bf16[384,768]{1,0:T(8,128)(2,1)S(1)}, u32[]{:S(2)}, u32[]{:S(2)}) collective-permute-start(bf16[384,768]{1,0:T(8,128)(2,1)S(1)} %get-tuple-element.85.refs_2_), channel_id=1, source_target_pairs={{0,1},{1,0},{2,3},{3,2},{4,5},{5,4},{6,7},{7,6},{8,9},{9,8},{10,11... | collective-permute-start | bytes 1769480 | tf_op jit(solution)/shard_map/ppermute | solution.py:491
  280.7 22.9 %collective-permute-start.26 = (bf16[384,768]{1,0:T(8,128)(2,1)S(1)}, bf16[384,768]{1,0:T(8,128)(2,1)S(1)}, u32[]{:S(2)}, u32[]{:S(2)}) collective-permute-start(bf16[384,768]{1,0:T(8,128)(2,1)S(1)} %get-tuple-element.85.refs_2_), channel_id=1, source_target_pairs={{0,2},{1,3},{2,0},{3,1},{4,6},{5,7},{6,4},{7,5},{8,10},{9,11},{10,... | collective-permute-start | bytes 1769480 | tf_op jit(solution)/shard_map/ppermute | solution.py:491
  293.4 26.8 %collective-permute-start.27 = (bf16[192,768]{1,0:T(8,128)(2,1)S(1)}, bf16[192,768]{1,0:T(8,128)(2,1)S(1)}, u32[]{:S(2)}, u32[]{:S(2)}) collective-permute-start(bf16[192,768]{1,0:T(8,128)(2,1)S(1)} %slice.63), channel_id=1, source_target_pairs={{0,2},{1,3},{2,0},{3,1},{4,6},{5,7},{6,4},{7,5},{8,10},{9,11},{10,... | collective-permute-start | bytes 884744 | tf_op jit(solution)/shard_map/ppermute | solution.py:491
  294.8 25.5 %collective-permute-start.28 = (bf16[192,768]{1,0:T(8,128)(2,1)S(1)}, bf16[192,768]{1,0:T(8,128)(2,1)S(1)}, u32[]{:S(2)}, u32[]{:S(2)}) collective-permute-start(bf16[192,768]{1,0:T(8,128)(2,1)S(1)} %slice.64), channel_id=1, source_target_pairs={{0,1},{1,0},{2,3},{3,2},{4,5},{5,4},{6,7},{7,6},{8,9},{9,8},{10,11... | collective-permute-start | bytes 884744 | tf_op jit(solution)/shard_map/ppermute | solution.py:491
  302.3 18.0 %collective-permute-start.29 = (bf16[192,768]{1,0:T(8,128)(2,1)S(1)}, bf16[192,768]{1,0:T(8,128)(2,1)S(1)}, u32[]{:S(2)}, u32[]{:S(2)}) collective-permute-start(bf16[192,768]{1,0:T(8,128)(2,1)S(1)} %slice.65), channel_id=1, source_target_pairs={{0,2},{1,3},{2,0},{3,1},{4,6},{5,7},{6,4},{7,5},{8,10},{9,11},{10,... | collective-permute-start | bytes 884744 | tf_op jit(solution)/shard_map/ppermute | solution.py:491
  303.7 16.6 %collective-permute-start.30 = (bf16[192,768]{1,0:T(8,128)(2,1)S(1)}, bf16[192,768]{1,0:T(8,128)(2,1)S(1)}, u32[]{:S(2)}, u32[]{:S(2)}) collective-permute-start(bf16[192,768]{1,0:T(8,128)(2,1)S(1)} %slice.66), channel_id=1, source_target_pairs={{0,1},{1,0},{2,3},{3,2},{4,5},{5,4},{6,7},{7,6},{8,9},{9,8},{10,11... | collective-permute-start | bytes 884744 | tf_op jit(solution)/shard_map/ppermute | solution.py:491
  (18 other events, 285.3 us)
